TPU v7x, 32 devices: a whole 2x2x4 slice. The times are simulated.
32 devices in a mesh: ctx: 4 (over y, x), tp: 2 (over core), dp: 4 (over z).
Axes of the slice: x: 2, y: 2, z: 4, core: 2. Of those that a mesh axis runs over, the one named last changes fastest.
Arguments:
- queries: bfloat16 [2048, 8192], P(('dp', 'ctx'), 'tp'), parts along dimension 0
- key_rows: bfloat16 [2048, 1024], P(('dp', 'ctx'), 'tp'), parts along dimension 0
- value_rows: bfloat16 [2048, 1024], P(('dp', 'ctx'), 'tp'), parts along dimension 0, may hold values from -6 to 6
- doc_lengths: int32 [32], P('dp'), parts along dimension 0, may hold values from 1 to 256, 512 in all
- unit_source: int32 [64], P('dp'), parts along dimension 0, may hold values from 0 to 15, as said below
- w_out: bfloat16 [8192, 16384], P('tp', 'ctx'), may hold values from -0.0625 to 0.0625
Outputs:
- projected: bfloat16 [2048, 16384], P(('dp', 'tp'), 'ctx'), parts along dimension 0
There are 4 independent parts, one for each index of `dp`. A program takes and returns all parts, laid end to end along the dimension named above; an argument that names none is the same for every part. Nothing has to cross between parts.
Inputs may be any that keep to these rules, and one draw needn't show every extreme that they name: `unit_source`: each run of 4 slots (one device's units in the balanced order) holds exactly one unit from every run of 4 units of the packed order; every unit appears once. `doc_lengths`: they sum to 512; the longest is exactly 256.
All inputs are finite; a program needn't handle non-finite values.
Results may differ from a plain program's by a relative error of at most 0.017.
Values may be sent and summed in bfloat16 or wider, within the bound.
No kernel may reach another device: no remote copies, remote signals or barrier semaphores. Data moves between devices by JAX's collectives and lax.ppermute only.
A program may use at most 128 MiB of HBM per device.

v0:
```python
import jax
import jax.numpy as jnp
from jax import lax
from jax.sharding import PartitionSpec as P

HD = 128


def doc_index(positions, doc_ends):
    return jnp.sum((positions[None, :] >= doc_ends[:, None]).astype(jnp.int32), axis=0)


def local(queries, key_rows, value_rows, doc_lengths, unit_source, w_out):
    ctx_count = lax.axis_size("ctx")
    ctx_index = lax.axis_index("ctx")
    tok_dev, columns = queries.shape
    unit_rows = tok_dev // ctx_count
    head_count = columns // HD
    kv_heads = key_rows.shape[1] // HD
    group_size = head_count // kv_heads
    unit_plan = unit_source.reshape(ctx_count, ctx_count)
    wanted = unit_plan // ctx_count == ctx_index
    send_order = jnp.sum(jnp.where(wanted, unit_plan % ctx_count, 0), axis=1)
    outgoing = jnp.take(queries.reshape(ctx_count, unit_rows, columns), send_order, axis=0)
    incoming = lax.all_to_all(outgoing, "ctx", split_axis=0, concat_axis=0, tiled=True)
    my_units = lax.dynamic_index_in_dim(unit_plan, ctx_index, 0, keepdims=False)
    arranged = jnp.take(incoming, my_units // ctx_count, axis=0).reshape(tok_dev, columns)
    positions = (
        my_units[:, None] * unit_rows + jnp.arange(unit_rows, dtype=jnp.int32)[None, :]
    ).reshape(tok_dev)
    doc_ends = jnp.cumsum(doc_lengths)
    query_doc = doc_index(positions, doc_ends)
    grouped = arranged.reshape(tok_dev, kv_heads, group_size, HD)
    score_scale = HD ** (-0.5)
    state_shape = (kv_heads, group_size, tok_dev)
    run_max = jnp.full(state_shape, -1e30, jnp.float32)
    key_piece = lax.all_gather(key_rows, "ctx", axis=0, tiled=True)
    value_piece = lax.all_gather(value_rows, "ctx", axis=0, tiled=True)
    extent = key_piece.shape[0]
    key_pos = jnp.arange(extent, dtype=jnp.int32)
    key_doc = doc_index(key_pos, doc_ends)
    visible = (key_doc[None, :] == query_doc[:, None]) & (key_pos[None, :] <= positions[:, None])
    scores = (
        jnp.einsum(
            "qkgd,pkd->kgqp",
            grouped,
            key_piece.reshape(extent, kv_heads, HD),
            preferred_element_type=jnp.float32,
        )
        * score_scale
    )
    scores = jnp.where(visible, scores, -1e30)
    new_max = jnp.maximum(run_max, jnp.max(scores, axis=3))
    weights = jnp.where(visible, jnp.exp(scores - new_max[..., None]), 0.0)
    new_sum = jnp.sum(weights, axis=3)
    blended = jnp.einsum(
        "kgqp,pkd->kgqd",
        weights.astype(jnp.bfloat16),
        value_piece.reshape(extent, kv_heads, HD),
        preferred_element_type=jnp.float32,
    )
    attended = (
        (blended / new_sum[..., None])
        .transpose(2, 0, 1, 3)
        .reshape(tok_dev, columns)
        .astype(jnp.bfloat16)
    )
    partial_value = jnp.dot(
        lax.all_gather(attended, "ctx", axis=0, tiled=True),
        w_out,
        preferred_element_type=jnp.float32,
    )
    summed = lax.psum_scatter(
        partial_value.astype(jnp.bfloat16), "tp", scatter_dimension=0, tiled=True
    )
    return summed


def solution(mesh):
    return jax.shard_map(
        local,
        mesh=mesh,
        in_specs=(
            P(("dp", "ctx"), "tp"),
            P(("dp", "ctx"), "tp"),
            P(("dp", "ctx"), "tp"),
            P("dp"),
            P("dp"),
            P("tp", "ctx"),
        ),
        out_specs=P(("dp", "tp"), "ctx"),
        check_vma=False,
    )
```

profile of v0, /device:TPU:0, one launch (start us, length us, event | category | flops | bytes accessed | tf_op | source)
XLA Modules:
  0.0 154.2 jit_solution(18268879868082175709)
XLA Ops:
  6.5 0.8 reshape.85
  7.4 0.1 fusion.16
  7.5 0.3 copy-done
  7.8 0.6 gather_fusion
  8.4 1.1 broadcast_select_fusion.1
  9.5 5.2 %all-to-all-start = ((bf16[4,32,4096]{2,1,0:T(8,128)(2,1)}), bf16[4,32,4096]{2,1,0:T(8,128)(2,1)S(1)}, u32[]{:S(2)}, u32[]{:S(2)}) async-start(bf16[4,32,4096]{2,1,0:T(8,128)(2,1)} %broadcast_select_fusion.1), calls=%async_computation | async-start | bytes 2097152 | tf_op jit(solution)/shard_map/all_to_all | solution.py:25
  14.8 19.4 %all_gather.10 = bf16[512,512]{1,0:T(8,128)(2,1)S(1)} all-gather(bf16[128,512]{1,0:T(8,128)(2,1)} %param.10), channel_id=1, replica_groups=mesh['ctx'=4,'tp'=2,'dp'=4] {'ctx'}, dimensions={0}, use_global_device_ids=true | all-gather | bytes 655360 | tf_op jit(solution)/shard_map/all_gather | solution.py:38
  34.1 0.1 add.45
  34.2 0.8 reduce-window.8
  35.1 1.0 copy.12
  36.1 1.0 copy.15
  37.1 10.5 %all_gather.9 = bf16[512,512]{0,1:T(8,128)(2,1)} all-gather(bf16[128,512]{0,1:T(8,128)(2,1)S(1)} %copy.12), channel_id=1, replica_groups=mesh['ctx'=4,'tp'=2,'dp'=4] {'ctx'}, dimensions={0}, use_global_device_ids=true | all-gather | bytes 655360 | tf_op jit(solution)/shard_map/all_gather | solution.py:37
  47.6 0.1 convert_reduce_fusion
  47.7 0.1 convert_reduce_fusion.1
  47.8 0.1 fusion.13
  47.9 0.6 gather_fusion.1
  48.5 0.2 broadcast_select_fusion
  48.7 0.2 copy.20
  49.0 3.1 %bitcast_reduce_fusion = (f32[4,8,128]{2,1,0:T(8,128)S(1)}, f32[4,128,8,512]{3,1,2,0:T(8,128)S(1)}) fusion(pred[128,512]{1,0:T(8,128)(4,1)S(1)} %fusion.13, bf16[512,4,128,1]{0,2,3,1:T(8,128)(2,1)} %bitcast.56, bf16[128,4,8,128]{3,2,1,0:T(8,128)(2,1)S(1)} %bitcast.54), kind=kOutput, calls=%fused_computation.3 | convolution fusion | flops 543158272 | bytes 10043392 | tf_op jit(solution)/shard_map/qkgd,pkd->kgqp/dot_general | solution.py:44
  52.1 2.7 %fusion.2 = f32[4,8,128]{2,1,0:T(8,128)S(1)} fusion(f32[4,128,8,512]{3,1,2,0:T(8,128)S(1)} %get-tuple-element.9, f32[4,8,128]{2,1,0:T(8,128)S(1)} %broadcast_maximum_fusion, pred[128,512]{1,0:T(8,128)(4,1)S(1)} %fusion.13), kind=kLoop, calls=%fused_computation.8 | loop fusion | flops 10481664 | bytes 8486912 | tf_op jit(solution)/shard_map/reduce_sum | solution.py:55
  54.8 3.6 %fusion.8 = bf16[128,4,8,128]{0,3,2,1:T(8,128)(2,1)} fusion(bf16[512,4,128,1]{0,2,3,1:T(8,128)(2,1)S(1)} %bitcast.58, f32[4,128,8,512]{3,1,2,0:T(8,128)S(1)} %get-tuple-element.9, f32[4,8,128]{2,1,0:T(8,128)S(1)} %broadcast_maximum_fusion, pred[128,512]{1,0:T(8,128)(4,1)S(1)} %fusion.13, f32[128,4,8]{0,2,1:T(8,128)S(1)} %bitcast.59), kind=kOutput, calls=%fused_computation.14 | convolution fusion | flops 548405248 | bytes 10059776 | tf_op jit(solution)/shard_map/kgqp,pkd->kgqd/dot_general | solution.py:56
  58.5 53.0 %all-gather.2.cloned.1.call-done = bf16[512,4096]{0,1:T(8,128)(2,1)} async-done(((bf16[128,4096]{0,1:T(8,128)(2,1)}), bf16[512,4096]{0,1:T(8,128)(2,1)}) %all-gather.2.cloned.1.call-update) | async-done | bytes 4194320 | tf_op jit(solution)/shard_map/all_gather | solution.py:69
  111.5 23.7 %convolution_convert_fusion = bf16[512,4096]{1,0:T(8,128)(2,1)} fusion(bf16[512,4096]{0,1:T(8,128)(2,1)} %all-gather.2.cloned.1.call-done, bf16[4096,4096]{1,0:T(8,128)(2,1)} %param.13), kind=kOutput, calls=%fused_computation.7 | convolution fusion | flops 17181966336 | bytes 41943040 | tf_op jit(solution)/shard_map/dot_general | solution.py:68
  135.2 12.2 %reduce-scatter.2.cloned.1.call-done = bf16[256,4096]{1,0:T(8,128)(2,1)} async-done(((bf16[512,4096]{1,0:T(8,128)(2,1)}), bf16[256,4096]{1,0:T(8,128)(2,1)}) %reduce-scatter.2.cloned.1.call-update) | async-done | bytes 2097168 | tf_op jit(solution)/shard_map/reduce_scatter | solution.py:73
  (16 shorter events, 0.2 us)
Async XLA Ops:
  6.5 1.2 copy-start
  9.5 38.4 %all-to-all-start = ((bf16[4,32,4096]{2,1,0:T(8,128)(2,1)}), bf16[4,32,4096]{2,1,0:T(8,128)(2,1)S(1)}, u32[]{:S(2)}, u32[]{:S(2)}) async-start(bf16[4,32,4096]{2,1,0:T(8,128)(2,1)} %broadcast_select_fusion.1), calls=%async_computation | async-start | bytes 2097152 | tf_op jit(solution)/shard_map/all_to_all | solution.py:25
  14.7 96.8 %all-gather.2.cloned.1.call-start = ((), (), s32[]{:S(2)}) async-start(), calls=%async_computation.2 | async-start | bytes 5242880 | tf_op jit(solution)/shard_map/all_gather | solution.py:69
  49.0 5.8 %copy-start.1 = (bf16[512,512]{0,1:T(8,128)(2,1)S(1)}, bf16[512,512]{0,1:T(8,128)(2,1)}, u32[]{:S(2)}) copy-start(bf16[512,512]{0,1:T(8,128)(2,1)} %copy.15) | copy-start | bytes 1572868
  58.5 89.0 %reduce-scatter.2.cloned.1.call-start = ((), (), s32[]{:S(2)}) async-start(), calls=%async_computation.3 | async-start | bytes 6291456 | tf_op jit(solution)/shard_map/reduce_scatter | solution.py:73
Sparse Core Ops, SparseCore 0:
  58.6 52.8 all-gather.1
  135.3 12.0 reduce-scatter.1
where the time goes:
time: 155 us; the launch traced here: 154 us
  waiting for transfers between devices  65.2 us (42%)
  matrix products  30.4 us (20%)
  blocking collectives  29.9 us (19%)
  between operations  13.5 us (9%)
  other arithmetic  5.34 us (3%)
  starting transfers between devices  5.21 us (3%)
  local copies, waits for them, and re-layouts  4.66 us (3%)
    all_gather x1, waiting for transfers between devices, local(): lax.all_gather(attended, 'ctx', axis=0, tiled=True)  53 us
    dot_general x1, matrix products, local(): jnp.dot(lax.all_gather(attended, 'ctx', axis=0, tiled=True), w_out, prefe...  23.7 us
    all_gather x1, blocking collectives, local(): value_piece = lax.all_gather(value_rows, 'ctx', axis=0, tiled=True)  19.4 us
    reduce_scatter x1, waiting for transfers between devices, local(): lax.psum_scatter(partial_value.astype(jnp.bfloat16), 'tp', scatter_dimens...  12.2 us
    all_gather x1, blocking collectives, local(): key_piece = lax.all_gather(key_rows, 'ctx', axis=0, tiled=True)  10.5 us
    all_to_all x1, starting transfers between devices, local(): lax.all_to_all(outgoing, 'ctx', split_axis=0, concat_axis=0, tiled=True)  5.16 us
    dot_general x1, matrix products, local(): jnp.einsum('kgqp,pkd->kgqd', weights.astype(jnp.bfloat16), value_piece.re...  3.61 us
    dot_general x1, matrix products, local(): jnp.einsum('qkgd,pkd->kgqp', grouped, key_piece.reshape(extent, kv_heads,...  3.15 us
  transfers between devices with their start and end apart: 3, of which 2 were waited for; matrix products, arithmetic and copies ran while one was open for 2% of the time, Pallas kernels for 0%

commit v1 on v0

v1 whole, which is shorter than its diff:
```python
import functools
import math

import jax
import jax.numpy as jnp
from jax import lax
from jax.experimental import pallas as pl
from jax.experimental.pallas import tpu as pltpu
from jax.sharding import PartitionSpec as P

HD = 128
MIB = 1 << 20
PARTS = ((0, 1), (1, 2), (2, 3), (3, 4))
PIECES = 2


def doc_index(positions, doc_ends):
    return jnp.sum((positions[None, :] >= doc_ends[:, None]).astype(jnp.int32), axis=0)


def general(queries, key_rows, value_rows, doc_lengths, unit_source, w_out):
    ctx_count = lax.axis_size("ctx")
    ctx_index = lax.axis_index("ctx")
    tok_dev, columns = queries.shape
    unit_rows = tok_dev // ctx_count
    head_count = columns // HD
    kv_heads = key_rows.shape[1] // HD
    group_size = head_count // kv_heads
    unit_plan = unit_source.reshape(ctx_count, ctx_count)
    positions = ctx_index * tok_dev + jnp.arange(tok_dev, dtype=jnp.int32)
    doc_ends = jnp.cumsum(doc_lengths)
    query_doc = doc_index(positions, doc_ends)
    grouped = queries.reshape(tok_dev, kv_heads, group_size, HD)
    key_all = lax.all_gather(key_rows, "ctx", axis=0, tiled=True)
    value_all = lax.all_gather(value_rows, "ctx", axis=0, tiled=True)
    extent = key_all.shape[0]
    key_pos = jnp.arange(extent, dtype=jnp.int32)
    key_doc = doc_index(key_pos, doc_ends)
    visible = (key_doc[None, :] == query_doc[:, None]) & (key_pos[None, :] <= positions[:, None])
    scores = jnp.einsum(
        "qkgd,pkd->kgqp",
        grouped,
        key_all.reshape(extent, kv_heads, HD),
        preferred_element_type=jnp.float32,
    ) * (HD ** -0.5)
    scores = jnp.where(visible, scores, -jnp.inf)
    row_max = jnp.max(scores, axis=3, keepdims=True)
    weights = jnp.where(visible, jnp.exp(scores - row_max), 0.0)
    totals = jnp.sum(weights, axis=3)
    blended = jnp.einsum(
        "kgqp,pkd->kgqd",
        weights.astype(jnp.bfloat16),
        value_all.reshape(extent, kv_heads, HD),
        preferred_element_type=jnp.float32,
    )
    attended = (
        (blended / totals[..., None])
        .transpose(2, 0, 1, 3)
        .reshape(tok_dev, columns)
        .astype(jnp.bfloat16)
    )
    gathered = lax.all_gather(attended, "ctx", axis=0, tiled=True)
    units = gathered.reshape(ctx_count * ctx_count, unit_rows, columns)
    balanced = jnp.take(units, unit_plan.reshape(-1), axis=0).reshape(extent, columns)
    partial_value = jnp.dot(balanced, w_out, preferred_element_type=jnp.float32)
    return lax.psum_scatter(
        partial_value.astype(jnp.bfloat16), "tp", scatter_dimension=0, tiled=True
    )


SMEM = pl.BlockSpec(memory_space=pltpu.SMEM)
VMEM = pl.BlockSpec(memory_space=pltpu.VMEM)
HBM = pl.BlockSpec(memory_space=pl.ANY)
TILE = 512


def in_hbm(x):
    return pltpu.with_memory_space_constraint(x, pltpu.HBM)


def pack_kernel(k_hbm, v_hbm, first_ref, sems):
    copies = [
        pltpu.make_async_copy(k_hbm.at[:, :HD], first_ref.at[:, :HD], sems.at[0]),
        pltpu.make_async_copy(v_hbm.at[:, :HD], first_ref.at[:, HD:], sems.at[1]),
    ]
    for copy in copies:
        copy.start()
    for copy in copies:
        copy.wait()


def pack(key_rows, value_rows):
    return pl.pallas_call(
        pack_kernel,
        out_shape=jax.ShapeDtypeStruct((key_rows.shape[0], 2 * HD), jnp.bfloat16),
        in_specs=[HBM, HBM],
        out_specs=VMEM,
        scratch_shapes=[pltpu.SemaphoreType.DMA((2,))],
        compiler_params=pltpu.CompilerParams(vmem_limit_bytes=4 * MIB),
        name="pack",
    )(in_hbm(key_rows), in_hbm(value_rows))


def prepare_kernel(docs_hbm, k_hbm, v_hbm, q_hbm, rest_ref, q_ref, mask_ref, docs, sems):
    more = k_hbm.shape[1] - HD
    lengths = pltpu.make_async_copy(docs_hbm, docs, sems.at[0])
    loads = [
        pltpu.make_async_copy(k_hbm.at[:, HD:], rest_ref.at[:, :more], sems.at[1]),
        pltpu.make_async_copy(v_hbm.at[:, HD:], rest_ref.at[:, more:], sems.at[2]),
        pltpu.make_async_copy(q_hbm, q_ref, sems.at[3]),
    ]
    lengths.start()
    for load in loads:
        load.start()
    lengths.wait()
    rows, window = mask_ref.shape
    base = lax.axis_index("ctx") * rows
    pos = base + lax.broadcasted_iota(jnp.int32, (rows, window), 0)
    start = jnp.zeros((rows, window), jnp.int32)
    end = jnp.int32(0)
    for d in range(docs.shape[0]):
        end = end + docs[d]
        start = jnp.where(pos >= end, end, start)
    key_pos = base + rows - window + lax.broadcasted_iota(jnp.int32, (rows, window), 1)
    mask_ref[...] = jnp.where((key_pos >= start) & (key_pos <= pos), 0.0, -jnp.inf)
    for load in loads:
        load.wait()


def prepare(doc_lengths, key_rows, value_rows, queries):
    rows, columns = key_rows.shape
    return pl.pallas_call(
        prepare_kernel,
        out_shape=[
            jax.ShapeDtypeStruct((rows, 2 * (columns - HD)), jnp.bfloat16),
            jax.ShapeDtypeStruct(queries.shape, jnp.bfloat16),
            jax.ShapeDtypeStruct((rows, 3 * rows), jnp.float32),
        ],
        in_specs=[HBM] * 4,
        out_specs=[VMEM] * 3,
        scratch_shapes=[
            pltpu.SMEM(doc_lengths.shape, jnp.int32),
            pltpu.SemaphoreType.DMA((4,)),
        ],
        compiler_params=pltpu.CompilerParams(vmem_limit_bytes=4 * MIB),
        cost_estimate=pl.CostEstimate(flops=0, bytes_accessed=0, transcendentals=0),
        name="prepare",
    )(in_hbm(doc_lengths), in_hbm(key_rows), in_hbm(value_rows), in_hbm(queries))


def attend_kernel(groups, count, q_ref, mask_ref, *refs):
    kv, out_ref = refs[:count], refs[-1]
    rows = q_ref.shape[0]
    width = out_ref.shape[1] // len(groups)
    heads = width // HD
    window = 3 * rows
    factor = HD ** -0.5 * math.log2(math.e)
    for i, g in enumerate(groups):
        kv0, kv1, kv2 = kv[:3] if g == 0 else kv[-3:]
        column = 0 if g == 0 else g - 1
        half = kv0.shape[1] // 2
        at_k = slice(column * HD, (column + 1) * HD)
        at_v = slice(half + column * HD, half + (column + 1) * HD)
        keys = jnp.concatenate([kv2[:, at_k], kv1[:, at_k], kv0[:, at_k]], axis=0)
        values = jnp.concatenate([kv2[:, at_v], kv1[:, at_v], kv0[:, at_v]], axis=0)
        stacked = jnp.concatenate(
            [q_ref[:, g * width + h * HD:g * width + (h + 1) * HD] for h in range(heads)], axis=0
        )
        scores = lax.dot_general(
            stacked, keys, (((1,), (1,)), ((), ())), preferred_element_type=jnp.float32
        ).reshape(heads, rows, window)
        scores = scores + mask_ref[...][None]
        top = jnp.max(scores, axis=2, keepdims=True)
        weights = jnp.exp2((scores - top) * factor)
        total = jnp.sum(weights, axis=2, keepdims=True)
        mixed = jnp.dot(
            weights.astype(jnp.bfloat16).reshape(heads * rows, window),
            values,
            preferred_element_type=jnp.float32,
        ).reshape(heads, rows, HD)
        result = (mixed / total).astype(jnp.bfloat16)
        for h in range(heads):
            out_ref[:, i * width + h * HD:i * width + (h + 1) * HD] = result[h]


def attend(groups, width, queries, mask, window, after):
    rows = queries.shape[0]
    kv = ([*window[0]] if 0 in groups else []) + ([*window[1]] if groups[-1] > 0 else [])
    count = len(groups)
    return pl.pallas_call(
        functools.partial(attend_kernel, groups, len(kv)),
        out_shape=jax.ShapeDtypeStruct((rows, count * width), jnp.bfloat16),
        in_specs=[VMEM] * (2 + len(kv)) + [HBM] * len(after),
        out_specs=VMEM,
        compiler_params=pltpu.CompilerParams(vmem_limit_bytes=16 * MIB),
        cost_estimate=pl.CostEstimate(flops=0, bytes_accessed=0, transcendentals=0),
        name=f"attend_{groups[0]}",
    )(queries, mask, *kv, *after)


def lay_out(plan, pieces, lhs):
    here = lax.axis_index("ctx")
    core = lax.axis_index("tp")
    first = jnp.where(core == 0, 1, 2)
    owners = [here, here ^ first, here ^ (3 - first), here ^ 3]
    unit_rows = lhs.shape[0] // 16
    swap = jnp.where(core == 0, 8, 0)
    wanted = [plan[slot] for slot in range(16)]
    for owner, piece in zip(owners, pieces):
        for u in range(4):
            slot = jnp.int32(0)
            for s in range(1, 16):
                slot = jnp.where(wanted[s] == owner * 4 + u, s, slot)
            slot = slot ^ swap
            at = pl.ds(pl.multiple_of(slot * unit_rows, unit_rows), unit_rows)
            lhs[at, :] = piece[u * unit_rows:(u + 1) * unit_rows, :]


def project(w_hbm, wbuf, sems, row, first, prologue, body):
    depth, columns = wbuf.shape
    cuts = [0, columns // 8, 3 * columns // 8, columns]
    copies = [
        pltpu.make_async_copy(
            w_hbm.at[row:row + depth, first + lo:first + hi], wbuf.at[:, lo:hi], sems.at[i]
        )
        for i, (lo, hi) in enumerate(zip(cuts, cuts[1:]))
    ]
    for copy in copies:
        copy.start()
    prologue()
    for copy, lo, hi in zip(copies, cuts, cuts[1:]):
        copy.wait()
        for at in range(lo, hi, TILE):
            end = min(at + TILE, hi)
            body(slice(first + at, first + end), slice(at, end), wbuf[:, at:end])


def chunk_kernel(row, has_acc, plan, p0, p1, p2, p3, w_hbm, *rest):
    acc_ref = rest[0]
    out_ref, lhs, wbuf, sems = rest[-4:]

    def body(at, to, tile):
        product = jnp.dot(lhs[...], tile, preferred_element_type=jnp.float32)
        if has_acc:
            product = product + acc_ref[:, at]
        out_ref[:, at] = product

    project(w_hbm, wbuf, sems, row, 0, lambda: lay_out(plan, (p0, p1, p2, p3), lhs), body)


def chunk(row, plan, pieces, w_out, acc, after):
    rows, width = pieces[0].shape
    total_rows, columns = 4 * rows, w_out.shape[1]
    has_acc = acc is not None
    return pl.pallas_call(
        functools.partial(chunk_kernel, row, has_acc),
        out_shape=jax.ShapeDtypeStruct((total_rows, columns), jnp.float32),
        in_specs=[SMEM] + [VMEM] * 4 + [HBM] + [VMEM] * has_acc + [HBM] * len(after),
        out_specs=VMEM,
        scratch_shapes=[
            pltpu.VMEM((total_rows, width), jnp.bfloat16),
            pltpu.VMEM((width, columns), jnp.bfloat16),
            pltpu.SemaphoreType.DMA((3,)),
        ],
        input_output_aliases={6: 0} if has_acc else {},
        compiler_params=pltpu.CompilerParams(vmem_limit_bytes=(4 + width // 128) * MIB),
        cost_estimate=pl.CostEstimate(
            flops=2 * total_rows * width * columns,
            bytes_accessed=2 * width * columns,
            transcendentals=0,
        ),
        name=f"chunk_{row // width}",
    )(plan, *pieces, w_out, *([acc] if has_acc else []), *after)


def last_kernel(row, first, plan, p0, p1, p2, p3, w_hbm, acc_ref, own_ref, sent_ref, lhs, wbuf, sems):
    rows = lhs.shape[0] // 2

    def body(at, to, tile):
        product = jnp.dot(lhs[...], tile, preferred_element_type=jnp.float32)
        product = product + acc_ref[:, at]
        sent_ref[:, to] = product[:rows].astype(jnp.bfloat16)
        own_ref[:, to] = product[rows:]

    project(w_hbm, wbuf, sems, row, first, lambda: lay_out(plan, (p0, p1, p2, p3), lhs), body)


def last(row, first, columns, plan, pieces, w_out, acc):
    rows, width = pieces[0].shape
    total_rows = 4 * rows
    return pl.pallas_call(
        functools.partial(last_kernel, row, first),
        out_shape=[
            jax.ShapeDtypeStruct((total_rows // 2, columns), jnp.float32),
            jax.ShapeDtypeStruct((total_rows // 2, columns), jnp.bfloat16),
        ],
        in_specs=[SMEM] + [VMEM] * 4 + [HBM, VMEM],
        out_specs=[VMEM, VMEM],
        scratch_shapes=[
            pltpu.VMEM((total_rows, width), jnp.bfloat16),
            pltpu.VMEM((width, columns), jnp.bfloat16),
            pltpu.SemaphoreType.DMA((3,)),
        ],
        compiler_params=pltpu.CompilerParams(vmem_limit_bytes=(4 + width // 128) * MIB),
        cost_estimate=pl.CostEstimate(
            flops=2 * total_rows * width * columns,
            bytes_accessed=2 * width * columns,
            transcendentals=0,
        ),
        name=f"last_{first // columns}",
    )(plan, *pieces, w_out, acc)


def total_kernel(first, has_out, own_ref, got_ref, *rest):
    out_hbm, buf, sems = rest[has_out:]
    columns = got_ref.shape[1]
    step = columns // 2
    writes = []
    for i in range(2):
        to = slice(i * step, (i + 1) * step)
        at = slice(first + i * step, first + (i + 1) * step)
        value = own_ref[:, to] + got_ref[:, to].astype(jnp.float32)
        buf[:, to] = value.astype(jnp.bfloat16)
        write = pltpu.make_async_copy(buf.at[:, to], out_hbm.at[:, at], sems.at[i])
        write.start()
        writes.append(write)
    for write in writes:
        write.wait()


def total(first, width, own, got, out):
    rows, columns = got.shape
    has_out = out is not None
    return pl.pallas_call(
        functools.partial(total_kernel, first, has_out),
        out_shape=jax.ShapeDtypeStruct((rows, width), jnp.bfloat16),
        in_specs=[VMEM, VMEM] + [HBM] * has_out,
        out_specs=HBM,
        scratch_shapes=[
            pltpu.VMEM((rows, columns), jnp.bfloat16),
            pltpu.SemaphoreType.DMA((2,)),
        ],
        input_output_aliases={2: 0} if has_out else {},
        compiler_params=pltpu.CompilerParams(vmem_limit_bytes=4 * MIB),
        cost_estimate=pl.CostEstimate(
            flops=rows * columns, bytes_accessed=2 * rows * columns, transcendentals=0
        ),
        name=f"total_{first // columns}",
    )(own, got, *([out] if has_out else []))


def gather_rows(own):
    def route(first):
        pairs = []
        for chip in range(4):
            for core in range(2):
                axis = 1 if (core == 0) == first else 2
                pairs.append((chip * 2 + core, (chip ^ axis) * 2 + core))
        return pairs

    near = lax.ppermute(own, ("ctx", "tp"), route(True))
    side = lax.ppermute(own, ("ctx", "tp"), route(False))
    far = lax.ppermute(near, ("ctx", "tp"), route(False))
    return own, near, side, far


def local(queries, key_rows, value_rows, doc_lengths, unit_source, w_out):
    if lax.axis_size("ctx") != 4 or lax.axis_size("tp") != 2 or key_rows.shape[1] != 4 * HD:
        return general(queries, key_rows, value_rows, doc_lengths, unit_source, w_out)
    w_out = in_hbm(w_out)
    kv_heads = key_rows.shape[1] // HD
    width = queries.shape[1] // kv_heads
    back_one = [(0, 1), (1, 2), (2, 3)]
    back_two = [(0, 2), (1, 3)]
    first = pack(key_rows, value_rows)
    rest, held, mask = prepare(doc_lengths, key_rows, value_rows, queries)
    window = [
        (part, lax.ppermute(part, "ctx", back_one), lax.ppermute(part, "ctx", back_two))
        for part in (first, rest)
    ]

    def rows_of(i, after):
        own = attend(tuple(range(*PARTS[i])), width, held, mask, window, after)
        return gather_rows(own)

    gathered = [rows_of(0, [])]
    gathered.append(rows_of(1, [gathered[0][0]]))
    gathered.append(rows_of(2, [gathered[1][0], gathered[0][2]]))
    acc = chunk(0, unit_source, gathered[0], w_out, None, [gathered[2][0]])
    gathered.append(rows_of(3, [acc, gathered[1][2]]))
    acc = chunk(width, unit_source, gathered[1], w_out, acc, [gathered[3][0], gathered[2][2]])
    acc = chunk(2 * width, unit_source, gathered[2], w_out, acc, [gathered[3][2]])
    columns = w_out.shape[1] // PIECES
    mine, got = [], []
    for i in range(PIECES):
        kept, sent = last(3 * width, i * columns, columns, unit_source, gathered[3], w_out, acc)
        mine.append(kept)
        got.append(lax.ppermute(sent, "tp", [(0, 1), (1, 0)]))
    out = None
    for i in range(PIECES):
        out = total(i * columns, w_out.shape[1], mine[i], got[i], out)
    return out


def solution(mesh):
    return jax.shard_map(
        local,
        mesh=mesh,
        in_specs=(
            P(("dp", "ctx"), "tp"),
            P(("dp", "ctx"), "tp"),
            P(("dp", "ctx"), "tp"),
            P("dp"),
            P("dp"),
            P("tp", "ctx"),
        ),
        out_specs=P(("dp", "tp"), "ctx"),
        check_vma=False,
    )
```

time: 155 us -> 78.1 us (0.50)
  waiting for transfers between devices: 65.2 us -> 8.85 us
  Pallas kernels: 0 us -> 39.5 us
  matrix products: 30.4 us -> 0 us
  blocking collectives: 29.9 us -> 0 us
  starting transfers between devices: 5.21 us -> 28.4 us
  between operations: 13.5 us -> 0.37 us
  other arithmetic: 5.34 us -> 0 us
  local copies, waits for them, and re-layouts: 4.66 us -> 0.66 us
    all_gather x1 -> x0, waiting for transfers between devices: 53 us -> none  [local(): lax.all_gather(attended, 'ctx', axis=0, tiled=True)]
    pallas_call x0 -> x13, Pallas kernels: none -> 39.5 us  [the longest x3 22.5 us: chunk(): pl.pallas_call(functools.partial(chunk_kernel, row, has_acc), out_shape=j...]
    dot_general x3 -> x0, matrix products: 30.4 us -> none  [the longest x1 23.7 us: local(): jnp.dot(lax.all_gather(attended, 'ctx', axis=0, tiled=True), w_out, prefe...]
    all_gather x2 -> x0, blocking collectives: 29.9 us -> none  [the longest x1 19.4 us: local(): value_piece = lax.all_gather(value_rows, 'ctx', axis=0, tiled=True)]
    ppermute x0 -> x18, starting transfers between devices: none -> 28.4 us  [the longest x2 8.76 us: local(): lax.ppermute(part, 'ctx', back_one)]
    reduce_scatter x1 -> x0, waiting for transfers between devices: 12.2 us -> none  [local(): lax.psum_scatter(partial_value.astype(jnp.bfloat16), 'tp', scatter_dimens...]
    ppermute x0 -> x18, waiting for transfers between devices: none -> 8.85 us  [the longest x2 3.42 us: local(): lax.ppermute(part, 'ctx', back_two)]
    all_to_all x1 -> x0, starting transfers between devices: 5.16 us -> none  [local(): lax.all_to_all(outgoing, 'ctx', split_axis=0, concat_axis=0, tiled=True)]
  transfers between devices with their start and end apart: 3 -> 18, of which waited for: 2 -> 6; matrix products, arithmetic and copies ran while one was open for 2% -> 0% of each run, Pallas kernels for 0% -> 41%
where the time goes in v1:
time: 78.1 us; the launch traced here: 77.8 us
  Pallas kernels  39.5 us (51%)
  starting transfers between devices  28.4 us (36%)
  waiting for transfers between devices  8.85 us (11%)
    pallas_call x3, Pallas kernels, chunk(): pl.pallas_call(functools.partial(chunk_kernel, row, has_acc), out_shape=j...  22.5 us
    pallas_call x2, Pallas kernels, last(): pl.pallas_call(functools.partial(last_kernel, row, first), out_shape=[jax...  9.93 us
    ppermute x2, starting transfers between devices, local(): lax.ppermute(part, 'ctx', back_one)  8.76 us
    ppermute x2, starting transfers between devices, local(): lax.ppermute(part, 'ctx', back_two)  7.7 us
    ppermute x4, starting transfers between devices, gather_rows(): far = lax.ppermute(near, ('ctx', 'tp'), route(False))  7.38 us
    ppermute x2, waiting for transfers between devices, local(): lax.ppermute(part, 'ctx', back_two)  3.42 us
    ppermute x4, starting transfers between devices, gather_rows(): side = lax.ppermute(own, ('ctx', 'tp'), route(False))  2.99 us
    pallas_call x4, Pallas kernels, attend(): pl.pallas_call(functools.partial(attend_kernel, groups, len(kv)), out_sha...  2.7 us
  transfers between devices with their start and end apart: 18, of which 6 were waited for; matrix products, arithmetic and copies ran while one was open for 0% of the time, Pallas kernels for 41%

profile of v1, /device:TPU:0, one launch (start us, length us, event | category | flops | bytes accessed | tf_op | source)
XLA Modules:
  0.0 77.8 jit_solution(7443278387973882577)
XLA Ops:
  0.0 0.8 %pack.1.refs_0_ = bf16[128,256]{1,0:T(8,128)(2,1)S(1)} custom-call(bf16[128,512]{1,0:T(8,128)(2,1)} %k_hbm.3, bf16[128,512]{1,0:T(8,128)(2,1)} %v_hbm.3), custom_call_target="tpu_custom_call" | custom-call | tf_op jit(solution)/shard_map/pack/pallas_call | solution.py:93
  0.8 4.8 %collective-permute-start.2 = (bf16[128,256]{1,0:T(8,128)(2,1)S(1)}, bf16[128,256]{1,0:T(8,128)(2,1)S(1)}, u32[]{:S(2)}, u32[]{:S(2)}) collective-permute-start(bf16[128,256]{1,0:T(8,128)(2,1)S(1)} %pack.1.refs_0_), channel_id=1, source_target_pairs={{0,8},{8,16},{16,24},{1,9},{9,17},{17,25},{2,10},{10,18},{18,26},{... | collective-permute-start | bytes 196616 | tf_op jit(solution)/shard_map/ppermute | solution.py:378
  5.7 3.4 %collective-permute-start.3 = (bf16[128,256]{1,0:T(8,128)(2,1)S(1)}, bf16[128,256]{1,0:T(8,128)(2,1)S(1)}, u32[]{:S(2)}, u32[]{:S(2)}) collective-permute-start(bf16[128,256]{1,0:T(8,128)(2,1)S(1)} %pack.1.refs_0_), channel_id=1, source_target_pairs={{0,16},{8,24},{1,17},{9,25},{2,18},{10,26},{3,19},{11,27},{4,20},{... | collective-permute-start | bytes 196616 | tf_op jit(solution)/shard_map/ppermute | solution.py:378
  9.1 1.4 %prepare.1 = (bf16[128,768]{1,0:T(8,128)(2,1)S(1)}, bf16[128,4096]{1,0:T(8,128)(2,1)S(1)}, f32[128,384]{1,0:T(8,128)S(1)}) custom-call(s32[8]{0:T(128)} %docs_hbm.1, bf16[128,512]{1,0:T(8,128)(2,1)} %k_hbm.3, bf16[128,512]{1,0:T(8,128)(2,1)} %v_hbm.3, bf16[128,4096]{1,0:T(8,128)(2,1)} %q_hbm.1), custom_call_target="tpu_custom_call" | custom-call | tf_op jit(solution)/shard_map/prepare/pallas_call | solution.py:132
  11.7 3.9 %collective-permute-start = (bf16[128,768]{1,0:T(8,128)(2,1)S(1)}, bf16[128,768]{1,0:T(8,128)(2,1)S(1)}, u32[]{:S(2)}, u32[]{:S(2)}) collective-permute-start(bf16[128,768]{1,0:T(8,128)(2,1)S(1)} %get-tuple-element.14.refs_0_), channel_id=1, source_target_pairs={{0,8},{8,16},{16,24},{1,9},{9,17},{17,25},{2,10},{10,18},{18,26},{... | collective-permute-start | bytes 589832 | tf_op jit(solution)/shard_map/ppermute | solution.py:378
  15.7 4.3 %collective-permute-start.1 = (bf16[128,768]{1,0:T(8,128)(2,1)S(1)}, bf16[128,768]{1,0:T(8,128)(2,1)S(1)}, u32[]{:S(2)}, u32[]{:S(2)}) collective-permute-start(bf16[128,768]{1,0:T(8,128)(2,1)S(1)} %get-tuple-element.14.refs_0_), channel_id=1, source_target_pairs={{0,16},{8,24},{1,17},{9,25},{2,18},{10,26},{3,19},{11,27},{4,20},{... | collective-permute-start | bytes 589832 | tf_op jit(solution)/shard_map/ppermute | solution.py:378
  20.0 1.4 %collective-permute-done.refs_1_ = bf16[128,768]{1,0:T(8,128)(2,1)S(1)} collective-permute-done((bf16[128,768]{1,0:T(8,128)(2,1)S(1)}, bf16[128,768]{1,0:T(8,128)(2,1)S(1)}, u32[]{:S(2)}, u32[]{:S(2)}) %collective-permute-start) | collective-permute-done | bytes 196640 | tf_op jit(solution)/shard_map/ppermute | solution.py:378
  21.4 2.9 %collective-permute-done.1.refs_2_ = bf16[128,768]{1,0:T(8,128)(2,1)S(1)} collective-permute-done((bf16[128,768]{1,0:T(8,128)(2,1)S(1)}, bf16[128,768]{1,0:T(8,128)(2,1)S(1)}, u32[]{:S(2)}, u32[]{:S(2)}) %collective-permute-start.1) | collective-permute-done | bytes 196640 | tf_op jit(solution)/shard_map/ppermute | solution.py:378
  25.1 2.7 %collective-permute-start.6 = (bf16[128,1024]{1,0:T(8,128)(2,1)S(1)}, bf16[128,1024]{1,0:T(8,128)(2,1)S(1)}, u32[]{:S(2)}, u32[]{:S(2)}) collective-permute-start(bf16[128,1024]{1,0:T(8,128)(2,1)S(1)} %collective-permute-done.4.p1), channel_id=1, source_target_pairs={{0,16},{4,12},{8,24},{12,4},{16,0},{20,28},{24,8},{28,20},{1,17},{... | collective-permute-start | bytes 786440 | tf_op jit(solution)/shard_map/ppermute | solution.py:363
  27.9 0.9 %collective-permute-done.5.refs_4_.p2 = bf16[128,1024]{1,0:T(8,128)(2,1)S(1)} collective-permute-done((bf16[128,1024]{1,0:T(8,128)(2,1)S(1)}, bf16[128,1024]{1,0:T(8,128)(2,1)S(1)}, u32[]{:S(2)}, u32[]{:S(2)}) %collective-permute-start.5) | collective-permute-done | bytes 262176 | tf_op jit(solution)/shard_map/ppermute | solution.py:362
  28.8 0.7 attend_2.1.rest_0_.p0
  29.5 2.5 %collective-permute-start.12 = (bf16[128,1024]{1,0:T(8,128)(2,1)S(1)}, bf16[128,1024]{1,0:T(8,128)(2,1)S(1)}, u32[]{:S(2)}, u32[]{:S(2)}) collective-permute-start(bf16[128,1024]{1,0:T(8,128)(2,1)S(1)} %attend_2.1.rest_0_.p0), channel_id=1, source_target_pairs={{0,16},{4,12},{8,24},{12,4},{16,0},{20,28},{24,8},{28,20},{1,17},{... | collective-permute-start | bytes 786440 | tf_op jit(solution)/shard_map/ppermute | solution.py:362
  32.4 1.9 %collective-permute-done.14.p1 = bf16[128,1024]{1,0:T(8,128)(2,1)S(1)} collective-permute-done((bf16[128,1024]{1,0:T(8,128)(2,1)S(1)}, bf16[128,1024]{1,0:T(8,128)(2,1)S(1)}, u32[]{:S(2)}, u32[]{:S(2)}) %collective-permute-start.14) | collective-permute-done | bytes 262176 | tf_op jit(solution)/shard_map/ppermute | solution.py:361
  34.3 2.6 %collective-permute-start.15 = (bf16[128,1024]{1,0:T(8,128)(2,1)S(1)}, bf16[128,1024]{1,0:T(8,128)(2,1)S(1)}, u32[]{:S(2)}, u32[]{:S(2)}) collective-permute-start(bf16[128,1024]{1,0:T(8,128)(2,1)S(1)} %collective-permute-done.14.p1), channel_id=1, source_target_pairs={{0,16},{4,12},{8,24},{12,4},{16,0},{20,28},{24,8},{28,20},{1,17},{... | collective-permute-start | bytes 786440 | tf_op jit(solution)/shard_map/ppermute | solution.py:363
  37.5 7.1 %chunk_0.1.refs_3_.rest_0_ = f32[512,4096]{1,0:T(8,128)S(1)} custom-call(s32[16]{0:T(128)S(1)} %copy-done, bf16[128,1024]{1,0:T(8,128)(2,1)S(1)} %attend_0.1.refs_3_.p0, bf16[128,1024]{1,0:T(8,128)(2,1)S(1)} %collective-permute-done.4.p1, bf16[128,1024]{1,0:T(8,128)(2,1)S(1)} %collective-permute-done.5.refs_4_.p2, ...), custom_call_target="tpu_custom_call" | custom-call | flops 4294967296 | bytes 8388608 | tf_op jit(solution)/shard_map/chunk_0/pallas_call | solution.py:255
  44.6 0.7 attend_3.1.rest_1_.p0
  46.1 1.5 %collective-permute-start.13 = (bf16[128,1024]{1,0:T(8,128)(2,1)S(1)}, bf16[128,1024]{1,0:T(8,128)(2,1)S(1)}, u32[]{:S(2)}, u32[]{:S(2)}) collective-permute-start(bf16[128,1024]{1,0:T(8,128)(2,1)S(1)} %collective-permute-done.11.p1), channel_id=1, source_target_pairs={{0,16},{4,12},{8,24},{12,4},{16,0},{20,28},{24,8},{28,20},{1,17},{... | collective-permute-start | bytes 786440 | tf_op jit(solution)/shard_map/ppermute | solution.py:363
  47.7 7.6 %chunk_1.1.rest_0_ = f32[512,4096]{1,0:T(8,128)S(1)} custom-call(s32[16]{0:T(128)S(1)} %copy-done, bf16[128,1024]{1,0:T(8,128)(2,1)S(1)} %attend_1.1.refs_3_.p0, bf16[128,1024]{1,0:T(8,128)(2,1)S(1)} %collective-permute-done.14.p1, bf16[128,1024]{1,0:T(8,128)(2,1)S(1)} %collective-permute-done.7.refs_4_.p2, ...), custom_call_target="tpu_custom_call", output_to_operand_aliasing={{}: (6, {})} | custom-call | flops 4294967296 | bytes 8388608 | tf_op jit(solution)/shard_map/chunk_1/pallas_call | solution.py:255
  55.9 7.8 %chunk_2.1.acc_ref = f32[512,4096]{1,0:T(8,128)S(1)} custom-call(s32[16]{0:T(128)S(1)} %copy-done, bf16[128,1024]{1,0:T(8,128)(2,1)S(1)} %attend_2.1.rest_0_.p0, bf16[128,1024]{1,0:T(8,128)(2,1)S(1)} %collective-permute-done.11.p1, bf16[128,1024]{1,0:T(8,128)(2,1)S(1)} %collective-permute-done.12.rest_2_.p2, ...), custom_call_target="tpu_custom_call", output_to_operand_aliasing={{}: (6, {})} | custom-call | flops 4294967296 | bytes 8388608 | tf_op jit(solution)/shard_map/chunk_2/pallas_call | solution.py:255
  63.7 5.0 %last_0.1 = (f32[256,2048]{1,0:T(8,128)S(1)}, bf16[256,2048]{1,0:T(8,128)(2,1)S(1)}) custom-call(s32[16]{0:T(128)S(1)} %copy-done, bf16[128,1024]{1,0:T(8,128)(2,1)S(1)} %attend_3.1.rest_1_.p0, bf16[128,1024]{1,0:T(8,128)(2,1)S(1)} %collective-permute-done.8.p1, bf16[128,1024]{1,0:T(8,128)(2,1)S(1)} %collective-permute-done.9.rest_1_.p2, ...), custom_call_target="tpu_custom_call" | custom-call | flops 2147483648 | bytes 4194304 | tf_op jit(solution)/shard_map/last_0/pallas_call | solution.py:291
  68.8 5.0 %last_1.1 = (f32[256,2048]{1,0:T(8,128)S(1)}, bf16[256,2048]{1,0:T(8,128)(2,1)S(1)}) custom-call(s32[16]{0:T(128)S(1)} %copy-done, bf16[128,1024]{1,0:T(8,128)(2,1)S(1)} %attend_3.1.rest_1_.p0, bf16[128,1024]{1,0:T(8,128)(2,1)S(1)} %collective-permute-done.8.p1, bf16[128,1024]{1,0:T(8,128)(2,1)S(1)} %collective-permute-done.9.rest_1_.p2, ...), custom_call_target="tpu_custom_call" | custom-call | flops 2147483648 | bytes 4194304 | tf_op jit(solution)/shard_map/last_1/pallas_call | solution.py:291
  74.3 1.1 %total_0.1.rest_0_ = bf16[256,4096]{1,0:T(8,128)(2,1)} custom-call(f32[256,2048]{1,0:T(8,128)S(1)} %get-tuple-element.17.own_ref, bf16[256,2048]{1,0:T(8,128)(2,1)S(1)} %collective-permute-done.17.got_ref), custom_call_target="tpu_custom_call" | custom-call | flops 524288 | bytes 1048576 | tf_op jit(solution)/shard_map/total_0/pallas_call | solution.py:334
  75.4 1.2 %collective-permute-done.16.got_ref = bf16[256,2048]{1,0:T(8,128)(2,1)S(1)} collective-permute-done((bf16[256,2048]{1,0:T(8,128)(2,1)S(1)}, bf16[256,2048]{1,0:T(8,128)(2,1)S(1)}, u32[]{:S(2)}, u32[]{:S(2)}) %collective-permute-start.16) | collective-permute-done | bytes 1048608 | tf_op jit(solution)/shard_map/ppermute | solution.py:398
  76.6 1.1 %total_1.1 = bf16[256,4096]{1,0:T(8,128)(2,1)} custom-call(f32[256,2048]{1,0:T(8,128)S(1)} %get-tuple-element.15.own_ref, bf16[256,2048]{1,0:T(8,128)(2,1)S(1)} %collective-permute-done.16.got_ref, bf16[256,4096]{1,0:T(8,128)(2,1)} %total_0.1.rest_0_), custom_call_target="tpu_custom_call", output_to_operand_aliasing={{}: (2, {})} | custom-call | flops 524288 | bytes 1048576 | tf_op jit(solution)/shard_map/total_1/pallas_call | solution.py:334
  (27 shorter events, 5.1 us)
Async XLA Ops:
  0.8 9.7 %collective-permute-start.2 = (bf16[128,256]{1,0:T(8,128)(2,1)S(1)}, bf16[128,256]{1,0:T(8,128)(2,1)S(1)}, u32[]{:S(2)}, u32[]{:S(2)}) collective-permute-start(bf16[128,256]{1,0:T(8,128)(2,1)S(1)} %pack.1.refs_0_), channel_id=1, source_target_pairs={{0,8},{8,16},{16,24},{1,9},{9,17},{17,25},{2,10},{10,18},{18,26},{... | collective-permute-start | bytes 196616 | tf_op jit(solution)/shard_map/ppermute | solution.py:378
  5.7 5.3 %collective-permute-start.3 = (bf16[128,256]{1,0:T(8,128)(2,1)S(1)}, bf16[128,256]{1,0:T(8,128)(2,1)S(1)}, u32[]{:S(2)}, u32[]{:S(2)}) collective-permute-start(bf16[128,256]{1,0:T(8,128)(2,1)S(1)} %pack.1.refs_0_), channel_id=1, source_target_pairs={{0,16},{8,24},{1,17},{9,25},{2,18},{10,26},{3,19},{11,27},{4,20},{... | collective-permute-start | bytes 196616 | tf_op jit(solution)/shard_map/ppermute | solution.py:378
  11.7 13.5 %collective-permute-start.4 = (bf16[128,1024]{1,0:T(8,128)(2,1)S(1)}, bf16[128,1024]{1,0:T(8,128)(2,1)S(1)}, u32[]{:S(2)}, u32[]{:S(2)}) collective-permute-start(bf16[128,1024]{1,0:T(8,128)(2,1)S(1)} %attend_0.1.refs_3_.p0), channel_id=1, source_target_pairs={{0,8},{4,20},{8,0},{12,28},{16,24},{20,4},{24,16},{28,12},{1,9},{5... | collective-permute-start | bytes 786440 | tf_op jit(solution)/shard_map/ppermute | solution.py:361
  11.7 9.7 %collective-permute-start = (bf16[128,768]{1,0:T(8,128)(2,1)S(1)}, bf16[128,768]{1,0:T(8,128)(2,1)S(1)}, u32[]{:S(2)}, u32[]{:S(2)}) collective-permute-start(bf16[128,768]{1,0:T(8,128)(2,1)S(1)} %get-tuple-element.14.refs_0_), channel_id=1, source_target_pairs={{0,8},{8,16},{16,24},{1,9},{9,17},{17,25},{2,10},{10,18},{18,26},{... | collective-permute-start | bytes 589832 | tf_op jit(solution)/shard_map/ppermute | solution.py:378
  15.7 8.7 %collective-permute-start.1 = (bf16[128,768]{1,0:T(8,128)(2,1)S(1)}, bf16[128,768]{1,0:T(8,128)(2,1)S(1)}, u32[]{:S(2)}, u32[]{:S(2)}) collective-permute-start(bf16[128,768]{1,0:T(8,128)(2,1)S(1)} %get-tuple-element.14.refs_0_), channel_id=1, source_target_pairs={{0,16},{8,24},{1,17},{9,25},{2,18},{10,26},{3,19},{11,27},{4,20},{... | collective-permute-start | bytes 589832 | tf_op jit(solution)/shard_map/ppermute | solution.py:378
  19.9 8.9 %collective-permute-start.5 = (bf16[128,1024]{1,0:T(8,128)(2,1)S(1)}, bf16[128,1024]{1,0:T(8,128)(2,1)S(1)}, u32[]{:S(2)}, u32[]{:S(2)}) collective-permute-start(bf16[128,1024]{1,0:T(8,128)(2,1)S(1)} %attend_0.1.refs_3_.p0), channel_id=1, source_target_pairs={{0,16},{4,12},{8,24},{12,4},{16,0},{20,28},{24,8},{28,20},{1,17},{... | collective-permute-start | bytes 786440 | tf_op jit(solution)/shard_map/ppermute | solution.py:362
  25.0 9.2 %collective-permute-start.14 = (bf16[128,1024]{1,0:T(8,128)(2,1)S(1)}, bf16[128,1024]{1,0:T(8,128)(2,1)S(1)}, u32[]{:S(2)}, u32[]{:S(2)}) collective-permute-start(bf16[128,1024]{1,0:T(8,128)(2,1)S(1)} %attend_1.1.refs_3_.p0), channel_id=1, source_target_pairs={{0,8},{4,20},{8,0},{12,28},{16,24},{20,4},{24,16},{28,12},{1,9},{5... | collective-permute-start | bytes 786440 | tf_op jit(solution)/shard_map/ppermute | solution.py:361
  25.1 11.7 %collective-permute-start.6 = (bf16[128,1024]{1,0:T(8,128)(2,1)S(1)}, bf16[128,1024]{1,0:T(8,128)(2,1)S(1)}, u32[]{:S(2)}, u32[]{:S(2)}) collective-permute-start(bf16[128,1024]{1,0:T(8,128)(2,1)S(1)} %collective-permute-done.4.p1), channel_id=1, source_target_pairs={{0,16},{4,12},{8,24},{12,4},{16,0},{20,28},{24,8},{28,20},{1,17},{... | collective-permute-start | bytes 786440 | tf_op jit(solution)/shard_map/ppermute | solution.py:363
  27.9 16.7 %collective-permute-start.7 = (bf16[128,1024]{1,0:T(8,128)(2,1)S(1)}, bf16[128,1024]{1,0:T(8,128)(2,1)S(1)}, u32[]{:S(2)}, u32[]{:S(2)}) collective-permute-start(bf16[128,1024]{1,0:T(8,128)(2,1)S(1)} %attend_1.1.refs_3_.p0), channel_id=1, source_target_pairs={{0,16},{4,12},{8,24},{12,4},{16,0},{20,28},{24,8},{28,20},{1,17},{... | collective-permute-start | bytes 786440 | tf_op jit(solution)/shard_map/ppermute | solution.py:362
  29.5 18.2 %collective-permute-start.12 = (bf16[128,1024]{1,0:T(8,128)(2,1)S(1)}, bf16[128,1024]{1,0:T(8,128)(2,1)S(1)}, u32[]{:S(2)}, u32[]{:S(2)}) collective-permute-start(bf16[128,1024]{1,0:T(8,128)(2,1)S(1)} %attend_2.1.rest_0_.p0), channel_id=1, source_target_pairs={{0,16},{4,12},{8,24},{12,4},{16,0},{20,28},{24,8},{28,20},{1,17},{... | collective-permute-start | bytes 786440 | tf_op jit(solution)/shard_map/ppermute | solution.py:362
  32.0 14.1 %collective-permute-start.11 = (bf16[128,1024]{1,0:T(8,128)(2,1)S(1)}, bf16[128,1024]{1,0:T(8,128)(2,1)S(1)}, u32[]{:S(2)}, u32[]{:S(2)}) collective-permute-start(bf16[128,1024]{1,0:T(8,128)(2,1)S(1)} %attend_2.1.rest_0_.p0), channel_id=1, source_target_pairs={{0,8},{4,20},{8,0},{12,28},{16,24},{20,4},{24,16},{28,12},{1,9},{5... | collective-permute-start | bytes 786440 | tf_op jit(solution)/shard_map/ppermute | solution.py:361
  34.3 13.4 %collective-permute-start.15 = (bf16[128,1024]{1,0:T(8,128)(2,1)S(1)}, bf16[128,1024]{1,0:T(8,128)(2,1)S(1)}, u32[]{:S(2)}, u32[]{:S(2)}) collective-permute-start(bf16[128,1024]{1,0:T(8,128)(2,1)S(1)} %collective-permute-done.14.p1), channel_id=1, source_target_pairs={{0,16},{4,12},{8,24},{12,4},{16,0},{20,28},{24,8},{28,20},{1,17},{... | collective-permute-start | bytes 786440 | tf_op jit(solution)/shard_map/ppermute | solution.py:363
  36.8 0.7 copy-start
  45.3 10.6 %collective-permute-start.9 = (bf16[128,1024]{1,0:T(8,128)(2,1)S(1)}, bf16[128,1024]{1,0:T(8,128)(2,1)S(1)}, u32[]{:S(2)}, u32[]{:S(2)}) collective-permute-start(bf16[128,1024]{1,0:T(8,128)(2,1)S(1)} %attend_3.1.rest_1_.p0), channel_id=1, source_target_pairs={{0,16},{4,12},{8,24},{12,4},{16,0},{20,28},{24,8},{28,20},{1,17},{... | collective-permute-start | bytes 786440 | tf_op jit(solution)/shard_map/ppermute | solution.py:362
  45.6 9.7 %collective-permute-start.8 = (bf16[128,1024]{1,0:T(8,128)(2,1)S(1)}, bf16[128,1024]{1,0:T(8,128)(2,1)S(1)}, u32[]{:S(2)}, u32[]{:S(2)}) collective-permute-start(bf16[128,1024]{1,0:T(8,128)(2,1)S(1)} %attend_3.1.rest_1_.p0), channel_id=1, source_target_pairs={{0,8},{4,20},{8,0},{12,28},{16,24},{20,4},{24,16},{28,12},{1,9},{5... | collective-permute-start | bytes 786440 | tf_op jit(solution)/shard_map/ppermute | solution.py:361
  46.1 9.7 %collective-permute-start.13 = (bf16[128,1024]{1,0:T(8,128)(2,1)S(1)}, bf16[128,1024]{1,0:T(8,128)(2,1)S(1)}, u32[]{:S(2)}, u32[]{:S(2)}) collective-permute-start(bf16[128,1024]{1,0:T(8,128)(2,1)S(1)} %collective-permute-done.11.p1), channel_id=1, source_target_pairs={{0,16},{4,12},{8,24},{12,4},{16,0},{20,28},{24,8},{28,20},{1,17},{... | collective-permute-start | bytes 786440 | tf_op jit(solution)/shard_map/ppermute | solution.py:363
  55.3 8.4 %collective-permute-start.10 = (bf16[128,1024]{1,0:T(8,128)(2,1)S(1)}, bf16[128,1024]{1,0:T(8,128)(2,1)S(1)}, u32[]{:S(2)}, u32[]{:S(2)}) collective-permute-start(bf16[128,1024]{1,0:T(8,128)(2,1)S(1)} %collective-permute-done.8.p1), channel_id=1, source_target_pairs={{0,16},{4,12},{8,24},{12,4},{16,0},{20,28},{24,8},{28,20},{1,17},{... | collective-permute-start | bytes 786440 | tf_op jit(solution)/shard_map/ppermute | solution.py:363
  68.7 5.6 %collective-permute-start.17 = (bf16[256,2048]{1,0:T(8,128)(2,1)S(1)}, bf16[256,2048]{1,0:T(8,128)(2,1)S(1)}, u32[]{:S(2)}, u32[]{:S(2)}) collective-permute-start(bf16[256,2048]{1,0:T(8,128)(2,1)S(1)} %get-tuple-element.18), channel_id=1, source_target_pairs={{0,4},{4,0},{1,5},{5,1},{2,6},{6,2},{3,7},{7,3},{8,12},{12,8},{9,1... | collective-permute-start | bytes 3145736 | tf_op jit(solution)/shard_map/ppermute | solution.py:398
  73.7 2.8 %collective-permute-start.16 = (bf16[256,2048]{1,0:T(8,128)(2,1)S(1)}, bf16[256,2048]{1,0:T(8,128)(2,1)S(1)}, u32[]{:S(2)}, u32[]{:S(2)}) collective-permute-start(bf16[256,2048]{1,0:T(8,128)(2,1)S(1)} %get-tuple-element.16), channel_id=1, source_target_pairs={{0,4},{4,0},{1,5},{5,1},{2,6},{6,2},{3,7},{7,3},{8,12},{12,8},{9,1... | collective-permute-start | bytes 3145736 | tf_op jit(solution)/shard_map/ppermute | solution.py:398

commit v2 on v1

v2 whole, which is shorter than its diff:
```python
import functools
import math

import jax
import jax.numpy as jnp
from jax import lax
from jax.experimental import pallas as pl
from jax.experimental.pallas import tpu as pltpu
from jax.sharding import PartitionSpec as P

HD = 128
MIB = 1 << 20
HALVES = 2


def doc_index(positions, doc_ends):
    return jnp.sum((positions[None, :] >= doc_ends[:, None]).astype(jnp.int32), axis=0)


def general(queries, key_rows, value_rows, doc_lengths, unit_source, w_out):
    ctx_count = lax.axis_size("ctx")
    ctx_index = lax.axis_index("ctx")
    tok_dev, columns = queries.shape
    unit_rows = tok_dev // ctx_count
    head_count = columns // HD
    kv_heads = key_rows.shape[1] // HD
    group_size = head_count // kv_heads
    unit_plan = unit_source.reshape(ctx_count, ctx_count)
    positions = ctx_index * tok_dev + jnp.arange(tok_dev, dtype=jnp.int32)
    doc_ends = jnp.cumsum(doc_lengths)
    query_doc = doc_index(positions, doc_ends)
    grouped = queries.reshape(tok_dev, kv_heads, group_size, HD)
    key_all = lax.all_gather(key_rows, "ctx", axis=0, tiled=True)
    value_all = lax.all_gather(value_rows, "ctx", axis=0, tiled=True)
    extent = key_all.shape[0]
    key_pos = jnp.arange(extent, dtype=jnp.int32)
    key_doc = doc_index(key_pos, doc_ends)
    visible = (key_doc[None, :] == query_doc[:, None]) & (key_pos[None, :] <= positions[:, None])
    scores = jnp.einsum(
        "qkgd,pkd->kgqp",
        grouped,
        key_all.reshape(extent, kv_heads, HD),
        preferred_element_type=jnp.float32,
    ) * (HD ** -0.5)
    scores = jnp.where(visible, scores, -jnp.inf)
    row_max = jnp.max(scores, axis=3, keepdims=True)
    weights = jnp.where(visible, jnp.exp(scores - row_max), 0.0)
    totals = jnp.sum(weights, axis=3)
    blended = jnp.einsum(
        "kgqp,pkd->kgqd",
        weights.astype(jnp.bfloat16),
        value_all.reshape(extent, kv_heads, HD),
        preferred_element_type=jnp.float32,
    )
    attended = (
        (blended / totals[..., None])
        .transpose(2, 0, 1, 3)
        .reshape(tok_dev, columns)
        .astype(jnp.bfloat16)
    )
    gathered = lax.all_gather(attended, "ctx", axis=0, tiled=True)
    units = gathered.reshape(ctx_count * ctx_count, unit_rows, columns)
    balanced = jnp.take(units, unit_plan.reshape(-1), axis=0).reshape(extent, columns)
    partial_value = jnp.dot(balanced, w_out, preferred_element_type=jnp.float32)
    return lax.psum_scatter(
        partial_value.astype(jnp.bfloat16), "tp", scatter_dimension=0, tiled=True
    )


SMEM = pl.BlockSpec(memory_space=pltpu.SMEM)
VMEM = pl.BlockSpec(memory_space=pltpu.VMEM)
HBM = pl.BlockSpec(memory_space=pl.ANY)
TILE = 512


def in_hbm(x):
    return pltpu.with_memory_space_constraint(x, pltpu.HBM)


def pack_kernel(k_hbm, v_hbm, kv_ref, sems):
    columns = k_hbm.shape[1]
    copies = [
        pltpu.make_async_copy(k_hbm, kv_ref.at[:, :columns], sems.at[0]),
        pltpu.make_async_copy(v_hbm, kv_ref.at[:, columns:], sems.at[1]),
    ]
    for copy in copies:
        copy.start()
    for copy in copies:
        copy.wait()


def pack(key_rows, value_rows):
    rows, columns = key_rows.shape
    return pl.pallas_call(
        pack_kernel,
        out_shape=jax.ShapeDtypeStruct((rows, 2 * columns), jnp.bfloat16),
        in_specs=[HBM, HBM],
        out_specs=VMEM,
        scratch_shapes=[pltpu.SemaphoreType.DMA((2,))],
        compiler_params=pltpu.CompilerParams(vmem_limit_bytes=4 * MIB),
        name="pack",
    )(in_hbm(key_rows), in_hbm(value_rows))


def prepare_kernel(docs_hbm, q_hbm, w_hbm, q_ref, mask_ref, w_ref, docs, sems):
    lengths = pltpu.make_async_copy(docs_hbm, docs, sems.at[0])
    loads = [
        pltpu.make_async_copy(q_hbm, q_ref, sems.at[1]),
        block_copy(w_hbm, 0, w_ref, sems.at[2]),
    ]
    lengths.start()
    for load in loads:
        load.start()
    lengths.wait()
    rows, window = mask_ref.shape
    base = lax.axis_index("ctx") * rows
    pos = base + lax.broadcasted_iota(jnp.int32, (rows, window), 0)
    start = jnp.zeros((rows, window), jnp.int32)
    end = jnp.int32(0)
    for d in range(docs.shape[0]):
        end = end + docs[d]
        start = jnp.where(pos >= end, end, start)
    key_pos = base + rows - window + lax.broadcasted_iota(jnp.int32, (rows, window), 1)
    mask_ref[...] = jnp.where((key_pos >= start) & (key_pos <= pos), 0.0, -jnp.inf)
    for load in loads:
        load.wait()


def block_shape(w_out, chunks):
    return w_out.shape[0] // chunks, w_out.shape[1] // HALVES


def block_copy(w_hbm, index, w_ref, sem):
    depth, columns = w_ref.shape
    row, column = index // HALVES * depth, index % HALVES * columns
    return pltpu.make_async_copy(
        w_hbm.at[row:row + depth, column:column + columns], w_ref, sem
    )


def prepare(doc_lengths, queries, w_out, chunks):
    rows = queries.shape[0]
    return pl.pallas_call(
        prepare_kernel,
        out_shape=[
            jax.ShapeDtypeStruct(queries.shape, jnp.bfloat16),
            jax.ShapeDtypeStruct((rows, 3 * rows), jnp.float32),
            jax.ShapeDtypeStruct(block_shape(w_out, chunks), jnp.bfloat16),
        ],
        in_specs=[HBM] * 3,
        out_specs=[VMEM] * 3,
        scratch_shapes=[
            pltpu.SMEM(doc_lengths.shape, jnp.int32),
            pltpu.SemaphoreType.DMA((3,)),
        ],
        compiler_params=pltpu.CompilerParams(vmem_limit_bytes=4 * MIB),
        cost_estimate=pl.CostEstimate(flops=0, bytes_accessed=0, transcendentals=0),
        name="prepare",
    )(in_hbm(doc_lengths), in_hbm(queries), w_out)


def attend_kernel(g, q_ref, mask_ref, kv0, kv1, kv2, *rest):
    out_ref = rest[-1]
    rows, width = out_ref.shape
    heads = width // HD
    window = 3 * rows
    factor = HD ** -0.5 * math.log2(math.e)
    half = kv0.shape[1] // 2
    at_k = slice(g * HD, (g + 1) * HD)
    at_v = slice(half + g * HD, half + (g + 1) * HD)
    keys = jnp.concatenate([kv2[:, at_k], kv1[:, at_k], kv0[:, at_k]], axis=0)
    values = jnp.concatenate([kv2[:, at_v], kv1[:, at_v], kv0[:, at_v]], axis=0)
    stacked = jnp.concatenate(
        [q_ref[:, g * width + h * HD:g * width + (h + 1) * HD] for h in range(heads)], axis=0
    )
    scores = lax.dot_general(
        stacked, keys, (((1,), (1,)), ((), ())), preferred_element_type=jnp.float32
    ).reshape(heads, rows, window)
    scores = scores + mask_ref[...][None]
    top = jnp.max(scores, axis=2, keepdims=True)
    weights = jnp.exp2((scores - top) * factor)
    total = jnp.sum(weights, axis=2, keepdims=True)
    mixed = jnp.dot(
        weights.astype(jnp.bfloat16).reshape(heads * rows, window),
        values,
        preferred_element_type=jnp.float32,
    ).reshape(heads, rows, HD)
    result = (mixed / total).astype(jnp.bfloat16)
    for h in range(heads):
        out_ref[:, h * HD:(h + 1) * HD] = result[h]


def attend(g, width, queries, mask, kv, after):
    rows = queries.shape[0]
    return pl.pallas_call(
        functools.partial(attend_kernel, g),
        out_shape=jax.ShapeDtypeStruct((rows, width), jnp.bfloat16),
        in_specs=[VMEM] * 5 + [HBM] * len(after),
        out_specs=VMEM,
        compiler_params=pltpu.CompilerParams(vmem_limit_bytes=16 * MIB),
        cost_estimate=pl.CostEstimate(flops=0, bytes_accessed=0, transcendentals=0),
        name=f"attend_{g}",
    )(queries, mask, *kv, *after)


def lay_out(plan, pieces, lhs):
    here = lax.axis_index("ctx")
    core = lax.axis_index("tp")
    first = jnp.where(core == 0, 1, 2)
    owners = [here, here ^ first, here ^ (3 - first), here ^ 3]
    unit_rows = lhs.shape[0] // 16
    swap = jnp.where(core == 0, 8, 0)
    wanted = [plan[slot] for slot in range(16)]
    for owner, piece in zip(owners, pieces):
        for u in range(4):
            slot = jnp.int32(0)
            for s in range(1, 16):
                slot = jnp.where(wanted[s] == owner * 4 + u, s, slot)
            slot = slot ^ swap
            at = pl.ds(pl.multiple_of(slot * unit_rows, unit_rows), unit_rows)
            lhs[at, :] = piece[u * unit_rows:(u + 1) * unit_rows, :]


def step_kernel(index, last, first_half, has_acc, *refs):
    refs = list(refs)
    if first_half:
        plan, *pieces = refs[:5]
        del refs[:5]
    else:
        lhs = refs.pop(0)
    w_ref, w_hbm = refs[:2]
    del refs[:2]
    acc_ref = refs.pop(0) if has_acc else None
    has_next = not (last and not first_half)
    sem = refs.pop() if has_next else None
    next_ref = refs.pop() if has_next else None
    if first_half:
        lhs = refs.pop()
    load = None
    if has_next:
        load = block_copy(w_hbm, index + 1, next_ref, sem)
        load.start()
    if first_half:
        lay_out(plan, pieces, lhs)
    rows = lhs.shape[0] // 2
    for at in range(0, w_ref.shape[1], TILE):
        to = slice(at, at + TILE)
        product = jnp.dot(lhs[...], w_ref[:, to], preferred_element_type=jnp.float32)
        if has_acc:
            product = product + acc_ref[:, to]
        if last:
            own_ref, sent_ref = refs
            own_ref[:, to] = product[rows:]
            sent_ref[:, to] = product[:rows].astype(jnp.bfloat16)
        else:
            refs[0][:, to] = product
    if load is not None:
        load.wait()


def step(index, last, rows_in, block, w_out, acc):
    first_half = index % HALVES == 0
    has_acc = acc is not None
    has_next = not (last and not first_half)
    depth, columns = block.shape
    if first_half:
        plan, pieces = rows_in
        total_rows = 4 * pieces[0].shape[0]
        operands, specs = [plan, *pieces], [SMEM] + [VMEM] * 4
    else:
        total_rows = rows_in.shape[0]
        operands, specs = [rows_in], [VMEM]
    if last:
        half = (total_rows // 2, columns)
        shapes = [jax.ShapeDtypeStruct(half, jnp.float32), jax.ShapeDtypeStruct(half, jnp.bfloat16)]
    else:
        shapes = [jax.ShapeDtypeStruct((total_rows, columns), jnp.float32)]
    if first_half:
        shapes.append(jax.ShapeDtypeStruct((total_rows, depth), jnp.bfloat16))
    if has_next:
        shapes.append(jax.ShapeDtypeStruct(block.shape, jnp.bfloat16))
    operands += [block, w_out] + [acc] * has_acc
    specs += [VMEM, HBM] + [VMEM] * has_acc
    alias = {len(operands) - 1: 0} if has_acc and not last else {}
    results = list(pl.pallas_call(
        functools.partial(step_kernel, index, last, first_half, has_acc),
        out_shape=shapes,
        in_specs=specs,
        out_specs=[VMEM] * len(shapes),
        scratch_shapes=[pltpu.SemaphoreType.DMA] * has_next,
        input_output_aliases=alias,
        compiler_params=pltpu.CompilerParams(vmem_limit_bytes=8 * MIB),
        cost_estimate=pl.CostEstimate(
            flops=2 * total_rows * depth * columns, bytes_accessed=0, transcendentals=0
        ),
        name=f"step_{index}",
    )(*operands))
    following = results.pop() if has_next else None
    lhs = results.pop() if first_half else None
    return results, lhs, following


def total_kernel(first, has_out, own_ref, got_ref, *rest):
    out_hbm, buf, sems = rest[has_out:]
    columns = got_ref.shape[1]
    step = columns // 2
    writes = []
    for i in range(2):
        to = slice(i * step, (i + 1) * step)
        at = slice(first + i * step, first + (i + 1) * step)
        value = own_ref[:, to] + got_ref[:, to].astype(jnp.float32)
        buf[:, to] = value.astype(jnp.bfloat16)
        write = pltpu.make_async_copy(buf.at[:, to], out_hbm.at[:, at], sems.at[i])
        write.start()
        writes.append(write)
    for write in writes:
        write.wait()


def total(first, width, own, got, out):
    rows, columns = got.shape
    has_out = out is not None
    return pl.pallas_call(
        functools.partial(total_kernel, first, has_out),
        out_shape=jax.ShapeDtypeStruct((rows, width), jnp.bfloat16),
        in_specs=[VMEM, VMEM] + [HBM] * has_out,
        out_specs=HBM,
        scratch_shapes=[
            pltpu.VMEM((rows, columns), jnp.bfloat16),
            pltpu.SemaphoreType.DMA((2,)),
        ],
        input_output_aliases={2: 0} if has_out else {},
        compiler_params=pltpu.CompilerParams(vmem_limit_bytes=4 * MIB),
        cost_estimate=pl.CostEstimate(
            flops=rows * columns, bytes_accessed=2 * rows * columns, transcendentals=0
        ),
        name=f"total_{first // columns}",
    )(own, got, *([out] if has_out else []))


def gather_rows(own):
    def route(first):
        pairs = []
        for chip in range(4):
            for core in range(2):
                axis = 1 if (core == 0) == first else 2
                pairs.append((chip * 2 + core, (chip ^ axis) * 2 + core))
        return pairs

    near = lax.ppermute(own, ("ctx", "tp"), route(True))
    side = lax.ppermute(own, ("ctx", "tp"), route(False))
    far = lax.ppermute(near, ("ctx", "tp"), route(False))
    return own, near, side, far


def local(queries, key_rows, value_rows, doc_lengths, unit_source, w_out):
    if lax.axis_size("ctx") != 4 or lax.axis_size("tp") != 2 or key_rows.shape[1] != 4 * HD:
        return general(queries, key_rows, value_rows, doc_lengths, unit_source, w_out)
    w_out = in_hbm(w_out)
    kv_heads = key_rows.shape[1] // HD
    width = queries.shape[1] // kv_heads
    kv = pack(key_rows, value_rows)
    held, mask, block = prepare(doc_lengths, queries, w_out, kv_heads)
    window = (
        kv,
        lax.ppermute(kv, "ctx", [(0, 1), (1, 2), (2, 3)]),
        lax.ppermute(kv, "ctx", [(0, 2), (1, 3)]),
    )
    gathered, after = [], []
    for g in range(kv_heads):
        own = attend(g, width, held, mask, window, after)
        gathered.append(gather_rows(own))
        after = [own]
    totals = [None] * HALVES
    mine, got = [], []
    for g in range(kv_heads):
        last = g == kv_heads - 1
        rows_in = (unit_source, gathered[g])
        for half in range(HALVES):
            results, lhs, block = step(
                g * HALVES + half, last, rows_in, block, w_out, totals[half]
            )
            rows_in = lhs
            if last:
                mine.append(results[0])
                got.append(lax.ppermute(results[1], "tp", [(0, 1), (1, 0)]))
            else:
                totals[half] = results[0]
    columns = w_out.shape[1] // HALVES
    out = None
    for half in range(HALVES):
        out = total(half * columns, w_out.shape[1], mine[half], got[half], out)
    return out


def solution(mesh):
    return jax.shard_map(
        local,
        mesh=mesh,
        in_specs=(
            P(("dp", "ctx"), "tp"),
            P(("dp", "ctx"), "tp"),
            P(("dp", "ctx"), "tp"),
            P("dp"),
            P("dp"),
            P("tp", "ctx"),
        ),
        out_specs=P(("dp", "tp"), "ctx"),
        check_vma=False,
    )
```

time: 78.1 us -> 75.8 us (0.971)
  starting transfers between devices: 28.4 us -> 25.3 us
  waiting for transfers between devices: 8.85 us -> 10.8 us
    ppermute x6 -> x4, starting transfers between devices: 17.1 us -> 8.92 us  [the longest x1 4.86 us: local(): lax.ppermute(kv, 'ctx', [(0, 1), (1, 2), (2, 3)])]
    ppermute x4, starting transfers between devices: 0.98 us -> 4.18 us  [gather_rows(): near = lax.ppermute(own, ('ctx', 'tp'), route(True))]
    ppermute x4, starting transfers between devices: 2.99 us -> 4.71 us  [gather_rows(): side = lax.ppermute(own, ('ctx', 'tp'), route(False))]
    ppermute x6 -> x4, waiting for transfers between devices: 6.04 us -> 7.29 us  [the longest x1 6.08 us: local(): lax.ppermute(kv, 'ctx', [(0, 2), (1, 3)])]
    ppermute x4, waiting for transfers between devices: 0.92 us -> 0.01 us  [gather_rows(): side = lax.ppermute(own, ('ctx', 'tp'), route(False))]
    ppermute x4, waiting for transfers between devices: 0.01 us -> 0.87 us  [gather_rows(): far = lax.ppermute(near, ('ctx', 'tp'), route(False))]
    pallas_call x11 -> x14, Pallas kernels: 37.3 us -> 36.8 us  [the longest x8 30.6 us: step(): pl.pallas_call(functools.partial(step_kernel, index, last, first_half, ha...]
  transfers between devices with their start and end apart: 18 -> 16, of which waited for: 6 -> 4; matrix products, arithmetic and copies ran while one was open for 0% -> 0% of each run, Pallas kernels for 41% -> 44%
where the time goes in v2:
time: 75.8 us; the launch traced here: 75.5 us
  Pallas kernels  39 us (51%)
  starting transfers between devices  25.3 us (33%)
  waiting for transfers between devices  10.8 us (14%)
    pallas_call x8, Pallas kernels, step(): pl.pallas_call(functools.partial(step_kernel, index, last, first_half, ha...  30.6 us
    ppermute x4, starting transfers between devices, gather_rows(): far = lax.ppermute(near, ('ctx', 'tp'), route(False))  7.47 us
    ppermute x1, waiting for transfers between devices, local(): lax.ppermute(kv, 'ctx', [(0, 2), (1, 3)])  6.08 us
    ppermute x1, starting transfers between devices, local(): lax.ppermute(kv, 'ctx', [(0, 1), (1, 2), (2, 3)])  4.86 us
    ppermute x4, starting transfers between devices, gather_rows(): side = lax.ppermute(own, ('ctx', 'tp'), route(False))  4.71 us
    ppermute x4, starting transfers between devices, gather_rows(): near = lax.ppermute(own, ('ctx', 'tp'), route(True))  4.18 us
    ppermute x1, starting transfers between devices, local(): lax.ppermute(kv, 'ctx', [(0, 2), (1, 3)])  3.43 us
    pallas_call x4, Pallas kernels, attend(): pl.pallas_call(functools.partial(attend_kernel, g), out_shape=jax.ShapeDt...  2.71 us
  transfers between devices with their start and end apart: 16, of which 4 were waited for; matrix products, arithmetic and copies ran while one was open for 0% of the time, Pallas kernels for 44%

profile of v2, /device:TPU:0, one launch (start us, length us, event | category | flops | bytes accessed | tf_op | source)
XLA Modules:
  0.0 75.5 jit_solution(8890587319567275434)
XLA Ops:
  0.0 1.0 %pack.1.kv0 = bf16[128,1024]{1,0:T(8,128)(2,1)S(1)} custom-call(bf16[128,512]{1,0:T(8,128)(2,1)} %k_hbm.1, bf16[128,512]{1,0:T(8,128)(2,1)} %v_hbm.1), custom_call_target="tpu_custom_call" | custom-call | tf_op jit(solution)/shard_map/pack/pallas_call | solution.py:94
  1.0 4.9 %collective-permute-start = (bf16[128,1024]{1,0:T(8,128)(2,1)S(1)}, bf16[128,1024]{1,0:T(8,128)(2,1)S(1)}, u32[]{:S(2)}, u32[]{:S(2)}) collective-permute-start(bf16[128,1024]{1,0:T(8,128)(2,1)S(1)} %pack.1.kv0), channel_id=1, source_target_pairs={{0,8},{8,16},{16,24},{1,9},{9,17},{17,25},{2,10},{10,18},{18,26},{... | collective-permute-start | bytes 786440 | tf_op jit(solution)/shard_map/ppermute | solution.py:366
  5.9 3.4 %collective-permute-start.1 = (bf16[128,1024]{1,0:T(8,128)(2,1)S(1)}, bf16[128,1024]{1,0:T(8,128)(2,1)S(1)}, u32[]{:S(2)}, u32[]{:S(2)}) collective-permute-start(bf16[128,1024]{1,0:T(8,128)(2,1)S(1)} %pack.1.kv0), channel_id=1, source_target_pairs={{0,16},{8,24},{1,17},{9,25},{2,18},{10,26},{3,19},{11,27},{4,20},{... | collective-permute-start | bytes 786440 | tf_op jit(solution)/shard_map/ppermute | solution.py:367
  9.3 2.5 %prepare.1 = (bf16[128,4096]{1,0:T(8,128)(2,1)S(1)}, f32[128,384]{1,0:T(8,128)S(1)}, bf16[1024,2048]{1,0:T(8,128)(2,1)S(1)}) custom-call(s32[8]{0:T(128)} %docs_hbm.1, bf16[128,4096]{1,0:T(8,128)(2,1)} %q_hbm.1, bf16[4096,4096]{1,0:T(8,128)(2,1)} %refs_2_.7), custom_call_target="tpu_custom_call" | custom-call | tf_op jit(solution)/shard_map/prepare/pallas_call | solution.py:143
  11.9 6.1 %collective-permute-done.1.kv2 = bf16[128,1024]{1,0:T(8,128)(2,1)S(1)} collective-permute-done((bf16[128,1024]{1,0:T(8,128)(2,1)S(1)}, bf16[128,1024]{1,0:T(8,128)(2,1)S(1)}, u32[]{:S(2)}, u32[]{:S(2)}) %collective-permute-start.1) | collective-permute-done | bytes 262176 | tf_op jit(solution)/shard_map/ppermute | solution.py:367
  18.7 2.5 %collective-permute-start.12 = (bf16[128,1024]{1,0:T(8,128)(2,1)S(1)}, bf16[128,1024]{1,0:T(8,128)(2,1)S(1)}, u32[]{:S(2)}, u32[]{:S(2)}) collective-permute-start(bf16[128,1024]{1,0:T(8,128)(2,1)S(1)} %attend_0.1.rest_0_.refs_1_), channel_id=1, source_target_pairs={{0,16},{4,12},{8,24},{12,4},{16,0},{20,28},{24,8},{28,20},{1,17},{... | collective-permute-start | bytes 786440 | tf_op jit(solution)/shard_map/ppermute | solution.py:351
  21.9 2.0 %collective-permute-start.8 = (bf16[128,1024]{1,0:T(8,128)(2,1)S(1)}, bf16[128,1024]{1,0:T(8,128)(2,1)S(1)}, u32[]{:S(2)}, u32[]{:S(2)}) collective-permute-start(bf16[128,1024]{1,0:T(8,128)(2,1)S(1)} %attend_1.1.rest_0_.refs_1_), channel_id=1, source_target_pairs={{0,8},{4,20},{8,0},{12,28},{16,24},{20,4},{24,16},{28,12},{1,9},{5... | collective-permute-start | bytes 786440 | tf_op jit(solution)/shard_map/ppermute | solution.py:350
  24.0 2.6 %collective-permute-done.11.refs_2_ = bf16[128,1024]{1,0:T(8,128)(2,1)S(1)} collective-permute-done((bf16[128,1024]{1,0:T(8,128)(2,1)S(1)}, bf16[128,1024]{1,0:T(8,128)(2,1)S(1)}, u32[]{:S(2)}, u32[]{:S(2)}) %collective-permute-start.11) | collective-permute-done | bytes 262176 | tf_op jit(solution)/shard_map/ppermute | solution.py:350
  26.6 2.9 %collective-permute-start.13 = (bf16[128,1024]{1,0:T(8,128)(2,1)S(1)}, bf16[128,1024]{1,0:T(8,128)(2,1)S(1)}, u32[]{:S(2)}, u32[]{:S(2)}) collective-permute-start(bf16[128,1024]{1,0:T(8,128)(2,1)S(1)} %collective-permute-done.11.refs_2_), channel_id=1, source_target_pairs={{0,16},{4,12},{8,24},{12,4},{16,0},{20,28},{24,8},{28,20},{1,17},{... | collective-permute-start | bytes 786440 | tf_op jit(solution)/shard_map/ppermute | solution.py:352
  31.3 2.1 %collective-permute-start.6 = (bf16[128,1024]{1,0:T(8,128)(2,1)S(1)}, bf16[128,1024]{1,0:T(8,128)(2,1)S(1)}, u32[]{:S(2)}, u32[]{:S(2)}) collective-permute-start(bf16[128,1024]{1,0:T(8,128)(2,1)S(1)} %attend_2.1.rest_0_.refs_1_), channel_id=1, source_target_pairs={{0,16},{4,12},{8,24},{12,4},{16,0},{20,28},{24,8},{28,20},{1,17},{... | collective-permute-start | bytes 786440 | tf_op jit(solution)/shard_map/ppermute | solution.py:351
  33.3 1.7 %collective-permute-start.2 = (bf16[128,1024]{1,0:T(8,128)(2,1)S(1)}, bf16[128,1024]{1,0:T(8,128)(2,1)S(1)}, u32[]{:S(2)}, u32[]{:S(2)}) collective-permute-start(bf16[128,1024]{1,0:T(8,128)(2,1)S(1)} %attend_3.1.refs_1_), channel_id=1, source_target_pairs={{0,8},{4,20},{8,0},{12,28},{16,24},{20,4},{24,16},{28,12},{1,9},{5... | collective-permute-start | bytes 786440 | tf_op jit(solution)/shard_map/ppermute | solution.py:350
  35.9 2.5 %collective-permute-start.10 = (bf16[128,1024]{1,0:T(8,128)(2,1)S(1)}, bf16[128,1024]{1,0:T(8,128)(2,1)S(1)}, u32[]{:S(2)}, u32[]{:S(2)}) collective-permute-start(bf16[128,1024]{1,0:T(8,128)(2,1)S(1)} %collective-permute-done.8.refs_2_), channel_id=1, source_target_pairs={{0,16},{4,12},{8,24},{12,4},{16,0},{20,28},{24,8},{28,20},{1,17},{... | collective-permute-start | bytes 786440 | tf_op jit(solution)/shard_map/ppermute | solution.py:352
  38.4 5.0 %step_0.1 = (f32[512,2048]{1,0:T(8,128)S(1)}, bf16[512,1024]{1,0:T(8,128)(2,1)S(1)}, bf16[1024,2048]{1,0:T(8,128)(2,1)S(1)}) custom-call(s32[16]{0:T(128)S(1)} %copy-done, bf16[128,1024]{1,0:T(8,128)(2,1)S(1)} %attend_0.1.rest_0_.refs_1_, bf16[128,1024]{1,0:T(8,128)(2,1)S(1)} %collective-permute-done.11.refs_2_, ...), custom_call_target="tpu_custom_call" | custom-call | flops 2147483648 | tf_op jit(solution)/shard_map/step_0/pallas_call | solution.py:285
  43.4 4.2 %step_1.1 = (f32[512,2048]{1,0:T(8,128)S(1)}, bf16[1024,2048]{1,0:T(8,128)(2,1)S(1)}) custom-call(bf16[512,1024]{1,0:T(8,128)(2,1)S(1)} %get-tuple-element.32.refs_0_, bf16[1024,2048]{1,0:T(8,128)(2,1)S(1)} %get-tuple-element.33.refs_1_, bf16[4096,4096]{1,0:T(8,128)(2,1)} %refs_2_.7), custom_call_target="tpu_custom_call" | custom-call | flops 2147483648 | tf_op jit(solution)/shard_map/step_1/pallas_call | solution.py:285
  47.7 2.0 %collective-permute-start.7 = (bf16[128,1024]{1,0:T(8,128)(2,1)S(1)}, bf16[128,1024]{1,0:T(8,128)(2,1)S(1)}, u32[]{:S(2)}, u32[]{:S(2)}) collective-permute-start(bf16[128,1024]{1,0:T(8,128)(2,1)S(1)} %collective-permute-done.5.refs_2_), channel_id=1, source_target_pairs={{0,16},{4,12},{8,24},{12,4},{16,0},{20,28},{24,8},{28,20},{1,17},{... | collective-permute-start | bytes 786440 | tf_op jit(solution)/shard_map/ppermute | solution.py:352
  49.8 3.4 %step_2.1 = (f32[512,2048]{1,0:T(8,128)S(1)}, bf16[512,1024]{1,0:T(8,128)(2,1)S(1)}, bf16[1024,2048]{1,0:T(8,128)(2,1)S(1)}) custom-call(s32[16]{0:T(128)S(1)} %copy-done, bf16[128,1024]{1,0:T(8,128)(2,1)S(1)} %attend_1.1.rest_0_.refs_1_, bf16[128,1024]{1,0:T(8,128)(2,1)S(1)} %collective-permute-done.8.refs_2_, ...), custom_call_target="tpu_custom_call", output_to_operand_aliasing={{0}: (7, {})} | custom-call | flops 2147483648 | tf_op jit(solution)/shard_map/step_2/pallas_call | solution.py:285
  53.2 4.6 %step_3.1 = (f32[512,2048]{1,0:T(8,128)S(1)}, bf16[1024,2048]{1,0:T(8,128)(2,1)S(1)}) custom-call(bf16[512,1024]{1,0:T(8,128)(2,1)S(1)} %get-tuple-element.36.refs_0_, bf16[1024,2048]{1,0:T(8,128)(2,1)S(1)} %get-tuple-element.37.refs_1_, bf16[4096,4096]{1,0:T(8,128)(2,1)} %refs_2_.7, ...), custom_call_target="tpu_custom_call", output_to_operand_aliasing={{0}: (3, {})} | custom-call | flops 2147483648 | tf_op jit(solution)/shard_map/step_3/pallas_call | solution.py:285
  57.8 3.3 %step_4.1 = (f32[512,2048]{1,0:T(8,128)S(1)}, bf16[512,1024]{1,0:T(8,128)(2,1)S(1)}, bf16[1024,2048]{1,0:T(8,128)(2,1)S(1)}) custom-call(s32[16]{0:T(128)S(1)} %copy-done, bf16[128,1024]{1,0:T(8,128)(2,1)S(1)} %attend_2.1.rest_0_.refs_1_, bf16[128,1024]{1,0:T(8,128)(2,1)S(1)} %collective-permute-done.5.refs_2_, ...), custom_call_target="tpu_custom_call", output_to_operand_aliasing={{0}: (7, {})} | custom-call | flops 2147483648 | tf_op jit(solution)/shard_map/step_4/pallas_call | solution.py:285
  61.2 4.7 %step_5.1 = (f32[512,2048]{1,0:T(8,128)S(1)}, bf16[1024,2048]{1,0:T(8,128)(2,1)S(1)}) custom-call(bf16[512,1024]{1,0:T(8,128)(2,1)S(1)} %get-tuple-element.41.refs_0_, bf16[1024,2048]{1,0:T(8,128)(2,1)S(1)} %get-tuple-element.42.refs_1_, bf16[4096,4096]{1,0:T(8,128)(2,1)} %refs_2_.7, ...), custom_call_target="tpu_custom_call", output_to_operand_aliasing={{0}: (3, {})} | custom-call | flops 2147483648 | tf_op jit(solution)/shard_map/step_5/pallas_call | solution.py:285
  65.9 3.1 %step_6.1 = (f32[256,2048]{1,0:T(8,128)S(1)}, bf16[256,2048]{1,0:T(8,128)(2,1)S(1)}, bf16[512,1024]{1,0:T(8,128)(2,1)S(1)}, bf16[1024,2048]{1,0:T(8,128)(2,1)S(1)}) custom-call(s32[16]{0:T(128)S(1)} %copy-done, bf16[128,1024]{1,0:T(8,128)(2,1)S(1)} %attend_3.1.refs_1_, bf16[128,1024]{1,0:T(8,128)(2,1)S(1)} %collective-permute-done.2.refs_2_, ...), custom_call_target="tpu_custom_call" | custom-call | flops 2147483648 | tf_op jit(solution)/shard_map/step_6/pallas_call | solution.py:285
  69.1 2.3 %step_7.1 = (f32[256,2048]{1,0:T(8,128)S(1)}, bf16[256,2048]{1,0:T(8,128)(2,1)S(1)}) custom-call(bf16[512,1024]{1,0:T(8,128)(2,1)S(1)} %get-tuple-element.46.refs_0_, bf16[1024,2048]{1,0:T(8,128)(2,1)S(1)} %get-tuple-element.47.refs_1_, bf16[4096,4096]{1,0:T(8,128)(2,1)} %refs_2_.7, f32[512,2048]{1,0:T(8,128)S(1)} %get-tuple-element.48.refs_3_), custom_call_target="tpu_custom_call" | custom-call | flops 2147483648 | tf_op jit(solution)/shard_map/step_7/pallas_call | solution.py:285
  72.0 1.1 %total_0.1.rest_0_ = bf16[256,4096]{1,0:T(8,128)(2,1)} custom-call(f32[256,2048]{1,0:T(8,128)S(1)} %get-tuple-element.51.own_ref, bf16[256,2048]{1,0:T(8,128)(2,1)S(1)} %collective-permute-done.15.got_ref), custom_call_target="tpu_custom_call" | custom-call | flops 524288 | bytes 1048576 | tf_op jit(solution)/shard_map/total_0/pallas_call | solution.py:323
  73.0 1.2 %collective-permute-done.14.got_ref = bf16[256,2048]{1,0:T(8,128)(2,1)S(1)} collective-permute-done((bf16[256,2048]{1,0:T(8,128)(2,1)S(1)}, bf16[256,2048]{1,0:T(8,128)(2,1)S(1)}, u32[]{:S(2)}, u32[]{:S(2)}) %collective-permute-start.14) | collective-permute-done | bytes 1048608 | tf_op jit(solution)/shard_map/ppermute | solution.py:386
  74.3 1.1 %total_1.1 = bf16[256,4096]{1,0:T(8,128)(2,1)} custom-call(f32[256,2048]{1,0:T(8,128)S(1)} %get-tuple-element.49.own_ref, bf16[256,2048]{1,0:T(8,128)(2,1)S(1)} %collective-permute-done.14.got_ref, bf16[256,4096]{1,0:T(8,128)(2,1)} %total_0.1.rest_0_), custom_call_target="tpu_custom_call", output_to_operand_aliasing={{}: (2, {})} | custom-call | flops 524288 | bytes 1048576 | tf_op jit(solution)/shard_map/total_1/pallas_call | solution.py:323
  (26 shorter events, 4.9 us)
Async XLA Ops:
  1.0 10.9 %collective-permute-start = (bf16[128,1024]{1,0:T(8,128)(2,1)S(1)}, bf16[128,1024]{1,0:T(8,128)(2,1)S(1)}, u32[]{:S(2)}, u32[]{:S(2)}) collective-permute-start(bf16[128,1024]{1,0:T(8,128)(2,1)S(1)} %pack.1.kv0), channel_id=1, source_target_pairs={{0,8},{8,16},{16,24},{1,9},{9,17},{17,25},{2,10},{10,18},{18,26},{... | collective-permute-start | bytes 786440 | tf_op jit(solution)/shard_map/ppermute | solution.py:366
  5.9 12.1 %collective-permute-start.1 = (bf16[128,1024]{1,0:T(8,128)(2,1)S(1)}, bf16[128,1024]{1,0:T(8,128)(2,1)S(1)}, u32[]{:S(2)}, u32[]{:S(2)}) collective-permute-start(bf16[128,1024]{1,0:T(8,128)(2,1)S(1)} %pack.1.kv0), channel_id=1, source_target_pairs={{0,16},{8,24},{1,17},{9,25},{2,18},{10,26},{3,19},{11,27},{4,20},{... | collective-permute-start | bytes 786440 | tf_op jit(solution)/shard_map/ppermute | solution.py:367
  18.6 19.8 %copy-start = (s32[16]{0:T(128)S(1)}, s32[16]{0:T(128)}, u32[]{:S(2)}) copy-start(s32[16]{0:T(128)} %refs_0_.7) | copy-start | bytes 196
  18.6 8.0 %collective-permute-start.11 = (bf16[128,1024]{1,0:T(8,128)(2,1)S(1)}, bf16[128,1024]{1,0:T(8,128)(2,1)S(1)}, u32[]{:S(2)}, u32[]{:S(2)}) collective-permute-start(bf16[128,1024]{1,0:T(8,128)(2,1)S(1)} %attend_0.1.rest_0_.refs_1_), channel_id=1, source_target_pairs={{0,8},{4,20},{8,0},{12,28},{16,24},{20,4},{24,16},{28,12},{1,9},{5... | collective-permute-start | bytes 786440 | tf_op jit(solution)/shard_map/ppermute | solution.py:350
  18.7 12.5 %collective-permute-start.12 = (bf16[128,1024]{1,0:T(8,128)(2,1)S(1)}, bf16[128,1024]{1,0:T(8,128)(2,1)S(1)}, u32[]{:S(2)}, u32[]{:S(2)}) collective-permute-start(bf16[128,1024]{1,0:T(8,128)(2,1)S(1)} %attend_0.1.rest_0_.refs_1_), channel_id=1, source_target_pairs={{0,16},{4,12},{8,24},{12,4},{16,0},{20,28},{24,8},{28,20},{1,17},{... | collective-permute-start | bytes 786440 | tf_op jit(solution)/shard_map/ppermute | solution.py:351
  21.9 11.4 %collective-permute-start.8 = (bf16[128,1024]{1,0:T(8,128)(2,1)S(1)}, bf16[128,1024]{1,0:T(8,128)(2,1)S(1)}, u32[]{:S(2)}, u32[]{:S(2)}) collective-permute-start(bf16[128,1024]{1,0:T(8,128)(2,1)S(1)} %attend_1.1.rest_0_.refs_1_), channel_id=1, source_target_pairs={{0,8},{4,20},{8,0},{12,28},{16,24},{20,4},{24,16},{28,12},{1,9},{5... | collective-permute-start | bytes 786440 | tf_op jit(solution)/shard_map/ppermute | solution.py:350
  26.6 9.3 %collective-permute-start.13 = (bf16[128,1024]{1,0:T(8,128)(2,1)S(1)}, bf16[128,1024]{1,0:T(8,128)(2,1)S(1)}, u32[]{:S(2)}, u32[]{:S(2)}) collective-permute-start(bf16[128,1024]{1,0:T(8,128)(2,1)S(1)} %collective-permute-done.11.refs_2_), channel_id=1, source_target_pairs={{0,16},{4,12},{8,24},{12,4},{16,0},{20,28},{24,8},{28,20},{1,17},{... | collective-permute-start | bytes 786440 | tf_op jit(solution)/shard_map/ppermute | solution.py:352
  29.5 18.2 %collective-permute-start.9 = (bf16[128,1024]{1,0:T(8,128)(2,1)S(1)}, bf16[128,1024]{1,0:T(8,128)(2,1)S(1)}, u32[]{:S(2)}, u32[]{:S(2)}) collective-permute-start(bf16[128,1024]{1,0:T(8,128)(2,1)S(1)} %attend_1.1.rest_0_.refs_1_), channel_id=1, source_target_pairs={{0,16},{4,12},{8,24},{12,4},{16,0},{20,28},{24,8},{28,20},{1,17},{... | collective-permute-start | bytes 786440 | tf_op jit(solution)/shard_map/ppermute | solution.py:351
  30.2 17.5 %collective-permute-start.5 = (bf16[128,1024]{1,0:T(8,128)(2,1)S(1)}, bf16[128,1024]{1,0:T(8,128)(2,1)S(1)}, u32[]{:S(2)}, u32[]{:S(2)}) collective-permute-start(bf16[128,1024]{1,0:T(8,128)(2,1)S(1)} %attend_2.1.rest_0_.refs_1_), channel_id=1, source_target_pairs={{0,8},{4,20},{8,0},{12,28},{16,24},{20,4},{24,16},{28,12},{1,9},{5... | collective-permute-start | bytes 786440 | tf_op jit(solution)/shard_map/ppermute | solution.py:350
  31.3 26.5 %collective-permute-start.6 = (bf16[128,1024]{1,0:T(8,128)(2,1)S(1)}, bf16[128,1024]{1,0:T(8,128)(2,1)S(1)}, u32[]{:S(2)}, u32[]{:S(2)}) collective-permute-start(bf16[128,1024]{1,0:T(8,128)(2,1)S(1)} %attend_2.1.rest_0_.refs_1_), channel_id=1, source_target_pairs={{0,16},{4,12},{8,24},{12,4},{16,0},{20,28},{24,8},{28,20},{1,17},{... | collective-permute-start | bytes 786440 | tf_op jit(solution)/shard_map/ppermute | solution.py:351
  33.3 16.4 %collective-permute-start.2 = (bf16[128,1024]{1,0:T(8,128)(2,1)S(1)}, bf16[128,1024]{1,0:T(8,128)(2,1)S(1)}, u32[]{:S(2)}, u32[]{:S(2)}) collective-permute-start(bf16[128,1024]{1,0:T(8,128)(2,1)S(1)} %attend_3.1.refs_1_), channel_id=1, source_target_pairs={{0,8},{4,20},{8,0},{12,28},{16,24},{20,4},{24,16},{28,12},{1,9},{5... | collective-permute-start | bytes 786440 | tf_op jit(solution)/shard_map/ppermute | solution.py:350
  35.9 13.9 %collective-permute-start.10 = (bf16[128,1024]{1,0:T(8,128)(2,1)S(1)}, bf16[128,1024]{1,0:T(8,128)(2,1)S(1)}, u32[]{:S(2)}, u32[]{:S(2)}) collective-permute-start(bf16[128,1024]{1,0:T(8,128)(2,1)S(1)} %collective-permute-done.8.refs_2_), channel_id=1, source_target_pairs={{0,16},{4,12},{8,24},{12,4},{16,0},{20,28},{24,8},{28,20},{1,17},{... | collective-permute-start | bytes 786440 | tf_op jit(solution)/shard_map/ppermute | solution.py:352
  47.7 18.2 %collective-permute-start.3 = (bf16[128,1024]{1,0:T(8,128)(2,1)S(1)}, bf16[128,1024]{1,0:T(8,128)(2,1)S(1)}, u32[]{:S(2)}, u32[]{:S(2)}) collective-permute-start(bf16[128,1024]{1,0:T(8,128)(2,1)S(1)} %attend_3.1.refs_1_), channel_id=1, source_target_pairs={{0,16},{4,12},{8,24},{12,4},{16,0},{20,28},{24,8},{28,20},{1,17},{... | collective-permute-start | bytes 786440 | tf_op jit(solution)/shard_map/ppermute | solution.py:351
  47.7 10.1 %collective-permute-start.7 = (bf16[128,1024]{1,0:T(8,128)(2,1)S(1)}, bf16[128,1024]{1,0:T(8,128)(2,1)S(1)}, u32[]{:S(2)}, u32[]{:S(2)}) collective-permute-start(bf16[128,1024]{1,0:T(8,128)(2,1)S(1)} %collective-permute-done.5.refs_2_), channel_id=1, source_target_pairs={{0,16},{4,12},{8,24},{12,4},{16,0},{20,28},{24,8},{28,20},{1,17},{... | collective-permute-start | bytes 786440 | tf_op jit(solution)/shard_map/ppermute | solution.py:352
  49.8 16.2 %collective-permute-start.4 = (bf16[128,1024]{1,0:T(8,128)(2,1)S(1)}, bf16[128,1024]{1,0:T(8,128)(2,1)S(1)}, u32[]{:S(2)}, u32[]{:S(2)}) collective-permute-start(bf16[128,1024]{1,0:T(8,128)(2,1)S(1)} %collective-permute-done.2.refs_2_), channel_id=1, source_target_pairs={{0,16},{4,12},{8,24},{12,4},{16,0},{20,28},{24,8},{28,20},{1,17},{... | collective-permute-start | bytes 786440 | tf_op jit(solution)/shard_map/ppermute | solution.py:352
  69.0 3.0 %collective-permute-start.15 = (bf16[256,2048]{1,0:T(8,128)(2,1)S(1)}, bf16[256,2048]{1,0:T(8,128)(2,1)S(1)}, u32[]{:S(2)}, u32[]{:S(2)}) collective-permute-start(bf16[256,2048]{1,0:T(8,128)(2,1)S(1)} %get-tuple-element.52), channel_id=1, source_target_pairs={{0,4},{4,0},{1,5},{5,1},{2,6},{6,2},{3,7},{7,3},{8,12},{12,8},{9,1... | collective-permute-start | bytes 3145736 | tf_op jit(solution)/shard_map/ppermute | solution.py:386
  71.4 2.8 %collective-permute-start.14 = (bf16[256,2048]{1,0:T(8,128)(2,1)S(1)}, bf16[256,2048]{1,0:T(8,128)(2,1)S(1)}, u32[]{:S(2)}, u32[]{:S(2)}) collective-permute-start(bf16[256,2048]{1,0:T(8,128)(2,1)S(1)} %get-tuple-element.50), channel_id=1, source_target_pairs={{0,4},{4,0},{1,5},{5,1},{2,6},{6,2},{3,7},{7,3},{8,12},{12,8},{9,1... | collective-permute-start | bytes 3145736 | tf_op jit(solution)/shard_map/ppermute | solution.py:386

commit v3 on v2

--- a/solution.py
+++ b/solution.py
@@ -77,36 +77,28 @@
     return pltpu.with_memory_space_constraint(x, pltpu.HBM)
 
 
-def pack_kernel(k_hbm, v_hbm, kv_ref, sems):
-    columns = k_hbm.shape[1]
-    copies = [
-        pltpu.make_async_copy(k_hbm, kv_ref.at[:, :columns], sems.at[0]),
-        pltpu.make_async_copy(v_hbm, kv_ref.at[:, columns:], sems.at[1]),
-    ]
-    for copy in copies:
-        copy.start()
-    for copy in copies:
-        copy.wait()
-
-
-def pack(key_rows, value_rows):
-    rows, columns = key_rows.shape
-    return pl.pallas_call(
-        pack_kernel,
-        out_shape=jax.ShapeDtypeStruct((rows, 2 * columns), jnp.bfloat16),
-        in_specs=[HBM, HBM],
-        out_specs=VMEM,
-        scratch_shapes=[pltpu.SemaphoreType.DMA((2,))],
-        compiler_params=pltpu.CompilerParams(vmem_limit_bytes=4 * MIB),
-        name="pack",
-    )(in_hbm(key_rows), in_hbm(value_rows))
-
-
-def prepare_kernel(docs_hbm, q_hbm, w_hbm, q_ref, mask_ref, w_ref, docs, sems):
+TOKEN = jax.ShapeDtypeStruct((8, 128), jnp.float32)
+
+
+def block_shape(w_out, chunks):
+    return w_out.shape[0] // chunks, w_out.shape[1] // HALVES
+
+
+def block_copy(w_hbm, index, w_ref, sem):
+    depth, columns = w_ref.shape
+    row, column = index // HALVES * depth, index % HALVES * columns
+    return pltpu.make_async_copy(
+        w_hbm.at[row:row + depth, column:column + columns], w_ref, sem
+    )
+
+
+def prepare_kernel(docs_hbm, k_hbm, v_hbm, q_hbm, w_hbm, after, k_ref, v_ref, q_ref, mask_ref, w_ref, docs, sems):
     lengths = pltpu.make_async_copy(docs_hbm, docs, sems.at[0])
     loads = [
-        pltpu.make_async_copy(q_hbm, q_ref, sems.at[1]),
-        block_copy(w_hbm, 0, w_ref, sems.at[2]),
+        pltpu.make_async_copy(k_hbm, k_ref, sems.at[1]),
+        pltpu.make_async_copy(v_hbm, v_ref, sems.at[2]),
+        pltpu.make_async_copy(q_hbm, q_ref, sems.at[3]),
+        block_copy(w_hbm, 0, w_ref, sems.at[4]),
     ]
     lengths.start()
     for load in loads:
@@ -126,84 +118,111 @@
         load.wait()
 
 
-def block_shape(w_out, chunks):
-    return w_out.shape[0] // chunks, w_out.shape[1] // HALVES
-
-
-def block_copy(w_hbm, index, w_ref, sem):
-    depth, columns = w_ref.shape
-    row, column = index // HALVES * depth, index % HALVES * columns
-    return pltpu.make_async_copy(
-        w_hbm.at[row:row + depth, column:column + columns], w_ref, sem
-    )
-
-
-def prepare(doc_lengths, queries, w_out, chunks):
+def prepare(doc_lengths, key_rows, value_rows, queries, w_out, chunks, after):
     rows = queries.shape[0]
     return pl.pallas_call(
         prepare_kernel,
         out_shape=[
+            jax.ShapeDtypeStruct(key_rows.shape, jnp.bfloat16),
+            jax.ShapeDtypeStruct(value_rows.shape, jnp.bfloat16),
             jax.ShapeDtypeStruct(queries.shape, jnp.bfloat16),
             jax.ShapeDtypeStruct((rows, 3 * rows), jnp.float32),
             jax.ShapeDtypeStruct(block_shape(w_out, chunks), jnp.bfloat16),
         ],
-        in_specs=[HBM] * 3,
-        out_specs=[VMEM] * 3,
+        in_specs=[HBM] * 6,
+        out_specs=[VMEM] * 5,
         scratch_shapes=[
             pltpu.SMEM(doc_lengths.shape, jnp.int32),
-            pltpu.SemaphoreType.DMA((3,)),
+            pltpu.SemaphoreType.DMA((5,)),
         ],
         compiler_params=pltpu.CompilerParams(vmem_limit_bytes=4 * MIB),
-        cost_estimate=pl.CostEstimate(flops=0, bytes_accessed=0, transcendentals=0),
+        cost_estimate=pl.CostEstimate(
+            flops=0, bytes_accessed=w_out.size // chunks, transcendentals=0
+        ),
         name="prepare",
-    )(in_hbm(doc_lengths), in_hbm(queries), w_out)
-
-
-def attend_kernel(g, q_ref, mask_ref, kv0, kv1, kv2, *rest):
+    )(
+        in_hbm(doc_lengths), in_hbm(key_rows), in_hbm(value_rows), in_hbm(queries), w_out, after
+    )
+
+
+def load_kernel(indexes, after, w_hbm, *refs):
+    *w_refs, token, sems = refs
+    loads = [
+        block_copy(w_hbm, index, w_ref, sems.at[i])
+        for i, (index, w_ref) in enumerate(zip(indexes, w_refs))
+    ]
+    for load in loads:
+        load.start()
+    token[...] = jnp.zeros_like(token)
+    for load in loads:
+        load.wait()
+
+
+def load_blocks(indexes, w_out, chunks, after):
+    shape = block_shape(w_out, chunks)
+    *blocks, token = pl.pallas_call(
+        functools.partial(load_kernel, indexes),
+        out_shape=[jax.ShapeDtypeStruct(shape, jnp.bfloat16)] * len(indexes) + [TOKEN],
+        in_specs=[HBM, HBM],
+        out_specs=[VMEM] * (len(indexes) + 1),
+        scratch_shapes=[pltpu.SemaphoreType.DMA((len(indexes),))],
+        compiler_params=pltpu.CompilerParams(vmem_limit_bytes=1 * MIB),
+        cost_estimate=pl.CostEstimate(
+            flops=0, bytes_accessed=4 * len(indexes) * shape[0] * shape[1], transcendentals=0
+        ),
+        name=f"load_{indexes[0]}",
+    )(after, w_out)
+    return blocks, token
+
+
+def attend_kernel(groups, q_ref, mask_ref, k0, k_near, k_far, k2, v0, v_near, v_far, v2, *rest):
     out_ref = rest[-1]
-    rows, width = out_ref.shape
+    rows = out_ref.shape[0]
+    width = out_ref.shape[1] // len(groups)
     heads = width // HD
     window = 3 * rows
     factor = HD ** -0.5 * math.log2(math.e)
-    half = kv0.shape[1] // 2
-    at_k = slice(g * HD, (g + 1) * HD)
-    at_v = slice(half + g * HD, half + (g + 1) * HD)
-    keys = jnp.concatenate([kv2[:, at_k], kv1[:, at_k], kv0[:, at_k]], axis=0)
-    values = jnp.concatenate([kv2[:, at_v], kv1[:, at_v], kv0[:, at_v]], axis=0)
-    stacked = jnp.concatenate(
-        [q_ref[:, g * width + h * HD:g * width + (h + 1) * HD] for h in range(heads)], axis=0
-    )
-    scores = lax.dot_general(
-        stacked, keys, (((1,), (1,)), ((), ())), preferred_element_type=jnp.float32
-    ).reshape(heads, rows, window)
-    scores = scores + mask_ref[...][None]
-    top = jnp.max(scores, axis=2, keepdims=True)
-    weights = jnp.exp2((scores - top) * factor)
-    total = jnp.sum(weights, axis=2, keepdims=True)
-    mixed = jnp.dot(
-        weights.astype(jnp.bfloat16).reshape(heads * rows, window),
-        values,
-        preferred_element_type=jnp.float32,
-    ).reshape(heads, rows, HD)
-    result = (mixed / total).astype(jnp.bfloat16)
-    for h in range(heads):
-        out_ref[:, h * HD:(h + 1) * HD] = result[h]
-
-
-def attend(g, width, queries, mask, kv, after):
+    across = lax.axis_index("ctx") == 2
+    for i, g in enumerate(groups):
+        at = slice(g * HD, (g + 1) * HD)
+        k1 = jnp.where(across, k_far[:, at], k_near[:, at])
+        v1 = jnp.where(across, v_far[:, at], v_near[:, at])
+        keys = jnp.concatenate([k2[:, at], k1, k0[:, at]], axis=0)
+        values = jnp.concatenate([v2[:, at], v1, v0[:, at]], axis=0)
+        stacked = jnp.concatenate(
+            [q_ref[:, g * width + h * HD:g * width + (h + 1) * HD] for h in range(heads)], axis=0
+        )
+        scores = lax.dot_general(
+            stacked, keys, (((1,), (1,)), ((), ())), preferred_element_type=jnp.float32
+        ).reshape(heads, rows, window)
+        scores = scores + mask_ref[...][None]
+        top = jnp.max(scores, axis=2, keepdims=True)
+        weights = jnp.exp2((scores - top) * factor)
+        total = jnp.sum(weights, axis=2, keepdims=True)
+        mixed = jnp.dot(
+            weights.astype(jnp.bfloat16).reshape(heads * rows, window),
+            values,
+            preferred_element_type=jnp.float32,
+        ).reshape(heads, rows, HD)
+        result = (mixed / total).astype(jnp.bfloat16)
+        for h in range(heads):
+            out_ref[:, i * width + h * HD:i * width + (h + 1) * HD] = result[h]
+
+
+def attend(groups, width, queries, mask, keys, values, after):
     rows = queries.shape[0]
     return pl.pallas_call(
-        functools.partial(attend_kernel, g),
-        out_shape=jax.ShapeDtypeStruct((rows, width), jnp.bfloat16),
-        in_specs=[VMEM] * 5 + [HBM] * len(after),
+        functools.partial(attend_kernel, groups),
+        out_shape=jax.ShapeDtypeStruct((rows, len(groups) * width), jnp.bfloat16),
+        in_specs=[VMEM] * 10 + [HBM] * len(after),
         out_specs=VMEM,
-        compiler_params=pltpu.CompilerParams(vmem_limit_bytes=16 * MIB),
+        compiler_params=pltpu.CompilerParams(vmem_limit_bytes=8 * MIB),
         cost_estimate=pl.CostEstimate(flops=0, bytes_accessed=0, transcendentals=0),
-        name=f"attend_{g}",
-    )(queries, mask, *kv, *after)
-
-
-def lay_out(plan, pieces, lhs):
+        name=f"attend_{groups[0]}",
+    )(queries, mask, *keys, *values, *after)
+
+
+def lay_out(plan, pieces, column, lhs):
     here = lax.axis_index("ctx")
     core = lax.axis_index("tp")
     first = jnp.where(core == 0, 1, 2)
@@ -218,30 +237,30 @@
                 slot = jnp.where(wanted[s] == owner * 4 + u, s, slot)
             slot = slot ^ swap
             at = pl.ds(pl.multiple_of(slot * unit_rows, unit_rows), unit_rows)
-            lhs[at, :] = piece[u * unit_rows:(u + 1) * unit_rows, :]
-
-
-def step_kernel(index, last, first_half, has_acc, *refs):
-    refs = list(refs)
+            lhs[at, :] = piece[u * unit_rows:(u + 1) * unit_rows, column:column + lhs.shape[1]]
+
+
+def step_kernel(index, last, column, has_acc, has_after, *refs):
+    refs = list(refs)[has_after:]
+    first_half = index % HALVES == 0
+    load = None
     if first_half:
         plan, *pieces = refs[:5]
-        del refs[:5]
-    else:
-        lhs = refs.pop(0)
-    w_ref, w_hbm = refs[:2]
-    del refs[:2]
-    acc_ref = refs.pop(0) if has_acc else None
-    has_next = not (last and not first_half)
-    sem = refs.pop() if has_next else None
-    next_ref = refs.pop() if has_next else None
-    if first_half:
+        w_hbm = refs[5]
+        del refs[:6]
+        sem = refs.pop()
+        token = refs.pop()
+        next_ref = refs.pop()
         lhs = refs.pop()
-    load = None
-    if has_next:
         load = block_copy(w_hbm, index + 1, next_ref, sem)
         load.start()
-    if first_half:
-        lay_out(plan, pieces, lhs)
+        lay_out(plan, pieces, column, lhs)
+    else:
+        token = refs.pop()
+        lhs = refs.pop(0)
+    token[...] = jnp.zeros_like(token)
+    w_ref = refs.pop(0)
+    acc_ref = refs.pop(0) if has_acc else None
     rows = lhs.shape[0] // 2
     for at in range(0, w_ref.shape[1], TILE):
         to = slice(at, at + TILE)
@@ -258,46 +277,45 @@
         load.wait()
 
 
-def step(index, last, rows_in, block, w_out, acc):
+def step(index, last, rows_in, column, block, w_out, acc, after):
     first_half = index % HALVES == 0
-    has_acc = acc is not None
-    has_next = not (last and not first_half)
+    has_acc, has_after = acc is not None, after is not None
     depth, columns = block.shape
     if first_half:
         plan, pieces = rows_in
         total_rows = 4 * pieces[0].shape[0]
-        operands, specs = [plan, *pieces], [SMEM] + [VMEM] * 4
+        operands, specs = [plan, *pieces, w_out], [SMEM] + [VMEM] * 4 + [HBM]
     else:
         total_rows = rows_in.shape[0]
         operands, specs = [rows_in], [VMEM]
     if last:
-        half = (total_rows // 2, columns)
-        shapes = [jax.ShapeDtypeStruct(half, jnp.float32), jax.ShapeDtypeStruct(half, jnp.bfloat16)]
+        part = (total_rows // 2, columns)
+        shapes = [jax.ShapeDtypeStruct(part, jnp.float32), jax.ShapeDtypeStruct(part, jnp.bfloat16)]
     else:
         shapes = [jax.ShapeDtypeStruct((total_rows, columns), jnp.float32)]
     if first_half:
         shapes.append(jax.ShapeDtypeStruct((total_rows, depth), jnp.bfloat16))
-    if has_next:
         shapes.append(jax.ShapeDtypeStruct(block.shape, jnp.bfloat16))
-    operands += [block, w_out] + [acc] * has_acc
-    specs += [VMEM, HBM] + [VMEM] * has_acc
-    alias = {len(operands) - 1: 0} if has_acc and not last else {}
+    shapes.append(TOKEN)
+    operands = [after] * has_after + operands + [block] + [acc] * has_acc
+    specs = [HBM] * has_after + specs + [VMEM] * (1 + has_acc)
     results = list(pl.pallas_call(
-        functools.partial(step_kernel, index, last, first_half, has_acc),
+        functools.partial(step_kernel, index, last, column, has_acc, has_after),
         out_shape=shapes,
         in_specs=specs,
         out_specs=[VMEM] * len(shapes),
-        scratch_shapes=[pltpu.SemaphoreType.DMA] * has_next,
-        input_output_aliases=alias,
-        compiler_params=pltpu.CompilerParams(vmem_limit_bytes=8 * MIB),
+        scratch_shapes=[pltpu.SemaphoreType.DMA] * first_half,
+        input_output_aliases={len(operands) - 1: 0} if has_acc and not last else {},
+        compiler_params=pltpu.CompilerParams(vmem_limit_bytes=6 * MIB),
         cost_estimate=pl.CostEstimate(
             flops=2 * total_rows * depth * columns, bytes_accessed=0, transcendentals=0
         ),
         name=f"step_{index}",
     )(*operands))
-    following = results.pop() if has_next else None
+    token = results.pop()
+    following = results.pop() if first_half else None
     lhs = results.pop() if first_half else None
-    return results, lhs, following
+    return results, lhs, following, token
 
 
 def total_kernel(first, has_out, own_ref, got_ref, *rest):
@@ -359,33 +377,52 @@
     w_out = in_hbm(w_out)
     kv_heads = key_rows.shape[1] // HD
     width = queries.shape[1] // kv_heads
-    kv = pack(key_rows, value_rows)
-    held, mask, block = prepare(doc_lengths, queries, w_out, kv_heads)
-    window = (
-        kv,
-        lax.ppermute(kv, "ctx", [(0, 1), (1, 2), (2, 3)]),
-        lax.ppermute(kv, "ctx", [(0, 2), (1, 3)]),
-    )
-    gathered, after = [], []
-    for g in range(kv_heads):
-        own = attend(g, width, held, mask, window, after)
+    two = [(0, 2), (1, 3)]
+    value_two = lax.ppermute(value_rows, "ctx", two)
+    key_two = lax.ppermute(key_rows, "ctx", two)
+    key_near = lax.ppermute(key_rows, "ctx", [(0, 1), (1, 2), (2, 3)])
+    value_near = lax.ppermute(value_rows, "ctx", [(0, 1), (2, 3)])
+    value_far = lax.ppermute(value_two, "ctx", [(3, 2)])
+    own_keys, own_values, held, mask, block = prepare(
+        doc_lengths, key_rows, value_rows, queries, w_out, kv_heads, value_two
+    )
+    keys = (own_keys, key_near, key_near, key_two)
+    values = (own_values, value_near, value_far, value_two)
+    state = {"blocks": {0: block}, "totals": [None] * HALVES, "before": None}
+    gathered, mine, got = [], [], []
+
+    def rows_of(g, after):
+        own = attend((g,), width, held, mask, keys, values, after)
         gathered.append(gather_rows(own))
-        after = [own]
-    totals = [None] * HALVES
-    mine, got = [], []
-    for g in range(kv_heads):
+        return own
+
+    def load(wanted, after):
+        loaded, token = load_blocks([g * HALVES for g in wanted], w_out, kv_heads, after)
+        state["blocks"].update(zip(wanted, loaded))
+        return token
+
+    def steps(g):
         last = g == kv_heads - 1
-        rows_in = (unit_source, gathered[g])
+        rows_in, block = (unit_source, gathered[g]), state["blocks"][g]
         for half in range(HALVES):
-            results, lhs, block = step(
-                g * HALVES + half, last, rows_in, block, w_out, totals[half]
+            results, rows_in, block, state["before"] = step(
+                g * HALVES + half, last, rows_in, 0, block, w_out,
+                state["totals"][half], state["before"],
             )
-            rows_in = lhs
             if last:
                 mine.append(results[0])
                 got.append(lax.ppermute(results[1], "tp", [(0, 1), (1, 0)]))
             else:
-                totals[half] = results[0]
+                state["totals"][half] = results[0]
+        return state["before"]
+
+    own = rows_of(0, [])
+    own = rows_of(1, [load((1,), own)])
+    own = rows_of(2, [load((2, 3), own), *gathered[0][1:2]])
+    done = steps(0)
+    rows_of(3, [own, done])
+    for g in range(1, kv_heads):
+        steps(g)
     columns = w_out.shape[1] // HALVES
     out = None
     for half in range(HALVES):

time: 75.8 us -> 70.2 us (0.926)
  waiting for transfers between devices: 10.8 us -> 3.33 us
  starting transfers between devices: 25.3 us -> 27.1 us
    ppermute x4 -> x7, waiting for transfers between devices: 7.29 us -> 1.43 us  [the longest x2 1.18 us: steps(): got.append(lax.ppermute(results[1], 'tp', [(0, 1), (1, 0)]))]
    ppermute x4, starting transfers between devices: 7.47 us -> 2.94 us  [gather_rows(): far = lax.ppermute(near, ('ctx', 'tp'), route(False))]
    ppermute x4 -> x7, starting transfers between devices: 8.92 us -> 12.7 us  [the longest x1 4.87 us: local(): value_two = lax.ppermute(value_rows, 'ctx', two)]
    ppermute x4, starting transfers between devices: 4.18 us -> 6.49 us  [gather_rows(): near = lax.ppermute(own, ('ctx', 'tp'), route(True))]
    ppermute x4, waiting for transfers between devices: 0.87 us -> 0.01 us  [gather_rows(): far = lax.ppermute(near, ('ctx', 'tp'), route(False))]
    ppermute x4, waiting for transfers between devices: 2.64 us -> 1.88 us  [gather_rows(): near = lax.ppermute(own, ('ctx', 'tp'), route(True))]
    pallas_call x14 -> x15, Pallas kernels: 36.8 us -> 36.9 us  [the longest x8 25.7 us: step(): pl.pallas_call(functools.partial(step_kernel, index, last, column, has_ac...]
  transfers between devices with their start and end apart: 16 -> 19, of which waited for: 4 -> 4; matrix products, arithmetic and copies ran while one was open for 0% -> 0% of each run, Pallas kernels for 44% -> 49%
where the time goes in v3:
time: 70.2 us; the launch traced here: 69.9 us
  Pallas kernels  39.1 us (56%)
  starting transfers between devices  27.1 us (39%)
  waiting for transfers between devices  3.33 us (5%)
    pallas_call x8, Pallas kernels, step(): pl.pallas_call(functools.partial(step_kernel, index, last, column, has_ac...  25.7 us
    ppermute x4, starting transfers between devices, gather_rows(): near = lax.ppermute(own, ('ctx', 'tp'), route(True))  6.49 us
    pallas_call x2, Pallas kernels, load_blocks(): pl.pallas_call(functools.partial(load_kernel, indexes), out_shape=[jax.Sh...  5.68 us
    ppermute x4, starting transfers between devices, gather_rows(): side = lax.ppermute(own, ('ctx', 'tp'), route(False))  4.92 us
    ppermute x1, starting transfers between devices, local(): value_two = lax.ppermute(value_rows, 'ctx', two)  4.87 us
    ppermute x1, starting transfers between devices, local(): key_near = lax.ppermute(key_rows, 'ctx', [(0, 1), (1, 2), (2, 3)])  3.4 us
    ppermute x4, starting transfers between devices, gather_rows(): far = lax.ppermute(near, ('ctx', 'tp'), route(False))  2.94 us
    pallas_call x4, Pallas kernels, attend(): pl.pallas_call(functools.partial(attend_kernel, groups), out_shape=jax.Sh...  2.81 us
  transfers between devices with their start and end apart: 19, of which 4 were waited for; matrix products, arithmetic and copies ran while one was open for 0% of the time, Pallas kernels for 49%

profile of v3, /device:TPU:0, one launch (start us, length us, event | category | flops | bytes accessed | tf_op | source)
XLA Modules:
  0.0 69.9 jit_solution(3309060443368596828)
XLA Ops:
  0.0 4.9 %collective-permute-start = (bf16[128,512]{1,0:T(8,128)(2,1)}, bf16[128,512]{1,0:T(8,128)(2,1)S(1)}, u32[]{:S(2)}, u32[]{:S(2)}) collective-permute-start(bf16[128,512]{1,0:T(8,128)(2,1)} %v_hbm.1), channel_id=1, source_target_pairs={{0,16},{8,24},{1,17},{9,25},{2,18},{10,26},{3,19},{11,27},{4,20},{... | collective-permute-start | bytes 393224 | tf_op jit(solution)/shard_map/ppermute | solution.py:381
  4.9 1.3 %collective-permute-start.2 = (bf16[128,512]{1,0:T(8,128)(2,1)}, bf16[128,512]{1,0:T(8,128)(2,1)S(1)}, u32[]{:S(2)}, u32[]{:S(2)}) collective-permute-start(bf16[128,512]{1,0:T(8,128)(2,1)} %k_hbm.1), channel_id=1, source_target_pairs={{0,16},{8,24},{1,17},{9,25},{2,18},{10,26},{3,19},{11,27},{4,20},{... | collective-permute-start | bytes 393224 | tf_op jit(solution)/shard_map/ppermute | solution.py:382
  6.2 3.4 %collective-permute-start.1 = (bf16[128,512]{1,0:T(8,128)(2,1)}, bf16[128,512]{1,0:T(8,128)(2,1)S(1)}, u32[]{:S(2)}, u32[]{:S(2)}) collective-permute-start(bf16[128,512]{1,0:T(8,128)(2,1)} %k_hbm.1), channel_id=1, source_target_pairs={{0,8},{8,16},{16,24},{1,9},{9,17},{17,25},{2,10},{10,18},{18,26},{... | collective-permute-start | bytes 393224 | tf_op jit(solution)/shard_map/ppermute | solution.py:383
  9.6 1.9 %collective-permute-start.3 = (bf16[128,512]{1,0:T(8,128)(2,1)}, bf16[128,512]{1,0:T(8,128)(2,1)S(1)}, u32[]{:S(2)}, u32[]{:S(2)}) collective-permute-start(bf16[128,512]{1,0:T(8,128)(2,1)} %v_hbm.1), channel_id=1, source_target_pairs={{0,8},{16,24},{1,9},{17,25},{2,10},{18,26},{3,11},{19,27},{4,12},{... | collective-permute-start | bytes 393224 | tf_op jit(solution)/shard_map/ppermute | solution.py:384
  12.2 2.7 %prepare.1 = (bf16[128,512]{1,0:T(8,128)(2,1)S(1)}, bf16[128,512]{1,0:T(8,128)(2,1)S(1)}, bf16[128,4096]{1,0:T(8,128)(2,1)S(1)}, f32[128,384]{1,0:T(8,128)S(1)}, bf16[1024,2048]{1,0:T(8,128)(2,1)S(1)}) custom-call(s32[8]{0:T(128)} %docs_hbm.1, bf16[128,512]{1,0:T(8,128)(2,1)} %k_hbm.1, bf16[128,512]{1,0:T(8,128)(2,1)} %v_hbm.1, bf16[128,4096]{1,0:T(8,128)(2,1)} %q_hbm.1, ...), custom_call_target="tpu_custom_call" | custom-call | bytes 4194304 | tf_op jit(solution)/shard_map/prepare/pallas_call | solution.py:123
  15.9 2.4 %collective-permute-start.5 = (bf16[128,1024]{1,0:T(8,128)(2,1)S(1)}, bf16[128,1024]{1,0:T(8,128)(2,1)S(1)}, u32[]{:S(2)}, u32[]{:S(2)}) collective-permute-start(bf16[128,1024]{1,0:T(8,128)(2,1)S(1)} %attend_0.1.refs_1_.after), channel_id=1, source_target_pairs={{0,8},{4,20},{8,0},{12,28},{16,24},{20,4},{24,16},{28,12},{1,9},{5... | collective-permute-start | bytes 786440 | tf_op jit(solution)/shard_map/ppermute | solution.py:368
  19.1 2.2 %load_2.1 = (bf16[1024,2048]{1,0:T(8,128)(2,1)S(1)}, f32[8,128]{1,0:T(8,128)S(1)}) custom-call(bf16[128,1024]{1,0:T(8,128)(2,1)S(1)} %attend_0.1.refs_1_.after, bf16[4096,4096]{1,0:T(8,128)(2,1)} %refs_6_.5), custom_call_target="tpu_custom_call" | custom-call | bytes 8388608 | tf_op jit(solution)/shard_map/load_2/pallas_call | solution.py:163
  22.1 2.0 %collective-permute-start.8 = (bf16[128,1024]{1,0:T(8,128)(2,1)S(1)}, bf16[128,1024]{1,0:T(8,128)(2,1)S(1)}, u32[]{:S(2)}, u32[]{:S(2)}) collective-permute-start(bf16[128,1024]{1,0:T(8,128)(2,1)S(1)} %attend_1.1.refs_2_.after), channel_id=1, source_target_pairs={{0,8},{4,20},{8,0},{12,28},{16,24},{20,4},{24,16},{28,12},{1,9},{5... | collective-permute-start | bytes 786440 | tf_op jit(solution)/shard_map/ppermute | solution.py:368
  24.8 1.9 %collective-permute-start.7 = (bf16[128,1024]{1,0:T(8,128)(2,1)S(1)}, bf16[128,1024]{1,0:T(8,128)(2,1)S(1)}, u32[]{:S(2)}, u32[]{:S(2)}) collective-permute-start(bf16[128,1024]{1,0:T(8,128)(2,1)S(1)} %collective-permute-done.5.refs_2_.rest_1_), channel_id=1, source_target_pairs={{0,16},{4,12},{8,24},{12,4},{16,0},{20,28},{24,8},{28,20},{1,17},{... | collective-permute-start | bytes 786440 | tf_op jit(solution)/shard_map/ppermute | solution.py:370
  26.8 3.5 %load_4.1 = (bf16[1024,2048]{1,0:T(8,128)(2,1)S(1)}, bf16[1024,2048]{1,0:T(8,128)(2,1)S(1)}, f32[8,128]{1,0:T(8,128)S(1)}) custom-call(bf16[128,1024]{1,0:T(8,128)(2,1)S(1)} %attend_1.1.refs_2_.after, bf16[4096,4096]{1,0:T(8,128)(2,1)} %refs_6_.5), custom_call_target="tpu_custom_call" | custom-call | bytes 16777216 | tf_op jit(solution)/shard_map/load_4/pallas_call | solution.py:163
  31.0 2.0 %collective-permute-start.12 = (bf16[128,1024]{1,0:T(8,128)(2,1)S(1)}, bf16[128,1024]{1,0:T(8,128)(2,1)S(1)}, u32[]{:S(2)}, u32[]{:S(2)}) collective-permute-start(bf16[128,1024]{1,0:T(8,128)(2,1)S(1)} %attend_2.1.refs_2_.rest_0_), channel_id=1, source_target_pairs={{0,16},{4,12},{8,24},{12,4},{16,0},{20,28},{24,8},{28,20},{1,17},{... | collective-permute-start | bytes 786440 | tf_op jit(solution)/shard_map/ppermute | solution.py:369
  33.0 1.5 %collective-permute-start.11 = (bf16[128,1024]{1,0:T(8,128)(2,1)S(1)}, bf16[128,1024]{1,0:T(8,128)(2,1)S(1)}, u32[]{:S(2)}, u32[]{:S(2)}) collective-permute-start(bf16[128,1024]{1,0:T(8,128)(2,1)S(1)} %attend_2.1.refs_2_.rest_0_), channel_id=1, source_target_pairs={{0,8},{4,20},{8,0},{12,28},{16,24},{20,4},{24,16},{28,12},{1,9},{5... | collective-permute-start | bytes 786440 | tf_op jit(solution)/shard_map/ppermute | solution.py:368
  34.6 5.0 %step_0.1 = (f32[512,2048]{1,0:T(8,128)S(1)}, bf16[512,1024]{1,0:T(8,128)(2,1)S(1)}, bf16[1024,2048]{1,0:T(8,128)(2,1)S(1)}, f32[8,128]{1,0:T(8,128)S(1)}) custom-call(s32[16]{0:T(128)S(1)} %copy-done, bf16[128,1024]{1,0:T(8,128)(2,1)S(1)} %attend_0.1.refs_1_.after, bf16[128,1024]{1,0:T(8,128)(2,1)S(1)} %collective-permute-done.5.refs_2_.rest_1_, ...), custom_call_target="tpu_custom_call" | custom-call | flops 2147483648 | tf_op jit(solution)/shard_map/step_0/pallas_call | solution.py:302
  39.6 2.3 %step_1.1 = (f32[512,2048]{1,0:T(8,128)S(1)}, f32[8,128]{1,0:T(8,128)S(1)}) custom-call(f32[8,128]{1,0:T(8,128)S(1)} %get-tuple-element.45.refs_0_, bf16[512,1024]{1,0:T(8,128)(2,1)S(1)} %get-tuple-element.46.refs_1_, bf16[1024,2048]{1,0:T(8,128)(2,1)S(1)} %get-tuple-element.47.refs_2_), custom_call_target="tpu_custom_call" | custom-call | flops 2147483648 | tf_op jit(solution)/shard_map/step_1/pallas_call | solution.py:302
  42.7 2.0 %collective-permute-start.15 = (bf16[128,1024]{1,0:T(8,128)(2,1)S(1)}, bf16[128,1024]{1,0:T(8,128)(2,1)S(1)}, u32[]{:S(2)}, u32[]{:S(2)}) collective-permute-start(bf16[128,1024]{1,0:T(8,128)(2,1)S(1)} %attend_3.1.refs_2_), channel_id=1, source_target_pairs={{0,16},{4,12},{8,24},{12,4},{16,0},{20,28},{24,8},{28,20},{1,17},{... | collective-permute-start | bytes 786440 | tf_op jit(solution)/shard_map/ppermute | solution.py:369
  45.3 3.4 %step_2.1 = (f32[512,2048]{1,0:T(8,128)S(1)}, bf16[512,1024]{1,0:T(8,128)(2,1)S(1)}, bf16[1024,2048]{1,0:T(8,128)(2,1)S(1)}, f32[8,128]{1,0:T(8,128)S(1)}) custom-call(f32[8,128]{1,0:T(8,128)S(1)} %get-tuple-element.48.refs_0_.rest_1_, s32[16]{0:T(128)S(1)} %copy-done, bf16[128,1024]{1,0:T(8,128)(2,1)S(1)} %attend_1.1.refs_2_.after, ...), custom_call_target="tpu_custom_call", output_to_operand_aliasing={{0}: (8, {})} | custom-call | flops 2147483648 | tf_op jit(solution)/shard_map/step_2/pallas_call | solution.py:302
  48.7 2.7 %step_3.1 = (f32[512,2048]{1,0:T(8,128)S(1)}, f32[8,128]{1,0:T(8,128)S(1)}) custom-call(f32[8,128]{1,0:T(8,128)S(1)} %get-tuple-element.52.refs_0_, bf16[512,1024]{1,0:T(8,128)(2,1)S(1)} %get-tuple-element.53.refs_1_, bf16[1024,2048]{1,0:T(8,128)(2,1)S(1)} %get-tuple-element.54.refs_2_, ...), custom_call_target="tpu_custom_call", output_to_operand_aliasing={{0}: (3, {})} | custom-call | flops 2147483648 | tf_op jit(solution)/shard_map/step_3/pallas_call | solution.py:302
  51.4 1.2 %collective-permute-done.14.refs_3_ = bf16[128,1024]{1,0:T(8,128)(2,1)S(1)} collective-permute-done((bf16[128,1024]{1,0:T(8,128)(2,1)S(1)}, bf16[128,1024]{1,0:T(8,128)(2,1)S(1)}, u32[]{:S(2)}, u32[]{:S(2)}) %collective-permute-start.14) | collective-permute-done | bytes 262176 | tf_op jit(solution)/shard_map/ppermute | solution.py:368
  53.5 3.4 %step_4.1 = (f32[512,2048]{1,0:T(8,128)S(1)}, bf16[512,1024]{1,0:T(8,128)(2,1)S(1)}, bf16[1024,2048]{1,0:T(8,128)(2,1)S(1)}, f32[8,128]{1,0:T(8,128)S(1)}) custom-call(f32[8,128]{1,0:T(8,128)S(1)} %get-tuple-element.56.refs_0_, s32[16]{0:T(128)S(1)} %copy-done, bf16[128,1024]{1,0:T(8,128)(2,1)S(1)} %attend_2.1.refs_2_.rest_0_, ...), custom_call_target="tpu_custom_call", output_to_operand_aliasing={{0}: (8, {})} | custom-call | flops 2147483648 | tf_op jit(solution)/shard_map/step_4/pallas_call | solution.py:302
  56.9 2.9 %step_5.1 = (f32[512,2048]{1,0:T(8,128)S(1)}, f32[8,128]{1,0:T(8,128)S(1)}) custom-call(f32[8,128]{1,0:T(8,128)S(1)} %get-tuple-element.60.refs_0_, bf16[512,1024]{1,0:T(8,128)(2,1)S(1)} %get-tuple-element.61.refs_1_, bf16[1024,2048]{1,0:T(8,128)(2,1)S(1)} %get-tuple-element.62.refs_2_, ...), custom_call_target="tpu_custom_call", output_to_operand_aliasing={{0}: (3, {})} | custom-call | flops 2147483648 | tf_op jit(solution)/shard_map/step_5/pallas_call | solution.py:302
  59.8 3.1 %step_6.1 = (f32[256,2048]{1,0:T(8,128)S(1)}, bf16[256,2048]{1,0:T(8,128)(2,1)S(1)}, bf16[512,1024]{1,0:T(8,128)(2,1)S(1)}, bf16[1024,2048]{1,0:T(8,128)(2,1)S(1)}, f32[8,128]{1,0:T(8,128)S(1)}) custom-call(f32[8,128]{1,0:T(8,128)S(1)} %get-tuple-element.64.refs_0_, s32[16]{0:T(128)S(1)} %copy-done, bf16[128,1024]{1,0:T(8,128)(2,1)S(1)} %attend_3.1.refs_2_, ...), custom_call_target="tpu_custom_call" | custom-call | flops 2147483648 | tf_op jit(solution)/shard_map/step_6/pallas_call | solution.py:302
  63.0 2.9 %step_7.1 = (f32[256,2048]{1,0:T(8,128)S(1)}, bf16[256,2048]{1,0:T(8,128)(2,1)S(1)}, f32[8,128]{1,0:T(8,128)}) custom-call(f32[8,128]{1,0:T(8,128)S(1)} %get-tuple-element.67.refs_0_, bf16[512,1024]{1,0:T(8,128)(2,1)S(1)} %get-tuple-element.68.refs_1_, bf16[1024,2048]{1,0:T(8,128)(2,1)S(1)} %get-tuple-element.69.refs_2_, ...), custom_call_target="tpu_custom_call" | custom-call | flops 2147483648 | tf_op jit(solution)/shard_map/step_7/pallas_call | solution.py:302
  66.4 1.1 %total_0.1.rest_0_ = bf16[256,4096]{1,0:T(8,128)(2,1)} custom-call(f32[256,2048]{1,0:T(8,128)S(1)} %get-tuple-element.73.own_ref, bf16[256,2048]{1,0:T(8,128)(2,1)S(1)} %collective-permute-done.18.got_ref), custom_call_target="tpu_custom_call" | custom-call | flops 524288 | bytes 1048576 | tf_op jit(solution)/shard_map/total_0/pallas_call | solution.py:341
  67.5 1.2 %collective-permute-done.17.got_ref = bf16[256,2048]{1,0:T(8,128)(2,1)S(1)} collective-permute-done((bf16[256,2048]{1,0:T(8,128)(2,1)S(1)}, bf16[256,2048]{1,0:T(8,128)(2,1)S(1)}, u32[]{:S(2)}, u32[]{:S(2)}) %collective-permute-start.17) | collective-permute-done | bytes 1048608 | tf_op jit(solution)/shard_map/ppermute | solution.py:414
  (33 shorter events, 8.5 us)
Async XLA Ops:
  0.0 11.5 %collective-permute-start = (bf16[128,512]{1,0:T(8,128)(2,1)}, bf16[128,512]{1,0:T(8,128)(2,1)S(1)}, u32[]{:S(2)}, u32[]{:S(2)}) collective-permute-start(bf16[128,512]{1,0:T(8,128)(2,1)} %v_hbm.1), channel_id=1, source_target_pairs={{0,16},{8,24},{1,17},{9,25},{2,18},{10,26},{3,19},{11,27},{4,20},{... | collective-permute-start | bytes 393224 | tf_op jit(solution)/shard_map/ppermute | solution.py:381
  4.9 10.0 %collective-permute-start.2 = (bf16[128,512]{1,0:T(8,128)(2,1)}, bf16[128,512]{1,0:T(8,128)(2,1)S(1)}, u32[]{:S(2)}, u32[]{:S(2)}) collective-permute-start(bf16[128,512]{1,0:T(8,128)(2,1)} %k_hbm.1), channel_id=1, source_target_pairs={{0,16},{8,24},{1,17},{9,25},{2,18},{10,26},{3,19},{11,27},{4,20},{... | collective-permute-start | bytes 393224 | tf_op jit(solution)/shard_map/ppermute | solution.py:382
  6.2 8.8 %collective-permute-start.1 = (bf16[128,512]{1,0:T(8,128)(2,1)}, bf16[128,512]{1,0:T(8,128)(2,1)S(1)}, u32[]{:S(2)}, u32[]{:S(2)}) collective-permute-start(bf16[128,512]{1,0:T(8,128)(2,1)} %k_hbm.1), channel_id=1, source_target_pairs={{0,8},{8,16},{16,24},{1,9},{9,17},{17,25},{2,10},{10,18},{18,26},{... | collective-permute-start | bytes 393224 | tf_op jit(solution)/shard_map/ppermute | solution.py:383
  9.6 5.6 %collective-permute-start.3 = (bf16[128,512]{1,0:T(8,128)(2,1)}, bf16[128,512]{1,0:T(8,128)(2,1)S(1)}, u32[]{:S(2)}, u32[]{:S(2)}) collective-permute-start(bf16[128,512]{1,0:T(8,128)(2,1)} %v_hbm.1), channel_id=1, source_target_pairs={{0,8},{16,24},{1,9},{17,25},{2,10},{18,26},{3,11},{19,27},{4,12},{... | collective-permute-start | bytes 393224 | tf_op jit(solution)/shard_map/ppermute | solution.py:384
  11.5 3.7 %collective-permute-start.4 = (bf16[128,512]{1,0:T(8,128)(2,1)S(1)}, bf16[128,512]{1,0:T(8,128)(2,1)S(1)}, u32[]{:S(2)}, u32[]{:S(2)}) collective-permute-start(bf16[128,512]{1,0:T(8,128)(2,1)S(1)} %collective-permute-done.after.v2), channel_id=1, source_target_pairs={{24,16},{25,17},{26,18},{27,19},{28,20},{29,21},{30,22},{31,23}} | collective-permute-start | bytes 393224 | tf_op jit(solution)/shard_map/ppermute | solution.py:385
  15.9 8.9 %collective-permute-start.5 = (bf16[128,1024]{1,0:T(8,128)(2,1)S(1)}, bf16[128,1024]{1,0:T(8,128)(2,1)S(1)}, u32[]{:S(2)}, u32[]{:S(2)}) collective-permute-start(bf16[128,1024]{1,0:T(8,128)(2,1)S(1)} %attend_0.1.refs_1_.after), channel_id=1, source_target_pairs={{0,8},{4,20},{8,0},{12,28},{16,24},{20,4},{24,16},{28,12},{1,9},{5... | collective-permute-start | bytes 786440 | tf_op jit(solution)/shard_map/ppermute | solution.py:368
  18.3 14.7 %collective-permute-start.6 = (bf16[128,1024]{1,0:T(8,128)(2,1)S(1)}, bf16[128,1024]{1,0:T(8,128)(2,1)S(1)}, u32[]{:S(2)}, u32[]{:S(2)}) collective-permute-start(bf16[128,1024]{1,0:T(8,128)(2,1)S(1)} %attend_0.1.refs_1_.after), channel_id=1, source_target_pairs={{0,16},{4,12},{8,24},{12,4},{16,0},{20,28},{24,8},{28,20},{1,17},{... | collective-permute-start | bytes 786440 | tf_op jit(solution)/shard_map/ppermute | solution.py:369
  22.1 12.6 %copy-start = (s32[16]{0:T(128)S(1)}, s32[16]{0:T(128)}, u32[]{:S(2)}) copy-start(s32[16]{0:T(128)} %refs_1_.5) | copy-start | bytes 196
  22.1 12.4 %collective-permute-start.8 = (bf16[128,1024]{1,0:T(8,128)(2,1)S(1)}, bf16[128,1024]{1,0:T(8,128)(2,1)S(1)}, u32[]{:S(2)}, u32[]{:S(2)}) collective-permute-start(bf16[128,1024]{1,0:T(8,128)(2,1)S(1)} %attend_1.1.refs_2_.after), channel_id=1, source_target_pairs={{0,8},{4,20},{8,0},{12,28},{16,24},{20,4},{24,16},{28,12},{1,9},{5... | collective-permute-start | bytes 786440 | tf_op jit(solution)/shard_map/ppermute | solution.py:368
  24.8 9.8 %collective-permute-start.7 = (bf16[128,1024]{1,0:T(8,128)(2,1)S(1)}, bf16[128,1024]{1,0:T(8,128)(2,1)S(1)}, u32[]{:S(2)}, u32[]{:S(2)}) collective-permute-start(bf16[128,1024]{1,0:T(8,128)(2,1)S(1)} %collective-permute-done.5.refs_2_.rest_1_), channel_id=1, source_target_pairs={{0,16},{4,12},{8,24},{12,4},{16,0},{20,28},{24,8},{28,20},{1,17},{... | collective-permute-start | bytes 786440 | tf_op jit(solution)/shard_map/ppermute | solution.py:370
  26.7 18.0 %collective-permute-start.9 = (bf16[128,1024]{1,0:T(8,128)(2,1)S(1)}, bf16[128,1024]{1,0:T(8,128)(2,1)S(1)}, u32[]{:S(2)}, u32[]{:S(2)}) collective-permute-start(bf16[128,1024]{1,0:T(8,128)(2,1)S(1)} %attend_1.1.refs_2_.after), channel_id=1, source_target_pairs={{0,16},{4,12},{8,24},{12,4},{16,0},{20,28},{24,8},{28,20},{1,17},{... | collective-permute-start | bytes 786440 | tf_op jit(solution)/shard_map/ppermute | solution.py:369
  31.0 22.5 %collective-permute-start.12 = (bf16[128,1024]{1,0:T(8,128)(2,1)S(1)}, bf16[128,1024]{1,0:T(8,128)(2,1)S(1)}, u32[]{:S(2)}, u32[]{:S(2)}) collective-permute-start(bf16[128,1024]{1,0:T(8,128)(2,1)S(1)} %attend_2.1.refs_2_.rest_0_), channel_id=1, source_target_pairs={{0,16},{4,12},{8,24},{12,4},{16,0},{20,28},{24,8},{28,20},{1,17},{... | collective-permute-start | bytes 786440 | tf_op jit(solution)/shard_map/ppermute | solution.py:369
  33.0 12.2 %collective-permute-start.11 = (bf16[128,1024]{1,0:T(8,128)(2,1)S(1)}, bf16[128,1024]{1,0:T(8,128)(2,1)S(1)}, u32[]{:S(2)}, u32[]{:S(2)}) collective-permute-start(bf16[128,1024]{1,0:T(8,128)(2,1)S(1)} %attend_2.1.refs_2_.rest_0_), channel_id=1, source_target_pairs={{0,8},{4,20},{8,0},{12,28},{16,24},{20,4},{24,16},{28,12},{1,9},{5... | collective-permute-start | bytes 786440 | tf_op jit(solution)/shard_map/ppermute | solution.py:368
  34.5 10.8 %collective-permute-start.10 = (bf16[128,1024]{1,0:T(8,128)(2,1)S(1)}, bf16[128,1024]{1,0:T(8,128)(2,1)S(1)}, u32[]{:S(2)}, u32[]{:S(2)}) collective-permute-start(bf16[128,1024]{1,0:T(8,128)(2,1)S(1)} %collective-permute-done.8.refs_3_), channel_id=1, source_target_pairs={{0,16},{4,12},{8,24},{12,4},{16,0},{20,28},{24,8},{28,20},{1,17},{... | collective-permute-start | bytes 786440 | tf_op jit(solution)/shard_map/ppermute | solution.py:370
  42.7 17.1 %collective-permute-start.15 = (bf16[128,1024]{1,0:T(8,128)(2,1)S(1)}, bf16[128,1024]{1,0:T(8,128)(2,1)S(1)}, u32[]{:S(2)}, u32[]{:S(2)}) collective-permute-start(bf16[128,1024]{1,0:T(8,128)(2,1)S(1)} %attend_3.1.refs_2_), channel_id=1, source_target_pairs={{0,16},{4,12},{8,24},{12,4},{16,0},{20,28},{24,8},{28,20},{1,17},{... | collective-permute-start | bytes 786440 | tf_op jit(solution)/shard_map/ppermute | solution.py:369
  44.7 7.9 %collective-permute-start.14 = (bf16[128,1024]{1,0:T(8,128)(2,1)S(1)}, bf16[128,1024]{1,0:T(8,128)(2,1)S(1)}, u32[]{:S(2)}, u32[]{:S(2)}) collective-permute-start(bf16[128,1024]{1,0:T(8,128)(2,1)S(1)} %attend_3.1.refs_2_), channel_id=1, source_target_pairs={{0,8},{4,20},{8,0},{12,28},{16,24},{20,4},{24,16},{28,12},{1,9},{5... | collective-permute-start | bytes 786440 | tf_op jit(solution)/shard_map/ppermute | solution.py:368
  45.2 8.2 %collective-permute-start.13 = (bf16[128,1024]{1,0:T(8,128)(2,1)S(1)}, bf16[128,1024]{1,0:T(8,128)(2,1)S(1)}, u32[]{:S(2)}, u32[]{:S(2)}) collective-permute-start(bf16[128,1024]{1,0:T(8,128)(2,1)S(1)} %collective-permute-done.11.refs_3_), channel_id=1, source_target_pairs={{0,16},{4,12},{8,24},{12,4},{16,0},{20,28},{24,8},{28,20},{1,17},{... | collective-permute-start | bytes 786440 | tf_op jit(solution)/shard_map/ppermute | solution.py:370
  52.6 7.2 %collective-permute-start.16 = (bf16[128,1024]{1,0:T(8,128)(2,1)S(1)}, bf16[128,1024]{1,0:T(8,128)(2,1)S(1)}, u32[]{:S(2)}, u32[]{:S(2)}) collective-permute-start(bf16[128,1024]{1,0:T(8,128)(2,1)S(1)} %collective-permute-done.14.refs_3_), channel_id=1, source_target_pairs={{0,16},{4,12},{8,24},{12,4},{16,0},{20,28},{24,8},{28,20},{1,17},{... | collective-permute-start | bytes 786440 | tf_op jit(solution)/shard_map/ppermute | solution.py:370
  62.9 3.5 %collective-permute-start.18 = (bf16[256,2048]{1,0:T(8,128)(2,1)S(1)}, bf16[256,2048]{1,0:T(8,128)(2,1)S(1)}, u32[]{:S(2)}, u32[]{:S(2)}) collective-permute-start(bf16[256,2048]{1,0:T(8,128)(2,1)S(1)} %get-tuple-element.74), channel_id=1, source_target_pairs={{0,4},{4,0},{1,5},{5,1},{2,6},{6,2},{3,7},{7,3},{8,12},{12,8},{9,1... | collective-permute-start | bytes 3145736 | tf_op jit(solution)/shard_map/ppermute | solution.py:414
  65.9 2.8 %collective-permute-start.17 = (bf16[256,2048]{1,0:T(8,128)(2,1)S(1)}, bf16[256,2048]{1,0:T(8,128)(2,1)S(1)}, u32[]{:S(2)}, u32[]{:S(2)}) collective-permute-start(bf16[256,2048]{1,0:T(8,128)(2,1)S(1)} %get-tuple-element.72), channel_id=1, source_target_pairs={{0,4},{4,0},{1,5},{5,1},{2,6},{6,2},{3,7},{7,3},{8,12},{12,8},{9,1... | collective-permute-start | bytes 3145736 | tf_op jit(solution)/shard_map/ppermute | solution.py:414

commit v4 on v3

--- a/solution.py
+++ b/solution.py
@@ -92,13 +92,14 @@
     )
 
 
-def prepare_kernel(docs_hbm, k_hbm, v_hbm, q_hbm, w_hbm, after, k_ref, v_ref, q_ref, mask_ref, w_ref, docs, sems):
+def prepare_kernel(docs_hbm, k_hbm, v_hbm, q_hbm, w_hbm, after, k_ref, v_ref, q_ref, mask_ref, left_ref, right_ref, docs, sems):
     lengths = pltpu.make_async_copy(docs_hbm, docs, sems.at[0])
     loads = [
         pltpu.make_async_copy(k_hbm, k_ref, sems.at[1]),
         pltpu.make_async_copy(v_hbm, v_ref, sems.at[2]),
         pltpu.make_async_copy(q_hbm, q_ref, sems.at[3]),
-        block_copy(w_hbm, 0, w_ref, sems.at[4]),
+        block_copy(w_hbm, 0, left_ref, sems.at[4]),
+        block_copy(w_hbm, 1, right_ref, sems.at[5]),
     ]
     lengths.start()
     for load in loads:
@@ -128,16 +129,17 @@
             jax.ShapeDtypeStruct(queries.shape, jnp.bfloat16),
             jax.ShapeDtypeStruct((rows, 3 * rows), jnp.float32),
             jax.ShapeDtypeStruct(block_shape(w_out, chunks), jnp.bfloat16),
+            jax.ShapeDtypeStruct(block_shape(w_out, chunks), jnp.bfloat16),
         ],
         in_specs=[HBM] * 6,
-        out_specs=[VMEM] * 5,
+        out_specs=[VMEM] * 6,
         scratch_shapes=[
             pltpu.SMEM(doc_lengths.shape, jnp.int32),
-            pltpu.SemaphoreType.DMA((5,)),
+            pltpu.SemaphoreType.DMA((6,)),
         ],
         compiler_params=pltpu.CompilerParams(vmem_limit_bytes=4 * MIB),
         cost_estimate=pl.CostEstimate(
-            flops=0, bytes_accessed=w_out.size // chunks, transcendentals=0
+            flops=0, bytes_accessed=2 * w_out.size // chunks, transcendentals=0
         ),
         name="prepare",
     )(
@@ -240,33 +242,33 @@
             lhs[at, :] = piece[u * unit_rows:(u + 1) * unit_rows, column:column + lhs.shape[1]]
 
 
-def step_kernel(index, last, column, has_acc, has_after, *refs):
+def step_kernel(index, last, column, first, columns, has_acc, has_after, has_load, *refs):
     refs = list(refs)[has_after:]
     first_half = index % HALVES == 0
     load = None
+    if has_load:
+        sem = refs.pop()
+    token = refs.pop()
+    if has_load:
+        load = block_copy(refs.pop(0), index + 1, refs.pop(), sem)
+        load.start()
     if first_half:
         plan, *pieces = refs[:5]
-        w_hbm = refs[5]
-        del refs[:6]
-        sem = refs.pop()
-        token = refs.pop()
-        next_ref = refs.pop()
+        del refs[:5]
         lhs = refs.pop()
-        load = block_copy(w_hbm, index + 1, next_ref, sem)
-        load.start()
         lay_out(plan, pieces, column, lhs)
     else:
-        token = refs.pop()
         lhs = refs.pop(0)
     token[...] = jnp.zeros_like(token)
     w_ref = refs.pop(0)
     acc_ref = refs.pop(0) if has_acc else None
     rows = lhs.shape[0] // 2
-    for at in range(0, w_ref.shape[1], TILE):
-        to = slice(at, at + TILE)
-        product = jnp.dot(lhs[...], w_ref[:, to], preferred_element_type=jnp.float32)
+    for start in range(0, columns, TILE):
+        to = slice(start, start + TILE)
+        at = slice(first + start, first + start + TILE)
+        product = jnp.dot(lhs[...], w_ref[:, at], preferred_element_type=jnp.float32)
         if has_acc:
-            product = product + acc_ref[:, to]
+            product = product + acc_ref[:, at]
         if last:
             own_ref, sent_ref = refs
             own_ref[:, to] = product[rows:]
@@ -277,14 +279,14 @@
         load.wait()
 
 
-def step(index, last, rows_in, column, block, w_out, acc, after):
+def step(index, last, rows_in, column, block, first, columns, w_out, acc, after):
     first_half = index % HALVES == 0
-    has_acc, has_after = acc is not None, after is not None
-    depth, columns = block.shape
+    has_acc, has_after, has_load = acc is not None, after is not None, w_out is not None
+    depth = block.shape[0]
     if first_half:
         plan, pieces = rows_in
         total_rows = 4 * pieces[0].shape[0]
-        operands, specs = [plan, *pieces, w_out], [SMEM] + [VMEM] * 4 + [HBM]
+        operands, specs = [plan, *pieces], [SMEM] + [VMEM] * 4
     else:
         total_rows = rows_in.shape[0]
         operands, specs = [rows_in], [VMEM]
@@ -295,65 +297,89 @@
         shapes = [jax.ShapeDtypeStruct((total_rows, columns), jnp.float32)]
     if first_half:
         shapes.append(jax.ShapeDtypeStruct((total_rows, depth), jnp.bfloat16))
+    if has_load:
         shapes.append(jax.ShapeDtypeStruct(block.shape, jnp.bfloat16))
     shapes.append(TOKEN)
-    operands = [after] * has_after + operands + [block] + [acc] * has_acc
-    specs = [HBM] * has_after + specs + [VMEM] * (1 + has_acc)
+    operands = [after] * has_after + [w_out] * has_load + operands + [block] + [acc] * has_acc
+    specs = [HBM] * (has_after + has_load) + specs + [VMEM] * (1 + has_acc)
     results = list(pl.pallas_call(
-        functools.partial(step_kernel, index, last, column, has_acc, has_after),
+        functools.partial(
+            step_kernel, index, last, column, first, columns, has_acc, has_after, has_load
+        ),
         out_shape=shapes,
         in_specs=specs,
         out_specs=[VMEM] * len(shapes),
-        scratch_shapes=[pltpu.SemaphoreType.DMA] * first_half,
+        scratch_shapes=[pltpu.SemaphoreType.DMA] * has_load,
         input_output_aliases={len(operands) - 1: 0} if has_acc and not last else {},
         compiler_params=pltpu.CompilerParams(vmem_limit_bytes=6 * MIB),
         cost_estimate=pl.CostEstimate(
             flops=2 * total_rows * depth * columns, bytes_accessed=0, transcendentals=0
         ),
-        name=f"step_{index}",
+        name=f"step_{index}_{first // columns}",
     )(*operands))
     token = results.pop()
-    following = results.pop() if first_half else None
-    lhs = results.pop() if first_half else None
+    following = results.pop() if has_load else None
+    lhs = results.pop() if first_half else rows_in
     return results, lhs, following, token
 
 
-def total_kernel(first, has_out, own_ref, got_ref, *rest):
-    out_hbm, buf, sems = rest[has_out:]
-    columns = got_ref.shape[1]
-    step = columns // 2
-    writes = []
-    for i in range(2):
-        to = slice(i * step, (i + 1) * step)
-        at = slice(first + i * step, first + (i + 1) * step)
-        value = own_ref[:, to] + got_ref[:, to].astype(jnp.float32)
-        buf[:, to] = value.astype(jnp.bfloat16)
-        write = pltpu.make_async_copy(buf.at[:, to], out_hbm.at[:, at], sems.at[i])
-        write.start()
-        writes.append(write)
+def total_kernel(first, count, has_out, *refs):
+    own_refs, got_refs = refs[:count], refs[count:2 * count]
+    out_hbm, buf, sems = refs[2 * count + has_out:]
+    writes, at = [], 0
+    for own_ref, got_ref in zip(own_refs, got_refs):
+        columns = own_ref.shape[1]
+        for start in range(0, columns, 2 * TILE):
+            to = slice(start, start + 2 * TILE)
+            value = own_ref[:, to] + got_ref[:, to].astype(jnp.float32)
+            here = slice(at + start, at + start + 2 * TILE)
+            there = slice(first + at + start, first + at + start + 2 * TILE)
+            buf[:, here] = value.astype(jnp.bfloat16)
+            write = pltpu.make_async_copy(buf.at[:, here], out_hbm.at[:, there], sems.at[len(writes)])
+            write.start()
+            writes.append(write)
+        at += columns
     for write in writes:
         write.wait()
 
 
 def total(first, width, own, got, out):
-    rows, columns = got.shape
-    has_out = out is not None
+    rows = own[0].shape[0]
+    columns = sum(x.shape[1] for x in own)
+    count, has_out = len(own), out is not None
     return pl.pallas_call(
-        functools.partial(total_kernel, first, has_out),
+        functools.partial(total_kernel, first, count, has_out),
         out_shape=jax.ShapeDtypeStruct((rows, width), jnp.bfloat16),
-        in_specs=[VMEM, VMEM] + [HBM] * has_out,
+        in_specs=[VMEM] * (2 * count) + [HBM] * has_out,
         out_specs=HBM,
         scratch_shapes=[
             pltpu.VMEM((rows, columns), jnp.bfloat16),
-            pltpu.SemaphoreType.DMA((2,)),
+            pltpu.SemaphoreType.DMA((columns // (2 * TILE),)),
         ],
-        input_output_aliases={2: 0} if has_out else {},
+        input_output_aliases={2 * count: 0} if has_out else {},
         compiler_params=pltpu.CompilerParams(vmem_limit_bytes=4 * MIB),
         cost_estimate=pl.CostEstimate(
             flops=rows * columns, bytes_accessed=2 * rows * columns, transcendentals=0
         ),
-        name=f"total_{first // columns}",
-    )(own, got, *([out] if has_out else []))
+        name=f"total_{first}",
+    )(*own, *got, *([out] if has_out else []))
+
+
+def gate_kernel(x, after, out):
+    pass
+
+
+def gate(x, after):
+    return pl.pallas_call(
+        gate_kernel,
+        out_shape=jax.ShapeDtypeStruct(x.shape, x.dtype),
+        in_specs=[HBM, HBM],
+        out_specs=HBM,
+        input_output_aliases={0: 0},
+        compiler_params=pltpu.CompilerParams(vmem_limit_bytes=1 * MIB),
+        cost_estimate=pl.CostEstimate(flops=0, bytes_accessed=0, transcendentals=0),
+        name="gate",
+    )(x, after)
 
 
 def gather_rows(own):
@@ -367,8 +393,12 @@
 
     near = lax.ppermute(own, ("ctx", "tp"), route(True))
     side = lax.ppermute(own, ("ctx", "tp"), route(False))
-    far = lax.ppermute(near, ("ctx", "tp"), route(False))
-    return own, near, side, far
+
+    def forward(after):
+        first = near if after is None else gate(near, after)
+        return own, first, side, lax.ppermute(first, ("ctx", "tp"), route(False))
+
+    return near, side, forward
 
 
 def local(queries, key_rows, value_rows, doc_lengths, unit_source, w_out):
@@ -383,51 +413,70 @@
     key_near = lax.ppermute(key_rows, "ctx", [(0, 1), (1, 2), (2, 3)])
     value_near = lax.ppermute(value_rows, "ctx", [(0, 1), (2, 3)])
     value_far = lax.ppermute(value_two, "ctx", [(3, 2)])
-    own_keys, own_values, held, mask, block = prepare(
+    own_keys, own_values, held, mask, left, right = prepare(
         doc_lengths, key_rows, value_rows, queries, w_out, kv_heads, value_two
     )
     keys = (own_keys, key_near, key_near, key_two)
     values = (own_values, value_near, value_far, value_two)
-    state = {"blocks": {0: block}, "totals": [None] * HALVES, "before": None}
-    gathered, mine, got = [], [], []
-
-    def rows_of(g, after):
-        own = attend((g,), width, held, mask, keys, values, after)
-        gathered.append(gather_rows(own))
-        return own
+    half_columns = w_out.shape[1] // HALVES
+    state = {"left": {0: left}, "right": {0: right}, "totals": [None] * HALVES, "before": None}
+    rows, mine, got = {}, [], []
+
+    def rows_of(groups, after):
+        own = attend(groups, width, held, mask, keys, values, after)
+        near, side, forward = gather_rows(own)
+
+        def arrive(after):
+            pieces = forward(after)
+            for i, g in enumerate(groups):
+                rows[g] = (pieces, i * width)
+            return pieces[1]
+
+        return own, arrive
 
     def load(wanted, after):
         loaded, token = load_blocks([g * HALVES for g in wanted], w_out, kv_heads, after)
-        state["blocks"].update(zip(wanted, loaded))
+        state["left"].update(zip(wanted, loaded))
         return token
 
     def steps(g):
         last = g == kv_heads - 1
-        rows_in, block = (unit_source, gathered[g]), state["blocks"][g]
-        for half in range(HALVES):
-            results, rows_in, block, state["before"] = step(
-                g * HALVES + half, last, rows_in, 0, block, w_out,
-                state["totals"][half], state["before"],
+        pieces, column = rows[g]
+        loads = g not in state["right"]
+        first, lhs, following, state["before"] = step(
+            g * HALVES, last, (unit_source, pieces), column, state["left"][g], 0, half_columns,
+            w_out if loads else None, state["totals"][0], state["before"],
+        )
+        if loads:
+            state["right"][g] = following
+        parts = 1
+        seconds = []
+        for i in range(parts):
+            second, lhs, _, state["before"] = step(
+                g * HALVES + 1, last, lhs, column, state["right"][g],
+                i * half_columns // parts, half_columns // parts, None,
+                state["totals"][1], state["before"],
             )
-            if last:
-                mine.append(results[0])
-                got.append(lax.ppermute(results[1], "tp", [(0, 1), (1, 0)]))
-            else:
-                state["totals"][half] = results[0]
+            seconds.append(second)
+        if last:
+            for kept, sent in [first, *seconds]:
+                mine.append(kept)
+                got.append(lax.ppermute(sent, "tp", [(0, 1), (1, 0)]))
+        else:
+            state["totals"] = [first[0], seconds[0][0]]
         return state["before"]
 
-    own = rows_of(0, [])
-    own = rows_of(1, [load((1,), own)])
-    own = rows_of(2, [load((2, 3), own), *gathered[0][1:2]])
+    own, arrive = rows_of((0,), [])
+    near = arrive(load((1, 2), own))
+    own, arrive = rows_of((1, 2), [near])
     done = steps(0)
-    rows_of(3, [own, done])
-    for g in range(1, kv_heads):
+    near = arrive(done)
+    _, arrive = rows_of((3,), [load((3,), near), done])
+    arrive(steps(1))
+    for g in range(2, kv_heads):
         steps(g)
-    columns = w_out.shape[1] // HALVES
-    out = None
-    for half in range(HALVES):
-        out = total(half * columns, w_out.shape[1], mine[half], got[half], out)
-    return out
+    out = total(0, w_out.shape[1], mine[:1], got[:1], None)
+    return total(half_columns, w_out.shape[1], mine[1:], got[1:], out)
 
 
 def solution(mesh):

time: 70.2 us -> 74.9 us (1.067)
  waiting for transfers between devices: 3.33 us -> 10.9 us
  starting transfers between devices: 27.1 us -> 24.9 us
    ppermute x6 -> x5, waiting for transfers between devices: 1.19 us -> 9.89 us  [the longest x3 8.7 us: forward(): return (own, first, side, lax.ppermute(first, ('ctx', 'tp'), route(False)))]
    ppermute x4 -> x3, starting transfers between devices: 4.92 us -> 1.91 us  [gather_rows(): side = lax.ppermute(own, ('ctx', 'tp'), route(False))]
    ppermute x6 -> x5, starting transfers between devices: 3.5 us -> 5.69 us  [the longest x3 5.12 us: forward(): return (own, first, side, lax.ppermute(first, ('ctx', 'tp'), route(False)))]
    pallas_call x10 -> x13, Pallas kernels: 27.9 us -> 26.1 us  [the longest x8 23.9 us: step(): pl.pallas_call(functools.partial(step_kernel, index, last, column, first,...]
    ppermute x4 -> x3, starting transfers between devices: 6.49 us -> 5.19 us  [gather_rows(): near = lax.ppermute(own, ('ctx', 'tp'), route(True))]
    pallas_call x1, Pallas kernels: 2.7 us -> 3.95 us  [prepare(): pl.pallas_call(prepare_kernel, out_shape=[jax.ShapeDtypeStruct(key_rows.s...]
    ppermute x4 -> x3, waiting for transfers between devices: 1.88 us -> 1.01 us  [gather_rows(): near = lax.ppermute(own, ('ctx', 'tp'), route(True))]
    pallas_call x4 -> x3, Pallas kernels: 2.81 us -> 2.64 us  [attend(): pl.pallas_call(functools.partial(attend_kernel, groups), out_shape=jax.Sh...]
  transfers between devices with their start and end apart: 19 -> 16, of which waited for: 4 -> 4; matrix products, arithmetic and copies ran while one was open for 0% -> 0% of each run, Pallas kernels for 49% -> 45%
where the time goes in v4:
time: 74.9 us; the launch traced here: 74.7 us
  Pallas kernels  38.4 us (51%)
  starting transfers between devices  24.9 us (33%)
  waiting for transfers between devices  10.9 us (15%)
    pallas_call x8, Pallas kernels, step(): pl.pallas_call(functools.partial(step_kernel, index, last, column, first,...  23.9 us
    ppermute x3, waiting for transfers between devices, forward(): return (own, first, side, lax.ppermute(first, ('ctx', 'tp'), route(False)))  8.7 us
    pallas_call x2, Pallas kernels, load_blocks(): pl.pallas_call(functools.partial(load_kernel, indexes), out_shape=[jax.Sh...  5.68 us
    ppermute x3, starting transfers between devices, gather_rows(): near = lax.ppermute(own, ('ctx', 'tp'), route(True))  5.19 us
    ppermute x3, starting transfers between devices, forward(): return (own, first, side, lax.ppermute(first, ('ctx', 'tp'), route(False)))  5.12 us
    ppermute x1, starting transfers between devices, local(): value_two = lax.ppermute(value_rows, 'ctx', two)  4.87 us
    pallas_call x1, Pallas kernels, prepare(): pl.pallas_call(prepare_kernel, out_shape=[jax.ShapeDtypeStruct(key_rows.s...  3.95 us
    ppermute x1, starting transfers between devices, local(): key_near = lax.ppermute(key_rows, 'ctx', [(0, 1), (1, 2), (2, 3)])  3.4 us
  transfers between devices with their start and end apart: 16, of which 4 were waited for; matrix products, arithmetic and copies ran while one was open for 0% of the time, Pallas kernels for 45%

profile of v4, /device:TPU:0, one launch (start us, length us, event | category | flops | bytes accessed | tf_op | source)
XLA Modules:
  0.0 74.7 jit_solution(14110590398845828850)
XLA Ops:
  0.0 4.9 %collective-permute-start = (bf16[128,512]{1,0:T(8,128)(2,1)}, bf16[128,512]{1,0:T(8,128)(2,1)S(1)}, u32[]{:S(2)}, u32[]{:S(2)}) collective-permute-start(bf16[128,512]{1,0:T(8,128)(2,1)} %v_hbm.1), channel_id=1, source_target_pairs={{0,16},{8,24},{1,17},{9,25},{2,18},{10,26},{3,19},{11,27},{4,20},{... | collective-permute-start | bytes 393224 | tf_op jit(solution)/shard_map/ppermute | solution.py:411
  4.9 1.3 %collective-permute-start.2 = (bf16[128,512]{1,0:T(8,128)(2,1)}, bf16[128,512]{1,0:T(8,128)(2,1)S(1)}, u32[]{:S(2)}, u32[]{:S(2)}) collective-permute-start(bf16[128,512]{1,0:T(8,128)(2,1)} %k_hbm.1), channel_id=1, source_target_pairs={{0,16},{8,24},{1,17},{9,25},{2,18},{10,26},{3,19},{11,27},{4,20},{... | collective-permute-start | bytes 393224 | tf_op jit(solution)/shard_map/ppermute | solution.py:412
  6.2 3.4 %collective-permute-start.1 = (bf16[128,512]{1,0:T(8,128)(2,1)}, bf16[128,512]{1,0:T(8,128)(2,1)S(1)}, u32[]{:S(2)}, u32[]{:S(2)}) collective-permute-start(bf16[128,512]{1,0:T(8,128)(2,1)} %k_hbm.1), channel_id=1, source_target_pairs={{0,8},{8,16},{16,24},{1,9},{9,17},{17,25},{2,10},{10,18},{18,26},{... | collective-permute-start | bytes 393224 | tf_op jit(solution)/shard_map/ppermute | solution.py:413
  9.6 1.9 %collective-permute-start.3 = (bf16[128,512]{1,0:T(8,128)(2,1)}, bf16[128,512]{1,0:T(8,128)(2,1)S(1)}, u32[]{:S(2)}, u32[]{:S(2)}) collective-permute-start(bf16[128,512]{1,0:T(8,128)(2,1)} %v_hbm.1), channel_id=1, source_target_pairs={{0,8},{16,24},{1,9},{17,25},{2,10},{18,26},{3,11},{19,27},{4,12},{... | collective-permute-start | bytes 393224 | tf_op jit(solution)/shard_map/ppermute | solution.py:414
  12.2 4.0 %prepare.1 = (bf16[128,512]{1,0:T(8,128)(2,1)S(1)}, bf16[128,512]{1,0:T(8,128)(2,1)S(1)}, bf16[128,4096]{1,0:T(8,128)(2,1)S(1)}, f32[128,384]{1,0:T(8,128)S(1)},...) custom-call(s32[8]{0:T(128)} %docs_hbm.1, bf16[128,512]{1,0:T(8,128)(2,1)} %k_hbm.1, ...), custom_call_target="tpu_custom_call" | custom-call | bytes 8388608 | tf_op jit(solution)/shard_map/prepare/pallas_call | solution.py:124
  16.9 1.4 %collective-permute-start.5 = (bf16[128,1024]{1,0:T(8,128)(2,1)S(1)}, bf16[128,1024]{1,0:T(8,128)(2,1)S(1)}, u32[]{:S(2)}, u32[]{:S(2)}) collective-permute-start(bf16[128,1024]{1,0:T(8,128)(2,1)S(1)} %attend_0.1.after.refs_1_), channel_id=1, source_target_pairs={{0,8},{4,20},{8,0},{12,28},{16,24},{20,4},{24,16},{28,12},{1,9},{5... | collective-permute-start | bytes 786440 | tf_op jit(solution)/shard_map/ppermute | solution.py:394
  18.3 1.8 %collective-permute-start.6 = (bf16[128,1024]{1,0:T(8,128)(2,1)S(1)}, bf16[128,1024]{1,0:T(8,128)(2,1)S(1)}, u32[]{:S(2)}, u32[]{:S(2)}) collective-permute-start(bf16[128,1024]{1,0:T(8,128)(2,1)S(1)} %attend_0.1.after.refs_1_), channel_id=1, source_target_pairs={{0,16},{4,12},{8,24},{12,4},{16,0},{20,28},{24,8},{28,20},{1,17},{... | collective-permute-start | bytes 786440 | tf_op jit(solution)/shard_map/ppermute | solution.py:395
  20.1 3.5 %load_2.1 = (bf16[1024,2048]{1,0:T(8,128)(2,1)S(1)}, bf16[1024,2048]{1,0:T(8,128)(2,1)S(1)}, f32[8,128]{1,0:T(8,128)S(1)}) custom-call(bf16[128,1024]{1,0:T(8,128)(2,1)S(1)} %attend_0.1.after.refs_1_, bf16[4096,4096]{1,0:T(8,128)(2,1)} %refs_1_.5), custom_call_target="tpu_custom_call" | custom-call | bytes 16777216 | tf_op jit(solution)/shard_map/load_2/pallas_call | solution.py:165
  24.6 2.6 %collective-permute-start.7 = (bf16[128,1024]{1,0:T(8,128)(2,1)S(1)}, bf16[128,1024]{1,0:T(8,128)(2,1)S(1)}, u32[]{:S(2)}, u32[]{:S(2)}) collective-permute-start(bf16[128,1024]{1,0:T(8,128)(2,1)S(1)} %gate.3.refs_2_.rest_0_), channel_id=1, source_target_pairs={{0,16},{4,12},{8,24},{12,4},{16,0},{20,28},{24,8},{28,20},{1,17},{... | collective-permute-start | bytes 786440 | tf_op jit(solution)/shard_map/ppermute | solution.py:399
  27.2 1.3 %attend_1.1.refs_3_ = bf16[128,2048]{1,0:T(8,128)(2,1)S(1)} custom-call(bf16[128,4096]{1,0:T(8,128)(2,1)S(1)} %get-tuple-element.40.q_ref, f32[128,384]{1,0:T(8,128)S(1)} %get-tuple-element.41.mask_ref, bf16[128,512]{1,0:T(8,128)(2,1)S(1)} %get-tuple-element.42.k0, bf16[128,512]{1,0:T(8,128)(2,1)S(1)} %collective-permute-done.1.k_near.k_far, ...), custom_call_target="tpu_custom_call" | custom-call | tf_op jit(solution)/shard_map/attend_1/pallas_call | solution.py:216
  28.5 1.5 %collective-permute-start.8 = (bf16[128,2048]{1,0:T(8,128)(2,1)S(1)}, bf16[128,2048]{1,0:T(8,128)(2,1)S(1)}, u32[]{:S(2)}, u32[]{:S(2)}) collective-permute-start(bf16[128,2048]{1,0:T(8,128)(2,1)S(1)} %attend_1.1.refs_3_), channel_id=1, source_target_pairs={{0,8},{4,20},{8,0},{12,28},{16,24},{20,4},{24,16},{28,12},{1,9},{5... | collective-permute-start | bytes 1572872 | tf_op jit(solution)/shard_map/ppermute | solution.py:394
  30.1 4.4 %collective-permute-done.7.refs_4_ = bf16[128,1024]{1,0:T(8,128)(2,1)S(1)} collective-permute-done((bf16[128,1024]{1,0:T(8,128)(2,1)S(1)}, bf16[128,1024]{1,0:T(8,128)(2,1)S(1)}, u32[]{:S(2)}, u32[]{:S(2)}) %collective-permute-start.7) | collective-permute-done | bytes 262176 | tf_op jit(solution)/shard_map/ppermute | solution.py:399
  34.5 3.1 %step_0_0.1 = (f32[512,2048]{1,0:T(8,128)S(1)}, bf16[512,1024]{1,0:T(8,128)(2,1)S(1)}, f32[8,128]{1,0:T(8,128)S(1)}) custom-call(s32[16]{0:T(128)S(1)} %copy-done, bf16[128,1024]{1,0:T(8,128)(2,1)S(1)} %attend_0.1.after.refs_1_, bf16[128,1024]{1,0:T(8,128)(2,1)S(1)} %gate.3.refs_2_.rest_0_, bf16[128,1024]{1,0:T(8,128)(2,1)S(1)} %collective-permute-done.6.refs_3_, ...), custom_call_target="tpu_custom_call" | custom-call | flops 2147483648 | tf_op jit(solution)/shard_map/step_0_0/pallas_call | solution.py:305
  37.5 2.4 %step_1_0.1 = (f32[512,2048]{1,0:T(8,128)S(1)}, f32[8,128]{1,0:T(8,128)S(1)}) custom-call(f32[8,128]{1,0:T(8,128)S(1)} %get-tuple-element.46.refs_0_, bf16[512,1024]{1,0:T(8,128)(2,1)S(1)} %get-tuple-element.47.refs_1_, bf16[1024,2048]{1,0:T(8,128)(2,1)S(1)} %get-tuple-element.48.refs_2_), custom_call_target="tpu_custom_call" | custom-call | flops 2147483648 | tf_op jit(solution)/shard_map/step_1_0/pallas_call | solution.py:305
  39.9 2.2 %collective-permute-start.10 = (bf16[128,2048]{1,0:T(8,128)(2,1)S(1)}, bf16[128,2048]{1,0:T(8,128)(2,1)S(1)}, u32[]{:S(2)}, u32[]{:S(2)}) collective-permute-start(bf16[128,2048]{1,0:T(8,128)(2,1)S(1)} %gate.4.refs_4_.after), channel_id=1, source_target_pairs={{0,16},{4,12},{8,24},{12,4},{16,0},{20,28},{24,8},{28,20},{1,17},{... | collective-permute-start | bytes 1572872 | tf_op jit(solution)/shard_map/ppermute | solution.py:399
  42.1 2.2 %load_6.1 = (bf16[1024,2048]{1,0:T(8,128)(2,1)S(1)}, f32[8,128]{1,0:T(8,128)S(1)}) custom-call(bf16[128,2048]{1,0:T(8,128)(2,1)S(1)} %gate.4.refs_4_.after, bf16[4096,4096]{1,0:T(8,128)(2,1)} %refs_1_.5), custom_call_target="tpu_custom_call" | custom-call | bytes 8388608 | tf_op jit(solution)/shard_map/load_6/pallas_call | solution.py:165
  45.1 2.2 %collective-permute-start.11 = (bf16[128,1024]{1,0:T(8,128)(2,1)S(1)}, bf16[128,1024]{1,0:T(8,128)(2,1)S(1)}, u32[]{:S(2)}, u32[]{:S(2)}) collective-permute-start(bf16[128,1024]{1,0:T(8,128)(2,1)S(1)} %attend_3.1.refs_3_), channel_id=1, source_target_pairs={{0,8},{4,20},{8,0},{12,28},{16,24},{20,4},{24,16},{28,12},{1,9},{5... | collective-permute-start | bytes 786440 | tf_op jit(solution)/shard_map/ppermute | solution.py:394
  47.3 4.3 %collective-permute-done.10.refs_6_ = bf16[128,2048]{1,0:T(8,128)(2,1)S(1)} collective-permute-done((bf16[128,2048]{1,0:T(8,128)(2,1)S(1)}, bf16[128,2048]{1,0:T(8,128)(2,1)S(1)}, u32[]{:S(2)}, u32[]{:S(2)}) %collective-permute-start.10) | collective-permute-done | bytes 524320 | tf_op jit(solution)/shard_map/ppermute | solution.py:399
  51.6 3.4 %step_2_0.1 = (f32[512,2048]{1,0:T(8,128)S(1)}, bf16[512,1024]{1,0:T(8,128)(2,1)S(1)}, bf16[1024,2048]{1,0:T(8,128)(2,1)S(1)}, f32[8,128]{1,0:T(8,128)S(1)}) custom-call(f32[8,128]{1,0:T(8,128)S(1)} %get-tuple-element.49.after.refs_0_.rest_1_, bf16[4096,4096]{1,0:T(8,128)(2,1)} %refs_1_.5, s32[16]{0:T(128)S(1)} %copy-done, ...), custom_call_target="tpu_custom_call", output_to_operand_aliasing={{0}: (8, {})} | custom-call | flops 2147483648 | tf_op jit(solution)/shard_map/step_2_0/pallas_call | solution.py:305
  55.0 2.8 %step_3_0.1 = (f32[512,2048]{1,0:T(8,128)S(1)}, f32[8,128]{1,0:T(8,128)S(1)}) custom-call(f32[8,128]{1,0:T(8,128)S(1)} %get-tuple-element.52.refs_0_, bf16[512,1024]{1,0:T(8,128)(2,1)S(1)} %get-tuple-element.53.refs_1_, bf16[1024,2048]{1,0:T(8,128)(2,1)S(1)} %get-tuple-element.54.refs_2_, ...), custom_call_target="tpu_custom_call", output_to_operand_aliasing={{0}: (3, {})} | custom-call | flops 2147483648 | tf_op jit(solution)/shard_map/step_3_0/pallas_call | solution.py:305
  58.2 3.4 %step_4_0.1 = (f32[512,2048]{1,0:T(8,128)S(1)}, bf16[512,1024]{1,0:T(8,128)(2,1)S(1)}, bf16[1024,2048]{1,0:T(8,128)(2,1)S(1)}, f32[8,128]{1,0:T(8,128)S(1)}) custom-call(f32[8,128]{1,0:T(8,128)S(1)} %get-tuple-element.56.refs_0_.after, bf16[4096,4096]{1,0:T(8,128)(2,1)} %refs_1_.5, s32[16]{0:T(128)S(1)} %copy-done, ...), custom_call_target="tpu_custom_call", output_to_operand_aliasing={{0}: (8, {})} | custom-call | flops 2147483648 | tf_op jit(solution)/shard_map/step_4_0/pallas_call | solution.py:305
  61.6 2.9 %step_5_0.1 = (f32[512,2048]{1,0:T(8,128)S(1)}, f32[8,128]{1,0:T(8,128)S(1)}) custom-call(f32[8,128]{1,0:T(8,128)S(1)} %get-tuple-element.59.refs_0_, bf16[512,1024]{1,0:T(8,128)(2,1)S(1)} %get-tuple-element.60.refs_1_, bf16[1024,2048]{1,0:T(8,128)(2,1)S(1)} %get-tuple-element.61.refs_2_, ...), custom_call_target="tpu_custom_call", output_to_operand_aliasing={{0}: (3, {})} | custom-call | flops 2147483648 | tf_op jit(solution)/shard_map/step_5_0/pallas_call | solution.py:305
  64.5 3.1 %step_6_0.1 = (f32[256,2048]{1,0:T(8,128)S(1)}, bf16[256,2048]{1,0:T(8,128)(2,1)S(1)}, bf16[512,1024]{1,0:T(8,128)(2,1)S(1)}, bf16[1024,2048]{1,0:T(8,128)(2,1)S(1)}, f32[8,128]{1,0:T(8,128)S(1)}) custom-call(f32[8,128]{1,0:T(8,128)S(1)} %get-tuple-element.63.refs_0_, bf16[4096,4096]{1,0:T(8,128)(2,1)} %refs_1_.5, s32[16]{0:T(128)S(1)} %copy-done, ...), custom_call_target="tpu_custom_call" | custom-call | flops 2147483648 | tf_op jit(solution)/shard_map/step_6_0/pallas_call | solution.py:305
  67.7 2.9 %step_7_0.1 = (f32[256,2048]{1,0:T(8,128)S(1)}, bf16[256,2048]{1,0:T(8,128)(2,1)S(1)}, f32[8,128]{1,0:T(8,128)}) custom-call(f32[8,128]{1,0:T(8,128)S(1)} %get-tuple-element.67.refs_0_, bf16[512,1024]{1,0:T(8,128)(2,1)S(1)} %get-tuple-element.68.refs_1_, bf16[1024,2048]{1,0:T(8,128)(2,1)S(1)} %get-tuple-element.69.refs_2_, ...), custom_call_target="tpu_custom_call" | custom-call | flops 2147483648 | tf_op jit(solution)/shard_map/step_7_0/pallas_call | solution.py:305
  (29 shorter events, 7.4 us)
Async XLA Ops:
  0.0 11.5 %collective-permute-start = (bf16[128,512]{1,0:T(8,128)(2,1)}, bf16[128,512]{1,0:T(8,128)(2,1)S(1)}, u32[]{:S(2)}, u32[]{:S(2)}) collective-permute-start(bf16[128,512]{1,0:T(8,128)(2,1)} %v_hbm.1), channel_id=1, source_target_pairs={{0,16},{8,24},{1,17},{9,25},{2,18},{10,26},{3,19},{11,27},{4,20},{... | collective-permute-start | bytes 393224 | tf_op jit(solution)/shard_map/ppermute | solution.py:411
  4.9 11.3 %collective-permute-start.2 = (bf16[128,512]{1,0:T(8,128)(2,1)}, bf16[128,512]{1,0:T(8,128)(2,1)S(1)}, u32[]{:S(2)}, u32[]{:S(2)}) collective-permute-start(bf16[128,512]{1,0:T(8,128)(2,1)} %k_hbm.1), channel_id=1, source_target_pairs={{0,16},{8,24},{1,17},{9,25},{2,18},{10,26},{3,19},{11,27},{4,20},{... | collective-permute-start | bytes 393224 | tf_op jit(solution)/shard_map/ppermute | solution.py:412
  6.2 10.0 %collective-permute-start.1 = (bf16[128,512]{1,0:T(8,128)(2,1)}, bf16[128,512]{1,0:T(8,128)(2,1)S(1)}, u32[]{:S(2)}, u32[]{:S(2)}) collective-permute-start(bf16[128,512]{1,0:T(8,128)(2,1)} %k_hbm.1), channel_id=1, source_target_pairs={{0,8},{8,16},{16,24},{1,9},{9,17},{17,25},{2,10},{10,18},{18,26},{... | collective-permute-start | bytes 393224 | tf_op jit(solution)/shard_map/ppermute | solution.py:413
  9.6 6.6 %collective-permute-start.3 = (bf16[128,512]{1,0:T(8,128)(2,1)}, bf16[128,512]{1,0:T(8,128)(2,1)S(1)}, u32[]{:S(2)}, u32[]{:S(2)}) collective-permute-start(bf16[128,512]{1,0:T(8,128)(2,1)} %v_hbm.1), channel_id=1, source_target_pairs={{0,8},{16,24},{1,9},{17,25},{2,10},{18,26},{3,11},{19,27},{4,12},{... | collective-permute-start | bytes 393224 | tf_op jit(solution)/shard_map/ppermute | solution.py:414
  11.5 4.7 %collective-permute-start.4 = (bf16[128,512]{1,0:T(8,128)(2,1)S(1)}, bf16[128,512]{1,0:T(8,128)(2,1)S(1)}, u32[]{:S(2)}, u32[]{:S(2)}) collective-permute-start(bf16[128,512]{1,0:T(8,128)(2,1)S(1)} %collective-permute-done.after.v2), channel_id=1, source_target_pairs={{24,16},{25,17},{26,18},{27,19},{28,20},{29,21},{30,22},{31,23}} | collective-permute-start | bytes 393224 | tf_op jit(solution)/shard_map/ppermute | solution.py:415
  16.9 17.6 %copy-start = (s32[16]{0:T(128)S(1)}, s32[16]{0:T(128)}, u32[]{:S(2)}) copy-start(s32[16]{0:T(128)} %refs_2_.5) | copy-start | bytes 196
  16.9 7.7 %collective-permute-start.5 = (bf16[128,1024]{1,0:T(8,128)(2,1)S(1)}, bf16[128,1024]{1,0:T(8,128)(2,1)S(1)}, u32[]{:S(2)}, u32[]{:S(2)}) collective-permute-start(bf16[128,1024]{1,0:T(8,128)(2,1)S(1)} %attend_0.1.after.refs_1_), channel_id=1, source_target_pairs={{0,8},{4,20},{8,0},{12,28},{16,24},{20,4},{24,16},{28,12},{1,9},{5... | collective-permute-start | bytes 786440 | tf_op jit(solution)/shard_map/ppermute | solution.py:394
  18.3 11.8 %collective-permute-start.6 = (bf16[128,1024]{1,0:T(8,128)(2,1)S(1)}, bf16[128,1024]{1,0:T(8,128)(2,1)S(1)}, u32[]{:S(2)}, u32[]{:S(2)}) collective-permute-start(bf16[128,1024]{1,0:T(8,128)(2,1)S(1)} %attend_0.1.after.refs_1_), channel_id=1, source_target_pairs={{0,16},{4,12},{8,24},{12,4},{16,0},{20,28},{24,8},{28,20},{1,17},{... | collective-permute-start | bytes 786440 | tf_op jit(solution)/shard_map/ppermute | solution.py:395
  24.6 9.8 %collective-permute-start.7 = (bf16[128,1024]{1,0:T(8,128)(2,1)S(1)}, bf16[128,1024]{1,0:T(8,128)(2,1)S(1)}, u32[]{:S(2)}, u32[]{:S(2)}) collective-permute-start(bf16[128,1024]{1,0:T(8,128)(2,1)S(1)} %gate.3.refs_2_.rest_0_), channel_id=1, source_target_pairs={{0,16},{4,12},{8,24},{12,4},{16,0},{20,28},{24,8},{28,20},{1,17},{... | collective-permute-start | bytes 786440 | tf_op jit(solution)/shard_map/ppermute | solution.py:399
  28.5 11.4 %collective-permute-start.8 = (bf16[128,2048]{1,0:T(8,128)(2,1)S(1)}, bf16[128,2048]{1,0:T(8,128)(2,1)S(1)}, u32[]{:S(2)}, u32[]{:S(2)}) collective-permute-start(bf16[128,2048]{1,0:T(8,128)(2,1)S(1)} %attend_1.1.refs_3_), channel_id=1, source_target_pairs={{0,8},{4,20},{8,0},{12,28},{16,24},{20,4},{24,16},{28,12},{1,9},{5... | collective-permute-start | bytes 1572872 | tf_op jit(solution)/shard_map/ppermute | solution.py:394
  30.1 17.2 %collective-permute-start.9 = (bf16[128,2048]{1,0:T(8,128)(2,1)S(1)}, bf16[128,2048]{1,0:T(8,128)(2,1)S(1)}, u32[]{:S(2)}, u32[]{:S(2)}) collective-permute-start(bf16[128,2048]{1,0:T(8,128)(2,1)S(1)} %attend_1.1.refs_3_), channel_id=1, source_target_pairs={{0,16},{4,12},{8,24},{12,4},{16,0},{20,28},{24,8},{28,20},{1,17},{... | collective-permute-start | bytes 1572872 | tf_op jit(solution)/shard_map/ppermute | solution.py:395
  39.9 11.7 %collective-permute-start.10 = (bf16[128,2048]{1,0:T(8,128)(2,1)S(1)}, bf16[128,2048]{1,0:T(8,128)(2,1)S(1)}, u32[]{:S(2)}, u32[]{:S(2)}) collective-permute-start(bf16[128,2048]{1,0:T(8,128)(2,1)S(1)} %gate.4.refs_4_.after), channel_id=1, source_target_pairs={{0,16},{4,12},{8,24},{12,4},{16,0},{20,28},{24,8},{28,20},{1,17},{... | collective-permute-start | bytes 1572872 | tf_op jit(solution)/shard_map/ppermute | solution.py:399
  45.0 19.5 %collective-permute-start.12 = (bf16[128,1024]{1,0:T(8,128)(2,1)S(1)}, bf16[128,1024]{1,0:T(8,128)(2,1)S(1)}, u32[]{:S(2)}, u32[]{:S(2)}) collective-permute-start(bf16[128,1024]{1,0:T(8,128)(2,1)S(1)} %attend_3.1.refs_3_), channel_id=1, source_target_pairs={{0,16},{4,12},{8,24},{12,4},{16,0},{20,28},{24,8},{28,20},{1,17},{... | collective-permute-start | bytes 786440 | tf_op jit(solution)/shard_map/ppermute | solution.py:395
  45.1 12.7 %collective-permute-start.11 = (bf16[128,1024]{1,0:T(8,128)(2,1)S(1)}, bf16[128,1024]{1,0:T(8,128)(2,1)S(1)}, u32[]{:S(2)}, u32[]{:S(2)}) collective-permute-start(bf16[128,1024]{1,0:T(8,128)(2,1)S(1)} %attend_3.1.refs_3_), channel_id=1, source_target_pairs={{0,8},{4,20},{8,0},{12,28},{16,24},{20,4},{24,16},{28,12},{1,9},{5... | collective-permute-start | bytes 786440 | tf_op jit(solution)/shard_map/ppermute | solution.py:394
  57.8 6.7 %collective-permute-start.13 = (bf16[128,1024]{1,0:T(8,128)(2,1)S(1)}, bf16[128,1024]{1,0:T(8,128)(2,1)S(1)}, u32[]{:S(2)}, u32[]{:S(2)}) collective-permute-start(bf16[128,1024]{1,0:T(8,128)(2,1)S(1)} %gate.5.refs_4_), channel_id=1, source_target_pairs={{0,16},{4,12},{8,24},{12,4},{16,0},{20,28},{24,8},{28,20},{1,17},{... | collective-permute-start | bytes 786440 | tf_op jit(solution)/shard_map/ppermute | solution.py:399
  67.6 3.5 %collective-permute-start.15 = (bf16[256,2048]{1,0:T(8,128)(2,1)S(1)}, bf16[256,2048]{1,0:T(8,128)(2,1)S(1)}, u32[]{:S(2)}, u32[]{:S(2)}) collective-permute-start(bf16[256,2048]{1,0:T(8,128)(2,1)S(1)} %get-tuple-element.74), channel_id=1, source_target_pairs={{0,4},{4,0},{1,5},{5,1},{2,6},{6,2},{3,7},{7,3},{8,12},{12,8},{9,1... | collective-permute-start | bytes 3145736 | tf_op jit(solution)/shard_map/ppermute | solution.py:464
  70.6 2.8 %collective-permute-start.14 = (bf16[256,2048]{1,0:T(8,128)(2,1)S(1)}, bf16[256,2048]{1,0:T(8,128)(2,1)S(1)}, u32[]{:S(2)}, u32[]{:S(2)}) collective-permute-start(bf16[256,2048]{1,0:T(8,128)(2,1)S(1)} %get-tuple-element.72), channel_id=1, source_target_pairs={{0,4},{4,0},{1,5},{5,1},{2,6},{6,2},{3,7},{7,3},{8,12},{12,8},{9,1... | collective-permute-start | bytes 3145736 | tf_op jit(solution)/shard_map/ppermute | solution.py:464

commit v5 on v4

--- a/solution.py
+++ b/solution.py
@@ -92,7 +92,7 @@
     )
 
 
-def prepare_kernel(docs_hbm, k_hbm, v_hbm, q_hbm, w_hbm, after, k_ref, v_ref, q_ref, mask_ref, left_ref, right_ref, docs, sems):
+def prepare_kernel(docs_hbm, k_hbm, v_hbm, q_hbm, w_hbm, k_ref, v_ref, q_ref, mask_ref, left_ref, right_ref, docs, sems):
     lengths = pltpu.make_async_copy(docs_hbm, docs, sems.at[0])
     loads = [
         pltpu.make_async_copy(k_hbm, k_ref, sems.at[1]),
@@ -119,7 +119,7 @@
         load.wait()
 
 
-def prepare(doc_lengths, key_rows, value_rows, queries, w_out, chunks, after):
+def prepare(doc_lengths, key_rows, value_rows, queries, w_out, chunks):
     rows = queries.shape[0]
     return pl.pallas_call(
         prepare_kernel,
@@ -131,7 +131,7 @@
             jax.ShapeDtypeStruct(block_shape(w_out, chunks), jnp.bfloat16),
             jax.ShapeDtypeStruct(block_shape(w_out, chunks), jnp.bfloat16),
         ],
-        in_specs=[HBM] * 6,
+        in_specs=[HBM] * 5,
         out_specs=[VMEM] * 6,
         scratch_shapes=[
             pltpu.SMEM(doc_lengths.shape, jnp.int32),
@@ -143,7 +143,7 @@
         ),
         name="prepare",
     )(
-        in_hbm(doc_lengths), in_hbm(key_rows), in_hbm(value_rows), in_hbm(queries), w_out, after
+        in_hbm(doc_lengths), in_hbm(key_rows), in_hbm(value_rows), in_hbm(queries), w_out
     )
 
 
@@ -392,13 +392,10 @@
         return pairs
 
     near = lax.ppermute(own, ("ctx", "tp"), route(True))
+    far = lax.ppermute(near, ("ctx", "tp"), route(False))
+    own = gate(own, near)
     side = lax.ppermute(own, ("ctx", "tp"), route(False))
-
-    def forward(after):
-        first = near if after is None else gate(near, after)
-        return own, first, side, lax.ppermute(first, ("ctx", "tp"), route(False))
-
-    return near, side, forward
+    return own, near, side, far
 
 
 def local(queries, key_rows, value_rows, doc_lengths, unit_source, w_out):
@@ -412,10 +409,11 @@
     key_two = lax.ppermute(key_rows, "ctx", two)
     key_near = lax.ppermute(key_rows, "ctx", [(0, 1), (1, 2), (2, 3)])
     value_near = lax.ppermute(value_rows, "ctx", [(0, 1), (2, 3)])
+    own_keys, own_values, held, mask, left, right = prepare(
+        doc_lengths, key_rows, value_rows, queries, w_out, kv_heads
+    )
+    value_two = gate(value_two, mask)
     value_far = lax.ppermute(value_two, "ctx", [(3, 2)])
-    own_keys, own_values, held, mask, left, right = prepare(
-        doc_lengths, key_rows, value_rows, queries, w_out, kv_heads, value_two
-    )
     keys = (own_keys, key_near, key_near, key_two)
     values = (own_values, value_near, value_far, value_two)
     half_columns = w_out.shape[1] // HALVES
@@ -424,15 +422,10 @@
 
     def rows_of(groups, after):
         own = attend(groups, width, held, mask, keys, values, after)
-        near, side, forward = gather_rows(own)
-
-        def arrive(after):
-            pieces = forward(after)
-            for i, g in enumerate(groups):
-                rows[g] = (pieces, i * width)
-            return pieces[1]
-
-        return own, arrive
+        pieces = gather_rows(own)
+        for i, g in enumerate(groups):
+            rows[g] = (pieces, i * width)
+        return own
 
     def load(wanted, after):
         loaded, token = load_blocks([g * HALVES for g in wanted], w_out, kv_heads, after)
@@ -449,31 +442,24 @@
         )
         if loads:
             state["right"][g] = following
-        parts = 1
-        seconds = []
-        for i in range(parts):
-            second, lhs, _, state["before"] = step(
-                g * HALVES + 1, last, lhs, column, state["right"][g],
-                i * half_columns // parts, half_columns // parts, None,
-                state["totals"][1], state["before"],
-            )
-            seconds.append(second)
+        second, _, _, state["before"] = step(
+            g * HALVES + 1, last, lhs, column, state["right"][g], 0, half_columns, None,
+            state["totals"][1], state["before"],
+        )
         if last:
-            for kept, sent in [first, *seconds]:
+            for kept, sent in (first, second):
                 mine.append(kept)
                 got.append(lax.ppermute(sent, "tp", [(0, 1), (1, 0)]))
         else:
-            state["totals"] = [first[0], seconds[0][0]]
+            state["totals"] = [first[0], second[0]]
         return state["before"]
 
-    own, arrive = rows_of((0,), [])
-    near = arrive(load((1, 2), own))
-    own, arrive = rows_of((1, 2), [near])
+    own = rows_of((0,), [])
+    own = rows_of((1,), [load((1,), own)])
+    own = rows_of((2,), [load((2, 3), own), rows[0][0][1]])
     done = steps(0)
-    near = arrive(done)
-    _, arrive = rows_of((3,), [load((3,), near), done])
-    arrive(steps(1))
-    for g in range(2, kv_heads):
+    rows_of((3,), [own, done])
+    for g in range(1, kv_heads):
         steps(g)
     out = total(0, w_out.shape[1], mine[:1], got[:1], None)
     return total(half_columns, w_out.shape[1], mine[1:], got[1:], out)

time: 74.9 us -> 73.2 us (0.977)
  waiting for transfers between devices: 10.9 us -> 5.64 us
  starting transfers between devices: 24.9 us -> 28.4 us
    ppermute x3 -> x4, starting transfers between devices: 1.91 us -> 10.4 us  [gather_rows(): side = lax.ppermute(own, ('ctx', 'tp'), route(False))]
    ppermute x3 -> x4, waiting for transfers between devices: 8.7 us -> 2.17 us  [gather_rows(): far = lax.ppermute(near, ('ctx', 'tp'), route(False))]
    ppermute x3 -> x4, starting transfers between devices: 5.12 us -> 0.96 us  [gather_rows(): far = lax.ppermute(near, ('ctx', 'tp'), route(False))]
    ppermute x3 -> x4, waiting for transfers between devices: 1.01 us -> 2.24 us  [gather_rows(): near = lax.ppermute(own, ('ctx', 'tp'), route(True))]
    ppermute x3 -> x4, starting transfers between devices: 5.19 us -> 4.36 us  [gather_rows(): near = lax.ppermute(own, ('ctx', 'tp'), route(True))]
    pallas_call x3 -> x4, Pallas kernels: 2.64 us -> 2.73 us  [attend(): pl.pallas_call(functools.partial(attend_kernel, groups), out_shape=jax.Sh...]
  transfers between devices with their start and end apart: 16 -> 19, of which waited for: 4 -> 5; matrix products, arithmetic and copies ran while one was open for 0% -> 0% of each run, Pallas kernels for 45% -> 46%
where the time goes in v5:
time: 73.2 us; the launch traced here: 73 us
  Pallas kernels  38.5 us (53%)
  starting transfers between devices  28.4 us (39%)
  waiting for transfers between devices  5.64 us (8%)
    pallas_call x8, Pallas kernels, step(): pl.pallas_call(functools.partial(step_kernel, index, last, column, first,...  23.9 us
    ppermute x4, starting transfers between devices, gather_rows(): side = lax.ppermute(own, ('ctx', 'tp'), route(False))  10.4 us
    pallas_call x2, Pallas kernels, load_blocks(): pl.pallas_call(functools.partial(load_kernel, indexes), out_shape=[jax.Sh...  5.68 us
    ppermute x1, starting transfers between devices, local(): value_two = lax.ppermute(value_rows, 'ctx', two)  4.87 us
    ppermute x4, starting transfers between devices, gather_rows(): near = lax.ppermute(own, ('ctx', 'tp'), route(True))  4.36 us
    pallas_call x1, Pallas kernels, prepare(): pl.pallas_call(prepare_kernel, out_shape=[jax.ShapeDtypeStruct(key_rows.s...  3.95 us
    ppermute x1, starting transfers between devices, local(): key_near = lax.ppermute(key_rows, 'ctx', [(0, 1), (1, 2), (2, 3)])  3.4 us
    pallas_call x4, Pallas kernels, attend(): pl.pallas_call(functools.partial(attend_kernel, groups), out_shape=jax.Sh...  2.73 us
  transfers between devices with their start and end apart: 19, of which 5 were waited for; matrix products, arithmetic and copies ran while one was open for 0% of the time, Pallas kernels for 46%

profile of v5, /device:TPU:0, one launch (start us, length us, event | category | flops | bytes accessed | tf_op | source)
XLA Modules:
  0.0 73.0 jit_solution(6482978044405001370)
XLA Ops:
  0.0 4.9 %collective-permute-start.3 = (bf16[128,512]{1,0:T(8,128)(2,1)}, bf16[128,512]{1,0:T(8,128)(2,1)S(1)}, u32[]{:S(2)}, u32[]{:S(2)}) collective-permute-start(bf16[128,512]{1,0:T(8,128)(2,1)} %v_hbm.1), channel_id=1, source_target_pairs={{0,16},{8,24},{1,17},{9,25},{2,18},{10,26},{3,19},{11,27},{4,20},{... | collective-permute-start | bytes 393224 | tf_op jit(solution)/shard_map/ppermute | solution.py:408
  4.9 3.4 %collective-permute-start = (bf16[128,512]{1,0:T(8,128)(2,1)}, bf16[128,512]{1,0:T(8,128)(2,1)S(1)}, u32[]{:S(2)}, u32[]{:S(2)}) collective-permute-start(bf16[128,512]{1,0:T(8,128)(2,1)} %k_hbm.1), channel_id=1, source_target_pairs={{0,8},{8,16},{16,24},{1,9},{9,17},{17,25},{2,10},{10,18},{18,26},{... | collective-permute-start | bytes 393224 | tf_op jit(solution)/shard_map/ppermute | solution.py:410
  8.3 1.3 %collective-permute-start.1 = (bf16[128,512]{1,0:T(8,128)(2,1)}, bf16[128,512]{1,0:T(8,128)(2,1)S(1)}, u32[]{:S(2)}, u32[]{:S(2)}) collective-permute-start(bf16[128,512]{1,0:T(8,128)(2,1)} %k_hbm.1), channel_id=1, source_target_pairs={{0,16},{8,24},{1,17},{9,25},{2,18},{10,26},{3,19},{11,27},{4,20},{... | collective-permute-start | bytes 393224 | tf_op jit(solution)/shard_map/ppermute | solution.py:409
  9.6 1.9 %collective-permute-start.2 = (bf16[128,512]{1,0:T(8,128)(2,1)}, bf16[128,512]{1,0:T(8,128)(2,1)S(1)}, u32[]{:S(2)}, u32[]{:S(2)}) collective-permute-start(bf16[128,512]{1,0:T(8,128)(2,1)} %v_hbm.1), channel_id=1, source_target_pairs={{0,8},{16,24},{1,9},{17,25},{2,10},{18,26},{3,11},{19,27},{4,12},{... | collective-permute-start | bytes 393224 | tf_op jit(solution)/shard_map/ppermute | solution.py:411
  11.5 4.0 %prepare.1 = (bf16[128,512]{1,0:T(8,128)(2,1)S(1)}, bf16[128,512]{1,0:T(8,128)(2,1)S(1)}, bf16[128,4096]{1,0:T(8,128)(2,1)S(1)}, f32[128,384]{1,0:T(8,128)S(1)},...) custom-call(s32[8]{0:T(128)} %docs_hbm.1, bf16[128,512]{1,0:T(8,128)(2,1)} %k_hbm.1, ...), custom_call_target="tpu_custom_call" | custom-call | bytes 8388608 | tf_op jit(solution)/shard_map/prepare/pallas_call | solution.py:124
  17.4 2.2 %load_2.1 = (bf16[1024,2048]{1,0:T(8,128)(2,1)S(1)}, f32[8,128]{1,0:T(8,128)S(1)}) custom-call(bf16[128,1024]{1,0:T(8,128)(2,1)S(1)} %attend_0.1.x.after, bf16[4096,4096]{1,0:T(8,128)(2,1)} %refs_1_.5), custom_call_target="tpu_custom_call" | custom-call | bytes 8388608 | tf_op jit(solution)/shard_map/load_2/pallas_call | solution.py:165
  20.3 1.6 %collective-permute-start.8 = (bf16[128,1024]{1,0:T(8,128)(2,1)S(1)}, bf16[128,1024]{1,0:T(8,128)(2,1)S(1)}, u32[]{:S(2)}, u32[]{:S(2)}) collective-permute-start(bf16[128,1024]{1,0:T(8,128)(2,1)S(1)} %attend_1.1.x.after), channel_id=1, source_target_pairs={{0,8},{4,20},{8,0},{12,28},{16,24},{20,4},{24,16},{28,12},{1,9},{5... | collective-permute-start | bytes 786440 | tf_op jit(solution)/shard_map/ppermute | solution.py:394
  22.0 1.4 %collective-permute-done.5.after.refs_2_.rest_1_ = bf16[128,1024]{1,0:T(8,128)(2,1)S(1)} collective-permute-done((bf16[128,1024]{1,0:T(8,128)(2,1)S(1)}, bf16[128,1024]{1,0:T(8,128)(2,1)S(1)}, u32[]{:S(2)}, u32[]{:S(2)}) %collective-permute-start.5) | collective-permute-done | bytes 262176 | tf_op jit(solution)/shard_map/ppermute | solution.py:394
  23.3 4.9 %collective-permute-start.6 = (bf16[128,1024]{1,0:T(8,128)(2,1)S(1)}, bf16[128,1024]{1,0:T(8,128)(2,1)S(1)}, u32[]{:S(2)}, u32[]{:S(2)}) collective-permute-start(bf16[128,1024]{1,0:T(8,128)(2,1)S(1)} %gate.6.refs_1_), channel_id=1, source_target_pairs={{0,16},{4,12},{8,24},{12,4},{16,0},{20,28},{24,8},{28,20},{1,17},{... | collective-permute-start | bytes 786440 | tf_op jit(solution)/shard_map/ppermute | solution.py:397
  28.3 3.5 %load_4.1 = (bf16[1024,2048]{1,0:T(8,128)(2,1)S(1)}, bf16[1024,2048]{1,0:T(8,128)(2,1)S(1)}, f32[8,128]{1,0:T(8,128)S(1)}) custom-call(bf16[128,1024]{1,0:T(8,128)(2,1)S(1)} %attend_1.1.x.after, bf16[4096,4096]{1,0:T(8,128)(2,1)} %refs_1_.5), custom_call_target="tpu_custom_call" | custom-call | bytes 16777216 | tf_op jit(solution)/shard_map/load_4/pallas_call | solution.py:165
  31.8 2.2 %collective-permute-start.9 = (bf16[128,1024]{1,0:T(8,128)(2,1)S(1)}, bf16[128,1024]{1,0:T(8,128)(2,1)S(1)}, u32[]{:S(2)}, u32[]{:S(2)}) collective-permute-start(bf16[128,1024]{1,0:T(8,128)(2,1)S(1)} %gate.7.refs_3_), channel_id=1, source_target_pairs={{0,16},{4,12},{8,24},{12,4},{16,0},{20,28},{24,8},{28,20},{1,17},{... | collective-permute-start | bytes 786440 | tf_op jit(solution)/shard_map/ppermute | solution.py:397
  34.7 2.1 %collective-permute-start.11 = (bf16[128,1024]{1,0:T(8,128)(2,1)S(1)}, bf16[128,1024]{1,0:T(8,128)(2,1)S(1)}, u32[]{:S(2)}, u32[]{:S(2)}) collective-permute-start(bf16[128,1024]{1,0:T(8,128)(2,1)S(1)} %attend_2.1.x.rest_0_), channel_id=1, source_target_pairs={{0,8},{4,20},{8,0},{12,28},{16,24},{20,4},{24,16},{28,12},{1,9},{5... | collective-permute-start | bytes 786440 | tf_op jit(solution)/shard_map/ppermute | solution.py:394
  36.9 1.4 %collective-permute-done.7.refs_4_ = bf16[128,1024]{1,0:T(8,128)(2,1)S(1)} collective-permute-done((bf16[128,1024]{1,0:T(8,128)(2,1)S(1)}, bf16[128,1024]{1,0:T(8,128)(2,1)S(1)}, u32[]{:S(2)}, u32[]{:S(2)}) %collective-permute-start.7) | collective-permute-done | bytes 262176 | tf_op jit(solution)/shard_map/ppermute | solution.py:395
  38.2 3.1 %step_0_0.1 = (f32[512,2048]{1,0:T(8,128)S(1)}, bf16[512,1024]{1,0:T(8,128)(2,1)S(1)}, f32[8,128]{1,0:T(8,128)S(1)}) custom-call(s32[16]{0:T(128)S(1)} %copy-done, bf16[128,1024]{1,0:T(8,128)(2,1)S(1)} %gate.6.refs_1_, bf16[128,1024]{1,0:T(8,128)(2,1)S(1)} %collective-permute-done.5.after.refs_2_.rest_1_, ...), custom_call_target="tpu_custom_call" | custom-call | flops 2147483648 | tf_op jit(solution)/shard_map/step_0_0/pallas_call | solution.py:305
  41.3 2.4 %step_1_0.1 = (f32[512,2048]{1,0:T(8,128)S(1)}, f32[8,128]{1,0:T(8,128)S(1)}) custom-call(f32[8,128]{1,0:T(8,128)S(1)} %get-tuple-element.45.refs_0_, bf16[512,1024]{1,0:T(8,128)(2,1)S(1)} %get-tuple-element.46.refs_1_, bf16[1024,2048]{1,0:T(8,128)(2,1)S(1)} %get-tuple-element.47.refs_2_), custom_call_target="tpu_custom_call" | custom-call | flops 2147483648 | tf_op jit(solution)/shard_map/step_1_0/pallas_call | solution.py:305
  44.4 2.1 %collective-permute-start.12 = (bf16[128,1024]{1,0:T(8,128)(2,1)S(1)}, bf16[128,1024]{1,0:T(8,128)(2,1)S(1)}, u32[]{:S(2)}, u32[]{:S(2)}) collective-permute-start(bf16[128,1024]{1,0:T(8,128)(2,1)S(1)} %gate.8.refs_3_), channel_id=1, source_target_pairs={{0,16},{4,12},{8,24},{12,4},{16,0},{20,28},{24,8},{28,20},{1,17},{... | collective-permute-start | bytes 786440 | tf_op jit(solution)/shard_map/ppermute | solution.py:397
  46.6 3.4 %step_2_0.1 = (f32[512,2048]{1,0:T(8,128)S(1)}, bf16[512,1024]{1,0:T(8,128)(2,1)S(1)}, bf16[1024,2048]{1,0:T(8,128)(2,1)S(1)}, f32[8,128]{1,0:T(8,128)S(1)}) custom-call(f32[8,128]{1,0:T(8,128)S(1)} %get-tuple-element.48.refs_0_.rest_1_, bf16[4096,4096]{1,0:T(8,128)(2,1)} %refs_1_.5, s32[16]{0:T(128)S(1)} %copy-done, ...), custom_call_target="tpu_custom_call", output_to_operand_aliasing={{0}: (8, {})} | custom-call | flops 2147483648 | tf_op jit(solution)/shard_map/step_2_0/pallas_call | solution.py:305
  50.0 2.8 %step_3_0.1 = (f32[512,2048]{1,0:T(8,128)S(1)}, f32[8,128]{1,0:T(8,128)S(1)}) custom-call(f32[8,128]{1,0:T(8,128)S(1)} %get-tuple-element.52.refs_0_, bf16[512,1024]{1,0:T(8,128)(2,1)S(1)} %get-tuple-element.53.refs_1_, bf16[1024,2048]{1,0:T(8,128)(2,1)S(1)} %get-tuple-element.54.refs_2_, ...), custom_call_target="tpu_custom_call", output_to_operand_aliasing={{0}: (3, {})} | custom-call | flops 2147483648 | tf_op jit(solution)/shard_map/step_3_0/pallas_call | solution.py:305
  53.6 1.2 %collective-permute-start.15 = (bf16[128,1024]{1,0:T(8,128)(2,1)S(1)}, bf16[128,1024]{1,0:T(8,128)(2,1)S(1)}, u32[]{:S(2)}, u32[]{:S(2)}) collective-permute-start(bf16[128,1024]{1,0:T(8,128)(2,1)S(1)} %gate.9.refs_3_), channel_id=1, source_target_pairs={{0,16},{4,12},{8,24},{12,4},{16,0},{20,28},{24,8},{28,20},{1,17},{... | collective-permute-start | bytes 786440 | tf_op jit(solution)/shard_map/ppermute | solution.py:397
  55.7 3.3 %step_4_0.1 = (f32[512,2048]{1,0:T(8,128)S(1)}, bf16[512,1024]{1,0:T(8,128)(2,1)S(1)}, bf16[1024,2048]{1,0:T(8,128)(2,1)S(1)}, f32[8,128]{1,0:T(8,128)S(1)}) custom-call(f32[8,128]{1,0:T(8,128)S(1)} %get-tuple-element.56.refs_0_, bf16[4096,4096]{1,0:T(8,128)(2,1)} %refs_1_.5, s32[16]{0:T(128)S(1)} %copy-done, ...), custom_call_target="tpu_custom_call", output_to_operand_aliasing={{0}: (8, {})} | custom-call | flops 2147483648 | tf_op jit(solution)/shard_map/step_4_0/pallas_call | solution.py:305
  59.0 3.0 %step_5_0.1 = (f32[512,2048]{1,0:T(8,128)S(1)}, f32[8,128]{1,0:T(8,128)S(1)}) custom-call(f32[8,128]{1,0:T(8,128)S(1)} %get-tuple-element.60.refs_0_, bf16[512,1024]{1,0:T(8,128)(2,1)S(1)} %get-tuple-element.61.refs_1_, bf16[1024,2048]{1,0:T(8,128)(2,1)S(1)} %get-tuple-element.62.refs_2_, ...), custom_call_target="tpu_custom_call", output_to_operand_aliasing={{0}: (3, {})} | custom-call | flops 2147483648 | tf_op jit(solution)/shard_map/step_5_0/pallas_call | solution.py:305
  62.8 3.1 %step_6_0.1 = (f32[256,2048]{1,0:T(8,128)S(1)}, bf16[256,2048]{1,0:T(8,128)(2,1)S(1)}, bf16[512,1024]{1,0:T(8,128)(2,1)S(1)}, bf16[1024,2048]{1,0:T(8,128)(2,1)S(1)}, f32[8,128]{1,0:T(8,128)S(1)}) custom-call(f32[8,128]{1,0:T(8,128)S(1)} %get-tuple-element.64.refs_0_, bf16[4096,4096]{1,0:T(8,128)(2,1)} %refs_1_.5, s32[16]{0:T(128)S(1)} %copy-done, ...), custom_call_target="tpu_custom_call" | custom-call | flops 2147483648 | tf_op jit(solution)/shard_map/step_6_0/pallas_call | solution.py:305
  66.0 2.9 %step_7_0.1 = (f32[256,2048]{1,0:T(8,128)S(1)}, bf16[256,2048]{1,0:T(8,128)(2,1)S(1)}, f32[8,128]{1,0:T(8,128)}) custom-call(f32[8,128]{1,0:T(8,128)S(1)} %get-tuple-element.67.refs_0_, bf16[512,1024]{1,0:T(8,128)(2,1)S(1)} %get-tuple-element.68.refs_1_, bf16[1024,2048]{1,0:T(8,128)(2,1)S(1)} %get-tuple-element.69.refs_2_, ...), custom_call_target="tpu_custom_call" | custom-call | flops 2147483648 | tf_op jit(solution)/shard_map/step_7_0/pallas_call | solution.py:305
  70.5 1.2 %collective-permute-done.17.refs_1_ = bf16[256,2048]{1,0:T(8,128)(2,1)S(1)} collective-permute-done((bf16[256,2048]{1,0:T(8,128)(2,1)S(1)}, bf16[256,2048]{1,0:T(8,128)(2,1)S(1)}, u32[]{:S(2)}, u32[]{:S(2)}) %collective-permute-start.17) | collective-permute-done | bytes 1048608 | tf_op jit(solution)/shard_map/ppermute | solution.py:452
  (38 shorter events, 9.4 us)
Async XLA Ops:
  0.0 15.5 %collective-permute-start.3 = (bf16[128,512]{1,0:T(8,128)(2,1)}, bf16[128,512]{1,0:T(8,128)(2,1)S(1)}, u32[]{:S(2)}, u32[]{:S(2)}) collective-permute-start(bf16[128,512]{1,0:T(8,128)(2,1)} %v_hbm.1), channel_id=1, source_target_pairs={{0,16},{8,24},{1,17},{9,25},{2,18},{10,26},{3,19},{11,27},{4,20},{... | collective-permute-start | bytes 393224 | tf_op jit(solution)/shard_map/ppermute | solution.py:408
  4.9 11.3 %collective-permute-start = (bf16[128,512]{1,0:T(8,128)(2,1)}, bf16[128,512]{1,0:T(8,128)(2,1)S(1)}, u32[]{:S(2)}, u32[]{:S(2)}) collective-permute-start(bf16[128,512]{1,0:T(8,128)(2,1)} %k_hbm.1), channel_id=1, source_target_pairs={{0,8},{8,16},{16,24},{1,9},{9,17},{17,25},{2,10},{10,18},{18,26},{... | collective-permute-start | bytes 393224 | tf_op jit(solution)/shard_map/ppermute | solution.py:410
  8.3 7.9 %collective-permute-start.1 = (bf16[128,512]{1,0:T(8,128)(2,1)}, bf16[128,512]{1,0:T(8,128)(2,1)S(1)}, u32[]{:S(2)}, u32[]{:S(2)}) collective-permute-start(bf16[128,512]{1,0:T(8,128)(2,1)} %k_hbm.1), channel_id=1, source_target_pairs={{0,16},{8,24},{1,17},{9,25},{2,18},{10,26},{3,19},{11,27},{4,20},{... | collective-permute-start | bytes 393224 | tf_op jit(solution)/shard_map/ppermute | solution.py:409
  9.6 6.6 %collective-permute-start.2 = (bf16[128,512]{1,0:T(8,128)(2,1)}, bf16[128,512]{1,0:T(8,128)(2,1)S(1)}, u32[]{:S(2)}, u32[]{:S(2)}) collective-permute-start(bf16[128,512]{1,0:T(8,128)(2,1)} %v_hbm.1), channel_id=1, source_target_pairs={{0,8},{16,24},{1,9},{17,25},{2,10},{18,26},{3,11},{19,27},{4,12},{... | collective-permute-start | bytes 393224 | tf_op jit(solution)/shard_map/ppermute | solution.py:411
  15.5 0.7 collective-permute-start.4
  16.9 6.4 %collective-permute-start.5 = (bf16[128,1024]{1,0:T(8,128)(2,1)S(1)}, bf16[128,1024]{1,0:T(8,128)(2,1)S(1)}, u32[]{:S(2)}, u32[]{:S(2)}) collective-permute-start(bf16[128,1024]{1,0:T(8,128)(2,1)S(1)} %attend_0.1.x.after), channel_id=1, source_target_pairs={{0,8},{4,20},{8,0},{12,28},{16,24},{20,4},{24,16},{28,12},{1,9},{5... | collective-permute-start | bytes 786440 | tf_op jit(solution)/shard_map/ppermute | solution.py:394
  20.3 11.4 %collective-permute-start.8 = (bf16[128,1024]{1,0:T(8,128)(2,1)S(1)}, bf16[128,1024]{1,0:T(8,128)(2,1)S(1)}, u32[]{:S(2)}, u32[]{:S(2)}) collective-permute-start(bf16[128,1024]{1,0:T(8,128)(2,1)S(1)} %attend_1.1.x.after), channel_id=1, source_target_pairs={{0,8},{4,20},{8,0},{12,28},{16,24},{20,4},{24,16},{28,12},{1,9},{5... | collective-permute-start | bytes 786440 | tf_op jit(solution)/shard_map/ppermute | solution.py:394
  23.3 14.9 %copy-start = (s32[16]{0:T(128)S(1)}, s32[16]{0:T(128)}, u32[]{:S(2)}) copy-start(s32[16]{0:T(128)} %refs_2_.5) | copy-start | bytes 196
  23.3 13.5 %collective-permute-start.6 = (bf16[128,1024]{1,0:T(8,128)(2,1)S(1)}, bf16[128,1024]{1,0:T(8,128)(2,1)S(1)}, u32[]{:S(2)}, u32[]{:S(2)}) collective-permute-start(bf16[128,1024]{1,0:T(8,128)(2,1)S(1)} %gate.6.refs_1_), channel_id=1, source_target_pairs={{0,16},{4,12},{8,24},{12,4},{16,0},{20,28},{24,8},{28,20},{1,17},{... | collective-permute-start | bytes 786440 | tf_op jit(solution)/shard_map/ppermute | solution.py:397
  28.2 10.0 %collective-permute-start.7 = (bf16[128,1024]{1,0:T(8,128)(2,1)S(1)}, bf16[128,1024]{1,0:T(8,128)(2,1)S(1)}, u32[]{:S(2)}, u32[]{:S(2)}) collective-permute-start(bf16[128,1024]{1,0:T(8,128)(2,1)S(1)} %collective-permute-done.5.after.refs_2_.rest_1_), channel_id=1, source_target_pairs={{0,16},{4,12},{8,24},{12,4},{16,0},{20,28},{24,8},{28,20},{1,17},{... | collective-permute-start | bytes 786440 | tf_op jit(solution)/shard_map/ppermute | solution.py:395
  31.8 14.8 %collective-permute-start.9 = (bf16[128,1024]{1,0:T(8,128)(2,1)S(1)}, bf16[128,1024]{1,0:T(8,128)(2,1)S(1)}, u32[]{:S(2)}, u32[]{:S(2)}) collective-permute-start(bf16[128,1024]{1,0:T(8,128)(2,1)S(1)} %gate.7.refs_3_), channel_id=1, source_target_pairs={{0,16},{4,12},{8,24},{12,4},{16,0},{20,28},{24,8},{28,20},{1,17},{... | collective-permute-start | bytes 786440 | tf_op jit(solution)/shard_map/ppermute | solution.py:397
  34.7 9.7 %collective-permute-start.11 = (bf16[128,1024]{1,0:T(8,128)(2,1)S(1)}, bf16[128,1024]{1,0:T(8,128)(2,1)S(1)}, u32[]{:S(2)}, u32[]{:S(2)}) collective-permute-start(bf16[128,1024]{1,0:T(8,128)(2,1)S(1)} %attend_2.1.x.rest_0_), channel_id=1, source_target_pairs={{0,8},{4,20},{8,0},{12,28},{16,24},{20,4},{24,16},{28,12},{1,9},{5... | collective-permute-start | bytes 786440 | tf_op jit(solution)/shard_map/ppermute | solution.py:394
  36.8 9.8 %collective-permute-start.10 = (bf16[128,1024]{1,0:T(8,128)(2,1)S(1)}, bf16[128,1024]{1,0:T(8,128)(2,1)S(1)}, u32[]{:S(2)}, u32[]{:S(2)}) collective-permute-start(bf16[128,1024]{1,0:T(8,128)(2,1)S(1)} %collective-permute-done.8.after.refs_4_), channel_id=1, source_target_pairs={{0,16},{4,12},{8,24},{12,4},{16,0},{20,28},{24,8},{28,20},{1,17},{... | collective-permute-start | bytes 786440 | tf_op jit(solution)/shard_map/ppermute | solution.py:395
  44.3 9.3 %collective-permute-start.14 = (bf16[128,1024]{1,0:T(8,128)(2,1)S(1)}, bf16[128,1024]{1,0:T(8,128)(2,1)S(1)}, u32[]{:S(2)}, u32[]{:S(2)}) collective-permute-start(bf16[128,1024]{1,0:T(8,128)(2,1)S(1)} %attend_3.1.x), channel_id=1, source_target_pairs={{0,8},{4,20},{8,0},{12,28},{16,24},{20,4},{24,16},{28,12},{1,9},{5... | collective-permute-start | bytes 786440 | tf_op jit(solution)/shard_map/ppermute | solution.py:394
  44.4 11.2 %collective-permute-start.12 = (bf16[128,1024]{1,0:T(8,128)(2,1)S(1)}, bf16[128,1024]{1,0:T(8,128)(2,1)S(1)}, u32[]{:S(2)}, u32[]{:S(2)}) collective-permute-start(bf16[128,1024]{1,0:T(8,128)(2,1)S(1)} %gate.8.refs_3_), channel_id=1, source_target_pairs={{0,16},{4,12},{8,24},{12,4},{16,0},{20,28},{24,8},{28,20},{1,17},{... | collective-permute-start | bytes 786440 | tf_op jit(solution)/shard_map/ppermute | solution.py:397
  46.5 9.2 %collective-permute-start.13 = (bf16[128,1024]{1,0:T(8,128)(2,1)S(1)}, bf16[128,1024]{1,0:T(8,128)(2,1)S(1)}, u32[]{:S(2)}, u32[]{:S(2)}) collective-permute-start(bf16[128,1024]{1,0:T(8,128)(2,1)S(1)} %collective-permute-done.11.after.refs_4_), channel_id=1, source_target_pairs={{0,16},{4,12},{8,24},{12,4},{16,0},{20,28},{24,8},{28,20},{1,17},{... | collective-permute-start | bytes 786440 | tf_op jit(solution)/shard_map/ppermute | solution.py:395
  53.6 8.4 %collective-permute-start.15 = (bf16[128,1024]{1,0:T(8,128)(2,1)S(1)}, bf16[128,1024]{1,0:T(8,128)(2,1)S(1)}, u32[]{:S(2)}, u32[]{:S(2)}) collective-permute-start(bf16[128,1024]{1,0:T(8,128)(2,1)S(1)} %gate.9.refs_3_), channel_id=1, source_target_pairs={{0,16},{4,12},{8,24},{12,4},{16,0},{20,28},{24,8},{28,20},{1,17},{... | collective-permute-start | bytes 786440 | tf_op jit(solution)/shard_map/ppermute | solution.py:397
  54.8 8.0 %collective-permute-start.16 = (bf16[128,1024]{1,0:T(8,128)(2,1)S(1)}, bf16[128,1024]{1,0:T(8,128)(2,1)S(1)}, u32[]{:S(2)}, u32[]{:S(2)}) collective-permute-start(bf16[128,1024]{1,0:T(8,128)(2,1)S(1)} %collective-permute-done.14.after.refs_4_), channel_id=1, source_target_pairs={{0,16},{4,12},{8,24},{12,4},{16,0},{20,28},{24,8},{28,20},{1,17},{... | collective-permute-start | bytes 786440 | tf_op jit(solution)/shard_map/ppermute | solution.py:395
  65.9 3.5 %collective-permute-start.18 = (bf16[256,2048]{1,0:T(8,128)(2,1)S(1)}, bf16[256,2048]{1,0:T(8,128)(2,1)S(1)}, u32[]{:S(2)}, u32[]{:S(2)}) collective-permute-start(bf16[256,2048]{1,0:T(8,128)(2,1)S(1)} %get-tuple-element.74), channel_id=1, source_target_pairs={{0,4},{4,0},{1,5},{5,1},{2,6},{6,2},{3,7},{7,3},{8,12},{12,8},{9,1... | collective-permute-start | bytes 3145736 | tf_op jit(solution)/shard_map/ppermute | solution.py:452
  68.9 2.8 %collective-permute-start.17 = (bf16[256,2048]{1,0:T(8,128)(2,1)S(1)}, bf16[256,2048]{1,0:T(8,128)(2,1)S(1)}, u32[]{:S(2)}, u32[]{:S(2)}) collective-permute-start(bf16[256,2048]{1,0:T(8,128)(2,1)S(1)} %get-tuple-element.72), channel_id=1, source_target_pairs={{0,4},{4,0},{1,5},{5,1},{2,6},{6,2},{3,7},{7,3},{8,12},{12,8},{9,1... | collective-permute-start | bytes 3145736 | tf_op jit(solution)/shard_map/ppermute | solution.py:452

commit v6 on v4

--- a/solution.py
+++ b/solution.py
@@ -92,14 +92,13 @@
     )
 
 
-def prepare_kernel(docs_hbm, k_hbm, v_hbm, q_hbm, w_hbm, after, k_ref, v_ref, q_ref, mask_ref, left_ref, right_ref, docs, sems):
+def prepare_kernel(docs_hbm, k_hbm, v_hbm, q_hbm, w_hbm, after, k_ref, v_ref, q_ref, mask_ref, w_ref, docs, sems):
     lengths = pltpu.make_async_copy(docs_hbm, docs, sems.at[0])
     loads = [
         pltpu.make_async_copy(k_hbm, k_ref, sems.at[1]),
         pltpu.make_async_copy(v_hbm, v_ref, sems.at[2]),
         pltpu.make_async_copy(q_hbm, q_ref, sems.at[3]),
-        block_copy(w_hbm, 0, left_ref, sems.at[4]),
-        block_copy(w_hbm, 1, right_ref, sems.at[5]),
+        block_copy(w_hbm, 0, w_ref, sems.at[4]),
     ]
     lengths.start()
     for load in loads:
@@ -129,17 +128,16 @@
             jax.ShapeDtypeStruct(queries.shape, jnp.bfloat16),
             jax.ShapeDtypeStruct((rows, 3 * rows), jnp.float32),
             jax.ShapeDtypeStruct(block_shape(w_out, chunks), jnp.bfloat16),
-            jax.ShapeDtypeStruct(block_shape(w_out, chunks), jnp.bfloat16),
         ],
         in_specs=[HBM] * 6,
-        out_specs=[VMEM] * 6,
+        out_specs=[VMEM] * 5,
         scratch_shapes=[
             pltpu.SMEM(doc_lengths.shape, jnp.int32),
-            pltpu.SemaphoreType.DMA((6,)),
+            pltpu.SemaphoreType.DMA((5,)),
         ],
         compiler_params=pltpu.CompilerParams(vmem_limit_bytes=4 * MIB),
         cost_estimate=pl.CostEstimate(
-            flops=0, bytes_accessed=2 * w_out.size // chunks, transcendentals=0
+            flops=0, bytes_accessed=w_out.size // chunks, transcendentals=0
         ),
         name="prepare",
     )(
@@ -177,7 +175,7 @@
     return blocks, token
 
 
-def attend_kernel(groups, q_ref, mask_ref, k0, k_near, k_far, k2, v0, v_near, v_far, v2, *rest):
+def attend_kernel(groups, q_ref, mask_ref, k0, k2, k_near, k_far, v0, v_near, v_far, v2, *rest):
     out_ref = rest[-1]
     rows = out_ref.shape[0]
     width = out_ref.shape[1] // len(groups)
@@ -413,13 +411,13 @@
     key_near = lax.ppermute(key_rows, "ctx", [(0, 1), (1, 2), (2, 3)])
     value_near = lax.ppermute(value_rows, "ctx", [(0, 1), (2, 3)])
     value_far = lax.ppermute(value_two, "ctx", [(3, 2)])
-    own_keys, own_values, held, mask, left, right = prepare(
+    own_keys, own_values, held, mask, block = prepare(
         doc_lengths, key_rows, value_rows, queries, w_out, kv_heads, value_two
     )
-    keys = (own_keys, key_near, key_near, key_two)
+    keys = (own_keys, key_two, key_near, key_near)
     values = (own_values, value_near, value_far, value_two)
     half_columns = w_out.shape[1] // HALVES
-    state = {"left": {0: left}, "right": {0: right}, "totals": [None] * HALVES, "before": None}
+    state = {"blocks": {0: block}, "totals": [None] * HALVES, "before": None}
     rows, mine, got = {}, [], []
 
     def rows_of(groups, after):
@@ -435,45 +433,41 @@
         return own, arrive
 
     def load(wanted, after):
-        loaded, token = load_blocks([g * HALVES for g in wanted], w_out, kv_heads, after)
-        state["left"].update(zip(wanted, loaded))
+        loaded, token = load_blocks(wanted, w_out, kv_heads, after)
+        state["blocks"].update(zip(wanted, loaded))
         return token
 
     def steps(g):
         last = g == kv_heads - 1
         pieces, column = rows[g]
-        loads = g not in state["right"]
+        loads = g * HALVES + 1 not in state["blocks"]
         first, lhs, following, state["before"] = step(
-            g * HALVES, last, (unit_source, pieces), column, state["left"][g], 0, half_columns,
+            g * HALVES, last, (unit_source, pieces), column, state["blocks"][g * HALVES], 0,
+            half_columns,
             w_out if loads else None, state["totals"][0], state["before"],
         )
         if loads:
-            state["right"][g] = following
-        parts = 1
-        seconds = []
-        for i in range(parts):
-            second, lhs, _, state["before"] = step(
-                g * HALVES + 1, last, lhs, column, state["right"][g],
-                i * half_columns // parts, half_columns // parts, None,
-                state["totals"][1], state["before"],
-            )
-            seconds.append(second)
+            state["blocks"][g * HALVES + 1] = following
+        second, _, _, state["before"] = step(
+            g * HALVES + 1, last, lhs, column, state["blocks"][g * HALVES + 1], 0,
+            half_columns, None,
+            state["totals"][1], state["before"],
+        )
         if last:
-            for kept, sent in [first, *seconds]:
+            for kept, sent in (first, second):
                 mine.append(kept)
                 got.append(lax.ppermute(sent, "tp", [(0, 1), (1, 0)]))
         else:
-            state["totals"] = [first[0], seconds[0][0]]
+            state["totals"] = [first[0], second[0]]
         return state["before"]
 
     own, arrive = rows_of((0,), [])
-    near = arrive(load((1, 2), own))
-    own, arrive = rows_of((1, 2), [near])
-    done = steps(0)
-    near = arrive(done)
-    _, arrive = rows_of((3,), [load((3,), near), done])
-    arrive(steps(1))
-    for g in range(2, kv_heads):
+    near = arrive(None)
+    own, arrive = rows_of((1,), [load((1, 2), own)])
+    arrive(None)
+    own, arrive = rows_of((2, 3), [load((4, 6), own), near])
+    arrive(steps(0))
+    for g in range(1, kv_heads):
         steps(g)
     out = total(0, w_out.shape[1], mine[:1], got[:1], None)
     return total(half_columns, w_out.shape[1], mine[1:], got[1:], out)

time: 74.9 us -> 70.9 us (0.947)
  waiting for transfers between devices: 10.9 us -> 8.71 us
  starting transfers between devices: 24.9 us -> 23.2 us
    ppermute x3, waiting for transfers between devices: 8.7 us -> 1.44 us  [forward(): return (own, first, side, lax.ppermute(first, ('ctx', 'tp'), route(False)))]
    ppermute x3, waiting for transfers between devices: 1.01 us -> 6.05 us  [gather_rows(): near = lax.ppermute(own, ('ctx', 'tp'), route(True))]
    ppermute x3, starting transfers between devices: 5.12 us -> 3.23 us  [forward(): return (own, first, side, lax.ppermute(first, ('ctx', 'tp'), route(False)))]
    pallas_call x2, Pallas kernels: 5.68 us -> 6.97 us  [load_blocks(): pl.pallas_call(functools.partial(load_kernel, indexes), out_shape=[jax.Sh...]
    pallas_call x1, Pallas kernels: 3.95 us -> 2.7 us  [prepare(): pl.pallas_call(prepare_kernel, out_shape=[jax.ShapeDtypeStruct(key_rows.s...]
  transfers between devices with their start and end apart: 16 -> 16, of which waited for: 4 -> 4; matrix products, arithmetic and copies ran while one was open for 0% -> 0% of each run, Pallas kernels for 45% -> 38%
where the time goes in v6:
time: 70.9 us; the launch traced here: 70.7 us
  Pallas kernels  38.4 us (54%)
  starting transfers between devices  23.2 us (33%)
  waiting for transfers between devices  8.71 us (12%)
    pallas_call x8, Pallas kernels, step(): pl.pallas_call(functools.partial(step_kernel, index, last, column, first,...  23.8 us
    pallas_call x2, Pallas kernels, load_blocks(): pl.pallas_call(functools.partial(load_kernel, indexes), out_shape=[jax.Sh...  6.97 us
    ppermute x3, waiting for transfers between devices, gather_rows(): near = lax.ppermute(own, ('ctx', 'tp'), route(True))  6.05 us
    ppermute x1, starting transfers between devices, local(): value_two = lax.ppermute(value_rows, 'ctx', two)  4.87 us
    ppermute x3, starting transfers between devices, gather_rows(): near = lax.ppermute(own, ('ctx', 'tp'), route(True))  4.71 us
    ppermute x1, starting transfers between devices, local(): key_near = lax.ppermute(key_rows, 'ctx', [(0, 1), (1, 2), (2, 3)])  3.4 us
    ppermute x3, starting transfers between devices, forward(): return (own, first, side, lax.ppermute(first, ('ctx', 'tp'), route(False)))  3.23 us
    pallas_call x3, Pallas kernels, attend(): pl.pallas_call(functools.partial(attend_kernel, groups), out_shape=jax.Sh...  2.72 us
  transfers between devices with their start and end apart: 16, of which 4 were waited for; matrix products, arithmetic and copies ran while one was open for 0% of the time, Pallas kernels for 38%

profile of v6, /device:TPU:0, one launch (start us, length us, event | category | flops | bytes accessed | tf_op | source)
XLA Modules:
  0.0 70.7 jit_solution(8353468629319613623)
XLA Ops:
  0.0 4.9 %collective-permute-start = (bf16[128,512]{1,0:T(8,128)(2,1)}, bf16[128,512]{1,0:T(8,128)(2,1)S(1)}, u32[]{:S(2)}, u32[]{:S(2)}) collective-permute-start(bf16[128,512]{1,0:T(8,128)(2,1)} %v_hbm.1), channel_id=1, source_target_pairs={{0,16},{8,24},{1,17},{9,25},{2,18},{10,26},{3,19},{11,27},{4,20},{... | collective-permute-start | bytes 393224 | tf_op jit(solution)/shard_map/ppermute | solution.py:409
  4.9 3.4 %collective-permute-start.2 = (bf16[128,512]{1,0:T(8,128)(2,1)}, bf16[128,512]{1,0:T(8,128)(2,1)S(1)}, u32[]{:S(2)}, u32[]{:S(2)}) collective-permute-start(bf16[128,512]{1,0:T(8,128)(2,1)} %k_hbm.1), channel_id=1, source_target_pairs={{0,8},{8,16},{16,24},{1,9},{9,17},{17,25},{2,10},{10,18},{18,26},{... | collective-permute-start | bytes 393224 | tf_op jit(solution)/shard_map/ppermute | solution.py:411
  8.3 1.3 %collective-permute-start.1 = (bf16[128,512]{1,0:T(8,128)(2,1)}, bf16[128,512]{1,0:T(8,128)(2,1)S(1)}, u32[]{:S(2)}, u32[]{:S(2)}) collective-permute-start(bf16[128,512]{1,0:T(8,128)(2,1)} %k_hbm.1), channel_id=1, source_target_pairs={{0,16},{8,24},{1,17},{9,25},{2,18},{10,26},{3,19},{11,27},{4,20},{... | collective-permute-start | bytes 393224 | tf_op jit(solution)/shard_map/ppermute | solution.py:410
  9.6 1.9 %collective-permute-start.3 = (bf16[128,512]{1,0:T(8,128)(2,1)}, bf16[128,512]{1,0:T(8,128)(2,1)S(1)}, u32[]{:S(2)}, u32[]{:S(2)}) collective-permute-start(bf16[128,512]{1,0:T(8,128)(2,1)} %v_hbm.1), channel_id=1, source_target_pairs={{0,8},{16,24},{1,9},{17,25},{2,10},{18,26},{3,11},{19,27},{4,12},{... | collective-permute-start | bytes 393224 | tf_op jit(solution)/shard_map/ppermute | solution.py:412
  12.2 2.7 %prepare.1 = (bf16[128,512]{1,0:T(8,128)(2,1)S(1)}, bf16[128,512]{1,0:T(8,128)(2,1)S(1)}, bf16[128,4096]{1,0:T(8,128)(2,1)S(1)}, f32[128,384]{1,0:T(8,128)S(1)}, bf16[1024,2048]{1,0:T(8,128)(2,1)S(1)}) custom-call(s32[8]{0:T(128)} %docs_hbm.1, bf16[128,512]{1,0:T(8,128)(2,1)} %k_hbm.1, bf16[128,512]{1,0:T(8,128)(2,1)} %v_hbm.1, bf16[128,4096]{1,0:T(8,128)(2,1)} %q_hbm.1, ...), custom_call_target="tpu_custom_call" | custom-call | bytes 4194304 | tf_op jit(solution)/shard_map/prepare/pallas_call | solution.py:123
  15.7 1.8 %collective-permute-start.5 = (bf16[128,1024]{1,0:T(8,128)(2,1)S(1)}, bf16[128,1024]{1,0:T(8,128)(2,1)S(1)}, u32[]{:S(2)}, u32[]{:S(2)}) collective-permute-start(bf16[128,1024]{1,0:T(8,128)(2,1)S(1)} %attend_0.1.refs_1_.after), channel_id=1, source_target_pairs={{0,8},{4,20},{8,0},{12,28},{16,24},{20,4},{24,16},{28,12},{1,9},{5... | collective-permute-start | bytes 786440 | tf_op jit(solution)/shard_map/ppermute | solution.py:392
  18.0 3.5 %load_1.1 = (bf16[1024,2048]{1,0:T(8,128)(2,1)S(1)}, bf16[1024,2048]{1,0:T(8,128)(2,1)S(1)}, f32[8,128]{1,0:T(8,128)S(1)}) custom-call(bf16[128,1024]{1,0:T(8,128)(2,1)S(1)} %attend_0.1.refs_1_.after, bf16[4096,4096]{1,0:T(8,128)(2,1)} %refs_1_.5), custom_call_target="tpu_custom_call" | custom-call | bytes 16777216 | tf_op jit(solution)/shard_map/load_1/pallas_call | solution.py:163
  22.2 2.0 %collective-permute-start.8 = (bf16[128,1024]{1,0:T(8,128)(2,1)S(1)}, bf16[128,1024]{1,0:T(8,128)(2,1)S(1)}, u32[]{:S(2)}, u32[]{:S(2)}) collective-permute-start(bf16[128,1024]{1,0:T(8,128)(2,1)S(1)} %attend_1.1.refs_3_.after), channel_id=1, source_target_pairs={{0,8},{4,20},{8,0},{12,28},{16,24},{20,4},{24,16},{28,12},{1,9},{5... | collective-permute-start | bytes 786440 | tf_op jit(solution)/shard_map/ppermute | solution.py:392
  25.0 3.5 %load_4.1 = (bf16[1024,2048]{1,0:T(8,128)(2,1)S(1)}, bf16[1024,2048]{1,0:T(8,128)(2,1)S(1)}, f32[8,128]{1,0:T(8,128)S(1)}) custom-call(bf16[128,1024]{1,0:T(8,128)(2,1)S(1)} %attend_1.1.refs_3_.after, bf16[4096,4096]{1,0:T(8,128)(2,1)} %refs_1_.5), custom_call_target="tpu_custom_call" | custom-call | bytes 16777216 | tf_op jit(solution)/shard_map/load_4/pallas_call | solution.py:163
  28.4 1.3 %attend_2.1.refs_3_ = bf16[128,2048]{1,0:T(8,128)(2,1)S(1)} custom-call(bf16[128,4096]{1,0:T(8,128)(2,1)S(1)} %get-tuple-element.40.q_ref, f32[128,384]{1,0:T(8,128)S(1)} %get-tuple-element.41.mask_ref, bf16[128,512]{1,0:T(8,128)(2,1)S(1)} %get-tuple-element.42.k0, bf16[128,512]{1,0:T(8,128)(2,1)S(1)} %collective-permute-done.1.k2, ...), custom_call_target="tpu_custom_call" | custom-call | tf_op jit(solution)/shard_map/attend_2/pallas_call | solution.py:214
  30.7 1.2 %collective-permute-start.9 = (bf16[128,1024]{1,0:T(8,128)(2,1)S(1)}, bf16[128,1024]{1,0:T(8,128)(2,1)S(1)}, u32[]{:S(2)}, u32[]{:S(2)}) collective-permute-start(bf16[128,1024]{1,0:T(8,128)(2,1)S(1)} %attend_1.1.refs_3_.after), channel_id=1, source_target_pairs={{0,16},{4,12},{8,24},{12,4},{16,0},{20,28},{24,8},{28,20},{1,17},{... | collective-permute-start | bytes 786440 | tf_op jit(solution)/shard_map/ppermute | solution.py:393
  32.7 1.2 %collective-permute-start.10 = (bf16[128,1024]{1,0:T(8,128)(2,1)S(1)}, bf16[128,1024]{1,0:T(8,128)(2,1)S(1)}, u32[]{:S(2)}, u32[]{:S(2)}) collective-permute-start(bf16[128,1024]{1,0:T(8,128)(2,1)S(1)} %collective-permute-done.8.refs_4_), channel_id=1, source_target_pairs={{0,16},{4,12},{8,24},{12,4},{16,0},{20,28},{24,8},{28,20},{1,17},{... | collective-permute-start | bytes 786440 | tf_op jit(solution)/shard_map/ppermute | solution.py:397
  34.0 3.1 %step_0_0.1 = (f32[512,2048]{1,0:T(8,128)S(1)}, bf16[512,1024]{1,0:T(8,128)(2,1)S(1)}, f32[8,128]{1,0:T(8,128)S(1)}) custom-call(s32[16]{0:T(128)S(1)} %copy-done, bf16[128,1024]{1,0:T(8,128)(2,1)S(1)} %attend_0.1.refs_1_.after, bf16[128,1024]{1,0:T(8,128)(2,1)S(1)} %collective-permute-done.5.refs_2_.rest_1_, ...), custom_call_target="tpu_custom_call" | custom-call | flops 2147483648 | tf_op jit(solution)/shard_map/step_0_0/pallas_call | solution.py:303
  37.0 2.4 %step_1_0.1 = (f32[512,2048]{1,0:T(8,128)S(1)}, f32[8,128]{1,0:T(8,128)S(1)}) custom-call(f32[8,128]{1,0:T(8,128)S(1)} %get-tuple-element.45.refs_0_, bf16[512,1024]{1,0:T(8,128)(2,1)S(1)} %get-tuple-element.46.refs_1_, bf16[1024,2048]{1,0:T(8,128)(2,1)S(1)} %get-tuple-element.47.refs_2_), custom_call_target="tpu_custom_call" | custom-call | flops 2147483648 | tf_op jit(solution)/shard_map/step_1_0/pallas_call | solution.py:303
  39.4 5.3 %collective-permute-done.11.x = bf16[128,2048]{1,0:T(8,128)(2,1)S(1)} collective-permute-done((bf16[128,2048]{1,0:T(8,128)(2,1)S(1)}, bf16[128,2048]{1,0:T(8,128)(2,1)S(1)}, u32[]{:S(2)}, u32[]{:S(2)}) %collective-permute-start.11) | collective-permute-done | bytes 524320 | tf_op jit(solution)/shard_map/ppermute | solution.py:392
  44.7 2.0 %collective-permute-start.13 = (bf16[128,2048]{1,0:T(8,128)(2,1)S(1)}, bf16[128,2048]{1,0:T(8,128)(2,1)S(1)}, u32[]{:S(2)}, u32[]{:S(2)}) collective-permute-start(bf16[128,2048]{1,0:T(8,128)(2,1)S(1)} %gate.1.refs_4_), channel_id=1, source_target_pairs={{0,16},{4,12},{8,24},{12,4},{16,0},{20,28},{24,8},{28,20},{1,17},{... | collective-permute-start | bytes 1572872 | tf_op jit(solution)/shard_map/ppermute | solution.py:397
  46.7 1.4 %collective-permute-done.10.refs_6_ = bf16[128,1024]{1,0:T(8,128)(2,1)S(1)} collective-permute-done((bf16[128,1024]{1,0:T(8,128)(2,1)S(1)}, bf16[128,1024]{1,0:T(8,128)(2,1)S(1)}, u32[]{:S(2)}, u32[]{:S(2)}) %collective-permute-start.10) | collective-permute-done | bytes 262176 | tf_op jit(solution)/shard_map/ppermute | solution.py:397
  48.1 3.4 %step_2_0.1 = (f32[512,2048]{1,0:T(8,128)S(1)}, bf16[512,1024]{1,0:T(8,128)(2,1)S(1)}, bf16[1024,2048]{1,0:T(8,128)(2,1)S(1)}, f32[8,128]{1,0:T(8,128)S(1)}) custom-call(f32[8,128]{1,0:T(8,128)S(1)} %get-tuple-element.48.refs_0_.after, bf16[4096,4096]{1,0:T(8,128)(2,1)} %refs_1_.5, s32[16]{0:T(128)S(1)} %copy-done, ...), custom_call_target="tpu_custom_call", output_to_operand_aliasing={{0}: (8, {})} | custom-call | flops 2147483648 | tf_op jit(solution)/shard_map/step_2_0/pallas_call | solution.py:303
  51.5 2.7 %step_3_0.1 = (f32[512,2048]{1,0:T(8,128)S(1)}, f32[8,128]{1,0:T(8,128)S(1)}) custom-call(f32[8,128]{1,0:T(8,128)S(1)} %get-tuple-element.52.refs_0_, bf16[512,1024]{1,0:T(8,128)(2,1)S(1)} %get-tuple-element.53.refs_1_, bf16[1024,2048]{1,0:T(8,128)(2,1)S(1)} %get-tuple-element.54.refs_2_, ...), custom_call_target="tpu_custom_call", output_to_operand_aliasing={{0}: (3, {})} | custom-call | flops 2147483648 | tf_op jit(solution)/shard_map/step_3_0/pallas_call | solution.py:303
  54.3 3.3 %step_4_0.1 = (f32[512,2048]{1,0:T(8,128)S(1)}, bf16[512,1024]{1,0:T(8,128)(2,1)S(1)}, bf16[1024,2048]{1,0:T(8,128)(2,1)S(1)}, f32[8,128]{1,0:T(8,128)S(1)}) custom-call(f32[8,128]{1,0:T(8,128)S(1)} %get-tuple-element.56.refs_0_, bf16[4096,4096]{1,0:T(8,128)(2,1)} %refs_1_.5, s32[16]{0:T(128)S(1)} %copy-done, ...), custom_call_target="tpu_custom_call", output_to_operand_aliasing={{0}: (8, {})} | custom-call | flops 2147483648 | tf_op jit(solution)/shard_map/step_4_0/pallas_call | solution.py:303
  57.6 3.0 %step_5_0.1 = (f32[512,2048]{1,0:T(8,128)S(1)}, f32[8,128]{1,0:T(8,128)S(1)}) custom-call(f32[8,128]{1,0:T(8,128)S(1)} %get-tuple-element.60.refs_0_, bf16[512,1024]{1,0:T(8,128)(2,1)S(1)} %get-tuple-element.61.refs_1_, bf16[1024,2048]{1,0:T(8,128)(2,1)S(1)} %get-tuple-element.62.refs_2_, ...), custom_call_target="tpu_custom_call", output_to_operand_aliasing={{0}: (3, {})} | custom-call | flops 2147483648 | tf_op jit(solution)/shard_map/step_5_0/pallas_call | solution.py:303
  60.6 3.1 %step_6_0.1 = (f32[256,2048]{1,0:T(8,128)S(1)}, bf16[256,2048]{1,0:T(8,128)(2,1)S(1)}, bf16[512,1024]{1,0:T(8,128)(2,1)S(1)}, bf16[1024,2048]{1,0:T(8,128)(2,1)S(1)}, f32[8,128]{1,0:T(8,128)S(1)}) custom-call(f32[8,128]{1,0:T(8,128)S(1)} %get-tuple-element.64.refs_0_, bf16[4096,4096]{1,0:T(8,128)(2,1)} %refs_1_.5, s32[16]{0:T(128)S(1)} %copy-done, ...), custom_call_target="tpu_custom_call" | custom-call | flops 2147483648 | tf_op jit(solution)/shard_map/step_6_0/pallas_call | solution.py:303
  63.8 2.9 %step_7_0.1 = (f32[256,2048]{1,0:T(8,128)S(1)}, bf16[256,2048]{1,0:T(8,128)(2,1)S(1)}, f32[8,128]{1,0:T(8,128)}) custom-call(f32[8,128]{1,0:T(8,128)S(1)} %get-tuple-element.67.refs_0_, bf16[512,1024]{1,0:T(8,128)(2,1)S(1)} %get-tuple-element.68.refs_1_, bf16[1024,2048]{1,0:T(8,128)(2,1)S(1)} %get-tuple-element.69.refs_2_, ...), custom_call_target="tpu_custom_call" | custom-call | flops 2147483648 | tf_op jit(solution)/shard_map/step_7_0/pallas_call | solution.py:303
  68.3 1.2 %collective-permute-done.14.refs_1_ = bf16[256,2048]{1,0:T(8,128)(2,1)S(1)} collective-permute-done((bf16[256,2048]{1,0:T(8,128)(2,1)S(1)}, bf16[256,2048]{1,0:T(8,128)(2,1)S(1)}, u32[]{:S(2)}, u32[]{:S(2)}) %collective-permute-start.14) | collective-permute-done | bytes 1048608 | tf_op jit(solution)/shard_map/ppermute | solution.py:459
  (27 shorter events, 7.8 us)
Async XLA Ops:
  0.0 11.5 %collective-permute-start = (bf16[128,512]{1,0:T(8,128)(2,1)}, bf16[128,512]{1,0:T(8,128)(2,1)S(1)}, u32[]{:S(2)}, u32[]{:S(2)}) collective-permute-start(bf16[128,512]{1,0:T(8,128)(2,1)} %v_hbm.1), channel_id=1, source_target_pairs={{0,16},{8,24},{1,17},{9,25},{2,18},{10,26},{3,19},{11,27},{4,20},{... | collective-permute-start | bytes 393224 | tf_op jit(solution)/shard_map/ppermute | solution.py:409
  4.9 10.0 %collective-permute-start.2 = (bf16[128,512]{1,0:T(8,128)(2,1)}, bf16[128,512]{1,0:T(8,128)(2,1)S(1)}, u32[]{:S(2)}, u32[]{:S(2)}) collective-permute-start(bf16[128,512]{1,0:T(8,128)(2,1)} %k_hbm.1), channel_id=1, source_target_pairs={{0,8},{8,16},{16,24},{1,9},{9,17},{17,25},{2,10},{10,18},{18,26},{... | collective-permute-start | bytes 393224 | tf_op jit(solution)/shard_map/ppermute | solution.py:411
  8.3 6.6 %collective-permute-start.1 = (bf16[128,512]{1,0:T(8,128)(2,1)}, bf16[128,512]{1,0:T(8,128)(2,1)S(1)}, u32[]{:S(2)}, u32[]{:S(2)}) collective-permute-start(bf16[128,512]{1,0:T(8,128)(2,1)} %k_hbm.1), channel_id=1, source_target_pairs={{0,16},{8,24},{1,17},{9,25},{2,18},{10,26},{3,19},{11,27},{4,20},{... | collective-permute-start | bytes 393224 | tf_op jit(solution)/shard_map/ppermute | solution.py:410
  9.6 5.4 %collective-permute-start.3 = (bf16[128,512]{1,0:T(8,128)(2,1)}, bf16[128,512]{1,0:T(8,128)(2,1)S(1)}, u32[]{:S(2)}, u32[]{:S(2)}) collective-permute-start(bf16[128,512]{1,0:T(8,128)(2,1)} %v_hbm.1), channel_id=1, source_target_pairs={{0,8},{16,24},{1,9},{17,25},{2,10},{18,26},{3,11},{19,27},{4,12},{... | collective-permute-start | bytes 393224 | tf_op jit(solution)/shard_map/ppermute | solution.py:412
  11.5 3.4 %collective-permute-start.4 = (bf16[128,512]{1,0:T(8,128)(2,1)S(1)}, bf16[128,512]{1,0:T(8,128)(2,1)S(1)}, u32[]{:S(2)}, u32[]{:S(2)}) collective-permute-start(bf16[128,512]{1,0:T(8,128)(2,1)S(1)} %collective-permute-done.after.v2), channel_id=1, source_target_pairs={{24,16},{25,17},{26,18},{27,19},{28,20},{29,21},{30,22},{31,23}} | collective-permute-start | bytes 393224 | tf_op jit(solution)/shard_map/ppermute | solution.py:413
  15.7 9.2 %collective-permute-start.5 = (bf16[128,1024]{1,0:T(8,128)(2,1)S(1)}, bf16[128,1024]{1,0:T(8,128)(2,1)S(1)}, u32[]{:S(2)}, u32[]{:S(2)}) collective-permute-start(bf16[128,1024]{1,0:T(8,128)(2,1)S(1)} %attend_0.1.refs_1_.after), channel_id=1, source_target_pairs={{0,8},{4,20},{8,0},{12,28},{16,24},{20,4},{24,16},{28,12},{1,9},{5... | collective-permute-start | bytes 786440 | tf_op jit(solution)/shard_map/ppermute | solution.py:392
  17.4 14.5 %collective-permute-start.6 = (bf16[128,1024]{1,0:T(8,128)(2,1)S(1)}, bf16[128,1024]{1,0:T(8,128)(2,1)S(1)}, u32[]{:S(2)}, u32[]{:S(2)}) collective-permute-start(bf16[128,1024]{1,0:T(8,128)(2,1)S(1)} %attend_0.1.refs_1_.after), channel_id=1, source_target_pairs={{0,16},{4,12},{8,24},{12,4},{16,0},{20,28},{24,8},{28,20},{1,17},{... | collective-permute-start | bytes 786440 | tf_op jit(solution)/shard_map/ppermute | solution.py:393
  22.2 11.8 %copy-start = (s32[16]{0:T(128)S(1)}, s32[16]{0:T(128)}, u32[]{:S(2)}) copy-start(s32[16]{0:T(128)} %refs_2_.5) | copy-start | bytes 196
  22.2 10.6 %collective-permute-start.8 = (bf16[128,1024]{1,0:T(8,128)(2,1)S(1)}, bf16[128,1024]{1,0:T(8,128)(2,1)S(1)}, u32[]{:S(2)}, u32[]{:S(2)}) collective-permute-start(bf16[128,1024]{1,0:T(8,128)(2,1)S(1)} %attend_1.1.refs_3_.after), channel_id=1, source_target_pairs={{0,8},{4,20},{8,0},{12,28},{16,24},{20,4},{24,16},{28,12},{1,9},{5... | collective-permute-start | bytes 786440 | tf_op jit(solution)/shard_map/ppermute | solution.py:392
  24.9 9.0 %collective-permute-start.7 = (bf16[128,1024]{1,0:T(8,128)(2,1)S(1)}, bf16[128,1024]{1,0:T(8,128)(2,1)S(1)}, u32[]{:S(2)}, u32[]{:S(2)}) collective-permute-start(bf16[128,1024]{1,0:T(8,128)(2,1)S(1)} %collective-permute-done.5.refs_2_.rest_1_), channel_id=1, source_target_pairs={{0,16},{4,12},{8,24},{12,4},{16,0},{20,28},{24,8},{28,20},{1,17},{... | collective-permute-start | bytes 786440 | tf_op jit(solution)/shard_map/ppermute | solution.py:397
  29.8 14.9 %collective-permute-start.11 = (bf16[128,2048]{1,0:T(8,128)(2,1)S(1)}, bf16[128,2048]{1,0:T(8,128)(2,1)S(1)}, u32[]{:S(2)}, u32[]{:S(2)}) collective-permute-start(bf16[128,2048]{1,0:T(8,128)(2,1)S(1)} %attend_2.1.refs_3_), channel_id=1, source_target_pairs={{0,8},{4,20},{8,0},{12,28},{16,24},{20,4},{24,16},{28,12},{1,9},{5... | collective-permute-start | bytes 1572872 | tf_op jit(solution)/shard_map/ppermute | solution.py:392
  30.7 16.0 %collective-permute-start.9 = (bf16[128,1024]{1,0:T(8,128)(2,1)S(1)}, bf16[128,1024]{1,0:T(8,128)(2,1)S(1)}, u32[]{:S(2)}, u32[]{:S(2)}) collective-permute-start(bf16[128,1024]{1,0:T(8,128)(2,1)S(1)} %attend_1.1.refs_3_.after), channel_id=1, source_target_pairs={{0,16},{4,12},{8,24},{12,4},{16,0},{20,28},{24,8},{28,20},{1,17},{... | collective-permute-start | bytes 786440 | tf_op jit(solution)/shard_map/ppermute | solution.py:393
  31.9 22.4 %collective-permute-start.12 = (bf16[128,2048]{1,0:T(8,128)(2,1)S(1)}, bf16[128,2048]{1,0:T(8,128)(2,1)S(1)}, u32[]{:S(2)}, u32[]{:S(2)}) collective-permute-start(bf16[128,2048]{1,0:T(8,128)(2,1)S(1)} %attend_2.1.refs_3_), channel_id=1, source_target_pairs={{0,16},{4,12},{8,24},{12,4},{16,0},{20,28},{24,8},{28,20},{1,17},{... | collective-permute-start | bytes 1572872 | tf_op jit(solution)/shard_map/ppermute | solution.py:393
  32.7 15.4 %collective-permute-start.10 = (bf16[128,1024]{1,0:T(8,128)(2,1)S(1)}, bf16[128,1024]{1,0:T(8,128)(2,1)S(1)}, u32[]{:S(2)}, u32[]{:S(2)}) collective-permute-start(bf16[128,1024]{1,0:T(8,128)(2,1)S(1)} %collective-permute-done.8.refs_4_), channel_id=1, source_target_pairs={{0,16},{4,12},{8,24},{12,4},{16,0},{20,28},{24,8},{28,20},{1,17},{... | collective-permute-start | bytes 786440 | tf_op jit(solution)/shard_map/ppermute | solution.py:397
  44.7 9.6 %collective-permute-start.13 = (bf16[128,2048]{1,0:T(8,128)(2,1)S(1)}, bf16[128,2048]{1,0:T(8,128)(2,1)S(1)}, u32[]{:S(2)}, u32[]{:S(2)}) collective-permute-start(bf16[128,2048]{1,0:T(8,128)(2,1)S(1)} %gate.1.refs_4_), channel_id=1, source_target_pairs={{0,16},{4,12},{8,24},{12,4},{16,0},{20,28},{24,8},{28,20},{1,17},{... | collective-permute-start | bytes 1572872 | tf_op jit(solution)/shard_map/ppermute | solution.py:397
  63.7 3.5 %collective-permute-start.15 = (bf16[256,2048]{1,0:T(8,128)(2,1)S(1)}, bf16[256,2048]{1,0:T(8,128)(2,1)S(1)}, u32[]{:S(2)}, u32[]{:S(2)}) collective-permute-start(bf16[256,2048]{1,0:T(8,128)(2,1)S(1)} %get-tuple-element.74), channel_id=1, source_target_pairs={{0,4},{4,0},{1,5},{5,1},{2,6},{6,2},{3,7},{7,3},{8,12},{12,8},{9,1... | collective-permute-start | bytes 3145736 | tf_op jit(solution)/shard_map/ppermute | solution.py:459
  66.7 2.8 %collective-permute-start.14 = (bf16[256,2048]{1,0:T(8,128)(2,1)S(1)}, bf16[256,2048]{1,0:T(8,128)(2,1)S(1)}, u32[]{:S(2)}, u32[]{:S(2)}) collective-permute-start(bf16[256,2048]{1,0:T(8,128)(2,1)S(1)} %get-tuple-element.72), channel_id=1, source_target_pairs={{0,4},{4,0},{1,5},{5,1},{2,6},{6,2},{3,7},{7,3},{8,12},{12,8},{9,1... | collective-permute-start | bytes 3145736 | tf_op jit(solution)/shard_map/ppermute | solution.py:459

commit v7 on v6

--- a/solution.py
+++ b/solution.py
@@ -465,8 +465,10 @@
     near = arrive(None)
     own, arrive = rows_of((1,), [load((1, 2), own)])
     arrive(None)
-    own, arrive = rows_of((2, 3), [load((4, 6), own), near])
-    arrive(steps(0))
+    own, arrive = rows_of((2,), [load((4, 6), own), near])
+    arrive(None)
+    own, arrive = rows_of((3,), [own, steps(0)])
+    arrive(None)
     for g in range(1, kv_heads):
         steps(g)
     out = total(0, w_out.shape[1], mine[:1], got[:1], None)

time: 70.9 us -> 68.3 us (0.963)
  waiting for transfers between devices: 8.71 us -> 3.77 us
  starting transfers between devices: 23.2 us -> 25.4 us
    ppermute x3 -> x4, waiting for transfers between devices: 6.05 us -> 0.71 us  [gather_rows(): near = lax.ppermute(own, ('ctx', 'tp'), route(True))]
    ppermute x3 -> x4, starting transfers between devices: 4.71 us -> 6 us  [gather_rows(): near = lax.ppermute(own, ('ctx', 'tp'), route(True))]
    ppermute x3 -> x4, starting transfers between devices: 2.57 us -> 3.53 us  [gather_rows(): side = lax.ppermute(own, ('ctx', 'tp'), route(False))]
    ppermute x3 -> x4, waiting for transfers between devices: 1.44 us -> 1.86 us  [forward(): return (own, first, side, lax.ppermute(first, ('ctx', 'tp'), route(False)))]
    ppermute x3 -> x4, starting transfers between devices: 3.23 us -> 3.12 us  [forward(): return (own, first, side, lax.ppermute(first, ('ctx', 'tp'), route(False)))]
    pallas_call x3 -> x4, Pallas kernels: 2.72 us -> 2.76 us  [attend(): pl.pallas_call(functools.partial(attend_kernel, groups), out_shape=jax.Sh...]
  transfers between devices with their start and end apart: 16 -> 19, of which waited for: 4 -> 3; matrix products, arithmetic and copies ran while one was open for 0% -> 0% of each run, Pallas kernels for 38% -> 49%
where the time goes in v7:
time: 68.3 us; the launch traced here: 68 us
  Pallas kernels  38.5 us (56%)
  starting transfers between devices  25.4 us (37%)
  waiting for transfers between devices  3.77 us (6%)
    pallas_call x8, Pallas kernels, step(): pl.pallas_call(functools.partial(step_kernel, index, last, column, first,...  23.8 us
    pallas_call x2, Pallas kernels, load_blocks(): pl.pallas_call(functools.partial(load_kernel, indexes), out_shape=[jax.Sh...  6.97 us
    ppermute x4, starting transfers between devices, gather_rows(): near = lax.ppermute(own, ('ctx', 'tp'), route(True))  6 us
    ppermute x1, starting transfers between devices, local(): value_two = lax.ppermute(value_rows, 'ctx', two)  4.87 us
    ppermute x4, starting transfers between devices, gather_rows(): side = lax.ppermute(own, ('ctx', 'tp'), route(False))  3.53 us
    ppermute x1, starting transfers between devices, local(): key_near = lax.ppermute(key_rows, 'ctx', [(0, 1), (1, 2), (2, 3)])  3.4 us
    ppermute x4, starting transfers between devices, forward(): return (own, first, side, lax.ppermute(first, ('ctx', 'tp'), route(False)))  3.12 us
    pallas_call x4, Pallas kernels, attend(): pl.pallas_call(functools.partial(attend_kernel, groups), out_shape=jax.Sh...  2.76 us
  transfers between devices with their start and end apart: 19, of which 3 were waited for; matrix products, arithmetic and copies ran while one was open for 0% of the time, Pallas kernels for 49%

profile of v7, /device:TPU:0, one launch (start us, length us, event | category | flops | bytes accessed | tf_op | source)
XLA Modules:
  0.0 68.0 jit_solution(11885258599152426370)
XLA Ops:
  0.0 4.9 %collective-permute-start = (bf16[128,512]{1,0:T(8,128)(2,1)}, bf16[128,512]{1,0:T(8,128)(2,1)S(1)}, u32[]{:S(2)}, u32[]{:S(2)}) collective-permute-start(bf16[128,512]{1,0:T(8,128)(2,1)} %v_hbm.1), channel_id=1, source_target_pairs={{0,16},{8,24},{1,17},{9,25},{2,18},{10,26},{3,19},{11,27},{4,20},{... | collective-permute-start | bytes 393224 | tf_op jit(solution)/shard_map/ppermute | solution.py:409
  4.9 3.4 %collective-permute-start.2 = (bf16[128,512]{1,0:T(8,128)(2,1)}, bf16[128,512]{1,0:T(8,128)(2,1)S(1)}, u32[]{:S(2)}, u32[]{:S(2)}) collective-permute-start(bf16[128,512]{1,0:T(8,128)(2,1)} %k_hbm.1), channel_id=1, source_target_pairs={{0,8},{8,16},{16,24},{1,9},{9,17},{17,25},{2,10},{10,18},{18,26},{... | collective-permute-start | bytes 393224 | tf_op jit(solution)/shard_map/ppermute | solution.py:411
  8.3 1.3 %collective-permute-start.1 = (bf16[128,512]{1,0:T(8,128)(2,1)}, bf16[128,512]{1,0:T(8,128)(2,1)S(1)}, u32[]{:S(2)}, u32[]{:S(2)}) collective-permute-start(bf16[128,512]{1,0:T(8,128)(2,1)} %k_hbm.1), channel_id=1, source_target_pairs={{0,16},{8,24},{1,17},{9,25},{2,18},{10,26},{3,19},{11,27},{4,20},{... | collective-permute-start | bytes 393224 | tf_op jit(solution)/shard_map/ppermute | solution.py:410
  9.6 1.9 %collective-permute-start.3 = (bf16[128,512]{1,0:T(8,128)(2,1)}, bf16[128,512]{1,0:T(8,128)(2,1)S(1)}, u32[]{:S(2)}, u32[]{:S(2)}) collective-permute-start(bf16[128,512]{1,0:T(8,128)(2,1)} %v_hbm.1), channel_id=1, source_target_pairs={{0,8},{16,24},{1,9},{17,25},{2,10},{18,26},{3,11},{19,27},{4,12},{... | collective-permute-start | bytes 393224 | tf_op jit(solution)/shard_map/ppermute | solution.py:412
  12.2 2.7 %prepare.1 = (bf16[128,512]{1,0:T(8,128)(2,1)S(1)}, bf16[128,512]{1,0:T(8,128)(2,1)S(1)}, bf16[128,4096]{1,0:T(8,128)(2,1)S(1)}, f32[128,384]{1,0:T(8,128)S(1)}, bf16[1024,2048]{1,0:T(8,128)(2,1)S(1)}) custom-call(s32[8]{0:T(128)} %docs_hbm.1, bf16[128,512]{1,0:T(8,128)(2,1)} %k_hbm.1, bf16[128,512]{1,0:T(8,128)(2,1)} %v_hbm.1, bf16[128,4096]{1,0:T(8,128)(2,1)} %q_hbm.1, ...), custom_call_target="tpu_custom_call" | custom-call | bytes 4194304 | tf_op jit(solution)/shard_map/prepare/pallas_call | solution.py:123
  15.7 1.8 %collective-permute-start.5 = (bf16[128,1024]{1,0:T(8,128)(2,1)S(1)}, bf16[128,1024]{1,0:T(8,128)(2,1)S(1)}, u32[]{:S(2)}, u32[]{:S(2)}) collective-permute-start(bf16[128,1024]{1,0:T(8,128)(2,1)S(1)} %attend_0.1.refs_1_.after), channel_id=1, source_target_pairs={{0,8},{4,20},{8,0},{12,28},{16,24},{20,4},{24,16},{28,12},{1,9},{5... | collective-permute-start | bytes 786440 | tf_op jit(solution)/shard_map/ppermute | solution.py:392
  18.0 3.5 %load_1.1 = (bf16[1024,2048]{1,0:T(8,128)(2,1)S(1)}, bf16[1024,2048]{1,0:T(8,128)(2,1)S(1)}, f32[8,128]{1,0:T(8,128)S(1)}) custom-call(bf16[128,1024]{1,0:T(8,128)(2,1)S(1)} %attend_0.1.refs_1_.after, bf16[4096,4096]{1,0:T(8,128)(2,1)} %refs_1_.5), custom_call_target="tpu_custom_call" | custom-call | bytes 16777216 | tf_op jit(solution)/shard_map/load_1/pallas_call | solution.py:163
  22.2 2.0 %collective-permute-start.8 = (bf16[128,1024]{1,0:T(8,128)(2,1)S(1)}, bf16[128,1024]{1,0:T(8,128)(2,1)S(1)}, u32[]{:S(2)}, u32[]{:S(2)}) collective-permute-start(bf16[128,1024]{1,0:T(8,128)(2,1)S(1)} %attend_1.1.refs_3_.after), channel_id=1, source_target_pairs={{0,8},{4,20},{8,0},{12,28},{16,24},{20,4},{24,16},{28,12},{1,9},{5... | collective-permute-start | bytes 786440 | tf_op jit(solution)/shard_map/ppermute | solution.py:392
  25.0 2.0 %collective-permute-start.9 = (bf16[128,1024]{1,0:T(8,128)(2,1)S(1)}, bf16[128,1024]{1,0:T(8,128)(2,1)S(1)}, u32[]{:S(2)}, u32[]{:S(2)}) collective-permute-start(bf16[128,1024]{1,0:T(8,128)(2,1)S(1)} %attend_1.1.refs_3_.after), channel_id=1, source_target_pairs={{0,16},{4,12},{8,24},{12,4},{16,0},{20,28},{24,8},{28,20},{1,17},{... | collective-permute-start | bytes 786440 | tf_op jit(solution)/shard_map/ppermute | solution.py:393
  26.9 3.5 %load_4.1 = (bf16[1024,2048]{1,0:T(8,128)(2,1)S(1)}, bf16[1024,2048]{1,0:T(8,128)(2,1)S(1)}, f32[8,128]{1,0:T(8,128)S(1)}) custom-call(bf16[128,1024]{1,0:T(8,128)(2,1)S(1)} %attend_1.1.refs_3_.after, bf16[4096,4096]{1,0:T(8,128)(2,1)} %refs_1_.5), custom_call_target="tpu_custom_call" | custom-call | bytes 16777216 | tf_op jit(solution)/shard_map/load_4/pallas_call | solution.py:163
  32.1 1.2 %collective-permute-start.10 = (bf16[128,1024]{1,0:T(8,128)(2,1)S(1)}, bf16[128,1024]{1,0:T(8,128)(2,1)S(1)}, u32[]{:S(2)}, u32[]{:S(2)}) collective-permute-start(bf16[128,1024]{1,0:T(8,128)(2,1)S(1)} %collective-permute-done.8.refs_4_), channel_id=1, source_target_pairs={{0,16},{4,12},{8,24},{12,4},{16,0},{20,28},{24,8},{28,20},{1,17},{... | collective-permute-start | bytes 786440 | tf_op jit(solution)/shard_map/ppermute | solution.py:397
  33.3 3.1 %step_0_0.1 = (f32[512,2048]{1,0:T(8,128)S(1)}, bf16[512,1024]{1,0:T(8,128)(2,1)S(1)}, f32[8,128]{1,0:T(8,128)S(1)}) custom-call(s32[16]{0:T(128)S(1)} %copy-done, bf16[128,1024]{1,0:T(8,128)(2,1)S(1)} %attend_0.1.refs_1_.after, bf16[128,1024]{1,0:T(8,128)(2,1)S(1)} %collective-permute-done.5.refs_2_.rest_1_, ...), custom_call_target="tpu_custom_call" | custom-call | flops 2147483648 | tf_op jit(solution)/shard_map/step_0_0/pallas_call | solution.py:303
  36.4 2.4 %step_1_0.1 = (f32[512,2048]{1,0:T(8,128)S(1)}, f32[8,128]{1,0:T(8,128)S(1)}) custom-call(f32[8,128]{1,0:T(8,128)S(1)} %get-tuple-element.45.refs_0_, bf16[512,1024]{1,0:T(8,128)(2,1)S(1)} %get-tuple-element.46.refs_1_, bf16[1024,2048]{1,0:T(8,128)(2,1)S(1)} %get-tuple-element.47.refs_2_), custom_call_target="tpu_custom_call" | custom-call | flops 2147483648 | tf_op jit(solution)/shard_map/step_1_0/pallas_call | solution.py:303
  40.3 1.4 %collective-permute-start.14 = (bf16[128,1024]{1,0:T(8,128)(2,1)S(1)}, bf16[128,1024]{1,0:T(8,128)(2,1)S(1)}, u32[]{:S(2)}, u32[]{:S(2)}) collective-permute-start(bf16[128,1024]{1,0:T(8,128)(2,1)S(1)} %attend_3.1.refs_3_), channel_id=1, source_target_pairs={{0,8},{4,20},{8,0},{12,28},{16,24},{20,4},{24,16},{28,12},{1,9},{5... | collective-permute-start | bytes 786440 | tf_op jit(solution)/shard_map/ppermute | solution.py:392
  41.7 1.8 %collective-permute-start.13 = (bf16[128,1024]{1,0:T(8,128)(2,1)S(1)}, bf16[128,1024]{1,0:T(8,128)(2,1)S(1)}, u32[]{:S(2)}, u32[]{:S(2)}) collective-permute-start(bf16[128,1024]{1,0:T(8,128)(2,1)S(1)} %collective-permute-done.11.refs_4_), channel_id=1, source_target_pairs={{0,16},{4,12},{8,24},{12,4},{16,0},{20,28},{24,8},{28,20},{1,17},{... | collective-permute-start | bytes 786440 | tf_op jit(solution)/shard_map/ppermute | solution.py:397
  43.5 1.8 %collective-permute-done.10.refs_6_ = bf16[128,1024]{1,0:T(8,128)(2,1)S(1)} collective-permute-done((bf16[128,1024]{1,0:T(8,128)(2,1)S(1)}, bf16[128,1024]{1,0:T(8,128)(2,1)S(1)}, u32[]{:S(2)}, u32[]{:S(2)}) %collective-permute-start.10) | collective-permute-done | bytes 262176 | tf_op jit(solution)/shard_map/ppermute | solution.py:397
  45.3 3.4 %step_2_0.1 = (f32[512,2048]{1,0:T(8,128)S(1)}, bf16[512,1024]{1,0:T(8,128)(2,1)S(1)}, bf16[1024,2048]{1,0:T(8,128)(2,1)S(1)}, f32[8,128]{1,0:T(8,128)S(1)}) custom-call(f32[8,128]{1,0:T(8,128)S(1)} %get-tuple-element.48.refs_0_.rest_1_, bf16[4096,4096]{1,0:T(8,128)(2,1)} %refs_1_.5, s32[16]{0:T(128)S(1)} %copy-done, ...), custom_call_target="tpu_custom_call", output_to_operand_aliasing={{0}: (8, {})} | custom-call | flops 2147483648 | tf_op jit(solution)/shard_map/step_2_0/pallas_call | solution.py:303
  48.7 2.7 %step_3_0.1 = (f32[512,2048]{1,0:T(8,128)S(1)}, f32[8,128]{1,0:T(8,128)S(1)}) custom-call(f32[8,128]{1,0:T(8,128)S(1)} %get-tuple-element.52.refs_0_, bf16[512,1024]{1,0:T(8,128)(2,1)S(1)} %get-tuple-element.53.refs_1_, bf16[1024,2048]{1,0:T(8,128)(2,1)S(1)} %get-tuple-element.54.refs_2_, ...), custom_call_target="tpu_custom_call", output_to_operand_aliasing={{0}: (3, {})} | custom-call | flops 2147483648 | tf_op jit(solution)/shard_map/step_3_0/pallas_call | solution.py:303
  51.6 3.4 %step_4_0.1 = (f32[512,2048]{1,0:T(8,128)S(1)}, bf16[512,1024]{1,0:T(8,128)(2,1)S(1)}, bf16[1024,2048]{1,0:T(8,128)(2,1)S(1)}, f32[8,128]{1,0:T(8,128)S(1)}) custom-call(f32[8,128]{1,0:T(8,128)S(1)} %get-tuple-element.56.refs_0_, bf16[4096,4096]{1,0:T(8,128)(2,1)} %refs_1_.5, s32[16]{0:T(128)S(1)} %copy-done, ...), custom_call_target="tpu_custom_call", output_to_operand_aliasing={{0}: (8, {})} | custom-call | flops 2147483648 | tf_op jit(solution)/shard_map/step_4_0/pallas_call | solution.py:303
  55.0 2.9 %step_5_0.1 = (f32[512,2048]{1,0:T(8,128)S(1)}, f32[8,128]{1,0:T(8,128)S(1)}) custom-call(f32[8,128]{1,0:T(8,128)S(1)} %get-tuple-element.60.refs_0_, bf16[512,1024]{1,0:T(8,128)(2,1)S(1)} %get-tuple-element.61.refs_1_, bf16[1024,2048]{1,0:T(8,128)(2,1)S(1)} %get-tuple-element.62.refs_2_, ...), custom_call_target="tpu_custom_call", output_to_operand_aliasing={{0}: (3, {})} | custom-call | flops 2147483648 | tf_op jit(solution)/shard_map/step_5_0/pallas_call | solution.py:303
  57.9 3.1 %step_6_0.1 = (f32[256,2048]{1,0:T(8,128)S(1)}, bf16[256,2048]{1,0:T(8,128)(2,1)S(1)}, bf16[512,1024]{1,0:T(8,128)(2,1)S(1)}, bf16[1024,2048]{1,0:T(8,128)(2,1)S(1)}, f32[8,128]{1,0:T(8,128)S(1)}) custom-call(f32[8,128]{1,0:T(8,128)S(1)} %get-tuple-element.64.refs_0_, bf16[4096,4096]{1,0:T(8,128)(2,1)} %refs_1_.5, s32[16]{0:T(128)S(1)} %copy-done, ...), custom_call_target="tpu_custom_call" | custom-call | flops 2147483648 | tf_op jit(solution)/shard_map/step_6_0/pallas_call | solution.py:303
  61.1 2.9 %step_7_0.1 = (f32[256,2048]{1,0:T(8,128)S(1)}, bf16[256,2048]{1,0:T(8,128)(2,1)S(1)}, f32[8,128]{1,0:T(8,128)}) custom-call(f32[8,128]{1,0:T(8,128)S(1)} %get-tuple-element.67.refs_0_, bf16[512,1024]{1,0:T(8,128)(2,1)S(1)} %get-tuple-element.68.refs_1_, bf16[1024,2048]{1,0:T(8,128)(2,1)S(1)} %get-tuple-element.69.refs_2_, ...), custom_call_target="tpu_custom_call" | custom-call | flops 2147483648 | tf_op jit(solution)/shard_map/step_7_0/pallas_call | solution.py:303
  64.5 1.1 %total_0.1.refs_2_ = bf16[256,4096]{1,0:T(8,128)(2,1)} custom-call(f32[256,2048]{1,0:T(8,128)S(1)} %get-tuple-element.73.refs_0_, bf16[256,2048]{1,0:T(8,128)(2,1)S(1)} %collective-permute-done.18.refs_1_), custom_call_target="tpu_custom_call" | custom-call | flops 524288 | bytes 1048576 | tf_op jit(solution)/shard_map/total_0/pallas_call | solution.py:348
  65.6 1.2 %collective-permute-done.17.refs_1_ = bf16[256,2048]{1,0:T(8,128)(2,1)S(1)} collective-permute-done((bf16[256,2048]{1,0:T(8,128)(2,1)S(1)}, bf16[256,2048]{1,0:T(8,128)(2,1)S(1)}, u32[]{:S(2)}, u32[]{:S(2)}) %collective-permute-start.17) | collective-permute-done | bytes 1048608 | tf_op jit(solution)/shard_map/ppermute | solution.py:459
  (33 shorter events, 8.4 us)
Async XLA Ops:
  0.0 11.5 %collective-permute-start = (bf16[128,512]{1,0:T(8,128)(2,1)}, bf16[128,512]{1,0:T(8,128)(2,1)S(1)}, u32[]{:S(2)}, u32[]{:S(2)}) collective-permute-start(bf16[128,512]{1,0:T(8,128)(2,1)} %v_hbm.1), channel_id=1, source_target_pairs={{0,16},{8,24},{1,17},{9,25},{2,18},{10,26},{3,19},{11,27},{4,20},{... | collective-permute-start | bytes 393224 | tf_op jit(solution)/shard_map/ppermute | solution.py:409
  4.9 10.0 %collective-permute-start.2 = (bf16[128,512]{1,0:T(8,128)(2,1)}, bf16[128,512]{1,0:T(8,128)(2,1)S(1)}, u32[]{:S(2)}, u32[]{:S(2)}) collective-permute-start(bf16[128,512]{1,0:T(8,128)(2,1)} %k_hbm.1), channel_id=1, source_target_pairs={{0,8},{8,16},{16,24},{1,9},{9,17},{17,25},{2,10},{10,18},{18,26},{... | collective-permute-start | bytes 393224 | tf_op jit(solution)/shard_map/ppermute | solution.py:411
  8.3 6.6 %collective-permute-start.1 = (bf16[128,512]{1,0:T(8,128)(2,1)}, bf16[128,512]{1,0:T(8,128)(2,1)S(1)}, u32[]{:S(2)}, u32[]{:S(2)}) collective-permute-start(bf16[128,512]{1,0:T(8,128)(2,1)} %k_hbm.1), channel_id=1, source_target_pairs={{0,16},{8,24},{1,17},{9,25},{2,18},{10,26},{3,19},{11,27},{4,20},{... | collective-permute-start | bytes 393224 | tf_op jit(solution)/shard_map/ppermute | solution.py:410
  9.6 5.4 %collective-permute-start.3 = (bf16[128,512]{1,0:T(8,128)(2,1)}, bf16[128,512]{1,0:T(8,128)(2,1)S(1)}, u32[]{:S(2)}, u32[]{:S(2)}) collective-permute-start(bf16[128,512]{1,0:T(8,128)(2,1)} %v_hbm.1), channel_id=1, source_target_pairs={{0,8},{16,24},{1,9},{17,25},{2,10},{18,26},{3,11},{19,27},{4,12},{... | collective-permute-start | bytes 393224 | tf_op jit(solution)/shard_map/ppermute | solution.py:412
  11.5 3.4 %collective-permute-start.4 = (bf16[128,512]{1,0:T(8,128)(2,1)S(1)}, bf16[128,512]{1,0:T(8,128)(2,1)S(1)}, u32[]{:S(2)}, u32[]{:S(2)}) collective-permute-start(bf16[128,512]{1,0:T(8,128)(2,1)S(1)} %collective-permute-done.after.v2), channel_id=1, source_target_pairs={{24,16},{25,17},{26,18},{27,19},{28,20},{29,21},{30,22},{31,23}} | collective-permute-start | bytes 393224 | tf_op jit(solution)/shard_map/ppermute | solution.py:413
  15.7 9.2 %collective-permute-start.5 = (bf16[128,1024]{1,0:T(8,128)(2,1)S(1)}, bf16[128,1024]{1,0:T(8,128)(2,1)S(1)}, u32[]{:S(2)}, u32[]{:S(2)}) collective-permute-start(bf16[128,1024]{1,0:T(8,128)(2,1)S(1)} %attend_0.1.refs_1_.after), channel_id=1, source_target_pairs={{0,8},{4,20},{8,0},{12,28},{16,24},{20,4},{24,16},{28,12},{1,9},{5... | collective-permute-start | bytes 786440 | tf_op jit(solution)/shard_map/ppermute | solution.py:392
  17.4 13.8 %collective-permute-start.6 = (bf16[128,1024]{1,0:T(8,128)(2,1)S(1)}, bf16[128,1024]{1,0:T(8,128)(2,1)S(1)}, u32[]{:S(2)}, u32[]{:S(2)}) collective-permute-start(bf16[128,1024]{1,0:T(8,128)(2,1)S(1)} %attend_0.1.refs_1_.after), channel_id=1, source_target_pairs={{0,16},{4,12},{8,24},{12,4},{16,0},{20,28},{24,8},{28,20},{1,17},{... | collective-permute-start | bytes 786440 | tf_op jit(solution)/shard_map/ppermute | solution.py:393
  22.2 11.1 %copy-start = (s32[16]{0:T(128)S(1)}, s32[16]{0:T(128)}, u32[]{:S(2)}) copy-start(s32[16]{0:T(128)} %refs_2_.5) | copy-start | bytes 196
  22.2 9.9 %collective-permute-start.8 = (bf16[128,1024]{1,0:T(8,128)(2,1)S(1)}, bf16[128,1024]{1,0:T(8,128)(2,1)S(1)}, u32[]{:S(2)}, u32[]{:S(2)}) collective-permute-start(bf16[128,1024]{1,0:T(8,128)(2,1)S(1)} %attend_1.1.refs_3_.after), channel_id=1, source_target_pairs={{0,8},{4,20},{8,0},{12,28},{16,24},{20,4},{24,16},{28,12},{1,9},{5... | collective-permute-start | bytes 786440 | tf_op jit(solution)/shard_map/ppermute | solution.py:392
  24.9 8.4 %collective-permute-start.7 = (bf16[128,1024]{1,0:T(8,128)(2,1)S(1)}, bf16[128,1024]{1,0:T(8,128)(2,1)S(1)}, u32[]{:S(2)}, u32[]{:S(2)}) collective-permute-start(bf16[128,1024]{1,0:T(8,128)(2,1)S(1)} %collective-permute-done.5.refs_2_.rest_1_), channel_id=1, source_target_pairs={{0,16},{4,12},{8,24},{12,4},{16,0},{20,28},{24,8},{28,20},{1,17},{... | collective-permute-start | bytes 786440 | tf_op jit(solution)/shard_map/ppermute | solution.py:397
  25.0 15.4 %collective-permute-start.9 = (bf16[128,1024]{1,0:T(8,128)(2,1)S(1)}, bf16[128,1024]{1,0:T(8,128)(2,1)S(1)}, u32[]{:S(2)}, u32[]{:S(2)}) collective-permute-start(bf16[128,1024]{1,0:T(8,128)(2,1)S(1)} %attend_1.1.refs_3_.after), channel_id=1, source_target_pairs={{0,16},{4,12},{8,24},{12,4},{16,0},{20,28},{24,8},{28,20},{1,17},{... | collective-permute-start | bytes 786440 | tf_op jit(solution)/shard_map/ppermute | solution.py:393
  31.1 20.4 %collective-permute-start.12 = (bf16[128,1024]{1,0:T(8,128)(2,1)S(1)}, bf16[128,1024]{1,0:T(8,128)(2,1)S(1)}, u32[]{:S(2)}, u32[]{:S(2)}) collective-permute-start(bf16[128,1024]{1,0:T(8,128)(2,1)S(1)} %attend_2.1.refs_3_.rest_0_), channel_id=1, source_target_pairs={{0,16},{4,12},{8,24},{12,4},{16,0},{20,28},{24,8},{28,20},{1,17},{... | collective-permute-start | bytes 786440 | tf_op jit(solution)/shard_map/ppermute | solution.py:393
  31.2 10.4 %collective-permute-start.11 = (bf16[128,1024]{1,0:T(8,128)(2,1)S(1)}, bf16[128,1024]{1,0:T(8,128)(2,1)S(1)}, u32[]{:S(2)}, u32[]{:S(2)}) collective-permute-start(bf16[128,1024]{1,0:T(8,128)(2,1)S(1)} %attend_2.1.refs_3_.rest_0_), channel_id=1, source_target_pairs={{0,8},{4,20},{8,0},{12,28},{16,24},{20,4},{24,16},{28,12},{1,9},{5... | collective-permute-start | bytes 786440 | tf_op jit(solution)/shard_map/ppermute | solution.py:392
  32.1 13.2 %collective-permute-start.10 = (bf16[128,1024]{1,0:T(8,128)(2,1)S(1)}, bf16[128,1024]{1,0:T(8,128)(2,1)S(1)}, u32[]{:S(2)}, u32[]{:S(2)}) collective-permute-start(bf16[128,1024]{1,0:T(8,128)(2,1)S(1)} %collective-permute-done.8.refs_4_), channel_id=1, source_target_pairs={{0,16},{4,12},{8,24},{12,4},{16,0},{20,28},{24,8},{28,20},{1,17},{... | collective-permute-start | bytes 786440 | tf_op jit(solution)/shard_map/ppermute | solution.py:397
  39.4 18.5 %collective-permute-start.15 = (bf16[128,1024]{1,0:T(8,128)(2,1)S(1)}, bf16[128,1024]{1,0:T(8,128)(2,1)S(1)}, u32[]{:S(2)}, u32[]{:S(2)}) collective-permute-start(bf16[128,1024]{1,0:T(8,128)(2,1)S(1)} %attend_3.1.refs_3_), channel_id=1, source_target_pairs={{0,16},{4,12},{8,24},{12,4},{16,0},{20,28},{24,8},{28,20},{1,17},{... | collective-permute-start | bytes 786440 | tf_op jit(solution)/shard_map/ppermute | solution.py:393
  40.3 11.2 %collective-permute-start.14 = (bf16[128,1024]{1,0:T(8,128)(2,1)S(1)}, bf16[128,1024]{1,0:T(8,128)(2,1)S(1)}, u32[]{:S(2)}, u32[]{:S(2)}) collective-permute-start(bf16[128,1024]{1,0:T(8,128)(2,1)S(1)} %attend_3.1.refs_3_), channel_id=1, source_target_pairs={{0,8},{4,20},{8,0},{12,28},{16,24},{20,4},{24,16},{28,12},{1,9},{5... | collective-permute-start | bytes 786440 | tf_op jit(solution)/shard_map/ppermute | solution.py:392
  41.7 9.9 %collective-permute-start.13 = (bf16[128,1024]{1,0:T(8,128)(2,1)S(1)}, bf16[128,1024]{1,0:T(8,128)(2,1)S(1)}, u32[]{:S(2)}, u32[]{:S(2)}) collective-permute-start(bf16[128,1024]{1,0:T(8,128)(2,1)S(1)} %collective-permute-done.11.refs_4_), channel_id=1, source_target_pairs={{0,16},{4,12},{8,24},{12,4},{16,0},{20,28},{24,8},{28,20},{1,17},{... | collective-permute-start | bytes 786440 | tf_op jit(solution)/shard_map/ppermute | solution.py:397
  51.5 6.4 %collective-permute-start.16 = (bf16[128,1024]{1,0:T(8,128)(2,1)S(1)}, bf16[128,1024]{1,0:T(8,128)(2,1)S(1)}, u32[]{:S(2)}, u32[]{:S(2)}) collective-permute-start(bf16[128,1024]{1,0:T(8,128)(2,1)S(1)} %collective-permute-done.14.refs_4_), channel_id=1, source_target_pairs={{0,16},{4,12},{8,24},{12,4},{16,0},{20,28},{24,8},{28,20},{1,17},{... | collective-permute-start | bytes 786440 | tf_op jit(solution)/shard_map/ppermute | solution.py:397
  61.0 3.5 %collective-permute-start.18 = (bf16[256,2048]{1,0:T(8,128)(2,1)S(1)}, bf16[256,2048]{1,0:T(8,128)(2,1)S(1)}, u32[]{:S(2)}, u32[]{:S(2)}) collective-permute-start(bf16[256,2048]{1,0:T(8,128)(2,1)S(1)} %get-tuple-element.74), channel_id=1, source_target_pairs={{0,4},{4,0},{1,5},{5,1},{2,6},{6,2},{3,7},{7,3},{8,12},{12,8},{9,1... | collective-permute-start | bytes 3145736 | tf_op jit(solution)/shard_map/ppermute | solution.py:459
  64.0 2.8 %collective-permute-start.17 = (bf16[256,2048]{1,0:T(8,128)(2,1)S(1)}, bf16[256,2048]{1,0:T(8,128)(2,1)S(1)}, u32[]{:S(2)}, u32[]{:S(2)}) collective-permute-start(bf16[256,2048]{1,0:T(8,128)(2,1)S(1)} %get-tuple-element.72), channel_id=1, source_target_pairs={{0,4},{4,0},{1,5},{5,1},{2,6},{6,2},{3,7},{7,3},{8,12},{12,8},{9,1... | collective-permute-start | bytes 3145736 | tf_op jit(solution)/shard_map/ppermute | solution.py:459

commit v8 on v7

--- a/solution.py
+++ b/solution.py
@@ -465,10 +465,11 @@
     near = arrive(None)
     own, arrive = rows_of((1,), [load((1, 2), own)])
     arrive(None)
-    own, arrive = rows_of((2,), [load((4, 6), own), near])
-    arrive(None)
+    own, arrive = rows_of((2,), [own, near])
+    near = arrive(None)
     own, arrive = rows_of((3,), [own, steps(0)])
     arrive(None)
+    state["before"] = load((4, 6), near)
     for g in range(1, kv_heads):
         steps(g)
     out = total(0, w_out.shape[1], mine[:1], got[:1], None)

time: 68.3 us -> 71.3 us (1.044)
  starting transfers between devices: 25.4 us -> 29 us
    ppermute x4, starting transfers between devices: 3.53 us -> 6.52 us  [gather_rows(): side = lax.ppermute(own, ('ctx', 'tp'), route(False))]
    ppermute x4, waiting for transfers between devices: 1.86 us -> 0.01 us  [forward(): return (own, first, side, lax.ppermute(first, ('ctx', 'tp'), route(False)))]
    ppermute x4, waiting for transfers between devices: 0.71 us -> 1.74 us  [gather_rows(): near = lax.ppermute(own, ('ctx', 'tp'), route(True))]
  transfers between devices with their start and end apart: 19 -> 19, of which waited for: 3 -> 3; matrix products, arithmetic and copies ran while one was open for 0% -> 0% of each run, Pallas kernels for 49% -> 47%
where the time goes in v8:
time: 71.3 us; the launch traced here: 71.1 us
  Pallas kernels  38.4 us (54%)
  starting transfers between devices  29 us (41%)
  waiting for transfers between devices  3.22 us (5%)
    pallas_call x8, Pallas kernels, step(): pl.pallas_call(functools.partial(step_kernel, index, last, column, first,...  23.8 us
    pallas_call x2, Pallas kernels, load_blocks(): pl.pallas_call(functools.partial(load_kernel, indexes), out_shape=[jax.Sh...  6.97 us
    ppermute x4, starting transfers between devices, gather_rows(): side = lax.ppermute(own, ('ctx', 'tp'), route(False))  6.52 us
    ppermute x4, starting transfers between devices, gather_rows(): near = lax.ppermute(own, ('ctx', 'tp'), route(True))  6.09 us
    ppermute x1, starting transfers between devices, local(): value_two = lax.ppermute(value_rows, 'ctx', two)  4.87 us
    ppermute x4, starting transfers between devices, forward(): return (own, first, side, lax.ppermute(first, ('ctx', 'tp'), route(False)))  3.68 us
    ppermute x1, starting transfers between devices, local(): key_near = lax.ppermute(key_rows, 'ctx', [(0, 1), (1, 2), (2, 3)])  3.4 us
    pallas_call x4, Pallas kernels, attend(): pl.pallas_call(functools.partial(attend_kernel, groups), out_shape=jax.Sh...  2.76 us
  transfers between devices with their start and end apart: 19, of which 3 were waited for; matrix products, arithmetic and copies ran while one was open for 0% of the time, Pallas kernels for 47%

profile of v8, /device:TPU:0, one launch (start us, length us, event | category | flops | bytes accessed | tf_op | source)
XLA Modules:
  0.0 71.1 jit_solution(7463207076237410060)
XLA Ops:
  0.0 4.9 %collective-permute-start = (bf16[128,512]{1,0:T(8,128)(2,1)}, bf16[128,512]{1,0:T(8,128)(2,1)S(1)}, u32[]{:S(2)}, u32[]{:S(2)}) collective-permute-start(bf16[128,512]{1,0:T(8,128)(2,1)} %v_hbm.1), channel_id=1, source_target_pairs={{0,16},{8,24},{1,17},{9,25},{2,18},{10,26},{3,19},{11,27},{4,20},{... | collective-permute-start | bytes 393224 | tf_op jit(solution)/shard_map/ppermute | solution.py:409
  4.9 1.3 %collective-permute-start.1 = (bf16[128,512]{1,0:T(8,128)(2,1)}, bf16[128,512]{1,0:T(8,128)(2,1)S(1)}, u32[]{:S(2)}, u32[]{:S(2)}) collective-permute-start(bf16[128,512]{1,0:T(8,128)(2,1)} %k_hbm.1), channel_id=1, source_target_pairs={{0,16},{8,24},{1,17},{9,25},{2,18},{10,26},{3,19},{11,27},{4,20},{... | collective-permute-start | bytes 393224 | tf_op jit(solution)/shard_map/ppermute | solution.py:410
  6.2 3.4 %collective-permute-start.2 = (bf16[128,512]{1,0:T(8,128)(2,1)}, bf16[128,512]{1,0:T(8,128)(2,1)S(1)}, u32[]{:S(2)}, u32[]{:S(2)}) collective-permute-start(bf16[128,512]{1,0:T(8,128)(2,1)} %k_hbm.1), channel_id=1, source_target_pairs={{0,8},{8,16},{16,24},{1,9},{9,17},{17,25},{2,10},{10,18},{18,26},{... | collective-permute-start | bytes 393224 | tf_op jit(solution)/shard_map/ppermute | solution.py:411
  9.6 1.9 %collective-permute-start.3 = (bf16[128,512]{1,0:T(8,128)(2,1)}, bf16[128,512]{1,0:T(8,128)(2,1)S(1)}, u32[]{:S(2)}, u32[]{:S(2)}) collective-permute-start(bf16[128,512]{1,0:T(8,128)(2,1)} %v_hbm.1), channel_id=1, source_target_pairs={{0,8},{16,24},{1,9},{17,25},{2,10},{18,26},{3,11},{19,27},{4,12},{... | collective-permute-start | bytes 393224 | tf_op jit(solution)/shard_map/ppermute | solution.py:412
  12.2 2.7 %prepare.1 = (bf16[128,512]{1,0:T(8,128)(2,1)S(1)}, bf16[128,512]{1,0:T(8,128)(2,1)S(1)}, bf16[128,4096]{1,0:T(8,128)(2,1)S(1)}, f32[128,384]{1,0:T(8,128)S(1)}, bf16[1024,2048]{1,0:T(8,128)(2,1)S(1)}) custom-call(s32[8]{0:T(128)} %docs_hbm.1, bf16[128,512]{1,0:T(8,128)(2,1)} %k_hbm.1, bf16[128,512]{1,0:T(8,128)(2,1)} %v_hbm.1, bf16[128,4096]{1,0:T(8,128)(2,1)} %q_hbm.1, ...), custom_call_target="tpu_custom_call" | custom-call | bytes 4194304 | tf_op jit(solution)/shard_map/prepare/pallas_call | solution.py:123
  15.9 2.4 %collective-permute-start.5 = (bf16[128,1024]{1,0:T(8,128)(2,1)S(1)}, bf16[128,1024]{1,0:T(8,128)(2,1)S(1)}, u32[]{:S(2)}, u32[]{:S(2)}) collective-permute-start(bf16[128,1024]{1,0:T(8,128)(2,1)S(1)} %attend_0.1.after.refs_1_), channel_id=1, source_target_pairs={{0,8},{4,20},{8,0},{12,28},{16,24},{20,4},{24,16},{28,12},{1,9},{5... | collective-permute-start | bytes 786440 | tf_op jit(solution)/shard_map/ppermute | solution.py:392
  19.1 3.5 %load_1.1 = (bf16[1024,2048]{1,0:T(8,128)(2,1)S(1)}, bf16[1024,2048]{1,0:T(8,128)(2,1)S(1)}, f32[8,128]{1,0:T(8,128)S(1)}) custom-call(bf16[128,1024]{1,0:T(8,128)(2,1)S(1)} %attend_0.1.after.refs_1_, bf16[4096,4096]{1,0:T(8,128)(2,1)} %refs_1_.5), custom_call_target="tpu_custom_call" | custom-call | bytes 16777216 | tf_op jit(solution)/shard_map/load_1/pallas_call | solution.py:163
  23.3 2.0 %collective-permute-start.7 = (bf16[128,1024]{1,0:T(8,128)(2,1)S(1)}, bf16[128,1024]{1,0:T(8,128)(2,1)S(1)}, u32[]{:S(2)}, u32[]{:S(2)}) collective-permute-start(bf16[128,1024]{1,0:T(8,128)(2,1)S(1)} %attend_1.1.rest_0_.refs_3_), channel_id=1, source_target_pairs={{0,8},{4,20},{8,0},{12,28},{16,24},{20,4},{24,16},{28,12},{1,9},{5... | collective-permute-start | bytes 786440 | tf_op jit(solution)/shard_map/ppermute | solution.py:392
  25.7 1.7 %collective-permute-start.8 = (bf16[128,1024]{1,0:T(8,128)(2,1)S(1)}, bf16[128,1024]{1,0:T(8,128)(2,1)S(1)}, u32[]{:S(2)}, u32[]{:S(2)}) collective-permute-start(bf16[128,1024]{1,0:T(8,128)(2,1)S(1)} %attend_1.1.rest_0_.refs_3_), channel_id=1, source_target_pairs={{0,16},{4,12},{8,24},{12,4},{16,0},{20,28},{24,8},{28,20},{1,17},{... | collective-permute-start | bytes 786440 | tf_op jit(solution)/shard_map/ppermute | solution.py:393
  28.9 2.0 %collective-permute-start.12 = (bf16[128,1024]{1,0:T(8,128)(2,1)S(1)}, bf16[128,1024]{1,0:T(8,128)(2,1)S(1)}, u32[]{:S(2)}, u32[]{:S(2)}) collective-permute-start(bf16[128,1024]{1,0:T(8,128)(2,1)S(1)} %attend_2.1.refs_3_.rest_0_), channel_id=1, source_target_pairs={{0,16},{4,12},{8,24},{12,4},{16,0},{20,28},{24,8},{28,20},{1,17},{... | collective-permute-start | bytes 786440 | tf_op jit(solution)/shard_map/ppermute | solution.py:393
  30.9 1.7 %collective-permute-done.7.refs_4_ = bf16[128,1024]{1,0:T(8,128)(2,1)S(1)} collective-permute-done((bf16[128,1024]{1,0:T(8,128)(2,1)S(1)}, bf16[128,1024]{1,0:T(8,128)(2,1)S(1)}, u32[]{:S(2)}, u32[]{:S(2)}) %collective-permute-start.7) | collective-permute-done | bytes 262176 | tf_op jit(solution)/shard_map/ppermute | solution.py:392
  32.6 1.2 %collective-permute-start.9 = (bf16[128,1024]{1,0:T(8,128)(2,1)S(1)}, bf16[128,1024]{1,0:T(8,128)(2,1)S(1)}, u32[]{:S(2)}, u32[]{:S(2)}) collective-permute-start(bf16[128,1024]{1,0:T(8,128)(2,1)S(1)} %collective-permute-done.7.refs_4_), channel_id=1, source_target_pairs={{0,16},{4,12},{8,24},{12,4},{16,0},{20,28},{24,8},{28,20},{1,17},{... | collective-permute-start | bytes 786440 | tf_op jit(solution)/shard_map/ppermute | solution.py:397
  33.9 3.0 %step_0_0.1 = (f32[512,2048]{1,0:T(8,128)S(1)}, bf16[512,1024]{1,0:T(8,128)(2,1)S(1)}, f32[8,128]{1,0:T(8,128)S(1)}) custom-call(s32[16]{0:T(128)S(1)} %copy-done, bf16[128,1024]{1,0:T(8,128)(2,1)S(1)} %attend_0.1.after.refs_1_, bf16[128,1024]{1,0:T(8,128)(2,1)S(1)} %collective-permute-done.5.rest_1_.refs_2_, ...), custom_call_target="tpu_custom_call" | custom-call | flops 2147483648 | tf_op jit(solution)/shard_map/step_0_0/pallas_call | solution.py:303
  36.9 2.4 %step_1_0.1 = (f32[512,2048]{1,0:T(8,128)S(1)}, f32[8,128]{1,0:T(8,128)S(1)}) custom-call(f32[8,128]{1,0:T(8,128)S(1)} %get-tuple-element.52.refs_0_, bf16[512,1024]{1,0:T(8,128)(2,1)S(1)} %get-tuple-element.53.refs_1_, bf16[1024,2048]{1,0:T(8,128)(2,1)S(1)} %get-tuple-element.54.refs_2_), custom_call_target="tpu_custom_call" | custom-call | flops 2147483648 | tf_op jit(solution)/shard_map/step_1_0/pallas_call | solution.py:303
  40.8 2.0 %collective-permute-start.15 = (bf16[128,1024]{1,0:T(8,128)(2,1)S(1)}, bf16[128,1024]{1,0:T(8,128)(2,1)S(1)}, u32[]{:S(2)}, u32[]{:S(2)}) collective-permute-start(bf16[128,1024]{1,0:T(8,128)(2,1)S(1)} %attend_3.1.refs_3_), channel_id=1, source_target_pairs={{0,16},{4,12},{8,24},{12,4},{16,0},{20,28},{24,8},{28,20},{1,17},{... | collective-permute-start | bytes 786440 | tf_op jit(solution)/shard_map/ppermute | solution.py:393
  42.8 3.5 %load_4.1 = (bf16[1024,2048]{1,0:T(8,128)(2,1)S(1)}, bf16[1024,2048]{1,0:T(8,128)(2,1)S(1)}, f32[8,128]{1,0:T(8,128)S(1)}) custom-call(bf16[128,1024]{1,0:T(8,128)(2,1)S(1)} %collective-permute-done.6.after.refs_4_, bf16[4096,4096]{1,0:T(8,128)(2,1)} %refs_1_.5), custom_call_target="tpu_custom_call" | custom-call | bytes 16777216 | tf_op jit(solution)/shard_map/load_4/pallas_call | solution.py:163
  46.4 3.4 %step_2_0.1 = (f32[512,2048]{1,0:T(8,128)S(1)}, bf16[512,1024]{1,0:T(8,128)(2,1)S(1)}, bf16[1024,2048]{1,0:T(8,128)(2,1)S(1)}, f32[8,128]{1,0:T(8,128)S(1)}) custom-call(f32[8,128]{1,0:T(8,128)S(1)} %get-tuple-element.45.refs_0_, bf16[4096,4096]{1,0:T(8,128)(2,1)} %refs_1_.5, s32[16]{0:T(128)S(1)} %copy-done, ...), custom_call_target="tpu_custom_call", output_to_operand_aliasing={{0}: (8, {})} | custom-call | flops 2147483648 | tf_op jit(solution)/shard_map/step_2_0/pallas_call | solution.py:303
  49.8 2.7 %step_3_0.1 = (f32[512,2048]{1,0:T(8,128)S(1)}, f32[8,128]{1,0:T(8,128)S(1)}) custom-call(f32[8,128]{1,0:T(8,128)S(1)} %get-tuple-element.49.refs_0_, bf16[512,1024]{1,0:T(8,128)(2,1)S(1)} %get-tuple-element.50.refs_1_, bf16[1024,2048]{1,0:T(8,128)(2,1)S(1)} %get-tuple-element.51.refs_2_, ...), custom_call_target="tpu_custom_call", output_to_operand_aliasing={{0}: (3, {})} | custom-call | flops 2147483648 | tf_op jit(solution)/shard_map/step_3_0/pallas_call | solution.py:303
  52.6 2.1 %collective-permute-start.16 = (bf16[128,1024]{1,0:T(8,128)(2,1)S(1)}, bf16[128,1024]{1,0:T(8,128)(2,1)S(1)}, u32[]{:S(2)}, u32[]{:S(2)}) collective-permute-start(bf16[128,1024]{1,0:T(8,128)(2,1)S(1)} %collective-permute-done.14.refs_4_), channel_id=1, source_target_pairs={{0,16},{4,12},{8,24},{12,4},{16,0},{20,28},{24,8},{28,20},{1,17},{... | collective-permute-start | bytes 786440 | tf_op jit(solution)/shard_map/ppermute | solution.py:397
  54.6 3.4 %step_4_0.1 = (f32[512,2048]{1,0:T(8,128)S(1)}, bf16[512,1024]{1,0:T(8,128)(2,1)S(1)}, bf16[1024,2048]{1,0:T(8,128)(2,1)S(1)}, f32[8,128]{1,0:T(8,128)S(1)}) custom-call(f32[8,128]{1,0:T(8,128)S(1)} %get-tuple-element.56.refs_0_, bf16[4096,4096]{1,0:T(8,128)(2,1)} %refs_1_.5, s32[16]{0:T(128)S(1)} %copy-done, ...), custom_call_target="tpu_custom_call", output_to_operand_aliasing={{0}: (8, {})} | custom-call | flops 2147483648 | tf_op jit(solution)/shard_map/step_4_0/pallas_call | solution.py:303
  58.0 2.9 %step_5_0.1 = (f32[512,2048]{1,0:T(8,128)S(1)}, f32[8,128]{1,0:T(8,128)S(1)}) custom-call(f32[8,128]{1,0:T(8,128)S(1)} %get-tuple-element.59.refs_0_, bf16[512,1024]{1,0:T(8,128)(2,1)S(1)} %get-tuple-element.60.refs_1_, bf16[1024,2048]{1,0:T(8,128)(2,1)S(1)} %get-tuple-element.61.refs_2_, ...), custom_call_target="tpu_custom_call", output_to_operand_aliasing={{0}: (3, {})} | custom-call | flops 2147483648 | tf_op jit(solution)/shard_map/step_5_0/pallas_call | solution.py:303
  60.9 3.1 %step_6_0.1 = (f32[256,2048]{1,0:T(8,128)S(1)}, bf16[256,2048]{1,0:T(8,128)(2,1)S(1)}, bf16[512,1024]{1,0:T(8,128)(2,1)S(1)}, bf16[1024,2048]{1,0:T(8,128)(2,1)S(1)}, f32[8,128]{1,0:T(8,128)S(1)}) custom-call(f32[8,128]{1,0:T(8,128)S(1)} %get-tuple-element.63.refs_0_, bf16[4096,4096]{1,0:T(8,128)(2,1)} %refs_1_.5, s32[16]{0:T(128)S(1)} %copy-done, ...), custom_call_target="tpu_custom_call" | custom-call | flops 2147483648 | tf_op jit(solution)/shard_map/step_6_0/pallas_call | solution.py:303
  64.1 2.9 %step_7_0.1 = (f32[256,2048]{1,0:T(8,128)S(1)}, bf16[256,2048]{1,0:T(8,128)(2,1)S(1)}, f32[8,128]{1,0:T(8,128)}) custom-call(f32[8,128]{1,0:T(8,128)S(1)} %get-tuple-element.67.refs_0_, bf16[512,1024]{1,0:T(8,128)(2,1)S(1)} %get-tuple-element.68.refs_1_, bf16[1024,2048]{1,0:T(8,128)(2,1)S(1)} %get-tuple-element.69.refs_2_, ...), custom_call_target="tpu_custom_call" | custom-call | flops 2147483648 | tf_op jit(solution)/shard_map/step_7_0/pallas_call | solution.py:303
  68.6 1.2 %collective-permute-done.17.refs_1_ = bf16[256,2048]{1,0:T(8,128)(2,1)S(1)} collective-permute-done((bf16[256,2048]{1,0:T(8,128)(2,1)S(1)}, bf16[256,2048]{1,0:T(8,128)(2,1)S(1)}, u32[]{:S(2)}, u32[]{:S(2)}) %collective-permute-start.17) | collective-permute-done | bytes 1048608 | tf_op jit(solution)/shard_map/ppermute | solution.py:459
  (33 shorter events, 9.3 us)
Async XLA Ops:
  0.0 11.5 %collective-permute-start = (bf16[128,512]{1,0:T(8,128)(2,1)}, bf16[128,512]{1,0:T(8,128)(2,1)S(1)}, u32[]{:S(2)}, u32[]{:S(2)}) collective-permute-start(bf16[128,512]{1,0:T(8,128)(2,1)} %v_hbm.1), channel_id=1, source_target_pairs={{0,16},{8,24},{1,17},{9,25},{2,18},{10,26},{3,19},{11,27},{4,20},{... | collective-permute-start | bytes 393224 | tf_op jit(solution)/shard_map/ppermute | solution.py:409
  4.9 10.0 %collective-permute-start.1 = (bf16[128,512]{1,0:T(8,128)(2,1)}, bf16[128,512]{1,0:T(8,128)(2,1)S(1)}, u32[]{:S(2)}, u32[]{:S(2)}) collective-permute-start(bf16[128,512]{1,0:T(8,128)(2,1)} %k_hbm.1), channel_id=1, source_target_pairs={{0,16},{8,24},{1,17},{9,25},{2,18},{10,26},{3,19},{11,27},{4,20},{... | collective-permute-start | bytes 393224 | tf_op jit(solution)/shard_map/ppermute | solution.py:410
  6.2 8.8 %collective-permute-start.2 = (bf16[128,512]{1,0:T(8,128)(2,1)}, bf16[128,512]{1,0:T(8,128)(2,1)S(1)}, u32[]{:S(2)}, u32[]{:S(2)}) collective-permute-start(bf16[128,512]{1,0:T(8,128)(2,1)} %k_hbm.1), channel_id=1, source_target_pairs={{0,8},{8,16},{16,24},{1,9},{9,17},{17,25},{2,10},{10,18},{18,26},{... | collective-permute-start | bytes 393224 | tf_op jit(solution)/shard_map/ppermute | solution.py:411
  9.6 5.6 %collective-permute-start.3 = (bf16[128,512]{1,0:T(8,128)(2,1)}, bf16[128,512]{1,0:T(8,128)(2,1)S(1)}, u32[]{:S(2)}, u32[]{:S(2)}) collective-permute-start(bf16[128,512]{1,0:T(8,128)(2,1)} %v_hbm.1), channel_id=1, source_target_pairs={{0,8},{16,24},{1,9},{17,25},{2,10},{18,26},{3,11},{19,27},{4,12},{... | collective-permute-start | bytes 393224 | tf_op jit(solution)/shard_map/ppermute | solution.py:412
  11.5 3.7 %collective-permute-start.4 = (bf16[128,512]{1,0:T(8,128)(2,1)S(1)}, bf16[128,512]{1,0:T(8,128)(2,1)S(1)}, u32[]{:S(2)}, u32[]{:S(2)}) collective-permute-start(bf16[128,512]{1,0:T(8,128)(2,1)S(1)} %collective-permute-done.after.v2), channel_id=1, source_target_pairs={{24,16},{25,17},{26,18},{27,19},{28,20},{29,21},{30,22},{31,23}} | collective-permute-start | bytes 393224 | tf_op jit(solution)/shard_map/ppermute | solution.py:413
  15.9 9.5 %collective-permute-start.5 = (bf16[128,1024]{1,0:T(8,128)(2,1)S(1)}, bf16[128,1024]{1,0:T(8,128)(2,1)S(1)}, u32[]{:S(2)}, u32[]{:S(2)}) collective-permute-start(bf16[128,1024]{1,0:T(8,128)(2,1)S(1)} %attend_0.1.after.refs_1_), channel_id=1, source_target_pairs={{0,8},{4,20},{8,0},{12,28},{16,24},{20,4},{24,16},{28,12},{1,9},{5... | collective-permute-start | bytes 786440 | tf_op jit(solution)/shard_map/ppermute | solution.py:392
  18.3 10.6 %collective-permute-start.10 = (bf16[128,1024]{1,0:T(8,128)(2,1)S(1)}, bf16[128,1024]{1,0:T(8,128)(2,1)S(1)}, u32[]{:S(2)}, u32[]{:S(2)}) collective-permute-start(bf16[128,1024]{1,0:T(8,128)(2,1)S(1)} %attend_0.1.after.refs_1_), channel_id=1, source_target_pairs={{0,16},{4,12},{8,24},{12,4},{16,0},{20,28},{24,8},{28,20},{1,17},{... | collective-permute-start | bytes 786440 | tf_op jit(solution)/shard_map/ppermute | solution.py:393
  22.6 11.2 %copy-start = (s32[16]{0:T(128)S(1)}, s32[16]{0:T(128)}, u32[]{:S(2)}) copy-start(s32[16]{0:T(128)} %refs_2_.5) | copy-start | bytes 196
  23.3 9.3 %collective-permute-start.7 = (bf16[128,1024]{1,0:T(8,128)(2,1)S(1)}, bf16[128,1024]{1,0:T(8,128)(2,1)S(1)}, u32[]{:S(2)}, u32[]{:S(2)}) collective-permute-start(bf16[128,1024]{1,0:T(8,128)(2,1)S(1)} %attend_1.1.rest_0_.refs_3_), channel_id=1, source_target_pairs={{0,8},{4,20},{8,0},{12,28},{16,24},{20,4},{24,16},{28,12},{1,9},{5... | collective-permute-start | bytes 786440 | tf_op jit(solution)/shard_map/ppermute | solution.py:392
  25.4 8.5 %collective-permute-start.11 = (bf16[128,1024]{1,0:T(8,128)(2,1)S(1)}, bf16[128,1024]{1,0:T(8,128)(2,1)S(1)}, u32[]{:S(2)}, u32[]{:S(2)}) collective-permute-start(bf16[128,1024]{1,0:T(8,128)(2,1)S(1)} %collective-permute-done.5.rest_1_.refs_2_), channel_id=1, source_target_pairs={{0,16},{4,12},{8,24},{12,4},{16,0},{20,28},{24,8},{28,20},{1,17},{... | collective-permute-start | bytes 786440 | tf_op jit(solution)/shard_map/ppermute | solution.py:397
  25.7 20.6 %collective-permute-start.8 = (bf16[128,1024]{1,0:T(8,128)(2,1)S(1)}, bf16[128,1024]{1,0:T(8,128)(2,1)S(1)}, u32[]{:S(2)}, u32[]{:S(2)}) collective-permute-start(bf16[128,1024]{1,0:T(8,128)(2,1)S(1)} %attend_1.1.rest_0_.refs_3_), channel_id=1, source_target_pairs={{0,16},{4,12},{8,24},{12,4},{16,0},{20,28},{24,8},{28,20},{1,17},{... | collective-permute-start | bytes 786440 | tf_op jit(solution)/shard_map/ppermute | solution.py:393
  28.1 12.7 %collective-permute-start.6 = (bf16[128,1024]{1,0:T(8,128)(2,1)S(1)}, bf16[128,1024]{1,0:T(8,128)(2,1)S(1)}, u32[]{:S(2)}, u32[]{:S(2)}) collective-permute-start(bf16[128,1024]{1,0:T(8,128)(2,1)S(1)} %attend_2.1.refs_3_.rest_0_), channel_id=1, source_target_pairs={{0,8},{4,20},{8,0},{12,28},{16,24},{20,4},{24,16},{28,12},{1,9},{5... | collective-permute-start | bytes 786440 | tf_op jit(solution)/shard_map/ppermute | solution.py:392
  28.9 25.7 %collective-permute-start.12 = (bf16[128,1024]{1,0:T(8,128)(2,1)S(1)}, bf16[128,1024]{1,0:T(8,128)(2,1)S(1)}, u32[]{:S(2)}, u32[]{:S(2)}) collective-permute-start(bf16[128,1024]{1,0:T(8,128)(2,1)S(1)} %attend_2.1.refs_3_.rest_0_), channel_id=1, source_target_pairs={{0,16},{4,12},{8,24},{12,4},{16,0},{20,28},{24,8},{28,20},{1,17},{... | collective-permute-start | bytes 786440 | tf_op jit(solution)/shard_map/ppermute | solution.py:393
  32.6 13.7 %collective-permute-start.9 = (bf16[128,1024]{1,0:T(8,128)(2,1)S(1)}, bf16[128,1024]{1,0:T(8,128)(2,1)S(1)}, u32[]{:S(2)}, u32[]{:S(2)}) collective-permute-start(bf16[128,1024]{1,0:T(8,128)(2,1)S(1)} %collective-permute-done.7.refs_4_), channel_id=1, source_target_pairs={{0,16},{4,12},{8,24},{12,4},{16,0},{20,28},{24,8},{28,20},{1,17},{... | collective-permute-start | bytes 786440 | tf_op jit(solution)/shard_map/ppermute | solution.py:397
  40.0 12.6 %collective-permute-start.14 = (bf16[128,1024]{1,0:T(8,128)(2,1)S(1)}, bf16[128,1024]{1,0:T(8,128)(2,1)S(1)}, u32[]{:S(2)}, u32[]{:S(2)}) collective-permute-start(bf16[128,1024]{1,0:T(8,128)(2,1)S(1)} %attend_3.1.refs_3_), channel_id=1, source_target_pairs={{0,8},{4,20},{8,0},{12,28},{16,24},{20,4},{24,16},{28,12},{1,9},{5... | collective-permute-start | bytes 786440 | tf_op jit(solution)/shard_map/ppermute | solution.py:392
  40.8 20.1 %collective-permute-start.15 = (bf16[128,1024]{1,0:T(8,128)(2,1)S(1)}, bf16[128,1024]{1,0:T(8,128)(2,1)S(1)}, u32[]{:S(2)}, u32[]{:S(2)}) collective-permute-start(bf16[128,1024]{1,0:T(8,128)(2,1)S(1)} %attend_3.1.refs_3_), channel_id=1, source_target_pairs={{0,16},{4,12},{8,24},{12,4},{16,0},{20,28},{24,8},{28,20},{1,17},{... | collective-permute-start | bytes 786440 | tf_op jit(solution)/shard_map/ppermute | solution.py:393
  46.3 8.3 %collective-permute-start.13 = (bf16[128,1024]{1,0:T(8,128)(2,1)S(1)}, bf16[128,1024]{1,0:T(8,128)(2,1)S(1)}, u32[]{:S(2)}, u32[]{:S(2)}) collective-permute-start(bf16[128,1024]{1,0:T(8,128)(2,1)S(1)} %collective-permute-done.6.after.refs_4_), channel_id=1, source_target_pairs={{0,16},{4,12},{8,24},{12,4},{16,0},{20,28},{24,8},{28,20},{1,17},{... | collective-permute-start | bytes 786440 | tf_op jit(solution)/shard_map/ppermute | solution.py:397
  52.6 8.4 %collective-permute-start.16 = (bf16[128,1024]{1,0:T(8,128)(2,1)S(1)}, bf16[128,1024]{1,0:T(8,128)(2,1)S(1)}, u32[]{:S(2)}, u32[]{:S(2)}) collective-permute-start(bf16[128,1024]{1,0:T(8,128)(2,1)S(1)} %collective-permute-done.14.refs_4_), channel_id=1, source_target_pairs={{0,16},{4,12},{8,24},{12,4},{16,0},{20,28},{24,8},{28,20},{1,17},{... | collective-permute-start | bytes 786440 | tf_op jit(solution)/shard_map/ppermute | solution.py:397
  64.1 3.5 %collective-permute-start.18 = (bf16[256,2048]{1,0:T(8,128)(2,1)S(1)}, bf16[256,2048]{1,0:T(8,128)(2,1)S(1)}, u32[]{:S(2)}, u32[]{:S(2)}) collective-permute-start(bf16[256,2048]{1,0:T(8,128)(2,1)S(1)} %get-tuple-element.74), channel_id=1, source_target_pairs={{0,4},{4,0},{1,5},{5,1},{2,6},{6,2},{3,7},{7,3},{8,12},{12,8},{9,1... | collective-permute-start | bytes 3145736 | tf_op jit(solution)/shard_map/ppermute | solution.py:459
  67.0 2.8 %collective-permute-start.17 = (bf16[256,2048]{1,0:T(8,128)(2,1)S(1)}, bf16[256,2048]{1,0:T(8,128)(2,1)S(1)}, u32[]{:S(2)}, u32[]{:S(2)}) collective-permute-start(bf16[256,2048]{1,0:T(8,128)(2,1)S(1)} %get-tuple-element.72), channel_id=1, source_target_pairs={{0,4},{4,0},{1,5},{5,1},{2,6},{6,2},{3,7},{7,3},{8,12},{12,8},{9,1... | collective-permute-start | bytes 3145736 | tf_op jit(solution)/shard_map/ppermute | solution.py:459

commit v9 on v6

--- a/solution.py
+++ b/solution.py
@@ -80,15 +80,10 @@
 TOKEN = jax.ShapeDtypeStruct((8, 128), jnp.float32)
 
 
-def block_shape(w_out, chunks):
-    return w_out.shape[0] // chunks, w_out.shape[1] // HALVES
-
-
-def block_copy(w_hbm, index, w_ref, sem):
+def block_copy(w_hbm, row, half, w_ref, sem):
     depth, columns = w_ref.shape
-    row, column = index // HALVES * depth, index % HALVES * columns
     return pltpu.make_async_copy(
-        w_hbm.at[row:row + depth, column:column + columns], w_ref, sem
+        w_hbm.at[row:row + depth, half * columns:(half + 1) * columns], w_ref, sem
     )
 
 
@@ -98,7 +93,7 @@
         pltpu.make_async_copy(k_hbm, k_ref, sems.at[1]),
         pltpu.make_async_copy(v_hbm, v_ref, sems.at[2]),
         pltpu.make_async_copy(q_hbm, q_ref, sems.at[3]),
-        block_copy(w_hbm, 0, w_ref, sems.at[4]),
+        block_copy(w_hbm, 0, 0, w_ref, sems.at[4]),
     ]
     lengths.start()
     for load in loads:
@@ -118,7 +113,7 @@
         load.wait()
 
 
-def prepare(doc_lengths, key_rows, value_rows, queries, w_out, chunks, after):
+def prepare(doc_lengths, key_rows, value_rows, queries, w_out, depth, after):
     rows = queries.shape[0]
     return pl.pallas_call(
         prepare_kernel,
@@ -127,7 +122,7 @@
             jax.ShapeDtypeStruct(value_rows.shape, jnp.bfloat16),
             jax.ShapeDtypeStruct(queries.shape, jnp.bfloat16),
             jax.ShapeDtypeStruct((rows, 3 * rows), jnp.float32),
-            jax.ShapeDtypeStruct(block_shape(w_out, chunks), jnp.bfloat16),
+            jax.ShapeDtypeStruct((depth, w_out.shape[1] // HALVES), jnp.bfloat16),
         ],
         in_specs=[HBM] * 6,
         out_specs=[VMEM] * 5,
@@ -137,7 +132,7 @@
         ],
         compiler_params=pltpu.CompilerParams(vmem_limit_bytes=4 * MIB),
         cost_estimate=pl.CostEstimate(
-            flops=0, bytes_accessed=w_out.size // chunks, transcendentals=0
+            flops=0, bytes_accessed=depth * w_out.shape[1], transcendentals=0
         ),
         name="prepare",
     )(
@@ -145,11 +140,11 @@
     )
 
 
-def load_kernel(indexes, after, w_hbm, *refs):
+def load_kernel(wanted, after, w_hbm, *refs):
     *w_refs, token, sems = refs
     loads = [
-        block_copy(w_hbm, index, w_ref, sems.at[i])
-        for i, (index, w_ref) in enumerate(zip(indexes, w_refs))
+        block_copy(w_hbm, row, half, w_ref, sems.at[i])
+        for i, ((row, depth, half), w_ref) in enumerate(zip(wanted, w_refs))
     ]
     for load in loads:
         load.start()
@@ -158,19 +153,23 @@
         load.wait()
 
 
-def load_blocks(indexes, w_out, chunks, after):
-    shape = block_shape(w_out, chunks)
+def load_blocks(wanted, w_out, after):
+    columns = w_out.shape[1] // HALVES
     *blocks, token = pl.pallas_call(
-        functools.partial(load_kernel, indexes),
-        out_shape=[jax.ShapeDtypeStruct(shape, jnp.bfloat16)] * len(indexes) + [TOKEN],
+        functools.partial(load_kernel, wanted),
+        out_shape=[
+            jax.ShapeDtypeStruct((depth, columns), jnp.bfloat16) for _, depth, _ in wanted
+        ] + [TOKEN],
         in_specs=[HBM, HBM],
-        out_specs=[VMEM] * (len(indexes) + 1),
-        scratch_shapes=[pltpu.SemaphoreType.DMA((len(indexes),))],
+        out_specs=[VMEM] * (len(wanted) + 1),
+        scratch_shapes=[pltpu.SemaphoreType.DMA((len(wanted),))],
         compiler_params=pltpu.CompilerParams(vmem_limit_bytes=1 * MIB),
         cost_estimate=pl.CostEstimate(
-            flops=0, bytes_accessed=4 * len(indexes) * shape[0] * shape[1], transcendentals=0
+            flops=0,
+            bytes_accessed=4 * columns * sum(depth for _, depth, _ in wanted),
+            transcendentals=0,
         ),
-        name=f"load_{indexes[0]}",
+        name=f"load_{wanted[0][0]}",
     )(after, w_out)
     return blocks, token
 
@@ -222,7 +221,7 @@
     )(queries, mask, *keys, *values, *after)
 
 
-def lay_out(plan, pieces, column, lhs):
+def lay_out(plan, pieces, lhs):
     here = lax.axis_index("ctx")
     core = lax.axis_index("tp")
     first = jnp.where(core == 0, 1, 2)
@@ -237,51 +236,48 @@
                 slot = jnp.where(wanted[s] == owner * 4 + u, s, slot)
             slot = slot ^ swap
             at = pl.ds(pl.multiple_of(slot * unit_rows, unit_rows), unit_rows)
-            lhs[at, :] = piece[u * unit_rows:(u + 1) * unit_rows, column:column + lhs.shape[1]]
-
-
-def step_kernel(index, last, column, first, columns, has_acc, has_after, has_load, *refs):
+            lhs[at, :] = piece[u * unit_rows:(u + 1) * unit_rows, :]
+
+
+def step_kernel(row, half, last, has_acc, has_after, has_load, *refs):
     refs = list(refs)[has_after:]
-    first_half = index % HALVES == 0
     load = None
     if has_load:
         sem = refs.pop()
     token = refs.pop()
     if has_load:
-        load = block_copy(refs.pop(0), index + 1, refs.pop(), sem)
+        load = block_copy(refs.pop(0), row, half + 1, refs.pop(), sem)
         load.start()
-    if first_half:
+    if half == 0:
         plan, *pieces = refs[:5]
         del refs[:5]
         lhs = refs.pop()
-        lay_out(plan, pieces, column, lhs)
+        lay_out(plan, pieces, lhs)
     else:
         lhs = refs.pop(0)
     token[...] = jnp.zeros_like(token)
     w_ref = refs.pop(0)
     acc_ref = refs.pop(0) if has_acc else None
     rows = lhs.shape[0] // 2
-    for start in range(0, columns, TILE):
-        to = slice(start, start + TILE)
-        at = slice(first + start, first + start + TILE)
+    for start in range(0, w_ref.shape[1], TILE):
+        at = slice(start, start + TILE)
         product = jnp.dot(lhs[...], w_ref[:, at], preferred_element_type=jnp.float32)
         if has_acc:
             product = product + acc_ref[:, at]
         if last:
             own_ref, sent_ref = refs
-            own_ref[:, to] = product[rows:]
-            sent_ref[:, to] = product[:rows].astype(jnp.bfloat16)
+            own_ref[:, at] = product[rows:]
+            sent_ref[:, at] = product[:rows].astype(jnp.bfloat16)
         else:
-            refs[0][:, to] = product
+            refs[0][:, at] = product
     if load is not None:
         load.wait()
 
 
-def step(index, last, rows_in, column, block, first, columns, w_out, acc, after):
-    first_half = index % HALVES == 0
+def step(row, half, last, rows_in, block, w_out, acc, after):
     has_acc, has_after, has_load = acc is not None, after is not None, w_out is not None
-    depth = block.shape[0]
-    if first_half:
+    depth, columns = block.shape
+    if half == 0:
         plan, pieces = rows_in
         total_rows = 4 * pieces[0].shape[0]
         operands, specs = [plan, *pieces], [SMEM] + [VMEM] * 4
@@ -293,7 +289,7 @@
         shapes = [jax.ShapeDtypeStruct(part, jnp.float32), jax.ShapeDtypeStruct(part, jnp.bfloat16)]
     else:
         shapes = [jax.ShapeDtypeStruct((total_rows, columns), jnp.float32)]
-    if first_half:
+    if half == 0:
         shapes.append(jax.ShapeDtypeStruct((total_rows, depth), jnp.bfloat16))
     if has_load:
         shapes.append(jax.ShapeDtypeStruct(block.shape, jnp.bfloat16))
@@ -301,9 +297,7 @@
     operands = [after] * has_after + [w_out] * has_load + operands + [block] + [acc] * has_acc
     specs = [HBM] * (has_after + has_load) + specs + [VMEM] * (1 + has_acc)
     results = list(pl.pallas_call(
-        functools.partial(
-            step_kernel, index, last, column, first, columns, has_acc, has_after, has_load
-        ),
+        functools.partial(step_kernel, row, half, last, has_acc, has_after, has_load),
         out_shape=shapes,
         in_specs=specs,
         out_specs=[VMEM] * len(shapes),
@@ -313,11 +307,11 @@
         cost_estimate=pl.CostEstimate(
             flops=2 * total_rows * depth * columns, bytes_accessed=0, transcendentals=0
         ),
-        name=f"step_{index}_{first // columns}",
+        name=f"step_{row}_{half}",
     )(*operands))
     token = results.pop()
     following = results.pop() if has_load else None
-    lhs = results.pop() if first_half else rows_in
+    lhs = results.pop() if half == 0 else rows_in
     return results, lhs, following, token
 
 
@@ -412,45 +406,43 @@
     value_near = lax.ppermute(value_rows, "ctx", [(0, 1), (2, 3)])
     value_far = lax.ppermute(value_two, "ctx", [(3, 2)])
     own_keys, own_values, held, mask, block = prepare(
-        doc_lengths, key_rows, value_rows, queries, w_out, kv_heads, value_two
+        doc_lengths, key_rows, value_rows, queries, w_out, width, value_two
     )
     keys = (own_keys, key_two, key_near, key_near)
     values = (own_values, value_near, value_far, value_two)
-    half_columns = w_out.shape[1] // HALVES
-    state = {"blocks": {0: block}, "totals": [None] * HALVES, "before": None}
+    state = {"blocks": {(0, 0): block}, "totals": [None] * HALVES, "before": None}
     rows, mine, got = {}, [], []
 
     def rows_of(groups, after):
         own = attend(groups, width, held, mask, keys, values, after)
-        near, side, forward = gather_rows(own)
+        _, _, forward = gather_rows(own)
 
         def arrive(after):
-            pieces = forward(after)
-            for i, g in enumerate(groups):
-                rows[g] = (pieces, i * width)
-            return pieces[1]
+            rows[groups] = forward(after)
+            return rows[groups]
 
         return own, arrive
 
     def load(wanted, after):
-        loaded, token = load_blocks(wanted, w_out, kv_heads, after)
-        state["blocks"].update(zip(wanted, loaded))
+        blocks, token = load_blocks(
+            [(groups[0] * width, len(groups) * width, half) for groups, half in wanted], w_out, after
+        )
+        for (groups, half), loaded in zip(wanted, blocks):
+            state["blocks"][groups[0], half] = loaded
         return token
 
-    def steps(g):
-        last = g == kv_heads - 1
-        pieces, column = rows[g]
-        loads = g * HALVES + 1 not in state["blocks"]
+    def steps(groups, between=None):
+        last = groups[-1] == kv_heads - 1
+        row = groups[0] * width
+        second_block = state["blocks"].get((groups[0], 1))
         first, lhs, following, state["before"] = step(
-            g * HALVES, last, (unit_source, pieces), column, state["blocks"][g * HALVES], 0,
-            half_columns,
-            w_out if loads else None, state["totals"][0], state["before"],
+            row, 0, last, (unit_source, rows[groups]), state["blocks"][groups[0], 0],
+            w_out if second_block is None else None, state["totals"][0], state["before"],
         )
-        if loads:
-            state["blocks"][g * HALVES + 1] = following
+        if between is not None:
+            between(state["before"])
         second, _, _, state["before"] = step(
-            g * HALVES + 1, last, lhs, column, state["blocks"][g * HALVES + 1], 0,
-            half_columns, None,
+            row, 1, last, lhs, following if second_block is None else second_block, None,
             state["totals"][1], state["before"],
         )
         if last:
@@ -461,14 +453,17 @@
             state["totals"] = [first[0], second[0]]
         return state["before"]
 
-    own, arrive = rows_of((0,), [])
-    near = arrive(None)
-    own, arrive = rows_of((1,), [load((1, 2), own)])
+    one, two, rest = (0,), (1,), (2, 3)
+    own, arrive = rows_of(one, [])
+    pieces = arrive(None)
+    own, arrive = rows_of(two, [load([(one, 1), (two, 0)], own)])
     arrive(None)
-    own, arrive = rows_of((2, 3), [load((4, 6), own), near])
-    arrive(steps(0))
-    for g in range(1, kv_heads):
-        steps(g)
+    token = load([(rest, 0)], own)
+    _, arrive = rows_of(rest, [token, pieces[3]])
+    steps(one)
+    steps(two, arrive)
+    steps(rest)
+    half_columns = w_out.shape[1] // HALVES
     out = total(0, w_out.shape[1], mine[:1], got[:1], None)
     return total(half_columns, w_out.shape[1], mine[1:], got[1:], out)
 

time: 70.9 us -> 73.3 us (1.034)
  waiting for transfers between devices: 8.71 us -> 14 us
  Pallas kernels: 38.4 us -> 36.5 us
  starting transfers between devices: 23.2 us -> 22.2 us
    ppermute x3, waiting for transfers between devices: 1.44 us -> 7.76 us  [forward(): return (own, first, side, lax.ppermute(first, ('ctx', 'tp'), route(False)))]
    ppermute x3, starting transfers between devices: 4.71 us -> 2.7 us  [gather_rows(): near = lax.ppermute(own, ('ctx', 'tp'), route(True))]
    pallas_call x10 -> x8, Pallas kernels: 30.8 us -> 28.9 us  [the longest x6 22.1 us: step(): pl.pallas_call(functools.partial(step_kernel, row, half, last, has_acc, h...]
    ppermute x3, starting transfers between devices: 2.57 us -> 3.73 us  [gather_rows(): side = lax.ppermute(own, ('ctx', 'tp'), route(False))]
    ppermute x3, waiting for transfers between devices: 6.05 us -> 5 us  [gather_rows(): near = lax.ppermute(own, ('ctx', 'tp'), route(True))]
  transfers between devices with their start and end apart: 16 -> 16, of which waited for: 4 -> 6; matrix products, arithmetic and copies ran while one was open for 0% -> 0% of each run, Pallas kernels for 38% -> 40%
where the time goes in v9:
time: 73.3 us; the launch traced here: 73.1 us
  Pallas kernels  36.5 us (50%)
  starting transfers between devices  22.2 us (30%)
  waiting for transfers between devices  14 us (19%)
    pallas_call x6, Pallas kernels, step(): pl.pallas_call(functools.partial(step_kernel, row, half, last, has_acc, h...  22.1 us
    ppermute x3, waiting for transfers between devices, forward(): return (own, first, side, lax.ppermute(first, ('ctx', 'tp'), route(False)))  7.76 us
    pallas_call x2, Pallas kernels, load_blocks(): pl.pallas_call(functools.partial(load_kernel, wanted), out_shape=[jax.Sha...  6.87 us
    ppermute x3, waiting for transfers between devices, gather_rows(): near = lax.ppermute(own, ('ctx', 'tp'), route(True))  5 us
    ppermute x1, starting transfers between devices, local(): value_two = lax.ppermute(value_rows, 'ctx', two)  4.87 us
    ppermute x3, starting transfers between devices, gather_rows(): side = lax.ppermute(own, ('ctx', 'tp'), route(False))  3.73 us
    ppermute x1, starting transfers between devices, local(): key_near = lax.ppermute(key_rows, 'ctx', [(0, 1), (1, 2), (2, 3)])  3.4 us
    ppermute x3, starting transfers between devices, forward(): return (own, first, side, lax.ppermute(first, ('ctx', 'tp'), route(False)))  3.05 us
  transfers between devices with their start and end apart: 16, of which 6 were waited for; matrix products, arithmetic and copies ran while one was open for 0% of the time, Pallas kernels for 40%

profile of v9, /device:TPU:0, one launch (start us, length us, event | category | flops | bytes accessed | tf_op | source)
XLA Modules:
  0.0 73.1 jit_solution(7537635905474954223)
XLA Ops:
  0.0 4.9 %collective-permute-start = (bf16[128,512]{1,0:T(8,128)(2,1)}, bf16[128,512]{1,0:T(8,128)(2,1)S(1)}, u32[]{:S(2)}, u32[]{:S(2)}) collective-permute-start(bf16[128,512]{1,0:T(8,128)(2,1)} %v_hbm.1), channel_id=1, source_target_pairs={{0,16},{8,24},{1,17},{9,25},{2,18},{10,26},{3,19},{11,27},{4,20},{... | collective-permute-start | bytes 393224 | tf_op jit(solution)/shard_map/ppermute | solution.py:403
  4.9 3.4 %collective-permute-start.2 = (bf16[128,512]{1,0:T(8,128)(2,1)}, bf16[128,512]{1,0:T(8,128)(2,1)S(1)}, u32[]{:S(2)}, u32[]{:S(2)}) collective-permute-start(bf16[128,512]{1,0:T(8,128)(2,1)} %k_hbm.1), channel_id=1, source_target_pairs={{0,8},{8,16},{16,24},{1,9},{9,17},{17,25},{2,10},{10,18},{18,26},{... | collective-permute-start | bytes 393224 | tf_op jit(solution)/shard_map/ppermute | solution.py:405
  8.3 1.3 %collective-permute-start.1 = (bf16[128,512]{1,0:T(8,128)(2,1)}, bf16[128,512]{1,0:T(8,128)(2,1)S(1)}, u32[]{:S(2)}, u32[]{:S(2)}) collective-permute-start(bf16[128,512]{1,0:T(8,128)(2,1)} %k_hbm.1), channel_id=1, source_target_pairs={{0,16},{8,24},{1,17},{9,25},{2,18},{10,26},{3,19},{11,27},{4,20},{... | collective-permute-start | bytes 393224 | tf_op jit(solution)/shard_map/ppermute | solution.py:404
  9.6 1.9 %collective-permute-start.3 = (bf16[128,512]{1,0:T(8,128)(2,1)}, bf16[128,512]{1,0:T(8,128)(2,1)S(1)}, u32[]{:S(2)}, u32[]{:S(2)}) collective-permute-start(bf16[128,512]{1,0:T(8,128)(2,1)} %v_hbm.1), channel_id=1, source_target_pairs={{0,8},{16,24},{1,9},{17,25},{2,10},{18,26},{3,11},{19,27},{4,12},{... | collective-permute-start | bytes 393224 | tf_op jit(solution)/shard_map/ppermute | solution.py:406
  12.2 2.7 %prepare.1 = (bf16[128,512]{1,0:T(8,128)(2,1)S(1)}, bf16[128,512]{1,0:T(8,128)(2,1)S(1)}, bf16[128,4096]{1,0:T(8,128)(2,1)S(1)}, f32[128,384]{1,0:T(8,128)S(1)}, bf16[1024,2048]{1,0:T(8,128)(2,1)S(1)}) custom-call(s32[8]{0:T(128)} %docs_hbm.1, bf16[128,512]{1,0:T(8,128)(2,1)} %k_hbm.1, bf16[128,512]{1,0:T(8,128)(2,1)} %v_hbm.1, bf16[128,4096]{1,0:T(8,128)(2,1)} %q_hbm.1, ...), custom_call_target="tpu_custom_call" | custom-call | bytes 4194304 | tf_op jit(solution)/shard_map/prepare/pallas_call | solution.py:118
  15.7 1.8 %collective-permute-start.5 = (bf16[128,1024]{1,0:T(8,128)(2,1)S(1)}, bf16[128,1024]{1,0:T(8,128)(2,1)S(1)}, u32[]{:S(2)}, u32[]{:S(2)}) collective-permute-start(bf16[128,1024]{1,0:T(8,128)(2,1)S(1)} %attend_0.1.refs_1_.after), channel_id=1, source_target_pairs={{0,8},{4,20},{8,0},{12,28},{16,24},{20,4},{24,16},{28,12},{1,9},{5... | collective-permute-start | bytes 786440 | tf_op jit(solution)/shard_map/ppermute | solution.py:386
  17.4 3.5 %load_0.1 = (bf16[1024,2048]{1,0:T(8,128)(2,1)S(1)}, bf16[1024,2048]{1,0:T(8,128)(2,1)S(1)}, f32[8,128]{1,0:T(8,128)S(1)}) custom-call(bf16[128,1024]{1,0:T(8,128)(2,1)S(1)} %attend_0.1.refs_1_.after, bf16[4096,4096]{1,0:T(8,128)(2,1)} %refs_1_.3), custom_call_target="tpu_custom_call" | custom-call | bytes 16777216 | tf_op jit(solution)/shard_map/load_0/pallas_call | solution.py:158
  22.1 2.2 %collective-permute-start.7 = (bf16[128,1024]{1,0:T(8,128)(2,1)S(1)}, bf16[128,1024]{1,0:T(8,128)(2,1)S(1)}, u32[]{:S(2)}, u32[]{:S(2)}) collective-permute-start(bf16[128,1024]{1,0:T(8,128)(2,1)S(1)} %collective-permute-done.5.refs_2_), channel_id=1, source_target_pairs={{0,16},{4,12},{8,24},{12,4},{16,0},{20,28},{24,8},{28,20},{1,17},{... | collective-permute-start | bytes 786440 | tf_op jit(solution)/shard_map/ppermute | solution.py:391
  24.3 2.0 %collective-permute-start.9 = (bf16[128,1024]{1,0:T(8,128)(2,1)S(1)}, bf16[128,1024]{1,0:T(8,128)(2,1)S(1)}, u32[]{:S(2)}, u32[]{:S(2)}) collective-permute-start(bf16[128,1024]{1,0:T(8,128)(2,1)S(1)} %attend_1.1.refs_3_.after), channel_id=1, source_target_pairs={{0,16},{4,12},{8,24},{12,4},{16,0},{20,28},{24,8},{28,20},{1,17},{... | collective-permute-start | bytes 786440 | tf_op jit(solution)/shard_map/ppermute | solution.py:387
  26.3 3.4 %load_2048.1 = (bf16[2048,2048]{1,0:T(8,128)(2,1)S(1)}, f32[8,128]{1,0:T(8,128)S(1)}) custom-call(bf16[128,1024]{1,0:T(8,128)(2,1)S(1)} %attend_1.1.refs_3_.after, bf16[4096,4096]{1,0:T(8,128)(2,1)} %refs_1_.3), custom_call_target="tpu_custom_call" | custom-call | bytes 16777216 | tf_op jit(solution)/shard_map/load_2048/pallas_call | solution.py:158
  29.7 1.2 %collective-permute-done.8.refs_4_ = bf16[128,1024]{1,0:T(8,128)(2,1)S(1)} collective-permute-done((bf16[128,1024]{1,0:T(8,128)(2,1)S(1)}, bf16[128,1024]{1,0:T(8,128)(2,1)S(1)}, u32[]{:S(2)}, u32[]{:S(2)}) %collective-permute-start.8) | collective-permute-done | bytes 262176 | tf_op jit(solution)/shard_map/ppermute | solution.py:386
  31.3 1.3 %attend_2.1.refs_3_ = bf16[128,2048]{1,0:T(8,128)(2,1)S(1)} custom-call(bf16[128,4096]{1,0:T(8,128)(2,1)S(1)} %get-tuple-element.33.q_ref, f32[128,384]{1,0:T(8,128)S(1)} %get-tuple-element.34.mask_ref, bf16[128,512]{1,0:T(8,128)(2,1)S(1)} %get-tuple-element.35.k0, bf16[128,512]{1,0:T(8,128)(2,1)S(1)} %collective-permute-done.1.k2, ...), custom_call_target="tpu_custom_call" | custom-call | tf_op jit(solution)/shard_map/attend_2/pallas_call | solution.py:213
  32.7 1.7 %collective-permute-start.12 = (bf16[128,2048]{1,0:T(8,128)(2,1)S(1)}, bf16[128,2048]{1,0:T(8,128)(2,1)S(1)}, u32[]{:S(2)}, u32[]{:S(2)}) collective-permute-start(bf16[128,2048]{1,0:T(8,128)(2,1)S(1)} %attend_2.1.refs_3_), channel_id=1, source_target_pairs={{0,16},{4,12},{8,24},{12,4},{16,0},{20,28},{24,8},{28,20},{1,17},{... | collective-permute-start | bytes 1572872 | tf_op jit(solution)/shard_map/ppermute | solution.py:387
  34.9 3.1 %step_0_0.1 = (f32[512,2048]{1,0:T(8,128)S(1)}, bf16[512,1024]{1,0:T(8,128)(2,1)S(1)}, f32[8,128]{1,0:T(8,128)S(1)}) custom-call(s32[16]{0:T(128)S(1)} %copy-done, bf16[128,1024]{1,0:T(8,128)(2,1)S(1)} %attend_0.1.refs_1_.after, bf16[128,1024]{1,0:T(8,128)(2,1)S(1)} %collective-permute-done.5.refs_2_, bf16[128,1024]{1,0:T(8,128)(2,1)S(1)} %collective-permute-done.6.refs_3_, ...), custom_call_target="tpu_custom_call" | custom-call | flops 2147483648 | tf_op jit(solution)/shard_map/step_0_0/pallas_call | solution.py:299
  38.0 2.4 %step_0_1.1 = (f32[512,2048]{1,0:T(8,128)S(1)}, f32[8,128]{1,0:T(8,128)S(1)}) custom-call(f32[8,128]{1,0:T(8,128)S(1)} %get-tuple-element.38.refs_0_, bf16[512,1024]{1,0:T(8,128)(2,1)S(1)} %get-tuple-element.39.refs_1_, bf16[1024,2048]{1,0:T(8,128)(2,1)S(1)} %get-tuple-element.40.refs_2_), custom_call_target="tpu_custom_call" | custom-call | flops 2147483648 | tf_op jit(solution)/shard_map/step_0_1/pallas_call | solution.py:299
  40.4 1.8 %collective-permute-done.10.refs_6_ = bf16[128,1024]{1,0:T(8,128)(2,1)S(1)} collective-permute-done((bf16[128,1024]{1,0:T(8,128)(2,1)S(1)}, bf16[128,1024]{1,0:T(8,128)(2,1)S(1)}, u32[]{:S(2)}, u32[]{:S(2)}) %collective-permute-start.10) | collective-permute-done | bytes 262176 | tf_op jit(solution)/shard_map/ppermute | solution.py:391
  42.2 3.4 %step_1024_0.1 = (f32[512,2048]{1,0:T(8,128)S(1)}, bf16[512,1024]{1,0:T(8,128)(2,1)S(1)}, bf16[1024,2048]{1,0:T(8,128)(2,1)S(1)}, f32[8,128]{1,0:T(8,128)S(1)}) custom-call(f32[8,128]{1,0:T(8,128)S(1)} %get-tuple-element.41.refs_0_, bf16[4096,4096]{1,0:T(8,128)(2,1)} %refs_1_.3, s32[16]{0:T(128)S(1)} %copy-done, ...), custom_call_target="tpu_custom_call", output_to_operand_aliasing={{0}: (8, {})} | custom-call | flops 2147483648 | tf_op jit(solution)/shard_map/step_1024_0/pallas_call | solution.py:299
  45.6 3.7 %collective-permute-done.11.x = bf16[128,2048]{1,0:T(8,128)(2,1)S(1)} collective-permute-done((bf16[128,2048]{1,0:T(8,128)(2,1)S(1)}, bf16[128,2048]{1,0:T(8,128)(2,1)S(1)}, u32[]{:S(2)}, u32[]{:S(2)}) %collective-permute-start.11) | collective-permute-done | bytes 524320 | tf_op jit(solution)/shard_map/ppermute | solution.py:386
  49.7 2.7 %step_1024_1.1 = (f32[512,2048]{1,0:T(8,128)S(1)}, f32[8,128]{1,0:T(8,128)S(1)}) custom-call(f32[8,128]{1,0:T(8,128)S(1)} %get-tuple-element.45.refs_0_.after, bf16[512,1024]{1,0:T(8,128)(2,1)S(1)} %get-tuple-element.46.refs_1_, bf16[1024,2048]{1,0:T(8,128)(2,1)S(1)} %get-tuple-element.47.refs_2_, ...), custom_call_target="tpu_custom_call", output_to_operand_aliasing={{0}: (3, {})} | custom-call | flops 2147483648 | tf_op jit(solution)/shard_map/step_1024_1/pallas_call | solution.py:299
  52.5 6.0 %collective-permute-done.13.refs_6_ = bf16[128,2048]{1,0:T(8,128)(2,1)S(1)} collective-permute-done((bf16[128,2048]{1,0:T(8,128)(2,1)S(1)}, bf16[128,2048]{1,0:T(8,128)(2,1)S(1)}, u32[]{:S(2)}, u32[]{:S(2)}) %collective-permute-start.13) | collective-permute-done | bytes 524320 | tf_op jit(solution)/shard_map/ppermute | solution.py:391
  58.4 5.5 %step_2048_0.1 = (f32[256,2048]{1,0:T(8,128)S(1)}, bf16[256,2048]{1,0:T(8,128)(2,1)S(1)}, bf16[512,2048]{1,0:T(8,128)(2,1)S(1)}, bf16[2048,2048]{1,0:T(8,128)(2,1)S(1)}, f32[8,128]{1,0:T(8,128)S(1)}) custom-call(f32[8,128]{1,0:T(8,128)S(1)} %get-tuple-element.49.refs_0_, bf16[4096,4096]{1,0:T(8,128)(2,1)} %refs_1_.3, s32[16]{0:T(128)S(1)} %copy-done, ...), custom_call_target="tpu_custom_call" | custom-call | flops 4294967296 | tf_op jit(solution)/shard_map/step_2048_0/pallas_call | solution.py:299
  64.0 5.1 %step_2048_1.1 = (f32[256,2048]{1,0:T(8,128)S(1)}, bf16[256,2048]{1,0:T(8,128)(2,1)S(1)}, f32[8,128]{1,0:T(8,128)}) custom-call(f32[8,128]{1,0:T(8,128)S(1)} %get-tuple-element.53.refs_0_, bf16[512,2048]{1,0:T(8,128)(2,1)S(1)} %get-tuple-element.54.refs_1_, bf16[2048,2048]{1,0:T(8,128)(2,1)S(1)} %get-tuple-element.55.refs_2_, ...), custom_call_target="tpu_custom_call" | custom-call | flops 4294967296 | tf_op jit(solution)/shard_map/step_2048_1/pallas_call | solution.py:299
  70.6 1.2 %collective-permute-done.14.refs_1_ = bf16[256,2048]{1,0:T(8,128)(2,1)S(1)} collective-permute-done((bf16[256,2048]{1,0:T(8,128)(2,1)S(1)}, bf16[256,2048]{1,0:T(8,128)(2,1)S(1)}, u32[]{:S(2)}, u32[]{:S(2)}) %collective-permute-start.14) | collective-permute-done | bytes 1048608 | tf_op jit(solution)/shard_map/ppermute | solution.py:451
  71.8 1.1 %total_2048.1 = bf16[256,4096]{1,0:T(8,128)(2,1)} custom-call(f32[256,2048]{1,0:T(8,128)S(1)} %get-tuple-element.57.refs_0_, bf16[256,2048]{1,0:T(8,128)(2,1)S(1)} %collective-permute-done.14.refs_1_, bf16[256,4096]{1,0:T(8,128)(2,1)} %total_0.1.refs_2_), custom_call_target="tpu_custom_call", output_to_operand_aliasing={{}: (2, {})} | custom-call | flops 524288 | bytes 1048576 | tf_op jit(solution)/shard_map/total_2048/pallas_call | solution.py:342
  (25 shorter events, 5.6 us)
Async XLA Ops:
  0.0 11.5 %collective-permute-start = (bf16[128,512]{1,0:T(8,128)(2,1)}, bf16[128,512]{1,0:T(8,128)(2,1)S(1)}, u32[]{:S(2)}, u32[]{:S(2)}) collective-permute-start(bf16[128,512]{1,0:T(8,128)(2,1)} %v_hbm.1), channel_id=1, source_target_pairs={{0,16},{8,24},{1,17},{9,25},{2,18},{10,26},{3,19},{11,27},{4,20},{... | collective-permute-start | bytes 393224 | tf_op jit(solution)/shard_map/ppermute | solution.py:403
  4.9 10.0 %collective-permute-start.2 = (bf16[128,512]{1,0:T(8,128)(2,1)}, bf16[128,512]{1,0:T(8,128)(2,1)S(1)}, u32[]{:S(2)}, u32[]{:S(2)}) collective-permute-start(bf16[128,512]{1,0:T(8,128)(2,1)} %k_hbm.1), channel_id=1, source_target_pairs={{0,8},{8,16},{16,24},{1,9},{9,17},{17,25},{2,10},{10,18},{18,26},{... | collective-permute-start | bytes 393224 | tf_op jit(solution)/shard_map/ppermute | solution.py:405
  8.3 6.6 %collective-permute-start.1 = (bf16[128,512]{1,0:T(8,128)(2,1)}, bf16[128,512]{1,0:T(8,128)(2,1)S(1)}, u32[]{:S(2)}, u32[]{:S(2)}) collective-permute-start(bf16[128,512]{1,0:T(8,128)(2,1)} %k_hbm.1), channel_id=1, source_target_pairs={{0,16},{8,24},{1,17},{9,25},{2,18},{10,26},{3,19},{11,27},{4,20},{... | collective-permute-start | bytes 393224 | tf_op jit(solution)/shard_map/ppermute | solution.py:404
  9.6 5.4 %collective-permute-start.3 = (bf16[128,512]{1,0:T(8,128)(2,1)}, bf16[128,512]{1,0:T(8,128)(2,1)S(1)}, u32[]{:S(2)}, u32[]{:S(2)}) collective-permute-start(bf16[128,512]{1,0:T(8,128)(2,1)} %v_hbm.1), channel_id=1, source_target_pairs={{0,8},{16,24},{1,9},{17,25},{2,10},{18,26},{3,11},{19,27},{4,12},{... | collective-permute-start | bytes 393224 | tf_op jit(solution)/shard_map/ppermute | solution.py:406
  11.5 3.4 %collective-permute-start.4 = (bf16[128,512]{1,0:T(8,128)(2,1)S(1)}, bf16[128,512]{1,0:T(8,128)(2,1)S(1)}, u32[]{:S(2)}, u32[]{:S(2)}) collective-permute-start(bf16[128,512]{1,0:T(8,128)(2,1)S(1)} %collective-permute-done.after.v2), channel_id=1, source_target_pairs={{24,16},{25,17},{26,18},{27,19},{28,20},{29,21},{30,22},{31,23}} | collective-permute-start | bytes 393224 | tf_op jit(solution)/shard_map/ppermute | solution.py:407
  15.7 6.4 %collective-permute-start.5 = (bf16[128,1024]{1,0:T(8,128)(2,1)S(1)}, bf16[128,1024]{1,0:T(8,128)(2,1)S(1)}, u32[]{:S(2)}, u32[]{:S(2)}) collective-permute-start(bf16[128,1024]{1,0:T(8,128)(2,1)S(1)} %attend_0.1.refs_1_.after), channel_id=1, source_target_pairs={{0,8},{4,20},{8,0},{12,28},{16,24},{20,4},{24,16},{28,12},{1,9},{5... | collective-permute-start | bytes 786440 | tf_op jit(solution)/shard_map/ppermute | solution.py:386
  21.6 13.3 %copy-start = (s32[16]{0:T(128)S(1)}, s32[16]{0:T(128)}, u32[]{:S(2)}) copy-start(s32[16]{0:T(128)} %refs_2_.3) | copy-start | bytes 196
  21.6 9.3 %collective-permute-start.8 = (bf16[128,1024]{1,0:T(8,128)(2,1)S(1)}, bf16[128,1024]{1,0:T(8,128)(2,1)S(1)}, u32[]{:S(2)}, u32[]{:S(2)}) collective-permute-start(bf16[128,1024]{1,0:T(8,128)(2,1)S(1)} %attend_1.1.refs_3_.after), channel_id=1, source_target_pairs={{0,8},{4,20},{8,0},{12,28},{16,24},{20,4},{24,16},{28,12},{1,9},{5... | collective-permute-start | bytes 786440 | tf_op jit(solution)/shard_map/ppermute | solution.py:386
  22.1 9.2 %collective-permute-start.7 = (bf16[128,1024]{1,0:T(8,128)(2,1)S(1)}, bf16[128,1024]{1,0:T(8,128)(2,1)S(1)}, u32[]{:S(2)}, u32[]{:S(2)}) collective-permute-start(bf16[128,1024]{1,0:T(8,128)(2,1)S(1)} %collective-permute-done.5.refs_2_), channel_id=1, source_target_pairs={{0,16},{4,12},{8,24},{12,4},{16,0},{20,28},{24,8},{28,20},{1,17},{... | collective-permute-start | bytes 786440 | tf_op jit(solution)/shard_map/ppermute | solution.py:391
  24.3 10.7 %collective-permute-start.6 = (bf16[128,1024]{1,0:T(8,128)(2,1)S(1)}, bf16[128,1024]{1,0:T(8,128)(2,1)S(1)}, u32[]{:S(2)}, u32[]{:S(2)}) collective-permute-start(bf16[128,1024]{1,0:T(8,128)(2,1)S(1)} %attend_0.1.refs_1_.after), channel_id=1, source_target_pairs={{0,16},{4,12},{8,24},{12,4},{16,0},{20,28},{24,8},{28,20},{1,17},{... | collective-permute-start | bytes 786440 | tf_op jit(solution)/shard_map/ppermute | solution.py:387
  24.3 16.1 %collective-permute-start.9 = (bf16[128,1024]{1,0:T(8,128)(2,1)S(1)}, bf16[128,1024]{1,0:T(8,128)(2,1)S(1)}, u32[]{:S(2)}, u32[]{:S(2)}) collective-permute-start(bf16[128,1024]{1,0:T(8,128)(2,1)S(1)} %attend_1.1.refs_3_.after), channel_id=1, source_target_pairs={{0,16},{4,12},{8,24},{12,4},{16,0},{20,28},{24,8},{28,20},{1,17},{... | collective-permute-start | bytes 786440 | tf_op jit(solution)/shard_map/ppermute | solution.py:387
  30.9 11.2 %collective-permute-start.10 = (bf16[128,1024]{1,0:T(8,128)(2,1)S(1)}, bf16[128,1024]{1,0:T(8,128)(2,1)S(1)}, u32[]{:S(2)}, u32[]{:S(2)}) collective-permute-start(bf16[128,1024]{1,0:T(8,128)(2,1)S(1)} %collective-permute-done.8.refs_4_), channel_id=1, source_target_pairs={{0,16},{4,12},{8,24},{12,4},{16,0},{20,28},{24,8},{28,20},{1,17},{... | collective-permute-start | bytes 786440 | tf_op jit(solution)/shard_map/ppermute | solution.py:391
  32.7 19.8 %collective-permute-start.12 = (bf16[128,2048]{1,0:T(8,128)(2,1)S(1)}, bf16[128,2048]{1,0:T(8,128)(2,1)S(1)}, u32[]{:S(2)}, u32[]{:S(2)}) collective-permute-start(bf16[128,2048]{1,0:T(8,128)(2,1)S(1)} %attend_2.1.refs_3_), channel_id=1, source_target_pairs={{0,16},{4,12},{8,24},{12,4},{16,0},{20,28},{24,8},{28,20},{1,17},{... | collective-permute-start | bytes 1572872 | tf_op jit(solution)/shard_map/ppermute | solution.py:387
  34.4 14.9 %collective-permute-start.11 = (bf16[128,2048]{1,0:T(8,128)(2,1)S(1)}, bf16[128,2048]{1,0:T(8,128)(2,1)S(1)}, u32[]{:S(2)}, u32[]{:S(2)}) collective-permute-start(bf16[128,2048]{1,0:T(8,128)(2,1)S(1)} %attend_2.1.refs_3_), channel_id=1, source_target_pairs={{0,8},{4,20},{8,0},{12,28},{16,24},{20,4},{24,16},{28,12},{1,9},{5... | collective-permute-start | bytes 1572872 | tf_op jit(solution)/shard_map/ppermute | solution.py:386
  49.3 9.2 %collective-permute-start.13 = (bf16[128,2048]{1,0:T(8,128)(2,1)S(1)}, bf16[128,2048]{1,0:T(8,128)(2,1)S(1)}, u32[]{:S(2)}, u32[]{:S(2)}) collective-permute-start(bf16[128,2048]{1,0:T(8,128)(2,1)S(1)} %gate.1.refs_4_), channel_id=1, source_target_pairs={{0,16},{4,12},{8,24},{12,4},{16,0},{20,28},{24,8},{28,20},{1,17},{... | collective-permute-start | bytes 1572872 | tf_op jit(solution)/shard_map/ppermute | solution.py:391
  63.9 5.6 %collective-permute-start.15 = (bf16[256,2048]{1,0:T(8,128)(2,1)S(1)}, bf16[256,2048]{1,0:T(8,128)(2,1)S(1)}, u32[]{:S(2)}, u32[]{:S(2)}) collective-permute-start(bf16[256,2048]{1,0:T(8,128)(2,1)S(1)} %get-tuple-element.60), channel_id=1, source_target_pairs={{0,4},{4,0},{1,5},{5,1},{2,6},{6,2},{3,7},{7,3},{8,12},{12,8},{9,1... | collective-permute-start | bytes 3145736 | tf_op jit(solution)/shard_map/ppermute | solution.py:451
  69.0 2.8 %collective-permute-start.14 = (bf16[256,2048]{1,0:T(8,128)(2,1)S(1)}, bf16[256,2048]{1,0:T(8,128)(2,1)S(1)}, u32[]{:S(2)}, u32[]{:S(2)}) collective-permute-start(bf16[256,2048]{1,0:T(8,128)(2,1)S(1)} %get-tuple-element.58), channel_id=1, source_target_pairs={{0,4},{4,0},{1,5},{5,1},{2,6},{6,2},{3,7},{7,3},{8,12},{12,8},{9,1... | collective-permute-start | bytes 3145736 | tf_op jit(solution)/shard_map/ppermute | solution.py:451

commit v10 on v9

--- a/solution.py
+++ b/solution.py
@@ -174,7 +174,7 @@
     return blocks, token
 
 
-def attend_kernel(groups, q_ref, mask_ref, k0, k2, k_near, k_far, v0, v_near, v_far, v2, *rest):
+def attend_kernel(groups, q_ref, mask_ref, k0, k_near, k_far, k2, v0, v_near, v_far, v2, *rest):
     out_ref = rest[-1]
     rows = out_ref.shape[0]
     width = out_ref.shape[1] // len(groups)
@@ -221,7 +221,7 @@
     )(queries, mask, *keys, *values, *after)
 
 
-def lay_out(plan, pieces, lhs):
+def lay_out(plan, pieces, column, lhs):
     here = lax.axis_index("ctx")
     core = lax.axis_index("tp")
     first = jnp.where(core == 0, 1, 2)
@@ -236,10 +236,10 @@
                 slot = jnp.where(wanted[s] == owner * 4 + u, s, slot)
             slot = slot ^ swap
             at = pl.ds(pl.multiple_of(slot * unit_rows, unit_rows), unit_rows)
-            lhs[at, :] = piece[u * unit_rows:(u + 1) * unit_rows, :]
-
-
-def step_kernel(row, half, last, has_acc, has_after, has_load, *refs):
+            lhs[at, column:column + piece.shape[1]] = piece[u * unit_rows:(u + 1) * unit_rows, :]
+
+
+def step_kernel(row, half, last, pieces_in, has_acc, has_after, has_load, *refs):
     refs = list(refs)[has_after:]
     load = None
     if has_load:
@@ -249,10 +249,12 @@
         load = block_copy(refs.pop(0), row, half + 1, refs.pop(), sem)
         load.start()
     if half == 0:
-        plan, *pieces = refs[:5]
-        del refs[:5]
+        plan, *pieces = refs[:1 + pieces_in]
+        del refs[:1 + pieces_in]
         lhs = refs.pop()
-        lay_out(plan, pieces, lhs)
+        width = pieces[0].shape[1]
+        for i in range(0, pieces_in, 4):
+            lay_out(plan, pieces[i:i + 4], i // 4 * width, lhs)
     else:
         lhs = refs.pop(0)
     token[...] = jnp.zeros_like(token)
@@ -275,13 +277,15 @@
 
 
 def step(row, half, last, rows_in, block, w_out, acc, after):
-    has_acc, has_after, has_load = acc is not None, after is not None, w_out is not None
+    has_acc, has_after, has_load = acc is not None, len(after), w_out is not None
     depth, columns = block.shape
     if half == 0:
         plan, pieces = rows_in
+        pieces_in = len(pieces)
         total_rows = 4 * pieces[0].shape[0]
-        operands, specs = [plan, *pieces], [SMEM] + [VMEM] * 4
+        operands, specs = [plan, *pieces], [SMEM] + [VMEM] * pieces_in
     else:
+        pieces_in = 0
         total_rows = rows_in.shape[0]
         operands, specs = [rows_in], [VMEM]
     if last:
@@ -294,10 +298,10 @@
     if has_load:
         shapes.append(jax.ShapeDtypeStruct(block.shape, jnp.bfloat16))
     shapes.append(TOKEN)
-    operands = [after] * has_after + [w_out] * has_load + operands + [block] + [acc] * has_acc
+    operands = [*after] + [w_out] * has_load + operands + [block] + [acc] * has_acc
     specs = [HBM] * (has_after + has_load) + specs + [VMEM] * (1 + has_acc)
     results = list(pl.pallas_call(
-        functools.partial(step_kernel, row, half, last, has_acc, has_after, has_load),
+        functools.partial(step_kernel, row, half, last, pieces_in, has_acc, has_after, has_load),
         out_shape=shapes,
         in_specs=specs,
         out_specs=[VMEM] * len(shapes),
@@ -408,9 +412,9 @@
     own_keys, own_values, held, mask, block = prepare(
         doc_lengths, key_rows, value_rows, queries, w_out, width, value_two
     )
-    keys = (own_keys, key_two, key_near, key_near)
+    keys = (own_keys, key_near, key_near, key_two)
     values = (own_values, value_near, value_far, value_two)
-    state = {"blocks": {(0, 0): block}, "totals": [None] * HALVES, "before": None}
+    state = {"blocks": {(0, 0): block}, "totals": [None] * HALVES, "before": []}
     rows, mine, got = {}, [], []
 
     def rows_of(groups, after):
@@ -435,33 +439,37 @@
         last = groups[-1] == kv_heads - 1
         row = groups[0] * width
         second_block = state["blocks"].get((groups[0], 1))
-        first, lhs, following, state["before"] = step(
+        first, lhs, following, token = step(
             row, 0, last, (unit_source, rows[groups]), state["blocks"][groups[0], 0],
             w_out if second_block is None else None, state["totals"][0], state["before"],
         )
         if between is not None:
-            between(state["before"])
-        second, _, _, state["before"] = step(
+            between(token)
+        second, _, _, token = step(
             row, 1, last, lhs, following if second_block is None else second_block, None,
-            state["totals"][1], state["before"],
+            state["totals"][1], [token],
         )
+        state["before"] = [token]
         if last:
             for kept, sent in (first, second):
                 mine.append(kept)
                 got.append(lax.ppermute(sent, "tp", [(0, 1), (1, 0)]))
         else:
             state["totals"] = [first[0], second[0]]
-        return state["before"]
-
-    one, two, rest = (0,), (1,), (2, 3)
+        return token
+
+    one, two, three, four = (0,), (1,), (2,), (3,)
+    rest = three + four
     own, arrive = rows_of(one, [])
     pieces = arrive(None)
     own, arrive = rows_of(two, [load([(one, 1), (two, 0)], own)])
     arrive(None)
-    token = load([(rest, 0)], own)
-    _, arrive = rows_of(rest, [token, pieces[3]])
-    steps(one)
+    own, arrive = rows_of(three, [load([(rest, 0)], own), pieces[1]])
+    side = arrive(None)[2]
+    _, arrive = rows_of(four, [own, steps(one)])
+    state["before"].append(side)
     steps(two, arrive)
+    rows[rest] = rows[three] + rows[four]
     steps(rest)
     half_columns = w_out.shape[1] // HALVES
     out = total(0, w_out.shape[1], mine[:1], got[:1], None)

time: 73.3 us -> 70.8 us (0.966)
  waiting for transfers between devices: 14 us -> 6.43 us
  starting transfers between devices: 22.2 us -> 26.9 us
    ppermute x3 -> x4, waiting for transfers between devices: 5 us -> 0.01 us  [gather_rows(): near = lax.ppermute(own, ('ctx', 'tp'), route(True))]
    ppermute x3 -> x4, starting transfers between devices: 2.7 us -> 6.52 us  [gather_rows(): near = lax.ppermute(own, ('ctx', 'tp'), route(True))]
    ppermute x3 -> x4, waiting for transfers between devices: 7.76 us -> 5.19 us  [forward(): return (own, first, side, lax.ppermute(first, ('ctx', 'tp'), route(False)))]
    ppermute x3 -> x4, starting transfers between devices: 3.05 us -> 4.48 us  [forward(): return (own, first, side, lax.ppermute(first, ('ctx', 'tp'), route(False)))]
    ppermute x3 -> x4, starting transfers between devices: 3.73 us -> 3.21 us  [gather_rows(): side = lax.ppermute(own, ('ctx', 'tp'), route(False))]
    pallas_call x3 -> x4, Pallas kernels: 2.72 us -> 2.79 us  [attend(): pl.pallas_call(functools.partial(attend_kernel, groups), out_shape=jax.Sh...]
  transfers between devices with their start and end apart: 16 -> 19, of which waited for: 6 -> 3; matrix products, arithmetic and copies ran while one was open for 0% -> 0% of each run, Pallas kernels for 40% -> 42%
where the time goes in v10:
time: 70.8 us; the launch traced here: 70.5 us
  Pallas kernels  36.8 us (52%)
  starting transfers between devices  26.9 us (38%)
  waiting for transfers between devices  6.43 us (9%)
    pallas_call x6, Pallas kernels, step(): pl.pallas_call(functools.partial(step_kernel, row, half, last, pieces_in,...  22.2 us
    pallas_call x2, Pallas kernels, load_blocks(): pl.pallas_call(functools.partial(load_kernel, wanted), out_shape=[jax.Sha...  6.87 us
    ppermute x4, starting transfers between devices, gather_rows(): near = lax.ppermute(own, ('ctx', 'tp'), route(True))  6.52 us
    ppermute x4, waiting for transfers between devices, forward(): return (own, first, side, lax.ppermute(first, ('ctx', 'tp'), route(False)))  5.19 us
    ppermute x1, starting transfers between devices, local(): value_two = lax.ppermute(value_rows, 'ctx', two)  4.87 us
    ppermute x4, starting transfers between devices, forward(): return (own, first, side, lax.ppermute(first, ('ctx', 'tp'), route(False)))  4.48 us
    ppermute x1, starting transfers between devices, local(): key_near = lax.ppermute(key_rows, 'ctx', [(0, 1), (1, 2), (2, 3)])  3.4 us
    ppermute x4, starting transfers between devices, gather_rows(): side = lax.ppermute(own, ('ctx', 'tp'), route(False))  3.21 us
  transfers between devices with their start and end apart: 19, of which 3 were waited for; matrix products, arithmetic and copies ran while one was open for 0% of the time, Pallas kernels for 42%

profile of v10, /device:TPU:0, one launch (start us, length us, event | category | flops | bytes accessed | tf_op | source)
XLA Modules:
  0.0 70.5 jit_solution(1474870940577570739)
XLA Ops:
  0.0 4.9 %collective-permute-start = (bf16[128,512]{1,0:T(8,128)(2,1)}, bf16[128,512]{1,0:T(8,128)(2,1)S(1)}, u32[]{:S(2)}, u32[]{:S(2)}) collective-permute-start(bf16[128,512]{1,0:T(8,128)(2,1)} %v_hbm.1), channel_id=1, source_target_pairs={{0,16},{8,24},{1,17},{9,25},{2,18},{10,26},{3,19},{11,27},{4,20},{... | collective-permute-start | bytes 393224 | tf_op jit(solution)/shard_map/ppermute | solution.py:407
  4.9 3.4 %collective-permute-start.1 = (bf16[128,512]{1,0:T(8,128)(2,1)}, bf16[128,512]{1,0:T(8,128)(2,1)S(1)}, u32[]{:S(2)}, u32[]{:S(2)}) collective-permute-start(bf16[128,512]{1,0:T(8,128)(2,1)} %k_hbm.1), channel_id=1, source_target_pairs={{0,8},{8,16},{16,24},{1,9},{9,17},{17,25},{2,10},{10,18},{18,26},{... | collective-permute-start | bytes 393224 | tf_op jit(solution)/shard_map/ppermute | solution.py:409
  8.3 1.3 %collective-permute-start.2 = (bf16[128,512]{1,0:T(8,128)(2,1)}, bf16[128,512]{1,0:T(8,128)(2,1)S(1)}, u32[]{:S(2)}, u32[]{:S(2)}) collective-permute-start(bf16[128,512]{1,0:T(8,128)(2,1)} %k_hbm.1), channel_id=1, source_target_pairs={{0,16},{8,24},{1,17},{9,25},{2,18},{10,26},{3,19},{11,27},{4,20},{... | collective-permute-start | bytes 393224 | tf_op jit(solution)/shard_map/ppermute | solution.py:408
  9.6 1.9 %collective-permute-start.3 = (bf16[128,512]{1,0:T(8,128)(2,1)}, bf16[128,512]{1,0:T(8,128)(2,1)S(1)}, u32[]{:S(2)}, u32[]{:S(2)}) collective-permute-start(bf16[128,512]{1,0:T(8,128)(2,1)} %v_hbm.1), channel_id=1, source_target_pairs={{0,8},{16,24},{1,9},{17,25},{2,10},{18,26},{3,11},{19,27},{4,12},{... | collective-permute-start | bytes 393224 | tf_op jit(solution)/shard_map/ppermute | solution.py:410
  12.2 2.7 %prepare.1 = (bf16[128,512]{1,0:T(8,128)(2,1)S(1)}, bf16[128,512]{1,0:T(8,128)(2,1)S(1)}, bf16[128,4096]{1,0:T(8,128)(2,1)S(1)}, f32[128,384]{1,0:T(8,128)S(1)}, bf16[1024,2048]{1,0:T(8,128)(2,1)S(1)}) custom-call(s32[8]{0:T(128)} %docs_hbm.1, bf16[128,512]{1,0:T(8,128)(2,1)} %k_hbm.1, bf16[128,512]{1,0:T(8,128)(2,1)} %v_hbm.1, bf16[128,4096]{1,0:T(8,128)(2,1)} %q_hbm.1, ...), custom_call_target="tpu_custom_call" | custom-call | bytes 4194304 | tf_op jit(solution)/shard_map/prepare/pallas_call | solution.py:118
  15.7 1.8 %collective-permute-start.5 = (bf16[128,1024]{1,0:T(8,128)(2,1)S(1)}, bf16[128,1024]{1,0:T(8,128)(2,1)S(1)}, u32[]{:S(2)}, u32[]{:S(2)}) collective-permute-start(bf16[128,1024]{1,0:T(8,128)(2,1)S(1)} %attend_0.1.refs_1_.after), channel_id=1, source_target_pairs={{0,8},{4,20},{8,0},{12,28},{16,24},{20,4},{24,16},{28,12},{1,9},{5... | collective-permute-start | bytes 786440 | tf_op jit(solution)/shard_map/ppermute | solution.py:390
  17.4 3.5 %load_0.1 = (bf16[1024,2048]{1,0:T(8,128)(2,1)S(1)}, bf16[1024,2048]{1,0:T(8,128)(2,1)S(1)}, f32[8,128]{1,0:T(8,128)S(1)}) custom-call(bf16[128,1024]{1,0:T(8,128)(2,1)S(1)} %attend_0.1.refs_1_.after, bf16[4096,4096]{1,0:T(8,128)(2,1)} %refs_1_.1), custom_call_target="tpu_custom_call" | custom-call | bytes 16777216 | tf_op jit(solution)/shard_map/load_0/pallas_call | solution.py:158
  22.2 2.1 %collective-permute-start.9 = (bf16[128,1024]{1,0:T(8,128)(2,1)S(1)}, bf16[128,1024]{1,0:T(8,128)(2,1)S(1)}, u32[]{:S(2)}, u32[]{:S(2)}) collective-permute-start(bf16[128,1024]{1,0:T(8,128)(2,1)S(1)} %attend_1.1.after.refs_4_), channel_id=1, source_target_pairs={{0,8},{4,20},{8,0},{12,28},{16,24},{20,4},{24,16},{28,12},{1,9},{5... | collective-permute-start | bytes 786440 | tf_op jit(solution)/shard_map/ppermute | solution.py:390
  24.3 1.3 %collective-permute-start.7 = (bf16[128,1024]{1,0:T(8,128)(2,1)S(1)}, bf16[128,1024]{1,0:T(8,128)(2,1)S(1)}, u32[]{:S(2)}, u32[]{:S(2)}) collective-permute-start(bf16[128,1024]{1,0:T(8,128)(2,1)S(1)} %collective-permute-done.5.refs_2_.rest_1_), channel_id=1, source_target_pairs={{0,16},{4,12},{8,24},{12,4},{16,0},{20,28},{24,8},{28,20},{1,17},{... | collective-permute-start | bytes 786440 | tf_op jit(solution)/shard_map/ppermute | solution.py:395
  25.6 3.4 %load_2048.1 = (bf16[2048,2048]{1,0:T(8,128)(2,1)S(1)}, f32[8,128]{1,0:T(8,128)S(1)}) custom-call(bf16[128,1024]{1,0:T(8,128)(2,1)S(1)} %attend_1.1.after.refs_4_, bf16[4096,4096]{1,0:T(8,128)(2,1)} %refs_1_.1), custom_call_target="tpu_custom_call" | custom-call | bytes 16777216 | tf_op jit(solution)/shard_map/load_2048/pallas_call | solution.py:158
  30.5 1.4 %collective-permute-start.8 = (bf16[128,1024]{1,0:T(8,128)(2,1)S(1)}, bf16[128,1024]{1,0:T(8,128)(2,1)S(1)}, u32[]{:S(2)}, u32[]{:S(2)}) collective-permute-start(bf16[128,1024]{1,0:T(8,128)(2,1)S(1)} %attend_2.1.rest_0_.refs_3_), channel_id=1, source_target_pairs={{0,16},{4,12},{8,24},{12,4},{16,0},{20,28},{24,8},{28,20},{1,17},{... | collective-permute-start | bytes 786440 | tf_op jit(solution)/shard_map/ppermute | solution.py:391
  33.1 3.1 %step_0_0.1 = (f32[512,2048]{1,0:T(8,128)S(1)}, bf16[512,1024]{1,0:T(8,128)(2,1)S(1)}, f32[8,128]{1,0:T(8,128)S(1)}) custom-call(s32[16]{0:T(128)S(1)} %copy-done, bf16[128,1024]{1,0:T(8,128)(2,1)S(1)} %attend_0.1.refs_1_.after, bf16[128,1024]{1,0:T(8,128)(2,1)S(1)} %collective-permute-done.5.refs_2_.rest_1_, ...), custom_call_target="tpu_custom_call" | custom-call | flops 2147483648 | tf_op jit(solution)/shard_map/step_0_0/pallas_call | solution.py:303
  36.1 2.4 %step_0_1.1 = (f32[512,2048]{1,0:T(8,128)S(1)}, f32[8,128]{1,0:T(8,128)S(1)}) custom-call(f32[8,128]{1,0:T(8,128)S(1)} %get-tuple-element.38.refs_0_, bf16[512,1024]{1,0:T(8,128)(2,1)S(1)} %get-tuple-element.39.refs_1_, bf16[1024,2048]{1,0:T(8,128)(2,1)S(1)} %get-tuple-element.40.refs_2_), custom_call_target="tpu_custom_call" | custom-call | flops 2147483648 | tf_op jit(solution)/shard_map/step_0_1/pallas_call | solution.py:303
  39.2 2.4 %collective-permute-start.14 = (bf16[128,1024]{1,0:T(8,128)(2,1)S(1)}, bf16[128,1024]{1,0:T(8,128)(2,1)S(1)}, u32[]{:S(2)}, u32[]{:S(2)}) collective-permute-start(bf16[128,1024]{1,0:T(8,128)(2,1)S(1)} %attend_3.1.refs_7_), channel_id=1, source_target_pairs={{0,8},{4,20},{8,0},{12,28},{16,24},{20,4},{24,16},{28,12},{1,9},{5... | collective-permute-start | bytes 786440 | tf_op jit(solution)/shard_map/ppermute | solution.py:390
  42.2 1.5 %collective-permute-start.13 = (bf16[128,1024]{1,0:T(8,128)(2,1)S(1)}, bf16[128,1024]{1,0:T(8,128)(2,1)S(1)}, u32[]{:S(2)}, u32[]{:S(2)}) collective-permute-start(bf16[128,1024]{1,0:T(8,128)(2,1)S(1)} %collective-permute-done.12.refs_4_), channel_id=1, source_target_pairs={{0,16},{4,12},{8,24},{12,4},{16,0},{20,28},{24,8},{28,20},{1,17},{... | collective-permute-start | bytes 786440 | tf_op jit(solution)/shard_map/ppermute | solution.py:395
  43.7 2.2 %collective-permute-done.11.refs_7_ = bf16[128,1024]{1,0:T(8,128)(2,1)S(1)} collective-permute-done((bf16[128,1024]{1,0:T(8,128)(2,1)S(1)}, bf16[128,1024]{1,0:T(8,128)(2,1)S(1)}, u32[]{:S(2)}, u32[]{:S(2)}) %collective-permute-start.11) | collective-permute-done | bytes 262176 | tf_op jit(solution)/shard_map/ppermute | solution.py:395
  45.9 3.4 %step_1024_0.1 = (f32[512,2048]{1,0:T(8,128)S(1)}, bf16[512,1024]{1,0:T(8,128)(2,1)S(1)}, bf16[1024,2048]{1,0:T(8,128)(2,1)S(1)}, f32[8,128]{1,0:T(8,128)S(1)}) custom-call(f32[8,128]{1,0:T(8,128)S(1)} %get-tuple-element.41.refs_0_.rest_1_, bf16[128,1024]{1,0:T(8,128)(2,1)S(1)} %collective-permute-done.8.refs_1_.refs_5_, ...), custom_call_target="tpu_custom_call", output_to_operand_aliasing={{0}: (9, {})} | custom-call | flops 2147483648 | tf_op jit(solution)/shard_map/step_1024_0/pallas_call | solution.py:303
  50.0 2.7 %step_1024_1.1 = (f32[512,2048]{1,0:T(8,128)S(1)}, f32[8,128]{1,0:T(8,128)S(1)}) custom-call(f32[8,128]{1,0:T(8,128)S(1)} %get-tuple-element.46.refs_0_.after, bf16[512,1024]{1,0:T(8,128)(2,1)S(1)} %get-tuple-element.47.refs_1_, bf16[1024,2048]{1,0:T(8,128)(2,1)S(1)} %get-tuple-element.48.refs_2_, ...), custom_call_target="tpu_custom_call", output_to_operand_aliasing={{0}: (3, {})} | custom-call | flops 2147483648 | tf_op jit(solution)/shard_map/step_1024_1/pallas_call | solution.py:303
  52.7 3.0 %collective-permute-done.16.refs_10_ = bf16[128,1024]{1,0:T(8,128)(2,1)S(1)} collective-permute-done((bf16[128,1024]{1,0:T(8,128)(2,1)S(1)}, bf16[128,1024]{1,0:T(8,128)(2,1)S(1)}, u32[]{:S(2)}, u32[]{:S(2)}) %collective-permute-start.16) | collective-permute-done | bytes 262176 | tf_op jit(solution)/shard_map/ppermute | solution.py:395
  55.7 5.6 %step_2048_0.1 = (f32[256,2048]{1,0:T(8,128)S(1)}, bf16[256,2048]{1,0:T(8,128)(2,1)S(1)}, bf16[512,2048]{1,0:T(8,128)(2,1)S(1)}, bf16[2048,2048]{1,0:T(8,128)(2,1)S(1)}, f32[8,128]{1,0:T(8,128)S(1)}) custom-call(f32[8,128]{1,0:T(8,128)S(1)} %get-tuple-element.50.refs_0_, bf16[4096,4096]{1,0:T(8,128)(2,1)} %refs_1_.1, s32[16]{0:T(128)S(1)} %copy-done, ...), custom_call_target="tpu_custom_call" | custom-call | flops 4294967296 | tf_op jit(solution)/shard_map/step_2048_0/pallas_call | solution.py:303
  61.4 5.1 %step_2048_1.1 = (f32[256,2048]{1,0:T(8,128)S(1)}, bf16[256,2048]{1,0:T(8,128)(2,1)S(1)}, f32[8,128]{1,0:T(8,128)}) custom-call(f32[8,128]{1,0:T(8,128)S(1)} %get-tuple-element.53.refs_0_, bf16[512,2048]{1,0:T(8,128)(2,1)S(1)} %get-tuple-element.54.refs_1_, bf16[2048,2048]{1,0:T(8,128)(2,1)S(1)} %get-tuple-element.55.refs_2_, ...), custom_call_target="tpu_custom_call" | custom-call | flops 4294967296 | tf_op jit(solution)/shard_map/step_2048_1/pallas_call | solution.py:303
  67.0 1.1 %total_0.1.refs_2_ = bf16[256,4096]{1,0:T(8,128)(2,1)} custom-call(f32[256,2048]{1,0:T(8,128)S(1)} %get-tuple-element.59.refs_0_, bf16[256,2048]{1,0:T(8,128)(2,1)S(1)} %collective-permute-done.18.refs_1_), custom_call_target="tpu_custom_call" | custom-call | flops 524288 | bytes 1048576 | tf_op jit(solution)/shard_map/total_0/pallas_call | solution.py:346
  68.1 1.2 %collective-permute-done.17.refs_1_ = bf16[256,2048]{1,0:T(8,128)(2,1)S(1)} collective-permute-done((bf16[256,2048]{1,0:T(8,128)(2,1)S(1)}, bf16[256,2048]{1,0:T(8,128)(2,1)S(1)}, u32[]{:S(2)}, u32[]{:S(2)}) %collective-permute-start.17) | collective-permute-done | bytes 1048608 | tf_op jit(solution)/shard_map/ppermute | solution.py:456
  69.3 1.1 %total_2048.1 = bf16[256,4096]{1,0:T(8,128)(2,1)} custom-call(f32[256,2048]{1,0:T(8,128)S(1)} %get-tuple-element.57.refs_0_, bf16[256,2048]{1,0:T(8,128)(2,1)S(1)} %collective-permute-done.17.refs_1_, bf16[256,4096]{1,0:T(8,128)(2,1)} %total_0.1.refs_2_), custom_call_target="tpu_custom_call", output_to_operand_aliasing={{}: (2, {})} | custom-call | flops 524288 | bytes 1048576 | tf_op jit(solution)/shard_map/total_2048/pallas_call | solution.py:346
  (32 shorter events, 7.7 us)
Async XLA Ops:
  0.0 11.5 %collective-permute-start = (bf16[128,512]{1,0:T(8,128)(2,1)}, bf16[128,512]{1,0:T(8,128)(2,1)S(1)}, u32[]{:S(2)}, u32[]{:S(2)}) collective-permute-start(bf16[128,512]{1,0:T(8,128)(2,1)} %v_hbm.1), channel_id=1, source_target_pairs={{0,16},{8,24},{1,17},{9,25},{2,18},{10,26},{3,19},{11,27},{4,20},{... | collective-permute-start | bytes 393224 | tf_op jit(solution)/shard_map/ppermute | solution.py:407
  4.9 10.0 %collective-permute-start.1 = (bf16[128,512]{1,0:T(8,128)(2,1)}, bf16[128,512]{1,0:T(8,128)(2,1)S(1)}, u32[]{:S(2)}, u32[]{:S(2)}) collective-permute-start(bf16[128,512]{1,0:T(8,128)(2,1)} %k_hbm.1), channel_id=1, source_target_pairs={{0,8},{8,16},{16,24},{1,9},{9,17},{17,25},{2,10},{10,18},{18,26},{... | collective-permute-start | bytes 393224 | tf_op jit(solution)/shard_map/ppermute | solution.py:409
  8.3 6.6 %collective-permute-start.2 = (bf16[128,512]{1,0:T(8,128)(2,1)}, bf16[128,512]{1,0:T(8,128)(2,1)S(1)}, u32[]{:S(2)}, u32[]{:S(2)}) collective-permute-start(bf16[128,512]{1,0:T(8,128)(2,1)} %k_hbm.1), channel_id=1, source_target_pairs={{0,16},{8,24},{1,17},{9,25},{2,18},{10,26},{3,19},{11,27},{4,20},{... | collective-permute-start | bytes 393224 | tf_op jit(solution)/shard_map/ppermute | solution.py:408
  9.6 5.4 %collective-permute-start.3 = (bf16[128,512]{1,0:T(8,128)(2,1)}, bf16[128,512]{1,0:T(8,128)(2,1)S(1)}, u32[]{:S(2)}, u32[]{:S(2)}) collective-permute-start(bf16[128,512]{1,0:T(8,128)(2,1)} %v_hbm.1), channel_id=1, source_target_pairs={{0,8},{16,24},{1,9},{17,25},{2,10},{18,26},{3,11},{19,27},{4,12},{... | collective-permute-start | bytes 393224 | tf_op jit(solution)/shard_map/ppermute | solution.py:410
  11.5 3.4 %collective-permute-start.4 = (bf16[128,512]{1,0:T(8,128)(2,1)S(1)}, bf16[128,512]{1,0:T(8,128)(2,1)S(1)}, u32[]{:S(2)}, u32[]{:S(2)}) collective-permute-start(bf16[128,512]{1,0:T(8,128)(2,1)S(1)} %collective-permute-done.after.v2), channel_id=1, source_target_pairs={{24,16},{25,17},{26,18},{27,19},{28,20},{29,21},{30,22},{31,23}} | collective-permute-start | bytes 393224 | tf_op jit(solution)/shard_map/ppermute | solution.py:411
  15.7 8.6 %collective-permute-start.5 = (bf16[128,1024]{1,0:T(8,128)(2,1)S(1)}, bf16[128,1024]{1,0:T(8,128)(2,1)S(1)}, u32[]{:S(2)}, u32[]{:S(2)}) collective-permute-start(bf16[128,1024]{1,0:T(8,128)(2,1)S(1)} %attend_0.1.refs_1_.after), channel_id=1, source_target_pairs={{0,8},{4,20},{8,0},{12,28},{16,24},{20,4},{24,16},{28,12},{1,9},{5... | collective-permute-start | bytes 786440 | tf_op jit(solution)/shard_map/ppermute | solution.py:390
  20.9 10.9 %collective-permute-start.6 = (bf16[128,1024]{1,0:T(8,128)(2,1)S(1)}, bf16[128,1024]{1,0:T(8,128)(2,1)S(1)}, u32[]{:S(2)}, u32[]{:S(2)}) collective-permute-start(bf16[128,1024]{1,0:T(8,128)(2,1)S(1)} %attend_0.1.refs_1_.after), channel_id=1, source_target_pairs={{0,16},{4,12},{8,24},{12,4},{16,0},{20,28},{24,8},{28,20},{1,17},{... | collective-permute-start | bytes 786440 | tf_op jit(solution)/shard_map/ppermute | solution.py:391
  22.2 10.9 %copy-start = (s32[16]{0:T(128)S(1)}, s32[16]{0:T(128)}, u32[]{:S(2)}) copy-start(s32[16]{0:T(128)} %refs_2_.3) | copy-start | bytes 196
  22.2 9.9 %collective-permute-start.9 = (bf16[128,1024]{1,0:T(8,128)(2,1)S(1)}, bf16[128,1024]{1,0:T(8,128)(2,1)S(1)}, u32[]{:S(2)}, u32[]{:S(2)}) collective-permute-start(bf16[128,1024]{1,0:T(8,128)(2,1)S(1)} %attend_1.1.after.refs_4_), channel_id=1, source_target_pairs={{0,8},{4,20},{8,0},{12,28},{16,24},{20,4},{24,16},{28,12},{1,9},{5... | collective-permute-start | bytes 786440 | tf_op jit(solution)/shard_map/ppermute | solution.py:390
  24.3 8.8 %collective-permute-start.7 = (bf16[128,1024]{1,0:T(8,128)(2,1)S(1)}, bf16[128,1024]{1,0:T(8,128)(2,1)S(1)}, u32[]{:S(2)}, u32[]{:S(2)}) collective-permute-start(bf16[128,1024]{1,0:T(8,128)(2,1)S(1)} %collective-permute-done.5.refs_2_.rest_1_), channel_id=1, source_target_pairs={{0,16},{4,12},{8,24},{12,4},{16,0},{20,28},{24,8},{28,20},{1,17},{... | collective-permute-start | bytes 786440 | tf_op jit(solution)/shard_map/ppermute | solution.py:395
  29.0 12.6 %collective-permute-start.10 = (bf16[128,1024]{1,0:T(8,128)(2,1)S(1)}, bf16[128,1024]{1,0:T(8,128)(2,1)S(1)}, u32[]{:S(2)}, u32[]{:S(2)}) collective-permute-start(bf16[128,1024]{1,0:T(8,128)(2,1)S(1)} %attend_1.1.after.refs_4_), channel_id=1, source_target_pairs={{0,16},{4,12},{8,24},{12,4},{16,0},{20,28},{24,8},{28,20},{1,17},{... | collective-permute-start | bytes 786440 | tf_op jit(solution)/shard_map/ppermute | solution.py:391
  30.5 13.2 %collective-permute-start.8 = (bf16[128,1024]{1,0:T(8,128)(2,1)S(1)}, bf16[128,1024]{1,0:T(8,128)(2,1)S(1)}, u32[]{:S(2)}, u32[]{:S(2)}) collective-permute-start(bf16[128,1024]{1,0:T(8,128)(2,1)S(1)} %attend_2.1.rest_0_.refs_3_), channel_id=1, source_target_pairs={{0,16},{4,12},{8,24},{12,4},{16,0},{20,28},{24,8},{28,20},{1,17},{... | collective-permute-start | bytes 786440 | tf_op jit(solution)/shard_map/ppermute | solution.py:391
  31.9 10.3 %collective-permute-start.12 = (bf16[128,1024]{1,0:T(8,128)(2,1)S(1)}, bf16[128,1024]{1,0:T(8,128)(2,1)S(1)}, u32[]{:S(2)}, u32[]{:S(2)}) collective-permute-start(bf16[128,1024]{1,0:T(8,128)(2,1)S(1)} %attend_2.1.rest_0_.refs_3_), channel_id=1, source_target_pairs={{0,8},{4,20},{8,0},{12,28},{16,24},{20,4},{24,16},{28,12},{1,9},{5... | collective-permute-start | bytes 786440 | tf_op jit(solution)/shard_map/ppermute | solution.py:390
  32.1 13.8 %collective-permute-start.11 = (bf16[128,1024]{1,0:T(8,128)(2,1)S(1)}, bf16[128,1024]{1,0:T(8,128)(2,1)S(1)}, u32[]{:S(2)}, u32[]{:S(2)}) collective-permute-start(bf16[128,1024]{1,0:T(8,128)(2,1)S(1)} %collective-permute-done.9.refs_5_), channel_id=1, source_target_pairs={{0,16},{4,12},{8,24},{12,4},{16,0},{20,28},{24,8},{28,20},{1,17},{... | collective-permute-start | bytes 786440 | tf_op jit(solution)/shard_map/ppermute | solution.py:395
  39.2 10.1 %collective-permute-start.14 = (bf16[128,1024]{1,0:T(8,128)(2,1)S(1)}, bf16[128,1024]{1,0:T(8,128)(2,1)S(1)}, u32[]{:S(2)}, u32[]{:S(2)}) collective-permute-start(bf16[128,1024]{1,0:T(8,128)(2,1)S(1)} %attend_3.1.refs_7_), channel_id=1, source_target_pairs={{0,8},{4,20},{8,0},{12,28},{16,24},{20,4},{24,16},{28,12},{1,9},{5... | collective-permute-start | bytes 786440 | tf_op jit(solution)/shard_map/ppermute | solution.py:390
  41.7 11.1 %collective-permute-start.15 = (bf16[128,1024]{1,0:T(8,128)(2,1)S(1)}, bf16[128,1024]{1,0:T(8,128)(2,1)S(1)}, u32[]{:S(2)}, u32[]{:S(2)}) collective-permute-start(bf16[128,1024]{1,0:T(8,128)(2,1)S(1)} %attend_3.1.refs_7_), channel_id=1, source_target_pairs={{0,16},{4,12},{8,24},{12,4},{16,0},{20,28},{24,8},{28,20},{1,17},{... | collective-permute-start | bytes 786440 | tf_op jit(solution)/shard_map/ppermute | solution.py:391
  42.2 10.6 %collective-permute-start.13 = (bf16[128,1024]{1,0:T(8,128)(2,1)S(1)}, bf16[128,1024]{1,0:T(8,128)(2,1)S(1)}, u32[]{:S(2)}, u32[]{:S(2)}) collective-permute-start(bf16[128,1024]{1,0:T(8,128)(2,1)S(1)} %collective-permute-done.12.refs_4_), channel_id=1, source_target_pairs={{0,16},{4,12},{8,24},{12,4},{16,0},{20,28},{24,8},{28,20},{1,17},{... | collective-permute-start | bytes 786440 | tf_op jit(solution)/shard_map/ppermute | solution.py:395
  49.3 6.4 %collective-permute-start.16 = (bf16[128,1024]{1,0:T(8,128)(2,1)S(1)}, bf16[128,1024]{1,0:T(8,128)(2,1)S(1)}, u32[]{:S(2)}, u32[]{:S(2)}) collective-permute-start(bf16[128,1024]{1,0:T(8,128)(2,1)S(1)} %gate.1.refs_8_), channel_id=1, source_target_pairs={{0,16},{4,12},{8,24},{12,4},{16,0},{20,28},{24,8},{28,20},{1,17},{... | collective-permute-start | bytes 786440 | tf_op jit(solution)/shard_map/ppermute | solution.py:395
  61.4 5.6 %collective-permute-start.18 = (bf16[256,2048]{1,0:T(8,128)(2,1)S(1)}, bf16[256,2048]{1,0:T(8,128)(2,1)S(1)}, u32[]{:S(2)}, u32[]{:S(2)}) collective-permute-start(bf16[256,2048]{1,0:T(8,128)(2,1)S(1)} %get-tuple-element.60), channel_id=1, source_target_pairs={{0,4},{4,0},{1,5},{5,1},{2,6},{6,2},{3,7},{7,3},{8,12},{12,8},{9,1... | collective-permute-start | bytes 3145736 | tf_op jit(solution)/shard_map/ppermute | solution.py:456
  66.5 2.8 %collective-permute-start.17 = (bf16[256,2048]{1,0:T(8,128)(2,1)S(1)}, bf16[256,2048]{1,0:T(8,128)(2,1)S(1)}, u32[]{:S(2)}, u32[]{:S(2)}) collective-permute-start(bf16[256,2048]{1,0:T(8,128)(2,1)S(1)} %get-tuple-element.58), channel_id=1, source_target_pairs={{0,4},{4,0},{1,5},{5,1},{2,6},{6,2},{3,7},{7,3},{8,12},{12,8},{9,1... | collective-permute-start | bytes 3145736 | tf_op jit(solution)/shard_map/ppermute | solution.py:456

commit v11 on v7

--- a/solution.py
+++ b/solution.py
@@ -70,7 +70,7 @@
 SMEM = pl.BlockSpec(memory_space=pltpu.SMEM)
 VMEM = pl.BlockSpec(memory_space=pltpu.VMEM)
 HBM = pl.BlockSpec(memory_space=pl.ANY)
-TILE = 512
+TILE = 256
 
 
 def in_hbm(x):

time: 68.3 us -> 68.2 us (level)
  no operation moved by 1% of the time
where the time goes in v11:
time: 68.2 us; the launch traced here: 68 us
  Pallas kernels  38.4 us (56%)
  starting transfers between devices  25.4 us (37%)
  waiting for transfers between devices  3.8 us (6%)
    pallas_call x8, Pallas kernels, step(): pl.pallas_call(functools.partial(step_kernel, index, last, column, first,...  23.8 us
    pallas_call x2, Pallas kernels, load_blocks(): pl.pallas_call(functools.partial(load_kernel, indexes), out_shape=[jax.Sh...  6.97 us
    ppermute x4, starting transfers between devices, gather_rows(): near = lax.ppermute(own, ('ctx', 'tp'), route(True))  6 us
    ppermute x1, starting transfers between devices, local(): value_two = lax.ppermute(value_rows, 'ctx', two)  4.87 us
    ppermute x4, starting transfers between devices, gather_rows(): side = lax.ppermute(own, ('ctx', 'tp'), route(False))  3.53 us
    ppermute x1, starting transfers between devices, local(): key_near = lax.ppermute(key_rows, 'ctx', [(0, 1), (1, 2), (2, 3)])  3.4 us
    ppermute x4, starting transfers between devices, forward(): return (own, first, side, lax.ppermute(first, ('ctx', 'tp'), route(False)))  3.12 us
    pallas_call x4, Pallas kernels, attend(): pl.pallas_call(functools.partial(attend_kernel, groups), out_shape=jax.Sh...  2.76 us
  transfers between devices with their start and end apart: 19, of which 3 were waited for; matrix products, arithmetic and copies ran while one was open for 0% of the time, Pallas kernels for 49%

profile of v11, /device:TPU:0, one launch (start us, length us, event | category | flops | bytes accessed | tf_op | source)
XLA Modules:
  0.0 68.0 jit_solution(4469381941847316914)
XLA Ops:
  0.0 4.9 %collective-permute-start = (bf16[128,512]{1,0:T(8,128)(2,1)}, bf16[128,512]{1,0:T(8,128)(2,1)S(1)}, u32[]{:S(2)}, u32[]{:S(2)}) collective-permute-start(bf16[128,512]{1,0:T(8,128)(2,1)} %v_hbm.1), channel_id=1, source_target_pairs={{0,16},{8,24},{1,17},{9,25},{2,18},{10,26},{3,19},{11,27},{4,20},{... | collective-permute-start | bytes 393224 | tf_op jit(solution)/shard_map/ppermute | solution.py:409
  4.9 3.4 %collective-permute-start.2 = (bf16[128,512]{1,0:T(8,128)(2,1)}, bf16[128,512]{1,0:T(8,128)(2,1)S(1)}, u32[]{:S(2)}, u32[]{:S(2)}) collective-permute-start(bf16[128,512]{1,0:T(8,128)(2,1)} %k_hbm.1), channel_id=1, source_target_pairs={{0,8},{8,16},{16,24},{1,9},{9,17},{17,25},{2,10},{10,18},{18,26},{... | collective-permute-start | bytes 393224 | tf_op jit(solution)/shard_map/ppermute | solution.py:411
  8.3 1.3 %collective-permute-start.1 = (bf16[128,512]{1,0:T(8,128)(2,1)}, bf16[128,512]{1,0:T(8,128)(2,1)S(1)}, u32[]{:S(2)}, u32[]{:S(2)}) collective-permute-start(bf16[128,512]{1,0:T(8,128)(2,1)} %k_hbm.1), channel_id=1, source_target_pairs={{0,16},{8,24},{1,17},{9,25},{2,18},{10,26},{3,19},{11,27},{4,20},{... | collective-permute-start | bytes 393224 | tf_op jit(solution)/shard_map/ppermute | solution.py:410
  9.6 1.9 %collective-permute-start.3 = (bf16[128,512]{1,0:T(8,128)(2,1)}, bf16[128,512]{1,0:T(8,128)(2,1)S(1)}, u32[]{:S(2)}, u32[]{:S(2)}) collective-permute-start(bf16[128,512]{1,0:T(8,128)(2,1)} %v_hbm.1), channel_id=1, source_target_pairs={{0,8},{16,24},{1,9},{17,25},{2,10},{18,26},{3,11},{19,27},{4,12},{... | collective-permute-start | bytes 393224 | tf_op jit(solution)/shard_map/ppermute | solution.py:412
  12.2 2.7 %prepare.1 = (bf16[128,512]{1,0:T(8,128)(2,1)S(1)}, bf16[128,512]{1,0:T(8,128)(2,1)S(1)}, bf16[128,4096]{1,0:T(8,128)(2,1)S(1)}, f32[128,384]{1,0:T(8,128)S(1)}, bf16[1024,2048]{1,0:T(8,128)(2,1)S(1)}) custom-call(s32[8]{0:T(128)} %docs_hbm.1, bf16[128,512]{1,0:T(8,128)(2,1)} %k_hbm.1, bf16[128,512]{1,0:T(8,128)(2,1)} %v_hbm.1, bf16[128,4096]{1,0:T(8,128)(2,1)} %q_hbm.1, ...), custom_call_target="tpu_custom_call" | custom-call | bytes 4194304 | tf_op jit(solution)/shard_map/prepare/pallas_call | solution.py:123
  15.7 1.8 %collective-permute-start.5 = (bf16[128,1024]{1,0:T(8,128)(2,1)S(1)}, bf16[128,1024]{1,0:T(8,128)(2,1)S(1)}, u32[]{:S(2)}, u32[]{:S(2)}) collective-permute-start(bf16[128,1024]{1,0:T(8,128)(2,1)S(1)} %attend_0.1.refs_1_.after), channel_id=1, source_target_pairs={{0,8},{4,20},{8,0},{12,28},{16,24},{20,4},{24,16},{28,12},{1,9},{5... | collective-permute-start | bytes 786440 | tf_op jit(solution)/shard_map/ppermute | solution.py:392
  18.0 3.5 %load_1.1 = (bf16[1024,2048]{1,0:T(8,128)(2,1)S(1)}, bf16[1024,2048]{1,0:T(8,128)(2,1)S(1)}, f32[8,128]{1,0:T(8,128)S(1)}) custom-call(bf16[128,1024]{1,0:T(8,128)(2,1)S(1)} %attend_0.1.refs_1_.after, bf16[4096,4096]{1,0:T(8,128)(2,1)} %refs_1_.5), custom_call_target="tpu_custom_call" | custom-call | bytes 16777216 | tf_op jit(solution)/shard_map/load_1/pallas_call | solution.py:163
  22.2 2.0 %collective-permute-start.8 = (bf16[128,1024]{1,0:T(8,128)(2,1)S(1)}, bf16[128,1024]{1,0:T(8,128)(2,1)S(1)}, u32[]{:S(2)}, u32[]{:S(2)}) collective-permute-start(bf16[128,1024]{1,0:T(8,128)(2,1)S(1)} %attend_1.1.refs_3_.after), channel_id=1, source_target_pairs={{0,8},{4,20},{8,0},{12,28},{16,24},{20,4},{24,16},{28,12},{1,9},{5... | collective-permute-start | bytes 786440 | tf_op jit(solution)/shard_map/ppermute | solution.py:392
  25.0 2.0 %collective-permute-start.9 = (bf16[128,1024]{1,0:T(8,128)(2,1)S(1)}, bf16[128,1024]{1,0:T(8,128)(2,1)S(1)}, u32[]{:S(2)}, u32[]{:S(2)}) collective-permute-start(bf16[128,1024]{1,0:T(8,128)(2,1)S(1)} %attend_1.1.refs_3_.after), channel_id=1, source_target_pairs={{0,16},{4,12},{8,24},{12,4},{16,0},{20,28},{24,8},{28,20},{1,17},{... | collective-permute-start | bytes 786440 | tf_op jit(solution)/shard_map/ppermute | solution.py:393
  26.9 3.5 %load_4.1 = (bf16[1024,2048]{1,0:T(8,128)(2,1)S(1)}, bf16[1024,2048]{1,0:T(8,128)(2,1)S(1)}, f32[8,128]{1,0:T(8,128)S(1)}) custom-call(bf16[128,1024]{1,0:T(8,128)(2,1)S(1)} %attend_1.1.refs_3_.after, bf16[4096,4096]{1,0:T(8,128)(2,1)} %refs_1_.5), custom_call_target="tpu_custom_call" | custom-call | bytes 16777216 | tf_op jit(solution)/shard_map/load_4/pallas_call | solution.py:163
  32.1 1.2 %collective-permute-start.10 = (bf16[128,1024]{1,0:T(8,128)(2,1)S(1)}, bf16[128,1024]{1,0:T(8,128)(2,1)S(1)}, u32[]{:S(2)}, u32[]{:S(2)}) collective-permute-start(bf16[128,1024]{1,0:T(8,128)(2,1)S(1)} %collective-permute-done.8.refs_4_), channel_id=1, source_target_pairs={{0,16},{4,12},{8,24},{12,4},{16,0},{20,28},{24,8},{28,20},{1,17},{... | collective-permute-start | bytes 786440 | tf_op jit(solution)/shard_map/ppermute | solution.py:397
  33.3 3.1 %step_0_0.1 = (f32[512,2048]{1,0:T(8,128)S(1)}, bf16[512,1024]{1,0:T(8,128)(2,1)S(1)}, f32[8,128]{1,0:T(8,128)S(1)}) custom-call(s32[16]{0:T(128)S(1)} %copy-done, bf16[128,1024]{1,0:T(8,128)(2,1)S(1)} %attend_0.1.refs_1_.after, bf16[128,1024]{1,0:T(8,128)(2,1)S(1)} %collective-permute-done.5.refs_2_.rest_1_, ...), custom_call_target="tpu_custom_call" | custom-call | flops 2147483648 | tf_op jit(solution)/shard_map/step_0_0/pallas_call | solution.py:303
  36.4 2.4 %step_1_0.1 = (f32[512,2048]{1,0:T(8,128)S(1)}, f32[8,128]{1,0:T(8,128)S(1)}) custom-call(f32[8,128]{1,0:T(8,128)S(1)} %get-tuple-element.45.refs_0_, bf16[512,1024]{1,0:T(8,128)(2,1)S(1)} %get-tuple-element.46.refs_1_, bf16[1024,2048]{1,0:T(8,128)(2,1)S(1)} %get-tuple-element.47.refs_2_), custom_call_target="tpu_custom_call" | custom-call | flops 2147483648 | tf_op jit(solution)/shard_map/step_1_0/pallas_call | solution.py:303
  40.3 1.4 %collective-permute-start.14 = (bf16[128,1024]{1,0:T(8,128)(2,1)S(1)}, bf16[128,1024]{1,0:T(8,128)(2,1)S(1)}, u32[]{:S(2)}, u32[]{:S(2)}) collective-permute-start(bf16[128,1024]{1,0:T(8,128)(2,1)S(1)} %attend_3.1.refs_3_), channel_id=1, source_target_pairs={{0,8},{4,20},{8,0},{12,28},{16,24},{20,4},{24,16},{28,12},{1,9},{5... | collective-permute-start | bytes 786440 | tf_op jit(solution)/shard_map/ppermute | solution.py:392
  41.7 1.8 %collective-permute-start.13 = (bf16[128,1024]{1,0:T(8,128)(2,1)S(1)}, bf16[128,1024]{1,0:T(8,128)(2,1)S(1)}, u32[]{:S(2)}, u32[]{:S(2)}) collective-permute-start(bf16[128,1024]{1,0:T(8,128)(2,1)S(1)} %collective-permute-done.11.refs_4_), channel_id=1, source_target_pairs={{0,16},{4,12},{8,24},{12,4},{16,0},{20,28},{24,8},{28,20},{1,17},{... | collective-permute-start | bytes 786440 | tf_op jit(solution)/shard_map/ppermute | solution.py:397
  43.5 1.8 %collective-permute-done.10.refs_6_ = bf16[128,1024]{1,0:T(8,128)(2,1)S(1)} collective-permute-done((bf16[128,1024]{1,0:T(8,128)(2,1)S(1)}, bf16[128,1024]{1,0:T(8,128)(2,1)S(1)}, u32[]{:S(2)}, u32[]{:S(2)}) %collective-permute-start.10) | collective-permute-done | bytes 262176 | tf_op jit(solution)/shard_map/ppermute | solution.py:397
  45.3 3.4 %step_2_0.1 = (f32[512,2048]{1,0:T(8,128)S(1)}, bf16[512,1024]{1,0:T(8,128)(2,1)S(1)}, bf16[1024,2048]{1,0:T(8,128)(2,1)S(1)}, f32[8,128]{1,0:T(8,128)S(1)}) custom-call(f32[8,128]{1,0:T(8,128)S(1)} %get-tuple-element.48.refs_0_.rest_1_, bf16[4096,4096]{1,0:T(8,128)(2,1)} %refs_1_.5, s32[16]{0:T(128)S(1)} %copy-done, ...), custom_call_target="tpu_custom_call", output_to_operand_aliasing={{0}: (8, {})} | custom-call | flops 2147483648 | tf_op jit(solution)/shard_map/step_2_0/pallas_call | solution.py:303
  48.7 2.7 %step_3_0.1 = (f32[512,2048]{1,0:T(8,128)S(1)}, f32[8,128]{1,0:T(8,128)S(1)}) custom-call(f32[8,128]{1,0:T(8,128)S(1)} %get-tuple-element.52.refs_0_, bf16[512,1024]{1,0:T(8,128)(2,1)S(1)} %get-tuple-element.53.refs_1_, bf16[1024,2048]{1,0:T(8,128)(2,1)S(1)} %get-tuple-element.54.refs_2_, ...), custom_call_target="tpu_custom_call", output_to_operand_aliasing={{0}: (3, {})} | custom-call | flops 2147483648 | tf_op jit(solution)/shard_map/step_3_0/pallas_call | solution.py:303
  51.6 3.4 %step_4_0.1 = (f32[512,2048]{1,0:T(8,128)S(1)}, bf16[512,1024]{1,0:T(8,128)(2,1)S(1)}, bf16[1024,2048]{1,0:T(8,128)(2,1)S(1)}, f32[8,128]{1,0:T(8,128)S(1)}) custom-call(f32[8,128]{1,0:T(8,128)S(1)} %get-tuple-element.56.refs_0_, bf16[4096,4096]{1,0:T(8,128)(2,1)} %refs_1_.5, s32[16]{0:T(128)S(1)} %copy-done, ...), custom_call_target="tpu_custom_call", output_to_operand_aliasing={{0}: (8, {})} | custom-call | flops 2147483648 | tf_op jit(solution)/shard_map/step_4_0/pallas_call | solution.py:303
  55.0 2.9 %step_5_0.1 = (f32[512,2048]{1,0:T(8,128)S(1)}, f32[8,128]{1,0:T(8,128)S(1)}) custom-call(f32[8,128]{1,0:T(8,128)S(1)} %get-tuple-element.60.refs_0_, bf16[512,1024]{1,0:T(8,128)(2,1)S(1)} %get-tuple-element.61.refs_1_, bf16[1024,2048]{1,0:T(8,128)(2,1)S(1)} %get-tuple-element.62.refs_2_, ...), custom_call_target="tpu_custom_call", output_to_operand_aliasing={{0}: (3, {})} | custom-call | flops 2147483648 | tf_op jit(solution)/shard_map/step_5_0/pallas_call | solution.py:303
  57.9 3.1 %step_6_0.1 = (f32[256,2048]{1,0:T(8,128)S(1)}, bf16[256,2048]{1,0:T(8,128)(2,1)S(1)}, bf16[512,1024]{1,0:T(8,128)(2,1)S(1)}, bf16[1024,2048]{1,0:T(8,128)(2,1)S(1)}, f32[8,128]{1,0:T(8,128)S(1)}) custom-call(f32[8,128]{1,0:T(8,128)S(1)} %get-tuple-element.64.refs_0_, bf16[4096,4096]{1,0:T(8,128)(2,1)} %refs_1_.5, s32[16]{0:T(128)S(1)} %copy-done, ...), custom_call_target="tpu_custom_call" | custom-call | flops 2147483648 | tf_op jit(solution)/shard_map/step_6_0/pallas_call | solution.py:303
  61.1 2.9 %step_7_0.1 = (f32[256,2048]{1,0:T(8,128)S(1)}, bf16[256,2048]{1,0:T(8,128)(2,1)S(1)}, f32[8,128]{1,0:T(8,128)}) custom-call(f32[8,128]{1,0:T(8,128)S(1)} %get-tuple-element.67.refs_0_, bf16[512,1024]{1,0:T(8,128)(2,1)S(1)} %get-tuple-element.68.refs_1_, bf16[1024,2048]{1,0:T(8,128)(2,1)S(1)} %get-tuple-element.69.refs_2_, ...), custom_call_target="tpu_custom_call" | custom-call | flops 2147483648 | tf_op jit(solution)/shard_map/step_7_0/pallas_call | solution.py:303
  64.5 1.1 %total_0.1.refs_2_ = bf16[256,4096]{1,0:T(8,128)(2,1)} custom-call(f32[256,2048]{1,0:T(8,128)S(1)} %get-tuple-element.73.refs_0_, bf16[256,2048]{1,0:T(8,128)(2,1)S(1)} %collective-permute-done.18.refs_1_), custom_call_target="tpu_custom_call" | custom-call | flops 524288 | bytes 1048576 | tf_op jit(solution)/shard_map/total_0/pallas_call | solution.py:348
  65.6 1.2 %collective-permute-done.17.refs_1_ = bf16[256,2048]{1,0:T(8,128)(2,1)S(1)} collective-permute-done((bf16[256,2048]{1,0:T(8,128)(2,1)S(1)}, bf16[256,2048]{1,0:T(8,128)(2,1)S(1)}, u32[]{:S(2)}, u32[]{:S(2)}) %collective-permute-start.17) | collective-permute-done | bytes 1048608 | tf_op jit(solution)/shard_map/ppermute | solution.py:459
  (33 shorter events, 8.3 us)
Async XLA Ops:
  0.0 11.5 %collective-permute-start = (bf16[128,512]{1,0:T(8,128)(2,1)}, bf16[128,512]{1,0:T(8,128)(2,1)S(1)}, u32[]{:S(2)}, u32[]{:S(2)}) collective-permute-start(bf16[128,512]{1,0:T(8,128)(2,1)} %v_hbm.1), channel_id=1, source_target_pairs={{0,16},{8,24},{1,17},{9,25},{2,18},{10,26},{3,19},{11,27},{4,20},{... | collective-permute-start | bytes 393224 | tf_op jit(solution)/shard_map/ppermute | solution.py:409
  4.9 10.0 %collective-permute-start.2 = (bf16[128,512]{1,0:T(8,128)(2,1)}, bf16[128,512]{1,0:T(8,128)(2,1)S(1)}, u32[]{:S(2)}, u32[]{:S(2)}) collective-permute-start(bf16[128,512]{1,0:T(8,128)(2,1)} %k_hbm.1), channel_id=1, source_target_pairs={{0,8},{8,16},{16,24},{1,9},{9,17},{17,25},{2,10},{10,18},{18,26},{... | collective-permute-start | bytes 393224 | tf_op jit(solution)/shard_map/ppermute | solution.py:411
  8.3 6.6 %collective-permute-start.1 = (bf16[128,512]{1,0:T(8,128)(2,1)}, bf16[128,512]{1,0:T(8,128)(2,1)S(1)}, u32[]{:S(2)}, u32[]{:S(2)}) collective-permute-start(bf16[128,512]{1,0:T(8,128)(2,1)} %k_hbm.1), channel_id=1, source_target_pairs={{0,16},{8,24},{1,17},{9,25},{2,18},{10,26},{3,19},{11,27},{4,20},{... | collective-permute-start | bytes 393224 | tf_op jit(solution)/shard_map/ppermute | solution.py:410
  9.6 5.4 %collective-permute-start.3 = (bf16[128,512]{1,0:T(8,128)(2,1)}, bf16[128,512]{1,0:T(8,128)(2,1)S(1)}, u32[]{:S(2)}, u32[]{:S(2)}) collective-permute-start(bf16[128,512]{1,0:T(8,128)(2,1)} %v_hbm.1), channel_id=1, source_target_pairs={{0,8},{16,24},{1,9},{17,25},{2,10},{18,26},{3,11},{19,27},{4,12},{... | collective-permute-start | bytes 393224 | tf_op jit(solution)/shard_map/ppermute | solution.py:412
  11.5 3.4 %collective-permute-start.4 = (bf16[128,512]{1,0:T(8,128)(2,1)S(1)}, bf16[128,512]{1,0:T(8,128)(2,1)S(1)}, u32[]{:S(2)}, u32[]{:S(2)}) collective-permute-start(bf16[128,512]{1,0:T(8,128)(2,1)S(1)} %collective-permute-done.after.v2), channel_id=1, source_target_pairs={{24,16},{25,17},{26,18},{27,19},{28,20},{29,21},{30,22},{31,23}} | collective-permute-start | bytes 393224 | tf_op jit(solution)/shard_map/ppermute | solution.py:413
  15.7 9.2 %collective-permute-start.5 = (bf16[128,1024]{1,0:T(8,128)(2,1)S(1)}, bf16[128,1024]{1,0:T(8,128)(2,1)S(1)}, u32[]{:S(2)}, u32[]{:S(2)}) collective-permute-start(bf16[128,1024]{1,0:T(8,128)(2,1)S(1)} %attend_0.1.refs_1_.after), channel_id=1, source_target_pairs={{0,8},{4,20},{8,0},{12,28},{16,24},{20,4},{24,16},{28,12},{1,9},{5... | collective-permute-start | bytes 786440 | tf_op jit(solution)/shard_map/ppermute | solution.py:392
  17.4 13.8 %collective-permute-start.6 = (bf16[128,1024]{1,0:T(8,128)(2,1)S(1)}, bf16[128,1024]{1,0:T(8,128)(2,1)S(1)}, u32[]{:S(2)}, u32[]{:S(2)}) collective-permute-start(bf16[128,1024]{1,0:T(8,128)(2,1)S(1)} %attend_0.1.refs_1_.after), channel_id=1, source_target_pairs={{0,16},{4,12},{8,24},{12,4},{16,0},{20,28},{24,8},{28,20},{1,17},{... | collective-permute-start | bytes 786440 | tf_op jit(solution)/shard_map/ppermute | solution.py:393
  22.2 11.1 %copy-start = (s32[16]{0:T(128)S(1)}, s32[16]{0:T(128)}, u32[]{:S(2)}) copy-start(s32[16]{0:T(128)} %refs_2_.5) | copy-start | bytes 196
  22.2 9.9 %collective-permute-start.8 = (bf16[128,1024]{1,0:T(8,128)(2,1)S(1)}, bf16[128,1024]{1,0:T(8,128)(2,1)S(1)}, u32[]{:S(2)}, u32[]{:S(2)}) collective-permute-start(bf16[128,1024]{1,0:T(8,128)(2,1)S(1)} %attend_1.1.refs_3_.after), channel_id=1, source_target_pairs={{0,8},{4,20},{8,0},{12,28},{16,24},{20,4},{24,16},{28,12},{1,9},{5... | collective-permute-start | bytes 786440 | tf_op jit(solution)/shard_map/ppermute | solution.py:392
  24.9 8.4 %collective-permute-start.7 = (bf16[128,1024]{1,0:T(8,128)(2,1)S(1)}, bf16[128,1024]{1,0:T(8,128)(2,1)S(1)}, u32[]{:S(2)}, u32[]{:S(2)}) collective-permute-start(bf16[128,1024]{1,0:T(8,128)(2,1)S(1)} %collective-permute-done.5.refs_2_.rest_1_), channel_id=1, source_target_pairs={{0,16},{4,12},{8,24},{12,4},{16,0},{20,28},{24,8},{28,20},{1,17},{... | collective-permute-start | bytes 786440 | tf_op jit(solution)/shard_map/ppermute | solution.py:397
  25.0 15.4 %collective-permute-start.9 = (bf16[128,1024]{1,0:T(8,128)(2,1)S(1)}, bf16[128,1024]{1,0:T(8,128)(2,1)S(1)}, u32[]{:S(2)}, u32[]{:S(2)}) collective-permute-start(bf16[128,1024]{1,0:T(8,128)(2,1)S(1)} %attend_1.1.refs_3_.after), channel_id=1, source_target_pairs={{0,16},{4,12},{8,24},{12,4},{16,0},{20,28},{24,8},{28,20},{1,17},{... | collective-permute-start | bytes 786440 | tf_op jit(solution)/shard_map/ppermute | solution.py:393
  31.1 20.4 %collective-permute-start.12 = (bf16[128,1024]{1,0:T(8,128)(2,1)S(1)}, bf16[128,1024]{1,0:T(8,128)(2,1)S(1)}, u32[]{:S(2)}, u32[]{:S(2)}) collective-permute-start(bf16[128,1024]{1,0:T(8,128)(2,1)S(1)} %attend_2.1.refs_3_.rest_0_), channel_id=1, source_target_pairs={{0,16},{4,12},{8,24},{12,4},{16,0},{20,28},{24,8},{28,20},{1,17},{... | collective-permute-start | bytes 786440 | tf_op jit(solution)/shard_map/ppermute | solution.py:393
  31.2 10.4 %collective-permute-start.11 = (bf16[128,1024]{1,0:T(8,128)(2,1)S(1)}, bf16[128,1024]{1,0:T(8,128)(2,1)S(1)}, u32[]{:S(2)}, u32[]{:S(2)}) collective-permute-start(bf16[128,1024]{1,0:T(8,128)(2,1)S(1)} %attend_2.1.refs_3_.rest_0_), channel_id=1, source_target_pairs={{0,8},{4,20},{8,0},{12,28},{16,24},{20,4},{24,16},{28,12},{1,9},{5... | collective-permute-start | bytes 786440 | tf_op jit(solution)/shard_map/ppermute | solution.py:392
  32.1 13.2 %collective-permute-start.10 = (bf16[128,1024]{1,0:T(8,128)(2,1)S(1)}, bf16[128,1024]{1,0:T(8,128)(2,1)S(1)}, u32[]{:S(2)}, u32[]{:S(2)}) collective-permute-start(bf16[128,1024]{1,0:T(8,128)(2,1)S(1)} %collective-permute-done.8.refs_4_), channel_id=1, source_target_pairs={{0,16},{4,12},{8,24},{12,4},{16,0},{20,28},{24,8},{28,20},{1,17},{... | collective-permute-start | bytes 786440 | tf_op jit(solution)/shard_map/ppermute | solution.py:397
  39.4 18.5 %collective-permute-start.15 = (bf16[128,1024]{1,0:T(8,128)(2,1)S(1)}, bf16[128,1024]{1,0:T(8,128)(2,1)S(1)}, u32[]{:S(2)}, u32[]{:S(2)}) collective-permute-start(bf16[128,1024]{1,0:T(8,128)(2,1)S(1)} %attend_3.1.refs_3_), channel_id=1, source_target_pairs={{0,16},{4,12},{8,24},{12,4},{16,0},{20,28},{24,8},{28,20},{1,17},{... | collective-permute-start | bytes 786440 | tf_op jit(solution)/shard_map/ppermute | solution.py:393
  40.3 11.2 %collective-permute-start.14 = (bf16[128,1024]{1,0:T(8,128)(2,1)S(1)}, bf16[128,1024]{1,0:T(8,128)(2,1)S(1)}, u32[]{:S(2)}, u32[]{:S(2)}) collective-permute-start(bf16[128,1024]{1,0:T(8,128)(2,1)S(1)} %attend_3.1.refs_3_), channel_id=1, source_target_pairs={{0,8},{4,20},{8,0},{12,28},{16,24},{20,4},{24,16},{28,12},{1,9},{5... | collective-permute-start | bytes 786440 | tf_op jit(solution)/shard_map/ppermute | solution.py:392
  41.7 9.9 %collective-permute-start.13 = (bf16[128,1024]{1,0:T(8,128)(2,1)S(1)}, bf16[128,1024]{1,0:T(8,128)(2,1)S(1)}, u32[]{:S(2)}, u32[]{:S(2)}) collective-permute-start(bf16[128,1024]{1,0:T(8,128)(2,1)S(1)} %collective-permute-done.11.refs_4_), channel_id=1, source_target_pairs={{0,16},{4,12},{8,24},{12,4},{16,0},{20,28},{24,8},{28,20},{1,17},{... | collective-permute-start | bytes 786440 | tf_op jit(solution)/shard_map/ppermute | solution.py:397
  51.5 6.4 %collective-permute-start.16 = (bf16[128,1024]{1,0:T(8,128)(2,1)S(1)}, bf16[128,1024]{1,0:T(8,128)(2,1)S(1)}, u32[]{:S(2)}, u32[]{:S(2)}) collective-permute-start(bf16[128,1024]{1,0:T(8,128)(2,1)S(1)} %collective-permute-done.14.refs_4_), channel_id=1, source_target_pairs={{0,16},{4,12},{8,24},{12,4},{16,0},{20,28},{24,8},{28,20},{1,17},{... | collective-permute-start | bytes 786440 | tf_op jit(solution)/shard_map/ppermute | solution.py:397
  61.0 3.5 %collective-permute-start.18 = (bf16[256,2048]{1,0:T(8,128)(2,1)S(1)}, bf16[256,2048]{1,0:T(8,128)(2,1)S(1)}, u32[]{:S(2)}, u32[]{:S(2)}) collective-permute-start(bf16[256,2048]{1,0:T(8,128)(2,1)S(1)} %get-tuple-element.74), channel_id=1, source_target_pairs={{0,4},{4,0},{1,5},{5,1},{2,6},{6,2},{3,7},{7,3},{8,12},{12,8},{9,1... | collective-permute-start | bytes 3145736 | tf_op jit(solution)/shard_map/ppermute | solution.py:459
  64.0 2.8 %collective-permute-start.17 = (bf16[256,2048]{1,0:T(8,128)(2,1)S(1)}, bf16[256,2048]{1,0:T(8,128)(2,1)S(1)}, u32[]{:S(2)}, u32[]{:S(2)}) collective-permute-start(bf16[256,2048]{1,0:T(8,128)(2,1)S(1)} %get-tuple-element.72), channel_id=1, source_target_pairs={{0,4},{4,0},{1,5},{5,1},{2,6},{6,2},{3,7},{7,3},{8,12},{12,8},{9,1... | collective-permute-start | bytes 3145736 | tf_op jit(solution)/shard_map/ppermute | solution.py:459
